TPU v7x, 32 devices: a whole 2x2x4 slice. The times are simulated.
32 devices in a mesh: dp: 16 (over z, y, core), tensor: 2 (over x).
Axes of the slice: x: 2, y: 2, z: 4, core: 2. Of those that a mesh axis runs over, the one named last changes fastest.
Arguments:
- target: bfloat16 [32768, 1024], P(('dp', 'tensor')), may hold values from -6 to 6
- memory: bfloat16 [32768, 1024], P(('dp', 'tensor')), may hold values from -6 to 6
- mem_len: int32 [32], P('dp'), may hold values from 512 to 1024, as said below
- grad_out: bfloat16 [32768, 1024], P(('dp', 'tensor')), may hold values from -6 to 6
- self_qkv: bfloat16 [3, 1024, 1024], P(None, None, 'tensor'), may hold values from -0.3125 to 0.3125
- self_out: bfloat16 [1024, 1024], P('tensor'), may hold values from -3 to 3
- cross_query: bfloat16 [1024, 1024], P(None, 'tensor'), may hold values from -0.3125 to 0.3125
- cross_kv: bfloat16 [2, 1024, 1024], P(None, None, 'tensor'), may hold values from -0.3125 to 0.3125
- cross_out: bfloat16 [1024, 1024], P('tensor'), may hold values from -3 to 3
- ffn_up: bfloat16 [1024, 4096], P(None, 'tensor'), may hold values from -0.1875 to 0.1875
- ffn_down: bfloat16 [4096, 1024], P('tensor'), may hold values from -0.75 to 0.75
- ln_gain: float32 [3, 1024], replicated, may hold values from 0.5 to 1.5
- ln_bias: float32 [3, 1024], replicated, may hold values from -3 to 3
Outputs:
- output: bfloat16 [32768, 1024], P(('dp', 'tensor'))
- grad_target: bfloat16 [32768, 1024], P(('dp', 'tensor'))
- grad_memory: bfloat16 [32768, 1024], P(('dp', 'tensor'))
- grad_self_qkv: float32 [3, 1024, 1024], P(None, None, 'tensor')
- grad_self_out: float32 [1024, 1024], P('tensor')
- grad_cross_query: float32 [1024, 1024], P(None, 'tensor')
- grad_cross_kv: float32 [2, 1024, 1024], P(None, None, 'tensor')
- grad_cross_out: float32 [1024, 1024], P('tensor')
- grad_ffn_up: float32 [1024, 4096], P(None, 'tensor')
- grad_ffn_down: float32 [4096, 1024], P('tensor')
- grad_ln_gain: float32 [3, 1024], replicated
- grad_ln_bias: float32 [3, 1024], replicated
Inputs may be any that keep to these rules, and one draw needn't show every extreme that they name: Queries of pair p read memory rows 0 to mem_len[p] - 1 of that pair; some pair reads all 1024 and some pair exactly half.
All inputs are finite; a program needn't handle non-finite values.
Results may differ from a plain program's by a relative error of at most 0.038.
The roundings to bfloat16 on the way count: a program that leaves them out, or rounds other values in their place, can miss the bound.
Values may be sent and summed in bfloat16 or wider, within the bound.
A program may use at most 320 MiB of HBM per device.

v0:
```python
import jax
import jax.numpy as jnp
from jax import lax
from jax.sharding import PartitionSpec as P

HD = 64


alpha_res = 300.0**0.25
norm_eps = 1e-05
mask_fill = -1e30
contract_rows = (((0,), (0,)), ((), ()))
contract_cols = (((1,), (1,)), ((), ()))


def norm_rows(resid, gain_vec, bias_vec):
    average = jnp.mean(resid, axis=-1, keepdims=True)
    centered = resid - average
    variance = jnp.mean(centered * centered, axis=-1, keepdims=True)
    return centered * lax.rsqrt(variance + norm_eps) * gain_vec + bias_vec


def exact_gelu(values_in):
    return jax.nn.gelu(values_in, approximate=False)


def gather_rows(local_rows):
    return lax.all_gather(local_rows, "tensor", axis=0, tiled=True)


def gather_grads(local_rows):
    return lax.all_gather(local_rows, "tensor", axis=0, tiled=True)


def scatter_branch(left_mat, right_mat, row_count):

    def partial_term(offset, num_rows):
        return jnp.dot(left_mat, right_mat, preferred_element_type=jnp.float32)

    return lax.psum_scatter(
        partial_term(jnp.int32(0), row_count * lax.axis_size("tensor")),
        "tensor",
        scatter_dimension=0,
        tiled=True,
    )


def project_context(context, weight_local, row_count):
    return scatter_branch(context, weight_local, row_count)


def scatter_inputs(factor_pairs, row_count):

    def partial_term(offset, num_rows):
        terms = [
            lax.dot_general(grad_mat, weight_mat, contract_cols, preferred_element_type=jnp.float32)
            for grad_mat, weight_mat in factor_pairs
        ]
        return sum(terms)

    return lax.psum_scatter(
        partial_term(jnp.int32(0), row_count * lax.axis_size("tensor")).astype(jnp.bfloat16),
        "tensor",
        scatter_dimension=0,
        tiled=True,
    ).astype(jnp.float32)


def block_view(flat, pair_count, block_rows):
    tok_count, col_count = flat.shape
    seq_len = tok_count // pair_count
    return flat.reshape(pair_count, seq_len // block_rows, block_rows, col_count // HD, HD)


def pair_view(flat, pair_count):
    tok_count, col_count = flat.shape
    return flat.reshape(pair_count, tok_count // pair_count, col_count // HD, HD)


def block_scores(query_blk, key_pair, start_row, key_len, causal):
    block_rows = query_blk.shape[0]
    seq_len = key_pair.shape[0]
    products = jnp.einsum(
        "qhd,khd->hqk", query_blk, key_pair, preferred_element_type=jnp.float32
    ) * HD ** (-0.5)
    key_pos = lax.broadcasted_iota(jnp.int32, (block_rows, seq_len), 1)
    query_pos = start_row + lax.broadcasted_iota(jnp.int32, (block_rows, seq_len), 0)
    allowed = key_pos < key_len
    if causal:
        allowed = allowed & (key_pos <= query_pos)
    return jnp.where(allowed[None], products, mask_fill)


def attend_forward(queries, key_rows, value_rows, key_lens, causal):
    pair_count = key_lens.shape[0]
    seq_len = queries.shape[0] // pair_count
    block_rows = min(512, seq_len)
    starts = lax.iota(jnp.int32, seq_len // block_rows) * block_rows

    def one_pair(packed):
        query_pair, key_pair, value_pair, key_len = packed

        def one_block(inner):
            query_blk, start_row = inner
            scores = block_scores(query_blk, key_pair, start_row, key_len, causal)
            row_max = jnp.max(scores, axis=-1, keepdims=True)
            shifted = jnp.exp(scores - row_max)
            row_total = jnp.sum(shifted, axis=-1, keepdims=True)
            attn_prob = (shifted / row_total).astype(jnp.bfloat16)
            context = jnp.einsum(
                "hqk,khd->qhd", attn_prob, value_pair, preferred_element_type=jnp.float32
            )
            return (context.astype(jnp.bfloat16), (row_max + jnp.log(row_total))[..., 0])

        return lax.map(one_block, (query_pair, starts))

    context, log_total = lax.map(
        one_pair,
        (
            block_view(queries, pair_count, block_rows),
            pair_view(key_rows, pair_count),
            pair_view(value_rows, pair_count),
            key_lens,
        ),
    )
    return (context.reshape(queries.shape), log_total)


def attend_backward(queries, key_rows, value_rows, key_lens, causal, log_total, grad_context):
    pair_count = key_lens.shape[0]
    seq_len = queries.shape[0] // pair_count
    block_rows = min(512, seq_len)
    starts = lax.iota(jnp.int32, seq_len // block_rows) * block_rows
    score_scale = HD ** (-0.5)

    def one_pair(packed):
        query_pair, key_pair, value_pair, key_len, total_pair, grad_pair = packed

        def one_block(carry, inner):
            key_grad, value_grad = carry
            query_blk, start_row, total_blk, grad_blk = inner
            scores = block_scores(query_blk, key_pair, start_row, key_len, causal)
            attn_prob = jnp.exp(scores - total_blk[..., None])
            value_grad = value_grad + jnp.einsum(
                "hqk,qhd->khd",
                attn_prob.astype(jnp.bfloat16),
                grad_blk,
                preferred_element_type=jnp.float32,
            )
            prob_grad = jnp.einsum(
                "qhd,khd->hqk", grad_blk, value_pair, preferred_element_type=jnp.float32
            )
            score_grad = (
                attn_prob * (prob_grad - jnp.sum(attn_prob * prob_grad, axis=-1, keepdims=True))
            ).astype(jnp.bfloat16)
            query_grad = (
                jnp.einsum("hqk,khd->qhd", score_grad, key_pair, preferred_element_type=jnp.float32)
                * score_scale
            )
            key_grad = (
                key_grad
                + jnp.einsum(
                    "hqk,qhd->khd", score_grad, query_blk, preferred_element_type=jnp.float32
                )
                * score_scale
            )
            return ((key_grad, value_grad), query_grad.astype(jnp.bfloat16))

        zeros = jnp.zeros(key_pair.shape, jnp.float32)
        (key_grad, value_grad), query_grad = lax.scan(
            one_block, (zeros, zeros), (query_pair, starts, total_pair, grad_pair)
        )
        return (query_grad, key_grad.astype(jnp.bfloat16), value_grad.astype(jnp.bfloat16))

    query_grad, key_grad, value_grad = lax.map(
        one_pair,
        (
            block_view(queries, pair_count, block_rows),
            pair_view(key_rows, pair_count),
            pair_view(value_rows, pair_count),
            key_lens,
            log_total,
            block_view(grad_context, pair_count, block_rows),
        ),
    )
    return (
        query_grad.reshape(queries.shape),
        key_grad.reshape(queries.shape),
        value_grad.reshape(queries.shape),
    )


def on_device(
    target,
    memory,
    mem_len,
    grad_out,
    self_qkv,
    self_out,
    cross_query,
    cross_kv,
    cross_out,
    ffn_up,
    ffn_down,
    ln_gain,
    ln_bias,
):
    row_count = target.shape[0]
    pair_count = mem_len.shape[0]
    seq_len = row_count * lax.axis_size("tensor") // pair_count
    full_lens = jnp.full((pair_count,), seq_len, jnp.int32)
    target_all = gather_rows(target)
    qkv_rows = jnp.einsum(
        "td,ide->ite", target_all, self_qkv, preferred_element_type=jnp.float32
    ).astype(jnp.bfloat16)
    context_one, total_one = attend_forward(qkv_rows[0], qkv_rows[1], qkv_rows[2], full_lens, True)
    branch_one = project_context(context_one, self_out, row_count)
    normed_one, norm_back_one = jax.vjp(
        norm_rows, alpha_res * target.astype(jnp.float32) + branch_one, ln_gain[0], ln_bias[0]
    )
    normed_one_all = gather_rows(normed_one.astype(jnp.bfloat16))
    memory_all = gather_rows(memory)
    query_two = jnp.dot(normed_one_all, cross_query, preferred_element_type=jnp.float32).astype(
        jnp.bfloat16
    )
    kv_two = jnp.einsum(
        "td,ide->ite", memory_all, cross_kv, preferred_element_type=jnp.float32
    ).astype(jnp.bfloat16)
    context_two, total_two = attend_forward(query_two, kv_two[0], kv_two[1], mem_len, False)
    branch_two = project_context(context_two, cross_out, row_count)
    normed_two, norm_back_two = jax.vjp(
        norm_rows, alpha_res * normed_one + branch_two, ln_gain[1], ln_bias[1]
    )
    normed_two_low = normed_two.astype(jnp.bfloat16)
    normed_two_all = gather_rows(normed_two_low)
    hidden = jnp.dot(normed_two_all, ffn_up, preferred_element_type=jnp.float32)
    activated, gelu_back = jax.vjp(exact_gelu, hidden)
    activated_low = activated.astype(jnp.bfloat16)
    branch_three = scatter_branch(activated_low, ffn_down, row_count)
    result, norm_back_three = jax.vjp(
        norm_rows, alpha_res * normed_two + branch_three, ln_gain[2], ln_bias[2]
    )
    grad_sum_three, gain_three, bias_three = norm_back_three(grad_out.astype(jnp.float32))
    branch_grad_three = gather_grads(grad_sum_three.astype(jnp.bfloat16))
    down_grad = lax.dot_general(
        activated_low, branch_grad_three, contract_rows, preferred_element_type=jnp.float32
    )
    act_grad = lax.dot_general(
        branch_grad_three, ffn_down, contract_cols, preferred_element_type=jnp.float32
    )
    hidden_grad = gelu_back(act_grad)[0].astype(jnp.bfloat16)
    up_grad = lax.dot_general(
        normed_two_all, hidden_grad, contract_rows, preferred_element_type=jnp.float32
    )
    normed_two_grad = alpha_res * grad_sum_three + scatter_inputs(
        ((hidden_grad, ffn_up),), row_count
    )
    grad_sum_two, gain_two, bias_two = norm_back_two(normed_two_grad)
    branch_grad_two = gather_grads(grad_sum_two.astype(jnp.bfloat16))
    cross_out_grad = lax.dot_general(
        context_two, branch_grad_two, contract_rows, preferred_element_type=jnp.float32
    )
    context_grad_two = lax.dot_general(
        branch_grad_two, cross_out, contract_cols, preferred_element_type=jnp.float32
    ).astype(jnp.bfloat16)
    query_grad_two, key_grad_two, value_grad_two = attend_backward(
        query_two, kv_two[0], kv_two[1], mem_len, False, total_two, context_grad_two
    )
    cross_query_grad = lax.dot_general(
        normed_one_all, query_grad_two, contract_rows, preferred_element_type=jnp.float32
    )
    cross_kv_grad = jnp.einsum(
        "td,ite->ide",
        memory_all,
        jnp.stack([key_grad_two, value_grad_two]),
        preferred_element_type=jnp.float32,
    )
    memory_grad = scatter_inputs(
        ((key_grad_two, cross_kv[0]), (value_grad_two, cross_kv[1])), row_count
    )
    normed_one_grad = alpha_res * grad_sum_two + scatter_inputs(
        ((query_grad_two, cross_query),), row_count
    )
    grad_sum_one, gain_one, bias_one = norm_back_one(normed_one_grad)
    branch_grad_one = gather_grads(grad_sum_one.astype(jnp.bfloat16))
    self_out_grad = lax.dot_general(
        context_one, branch_grad_one, contract_rows, preferred_element_type=jnp.float32
    )
    context_grad_one = lax.dot_general(
        branch_grad_one, self_out, contract_cols, preferred_element_type=jnp.float32
    ).astype(jnp.bfloat16)
    query_grad_one, key_grad_one, value_grad_one = attend_backward(
        qkv_rows[0], qkv_rows[1], qkv_rows[2], full_lens, True, total_one, context_grad_one
    )
    self_qkv_grad = jnp.einsum(
        "td,ite->ide",
        target_all,
        jnp.stack([query_grad_one, key_grad_one, value_grad_one]),
        preferred_element_type=jnp.float32,
    )
    target_grad = alpha_res * grad_sum_one + scatter_inputs(
        ((query_grad_one, self_qkv[0]), (key_grad_one, self_qkv[1]), (value_grad_one, self_qkv[2])),
        row_count,
    )
    (
        self_qkv_total,
        self_out_total,
        cross_query_total,
        cross_kv_total,
        cross_out_total,
        up_total,
        down_total,
    ) = (
        lax.psum(self_qkv_grad.astype(jnp.bfloat16), "dp").astype(jnp.float32),
        lax.psum(self_out_grad.astype(jnp.bfloat16), "dp").astype(jnp.float32),
        lax.psum(cross_query_grad.astype(jnp.bfloat16), "dp").astype(jnp.float32),
        lax.psum(cross_kv_grad.astype(jnp.bfloat16), "dp").astype(jnp.float32),
        lax.psum(cross_out_grad.astype(jnp.bfloat16), "dp").astype(jnp.float32),
        lax.psum(up_grad.astype(jnp.bfloat16), "dp").astype(jnp.float32),
        lax.psum(down_grad.astype(jnp.bfloat16), "dp").astype(jnp.float32),
    )
    gain_total, bias_total = lax.psum(
        (jnp.stack([gain_one, gain_two, gain_three]), jnp.stack([bias_one, bias_two, bias_three])),
        ("dp", "tensor"),
    )
    return (
        result.astype(jnp.bfloat16),
        target_grad.astype(jnp.bfloat16),
        memory_grad.astype(jnp.bfloat16),
        self_qkv_total,
        self_out_total,
        cross_query_total,
        cross_kv_total,
        cross_out_total,
        up_total,
        down_total,
        gain_total,
        bias_total,
    )


def solution(mesh):
    placed = (
        P(("dp", "tensor"), None),
        P(("dp", "tensor"), None),
        P("dp"),
        P(("dp", "tensor"), None),
        P(None, None, "tensor"),
        P("tensor", None),
        P(None, "tensor"),
        P(None, None, "tensor"),
        P("tensor", None),
        P(None, "tensor"),
        P("tensor", None),
        P(),
        P(),
    )
    return jax.shard_map(
        on_device,
        mesh=mesh,
        in_specs=placed,
        out_specs=(
            P(("dp", "tensor"), None),
            P(("dp", "tensor"), None),
            P(("dp", "tensor"), None),
            P(None, None, "tensor"),
            P("tensor", None),
            P(None, "tensor"),
            P(None, None, "tensor"),
            P("tensor", None),
            P(None, "tensor"),
            P("tensor", None),
            P(),
            P(),
        ),
        check_vma=False,
    )
```

profile of v0, /device:TPU:0, one launch (start us, length us, event | category | flops | bytes accessed | tf_op | source)
XLA Modules:
  0.0 2073.0 jit_solution(4765463061131379736)
XLA Ops:
  8.0 61.1 %all-gather.8.cloned.1.call-done = bf16[2048,1024]{1,0:T(8,128)(2,1)} async-done(((bf16[1024,1024]{1,0:T(8,128)(2,1)}), bf16[2048,1024]{1,0:T(8,128)(2,1)}) %all-gather.8.cloned.1.call-update) | async-done | bytes 4194320 | tf_op jit(solution)/shard_map/all_gather | solution.py:28
  69.0 9.6 convert_bitcast_fusion
  100.3 76.4 %while.117 = (s32[]{:T(128)}, bf16[2,2,512,8,64]{2,1,0,4,3:T(2,128)(2,1)}, f32[2,2,8,512]{3,2,1,0:T(8,128)}, bf16[2,2,512,8,64]{2,4,3,1,0:T(8,128)(2,1)}, bf16[2...) while((s32[]{:T(128)}, ...), condition=%wide.region_5.6_spmd.clone, body=%wide.region_0.5_spmd.clone.sunk | while | flops 1125381632 | bytes 77273528 | solution.py:117
  104.6 30.6 %while.122 = (s32[]{:T(128)}, bf16[2,512,8,64]{1,3,2,0:T(8,128)(2,1)}, f32[2,8,512]{2,1,0:T(8,128)S(1)}, s32[2]{0:T(128)S(1)}, bf16[2,512,8,64]{1,3,2,0:T(8,128)...) while((s32[]{:T(128)}, bf16[2,512,8,64]{1,3,2,0:T(8,128)(2,1)}, ...), condition=%wide.region_4.4_spmd, body=%wide.region_1.3_spmd.sunk | while | flops 1125381632 | bytes 68294856 | solution.py:115
  142.7 30.6 %while.122 = (s32[]{:T(128)}, bf16[2,512,8,64]{1,3,2,0:T(8,128)(2,1)}, f32[2,8,512]{2,1,0:T(8,128)S(1)}, s32[2]{0:T(128)S(1)}, bf16[2,512,8,64]{1,3,2,0:T(8,128)...) while((s32[]{:T(128)}, bf16[2,512,8,64]{1,3,2,0:T(8,128)(2,1)}, ...), condition=%wide.region_4.4_spmd, body=%wide.region_1.3_spmd.sunk | while | flops 1125381632 | bytes 68294856 | solution.py:115
  180.0 7.8 fusion.138
  190.2 97.0 %reduce-scatter.8.cloned.1.call-done = f32[1024,1024]{1,0:T(8,128)} async-done(((f32[2048,1024]{1,0:T(8,128)}), f32[1024,1024]{1,0:T(8,128)}) %reduce-scatter.8.cloned.1.call-update) | async-done | bytes 4194320 | tf_op jit(solution)/shard_map/reduce_scatter | solution.py:40
  294.3 51.3 %all-gather.12.cloned.1.call-done = bf16[2048,1024]{1,0:T(8,128)(2,1)} async-done(((bf16[1024,1024]{1,0:T(8,128)(2,1)}), bf16[2048,1024]{1,0:T(8,128)(2,1)}) %all-gather.12.cloned.1.call-update) | async-done | bytes 4194320 | tf_op jit(solution)/shard_map/all_gather | solution.py:28
  345.6 7.0 convert_bitcast_fusion.1
  365.7 38.8 %all-gather.10.cloned.1.call-done = bf16[2048,1024]{1,0:T(8,128)(2,1)} async-done(((bf16[1024,1024]{1,0:T(8,128)(2,1)}), bf16[2048,1024]{1,0:T(8,128)(2,1)}) %all-gather.10.cloned.1.call-update) | async-done | bytes 4194320 | tf_op jit(solution)/shard_map/all_gather | solution.py:28
  421.3 68.6 %while.113 = (s32[]{:T(128)}, bf16[2,2,512,8,64]{2,1,0,4,3:T(2,128)(2,1)}, f32[2,2,8,512]{3,2,1,0:T(8,128)}, bf16[2,2,512,8,64]{2,4,3,1,0:T(8,128)(2,1)}, bf16[2...) while((s32[]{:T(128)}, ...), condition=%wide.region_14.15_spmd, body=%wide.region_9.14_spmd.sunk | while | flops 1124332544 | bytes 75174336 | solution.py:117
  426.8 25.6 %while.120 = (s32[]{:T(128)}, bf16[2,512,8,64]{1,3,2,0:T(8,128)(2,1)}, f32[2,8,512]{2,1,0:T(8,128)S(1)}, s32[]{:T(128)}, bf16[2,512,8,64]{1,3,2,0:T(8,128)(2,1)S...) while((s32[]{:T(128)}, bf16[2,512,8,64]{1,3,2,0:T(8,128)(2,1)}, ...), condition=%wide.region_13.13_spmd, body=%wide.region_10.12_spmd.sunk | while | flops 1124332544 | bytes 66195648 | solution.py:115
  461.0 25.6 %while.120 = (s32[]{:T(128)}, bf16[2,512,8,64]{1,3,2,0:T(8,128)(2,1)}, f32[2,8,512]{2,1,0:T(8,128)S(1)}, s32[]{:T(128)}, bf16[2,512,8,64]{1,3,2,0:T(8,128)(2,1)S...) while((s32[]{:T(128)}, bf16[2,512,8,64]{1,3,2,0:T(8,128)(2,1)}, ...), condition=%wide.region_13.13_spmd, body=%wide.region_10.12_spmd.sunk | while | flops 1124332544 | bytes 66195648 | solution.py:115
  499.1 99.3 %reduce-scatter.10.cloned.1.call-done = f32[1024,1024]{1,0:T(8,128)} async-done(((f32[2048,1024]{1,0:T(8,128)}), f32[1024,1024]{1,0:T(8,128)}) %reduce-scatter.10.cloned.1.call-update) | async-done | bytes 4194320 | tf_op jit(solution)/shard_map/reduce_scatter | solution.py:40
  606.9 56.9 %all-gather.14.cloned.1.call-done = bf16[2048,1024]{1,0:T(8,128)(2,1)} async-done(((bf16[1024,1024]{1,0:T(8,128)(2,1)}), bf16[2048,1024]{1,0:T(8,128)(2,1)}) %all-gather.14.cloned.1.call-update) | async-done | bytes 4194320 | tf_op jit(solution)/shard_map/all_gather | solution.py:28
  663.8 48.6 %multiply_convert_fusion.2 = (bf16[2048,2048]{1,0:T(8,128)(2,1)S(1)}, f32[2048,2048]{1,0:T(8,128)}, f32[2048,2048]{1,0:T(8,128)}) fusion(bf16[2048,1024]{1,0:T(8,128)(2,1)} %all-gather.14.cloned.1.call-done, bf16[1024,2048]{1,0:T(8,128)(2,1)} %param.38), kind=kOutput, calls=%fused_computation.125 | convolution fusion | flops 8862564352 | bytes 50331648 | tf_op jit(solution)/shard_map/dot_general | solution.py:236
  715.8 11.0 fusion.140
  726.9 99.4 %reduce-scatter.12.cloned.1.call-done = f32[1024,1024]{1,0:T(8,128)} async-done(((f32[2048,1024]{1,0:T(8,128)}), f32[1024,1024]{1,0:T(8,128)}) %reduce-scatter.12.cloned.1.call-update) | async-done | bytes 4194320 | tf_op jit(solution)/shard_map/reduce_scatter | solution.py:40
  841.9 56.9 %all-gather.16.cloned.1.call-done = bf16[2048,1024]{1,0:T(8,128)(2,1)} async-done(((bf16[1024,1024]{1,0:T(8,128)(2,1)}), bf16[2048,1024]{1,0:T(8,128)(2,1)}) %all-gather.16.cloned.1.call-update) | async-done | bytes 4194320 | tf_op jit(solution)/shard_map/all_gather | solution.py:32
  898.8 22.2 %add_convert_fusion = bf16[2048,2048]{1,0:T(8,128)(2,1)} fusion(f32[2048,2048]{1,0:T(8,128)} %get-tuple-element.813, f32[2048,2048]{1,0:T(8,128)} %get-tuple-element.846, bf16[2048,1024]{1,0:T(8,128)(2,1)} %all-gather.16.cloned.1.call-done, bf16[2048,1024]{1,0:T(8,128)(2,1)} %param.39), kind=kOutput, calls=%fused_computation.124 | convolution fusion | flops 8648654848 | bytes 50331648 | tf_op jit(solution)/shard_map/dot_general | solution.py:248
  921.0 13.9 convolution_convert_fusion.2
  935.0 54.4 %reduce-scatter.14.cloned.1.call-done = bf16[1024,1024]{1,0:T(8,128)(2,1)} async-done(((bf16[2048,1024]{1,0:T(8,128)(2,1)}), bf16[1024,1024]{1,0:T(8,128)(2,1)}) %reduce-scatter.14.cloned.1.call-update) | async-done | bytes 2097168 | tf_op jit(solution)/shard_map/reduce_scatter | solution.py:61
  1002.6 56.9 %all-gather.18.cloned.1.call-done = bf16[2048,1024]{1,0:T(8,128)(2,1)} async-done(((bf16[1024,1024]{1,0:T(8,128)(2,1)}), bf16[2048,1024]{1,0:T(8,128)(2,1)}) %all-gather.18.cloned.1.call-update) | async-done | bytes 4194320 | tf_op jit(solution)/shard_map/all_gather | solution.py:32
  1078.7 181.9 %while.115 = (s32[]{:T(128)}, bf16[2,2,512,8,64]{2,1,0,4,3:T(2,128)(2,1)}, bf16[2,1024,8,64]{1,3,2,0:T(8,128)(2,1)}, bf16[2,1024,8,64]{1,3,2,0:T(8,128)(2,1)}, b...) while((s32[]{:T(128)}, ...), condition=%wide.region_30.31_spmd, body=%wide.region_26.30_spmd.sunk | while | flops 2726294528 | bytes 240798400 | solution.py:175
  1085.9 76.7 %while.121 = (s32[]{:T(128)}, f32[1024,8,64]{0,2,1:T(8,128)}, f32[1024,8,64]{0,2,1:T(8,128)}, bf16[2,512,8,64]{1,3,2,0:T(8,128)(2,1)}, bf16[2,512,8,64]{1,3,2,0:...) while((s32[]{:T(128)}, f32[1024,8,64]{0,2,1:T(8,128)}, ...), condition=%wide.region_29.29_spmd.clone, body=%wide.region_27.28_spmd.clone.sunk | while | flops 2725245952 | bytes 207178096 | solution.py:170
  1088.9 10.5 multiply_reduce_fusion.12
  1099.4 9.4 multiply_convert_fusion.6
  1108.8 8.8 bitcast_add_fusion.11
  1126.9 10.5 multiply_reduce_fusion.12
  1137.4 9.4 multiply_convert_fusion.6
  1146.9 9.4 bitcast_add_fusion.11
  1176.7 76.7 %while.121 = (s32[]{:T(128)}, f32[1024,8,64]{0,2,1:T(8,128)}, f32[1024,8,64]{0,2,1:T(8,128)}, bf16[2,512,8,64]{1,3,2,0:T(8,128)(2,1)}, bf16[2,512,8,64]{1,3,2,0:...) while((s32[]{:T(128)}, f32[1024,8,64]{0,2,1:T(8,128)}, ...), condition=%wide.region_29.29_spmd.clone, body=%wide.region_27.28_spmd.clone.sunk | while | flops 2725245952 | bytes 207178096 | solution.py:170
  1179.7 10.5 multiply_reduce_fusion.12
  1190.2 9.4 multiply_convert_fusion.6
  1199.7 8.8 bitcast_add_fusion.11
  1217.8 10.5 multiply_reduce_fusion.12
  1228.3 9.4 multiply_convert_fusion.6
  1237.7 9.4 bitcast_add_fusion.11
  1269.0 14.1 convolution_convert_fusion
  1283.0 40.3 %reduce-scatter.16.cloned.1.call-done = bf16[1024,1024]{1,0:T(8,128)(2,1)} async-done(((bf16[2048,1024]{1,0:T(8,128)(2,1)}), bf16[1024,1024]{1,0:T(8,128)(2,1)}) %reduce-scatter.16.cloned.1.call-update) | async-done | bytes 2097168 | tf_op jit(solution)/shard_map/reduce_scatter | solution.py:61
  1336.6 14.2 convolution_convert_fusion.3
  1364.0 6.4 convolution_convert_fusion.7
  1379.5 13.9 all-gather.20.cloned.1.call-done
  1411.6 203.5 %while.119 = (s32[]{:T(128)}, bf16[2,2,512,8,64]{2,1,0,4,3:T(2,128)(2,1)}, bf16[2,1024,8,64]{1,3,2,0:T(8,128)(2,1)}, bf16[2,1024,8,64]{1,3,2,0:T(8,128)(2,1)}, b...) while((s32[]{:T(128)}, ...), condition=%wide.region_38.39_spmd.clone, body=%wide.region_34.38_spmd.clone.sunk | while | flops 2727343616 | bytes 246307600 | solution.py:175
  1419.8 86.4 %while.123 = (s32[]{:T(128)}, f32[1024,8,64]{0,2,1:T(8,128)}, f32[1024,8,64]{0,2,1:T(8,128)}, bf16[2,512,8,64]{1,3,2,0:T(8,128)(2,1)}, bf16[2,512,8,64]{1,3,2,0:...) while((s32[]{:T(128)}, f32[1024,8,64]{0,2,1:T(8,128)}, ...), condition=%wide.region_37.37_spmd.clone, body=%wide.region_35.36_spmd.clone.sunk | while | flops 2726295040 | bytes 212687312 | solution.py:170
  1426.3 11.8 multiply_reduce_fusion.11
  1438.1 9.4 multiply_convert_fusion.5
  1447.5 8.8 bitcast_add_fusion.9
  1469.1 11.8 multiply_reduce_fusion.11
  1481.0 9.4 multiply_convert_fusion.5
  1490.4 9.4 bitcast_add_fusion.9
  1521.2 86.4 %while.123 = (s32[]{:T(128)}, f32[1024,8,64]{0,2,1:T(8,128)}, f32[1024,8,64]{0,2,1:T(8,128)}, bf16[2,512,8,64]{1,3,2,0:T(8,128)(2,1)}, bf16[2,512,8,64]{1,3,2,0:...) while((s32[]{:T(128)}, f32[1024,8,64]{0,2,1:T(8,128)}, ...), condition=%wide.region_37.37_spmd.clone, body=%wide.region_35.36_spmd.clone.sunk | while | flops 2726295040 | bytes 212687312 | solution.py:170
  1527.7 11.8 multiply_reduce_fusion.11
  1539.5 9.4 multiply_convert_fusion.5
  1549.0 8.8 bitcast_add_fusion.9
  1570.6 11.8 multiply_reduce_fusion.11
  1582.4 9.4 multiply_convert_fusion.5
  1591.9 9.4 bitcast_add_fusion.9
  1640.5 8.0 convert_bitcast_fusion.2
  1680.2 41.3 %all-reduce = (f32[3,1024]{1,0:T(4,128)}, f32[3,1024]{1,0:T(4,128)}) all-reduce(f32[3,1024]{1,0:T(4,128)S(1)} %get-tuple-element.847, f32[3,1024]{1,0:T(4,128)S(1)} %get-tuple-element.848), channel_id=1, replica_groups=mesh['dp'=16,'tensor'=2] {'dp','tensor'}, use_global_device_ids=true, to_apply=%region_51.52 | all-reduce | flops 6144 | bytes 49152 | tf_op jit(solution)/shard_map/psum | solution.py:322
  1721.5 231.2 %all-reduce.4.cloned.1.call-done = (bf16[3,1024,512]{1,2,0:T(8,128)(2,1)}, bf16[2,1024,512]{1,2,0:T(8,128)(2,1)}, bf16[512,1024]{1,0:T(8,128)(2,1)}, bf16[1024,5...) async-done(((bf16[3,1024,512]{1,2,0:T(8,128)(2,1)}, bf16[2,1024,512]{1,2,0:T(8,128)(2,1)}, ...) | async-done | bytes 16777232 | tf_op jit(solution)/shard_map/psum | solution.py:314
  1968.7 7.1 convert_element_type.227
  1980.2 28.7 %reduce-scatter.18.cloned.1.call-done = bf16[1024,1024]{1,0:T(8,128)(2,1)} async-done(((bf16[2048,1024]{1,0:T(8,128)(2,1)}), bf16[1024,1024]{1,0:T(8,128)(2,1)}) %reduce-scatter.18.cloned.1.call-update) | async-done | bytes 2097168 | tf_op jit(solution)/shard_map/reduce_scatter | solution.py:61
  2013.8 52.2 %reduce-scatter.20.cloned.1.call-done = bf16[1024,1024]{1,0:T(8,128)(2,1)} async-done(((bf16[2048,1024]{1,0:T(8,128)(2,1)}), bf16[1024,1024]{1,0:T(8,128)(2,1)}) %reduce-scatter.20.cloned.1.call-update) | async-done | bytes 2097168 | tf_op jit(solution)/shard_map/reduce_scatter | solution.py:61
  (669 shorter events, 568.0 us)
Async XLA Ops:
  7.2 486.0 %copy-start = (bf16[512,1024]{1,0:T(8,128)(2,1)S(1)}, bf16[512,1024]{1,0:T(8,128)(2,1)}, u32[]{:S(2)}) copy-start(bf16[512,1024]{1,0:T(8,128)(2,1)} %param.37) | copy-start | bytes 3145732
  7.2 61.9 %all-gather.8.cloned.1.call-start = ((), (), s32[]{:S(2)}) async-start(), calls=%async_computation.7 | async-start | bytes 6291456 | tf_op jit(solution)/shard_map/all_gather | solution.py:28
  7.9 279.3 %reduce-scatter.8.cloned.1.call-start = ((), (), s32[]{:S(2)}) async-start(), calls=%async_computation.8 | async-start | bytes 12582912 | tf_op jit(solution)/shard_map/reduce_scatter | solution.py:40
  104.6 30.6 %copy-start.63 = (f32[2,2,8,512]{3,2,1,0:T(8,128)S(1)}, f32[2,2,8,512]{3,2,1,0:T(8,128)}, u32[]{:S(2)}) copy-start(f32[2,2,8,512]{3,2,1,0:T(8,128)} %get-tuple-element.1508) | copy-start | bytes 196612 | tf_op jit(solution)/shard_map/while
  142.7 30.6 %copy-start.63 = (f32[2,2,8,512]{3,2,1,0:T(8,128)S(1)}, f32[2,2,8,512]{3,2,1,0:T(8,128)}, u32[]{:S(2)}) copy-start(f32[2,2,8,512]{3,2,1,0:T(8,128)} %get-tuple-element.1508) | copy-start | bytes 196612 | tf_op jit(solution)/shard_map/while
  187.8 99.4 %copy-start.40 = (bf16[1024,1024]{1,0:T(8,128)(2,1)S(1)}, bf16[1024,1024]{1,0:T(8,128)(2,1)}, u32[]{:S(2)}) copy-start(bf16[1024,1024]{1,0:T(8,128)(2,1)} %param.29) | copy-start | bytes 6291460
  187.8 157.8 %all-gather.12.cloned.1.call-start = ((), (), s32[]{:S(2)}) async-start(), calls=%async_computation.10 | async-start | bytes 6291456 | tf_op jit(solution)/shard_map/all_gather | solution.py:28
  188.5 215.9 %all-gather.10.cloned.1.call-start = ((), (), s32[]{:S(2)}) async-start(), calls=%async_computation.9 | async-start | bytes 6291456 | tf_op jit(solution)/shard_map/all_gather | solution.py:28
  189.6 102.0 %copy-start.72 = (f32[1,1024]{1,0:T(1,128)}, f32[1,1024]{1,0:T(1,128)S(1)}, u32[]{:S(2)}) copy-start(f32[1,1024]{1,0:T(1,128)S(1)} %get-tuple-element.841) | copy-start | bytes 12292
  190.2 101.4 %copy-start.80 = (f32[1,1024]{1,0:T(1,128)}, f32[1,1024]{1,0:T(1,128)S(1)}, u32[]{:S(2)}) copy-start(f32[1,1024]{1,0:T(1,128)S(1)} %get-tuple-element.844) | copy-start | bytes 12292
  292.2 53.4 %copy-start.101 = (bf16[2,1024,512]{2,1,0:T(8,128)(2,1)S(1)}, bf16[2,1024,512]{2,1,0:T(8,128)(2,1)}, u32[]{:S(2)}) copy-start(bf16[2,1024,512]{2,1,0:T(8,128)(2,1)} %param.36) | copy-start | bytes 6291460
  294.3 304.2 %reduce-scatter.10.cloned.1.call-start = ((), (), s32[]{:S(2)}) async-start(), calls=%async_computation.11 | async-start | bytes 12582912 | tf_op jit(solution)/shard_map/reduce_scatter | solution.py:40
  426.8 25.6 %copy-start.61 = (f32[2,2,8,512]{3,2,1,0:T(8,128)S(1)}, f32[2,2,8,512]{3,2,1,0:T(8,128)}, u32[]{:S(2)}) copy-start(f32[2,2,8,512]{3,2,1,0:T(8,128)} %get-tuple-element.1536) | copy-start | bytes 196612 | tf_op jit(solution)/shard_map/while
  461.0 25.6 %copy-start.61 = (f32[2,2,8,512]{3,2,1,0:T(8,128)S(1)}, f32[2,2,8,512]{3,2,1,0:T(8,128)}, u32[]{:S(2)}) copy-start(f32[2,2,8,512]{3,2,1,0:T(8,128)} %get-tuple-element.1536) | copy-start | bytes 196612 | tf_op jit(solution)/shard_map/while
  499.0 99.4 %copy-start.67 = (f32[1024]{0:T(1024)S(1)}, f32[1024]{0:T(1024)}, u32[]{:S(2)}) copy-start(f32[1024]{0:T(1024)} %copy-done.66) | copy-start | bytes 12292
  499.0 99.4 %copy-start.70 = (f32[1024]{0:T(1024)S(1)}, f32[1024]{0:T(1024)}, u32[]{:S(2)}) copy-start(f32[1024]{0:T(1024)} %copy-done.69) | copy-start | bytes 12292
  499.0 99.4 %copy-start.73 = (f32[1,1024]{1,0:T(1,128)S(1)}, f32[1,1024]{1,0:T(1,128)}, u32[]{:S(2)}) copy-start(f32[1,1024]{1,0:T(1,128)} %copy-done.72) | copy-start | bytes 12292
  499.0 99.4 %copy-start.81 = (f32[1,1024]{1,0:T(1,128)S(1)}, f32[1,1024]{1,0:T(1,128)}, u32[]{:S(2)}) copy-start(f32[1,1024]{1,0:T(1,128)} %copy-done.80) | copy-start | bytes 12292
  499.1 164.7 %all-gather.14.cloned.1.call-start = ((), (), s32[]{:S(2)}) async-start(), calls=%async_computation.12 | async-start | bytes 6291456 | tf_op jit(solution)/shard_map/all_gather | solution.py:28
  606.9 219.4 %reduce-scatter.12.cloned.1.call-start = ((), (), s32[]{:S(2)}) async-start(), calls=%async_computation.13 | async-start | bytes 12582912 | tf_op jit(solution)/shard_map/reduce_scatter | solution.py:40
  663.8 52.0 %copy-start.97 = (bf16[2048,1024]{1,0:T(8,128)(2,1)S(1)}, bf16[2048,1024]{1,0:T(8,128)(2,1)}, u32[]{:S(2)}) copy-start(bf16[2048,1024]{1,0:T(8,128)(2,1)} %param.39) | copy-start | bytes 12582916
  726.8 171.9 %all-gather.16.cloned.1.call-start = ((), (), s32[]{:S(2)}) async-start(), calls=%async_computation.14 | async-start | bytes 6291456 | tf_op jit(solution)/shard_map/all_gather | solution.py:32
  841.9 147.5 %reduce-scatter.14.cloned.1.call-start = ((), (), s32[]{:S(2)}) async-start(), calls=%async_computation.15 | async-start | bytes 6291456 | tf_op jit(solution)/shard_map/reduce_scatter | solution.py:61
  934.9 60.5 %copy-start.87 = (f32[1024]{0:T(1024)S(1)}, f32[1024]{0:T(1024)}, u32[]{:S(2)}) copy-start(f32[1024]{0:T(1024)} %copy-done.86) | copy-start | bytes 12292
  934.9 124.5 %all-gather.18.cloned.1.call-start = ((), (), s32[]{:S(2)}) async-start(), calls=%async_computation.16 | async-start | bytes 6291456 | tf_op jit(solution)/shard_map/all_gather | solution.py:32
  1002.5 320.8 %reduce-scatter.16.cloned.1.call-start = ((), (), s32[]{:S(2)}) async-start(), calls=%async_computation.17 | async-start | bytes 6291456 | tf_op jit(solution)/shard_map/reduce_scatter | solution.py:61
  1108.8 8.8 copy-start.12
  1108.8 9.3 copy-start.29
  1146.9 9.4 copy-start.2
  1146.9 9.4 copy-start.12
  1146.9 9.9 copy-start.29
  1199.7 9.3 copy-start.29
  1237.7 9.4 copy-start.2
  1237.7 9.4 copy-start.12
  1237.7 9.9 copy-start.29
  1268.9 124.5 %all-gather.20.cloned.1.call-start = ((), (), s32[]{:S(2)}) async-start(), calls=%async_computation.18 | async-start | bytes 6291456 | tf_op jit(solution)/shard_map/all_gather | solution.py:32
  1268.9 54.4 %copy-start.68 = (f32[1024]{0:T(1024)S(1)}, f32[1024]{0:T(1024)}, u32[]{:S(2)}) copy-start(f32[1024]{0:T(1024)} %copy-done.66) | copy-start | bytes 12292
  1268.9 54.4 %copy-start.71 = (f32[1024]{0:T(1024)S(1)}, f32[1024]{0:T(1024)}, u32[]{:S(2)}) copy-start(f32[1024]{0:T(1024)} %copy-done.69) | copy-start | bytes 12292
  1268.9 54.4 %copy-start.74 = (f32[1,1024]{1,0:T(1,128)S(1)}, f32[1,1024]{1,0:T(1,128)}, u32[]{:S(2)}) copy-start(f32[1,1024]{1,0:T(1,128)} %copy-done.72) | copy-start | bytes 12292
  1268.9 54.4 %copy-start.77 = (f32[1024]{0:T(1024)S(1)}, f32[1024]{0:T(1024)}, u32[]{:S(2)}) copy-start(f32[1024]{0:T(1024)} %copy-done.76) | copy-start | bytes 12292
  1283.0 46.2 %copy-start.85 = (f32[1024]{0:T(1024)S(1)}, f32[1024]{0:T(1024)}, u32[]{:S(2)}) copy-start(f32[1024]{0:T(1024)} %copy-done.84) | copy-start | bytes 12292
  1336.5 616.1 %all-reduce.4.cloned.1.call-start = ((), (), s32[]{:S(2)}) async-start(), calls=%async_computation.21 | async-start | bytes 33554432 | tf_op jit(solution)/shard_map/psum | solution.py:314
  1336.6 14.3 copy-start.43
  1373.8 19.6 copy-start.104
  1438.1 9.4 copy-start.8
  1447.5 8.9 copy-start.3
  1447.5 8.9 copy-start.11
  1447.5 9.2 copy-start.31
  1481.0 9.4 copy-start.8
  1490.4 9.4 copy-start.3
  1490.4 9.4 copy-start.11
  1490.4 9.8 copy-start.31
  1539.5 9.4 copy-start.8
  1548.9 8.9 copy-start.3
  1548.9 8.9 copy-start.11
  1549.0 9.2 copy-start.31
  1582.4 9.4 copy-start.8
  1591.8 9.4 copy-start.3
  1591.8 9.4 copy-start.11
  1591.8 9.8 copy-start.31
  1648.5 360.4 %reduce-scatter.18.cloned.1.call-start = ((), (), s32[]{:S(2)}) async-start(), calls=%async_computation.19 | async-start | bytes 6291456 | tf_op jit(solution)/shard_map/reduce_scatter | solution.py:61
  1669.0 397.0 %reduce-scatter.20.cloned.1.call-start = ((), (), s32[]{:S(2)}) async-start(), calls=%async_computation.20 | async-start | bytes 6291456 | tf_op jit(solution)/shard_map/reduce_scatter | solution.py:61
  1975.8 33.2 %copy-start.83 = (f32[1024]{0:T(1024)S(1)}, f32[1024]{0:T(1024)}, u32[]{:S(2)}) copy-start(f32[1024]{0:T(1024)} %copy-done.82) | copy-start | bytes 12292
  1975.8 90.3 %copy-start.1 = (bf16[512,1024]{1,0:T(8,128)(2,1)S(1)}, bf16[512,1024]{1,0:T(8,128)(2,1)}, u32[]{:S(2)}) copy-start(bf16[512,1024]{1,0:T(8,128)(2,1)} %param.37) | copy-start | bytes 3145732
  (134 other events, 457.2 us)
Sparse Core Ops, SparseCore 0:
  9.6 59.4 all-gather.7
  187.9 99.2 reduce-scatter.7
  288.8 56.7 all-gather.11
  347.7 56.7 all-gather.9
  499.2 99.2 reduce-scatter.9
  607.0 56.7 all-gather.13
  727.0 99.2 reduce-scatter.11
  842.0 56.7 all-gather.15
  935.1 54.3 reduce-scatter.13
  1002.7 56.7 all-gather.17
  1269.0 54.2 reduce-scatter.15
  1336.6 56.7 all-gather.19
  1648.7 303.9 all-reduce.3
  1954.9 53.9 reduce-scatter.17
  2011.7 54.3 reduce-scatter.19
where the time goes:
time: 2080 us; the launch traced here: 2070 us
  waiting for transfers between devices  1040 us (50%)
  matrix products  504 us (24%)
  local copies, waits for them, and re-layouts  261 us (13%)
  other arithmetic  209 us (10%)
  blocking collectives  41.3 us (2%)
    reduce_scatter x3, waiting for transfers between devices, scatter_branch(): lax.psum_scatter(partial_term(jnp.int32(0), row_count * lax.axis_size('te...  296 us
    psum x1, waiting for transfers between devices, on_device(): lax.psum(self_qkv_grad.astype(jnp.bfloat16), 'dp').astype(jnp.float32)  231 us
    all_gather x4, waiting for transfers between devices, gather_rows(): return lax.all_gather(local_rows, 'tensor', axis=0, tiled=True)  208 us
    reduce_scatter x4, waiting for transfers between devices, scatter_inputs(): lax.psum_scatter(partial_term(jnp.int32(0), row_count * lax.axis_size('te...  176 us
    all_gather x3, waiting for transfers between devices, gather_grads(): return lax.all_gather(local_rows, 'tensor', axis=0, tiled=True)  128 us
    dot_general x16, matrix products, block_scores(): jnp.einsum('qhd,khd->hqk', query_blk, key_pair, preferred_element_type=jn...  111 us
    convert_element_type x8, other arithmetic, one_block(): score_grad = (attn_prob * (prob_grad - jnp.sum(attn_prob * prob_grad, axi...  75.4 us
    dot_general x8, matrix products, one_block(): jnp.einsum('hqk,qhd->khd', attn_prob.astype(jnp.bfloat16), grad_blk, pref...  73 us
  transfers between devices with their start and end apart: 15, of which 15 were waited for; matrix products, arithmetic and copies ran while one was open for 7% of the time, Pallas kernels for 0%

commit v1 on v0

--- a/solution.py
+++ b/solution.py
@@ -1,6 +1,10 @@
+import functools
+
 import jax
 import jax.numpy as jnp
 from jax import lax
+from jax.experimental import pallas as pl
+from jax.experimental.pallas import tpu as pltpu
 from jax.sharding import PartitionSpec as P
 
 HD = 64
@@ -339,6 +343,694 @@
     )
 
 
+BLK = 256
+f32 = jnp.float32
+bf16 = jnp.bfloat16
+NN = (((1,), (0,)), ((), ()))
+NT = (((1,), (1,)), ((), ()))
+TN = (((0,), (0,)), ((), ()))
+
+
+def dot(a, b, dims=NN):
+    return lax.dot_general(a, b, dims, preferred_element_type=f32)
+
+
+def lanes(rows):
+    return lax.broadcasted_iota(jnp.int32, (rows, 128), 1)
+
+
+def place3(x, rows):
+    hi = x.astype(bf16)
+    rest = x - hi.astype(f32)
+    mid = rest.astype(bf16)
+    lo = (rest - mid.astype(f32)).astype(bf16)
+    at = lanes(rows) % 64
+    return jnp.where(at == 0, hi, jnp.where(at == 1, mid, jnp.where(at == 2, lo, jnp.zeros_like(hi))))
+
+
+def fwd_kernel(causal, len_ref, *refs):
+    if causal:
+        qkv_ref, c_ref, lse_ref, kaug, vaug = refs
+        q_ref, k2, v2 = qkv_ref.at[:, :128], qkv_ref[:, 128:256], qkv_ref[:, 256:]
+    else:
+        q_ref, kv_ref, c_ref, lse_ref, kaug, vaug = refs
+        k2, v2 = kv_ref[:, :128], kv_ref[:, 128:]
+    seq = k2.shape[0]
+    lane = lanes(seq)
+    zero = jnp.zeros_like(k2)
+    if not causal:
+        pos = lax.broadcasted_iota(jnp.int32, (seq, 128), 0)
+        bias = jnp.where((pos >= len_ref[0]) & (lane == 0), -1e30, 0.0).astype(bf16)
+    for h in range(2):
+        own = (lane // 64) == h
+        kaug[h, :, :128] = jnp.where(own, k2, zero)
+        if not causal:
+            kaug[h, :, 128:] = bias
+        vaug[h, :, :128] = jnp.where(own, v2, zero)
+        vaug[h, :, 128:] = jnp.where(own, jnp.ones_like(v2), zero)
+    lb = lanes(BLK)
+    for i in range(seq // BLK):
+        rows = slice(i * BLK, (i + 1) * BLK)
+        q = q_ref[rows, :] * jnp.asarray(HD**-0.5, bf16)
+        if not causal:
+            q = jnp.concatenate([q, jnp.where(lb == 0, 1.0, 0.0).astype(bf16)], axis=1)
+        nk = (i + 1) * BLK if causal else seq
+        acc = None
+        ms = []
+        for h in range(2):
+            s = dot(q, kaug[h, :nk, :128] if causal else kaug[h], NT)
+            if causal:
+                a = lax.broadcasted_iota(jnp.int32, (BLK, BLK), 0)
+                b = lax.broadcasted_iota(jnp.int32, (BLK, BLK), 1)
+                d = jnp.where(b <= a, s[:, nk - BLK :], mask_fill)
+                s = d if nk == BLK else jnp.concatenate([s[:, : nk - BLK], d], axis=1)
+            m = jnp.max(s, axis=1, keepdims=True)
+            p = jnp.exp(s - m).astype(bf16)
+            o = dot(p, vaug[h, :nk])
+            acc = o if acc is None else acc + o
+            ms.append(m)
+        total = acc[:, 128:]
+        c_ref[rows, :] = (acc[:, :128] / total).astype(bf16)
+        lse_ref[rows, :] = place3(-(jnp.where(lb < 64, ms[0], ms[1]) + jnp.log(total)), BLK)
+
+
+def cost(matmuls, blocks, seq, causal):
+    area = seq * seq * blocks * 2 * (0.625 if causal else 1)
+    return pl.CostEstimate(
+        flops=int(matmuls * area * 2 * 256), bytes_accessed=16 * seq * 128 * blocks, transcendentals=int(area)
+    )
+
+
+def columns(seq, width, first=0):
+    return pl.BlockSpec((seq, width), lambda i: (0, i + first))
+
+
+def attend_fwd(arrays, length, causal):
+    seq = arrays[0].shape[0]
+    widths = (384,) if causal else (128, 256)
+    blocks = arrays[0].shape[1] // widths[0]
+    return pl.pallas_call(
+        functools.partial(fwd_kernel, causal),
+        grid=(blocks,),
+        in_specs=[pl.BlockSpec(memory_space=pltpu.SMEM)] + [columns(seq, w) for w in widths],
+        out_specs=[columns(seq, 128)] * 2,
+        out_shape=[jax.ShapeDtypeStruct((seq, 128 * blocks), bf16)] * 2,
+        scratch_shapes=[pltpu.VMEM((2, seq, 256), bf16)] * 2,
+        compiler_params=pltpu.CompilerParams(vmem_limit_bytes=48 * 2**20),
+        cost_estimate=cost(2, blocks, seq, causal),
+        name="attend_causal" if causal else "attend_memory",
+    )(length, *arrays)
+
+
+def bwd_kernel(causal, len_ref, *refs):
+    if causal:
+        qkv_ref, c_ref, lse_ref, g_ref, d_ref, qs, qm, ka, gs, gm, va, dqa = refs
+        q2, k2, v2 = qkv_ref[:, :128], qkv_ref[:, 128:256], qkv_ref[:, 256:]
+        dq_ref, dk_ref, dv_ref = d_ref.at[:, :128], d_ref.at[:, 128:256], d_ref.at[:, 256:]
+    else:
+        q_ref, kv_ref, c_ref, lse_ref, g_ref, dq_ref, dkv_ref, qs, qm, ka, gs, gm, va, dqa = refs
+        q2, k2, v2 = q_ref[...], kv_ref[:, :128], kv_ref[:, 128:]
+        dk_ref, dv_ref = dkv_ref.at[:, :128], dkv_ref.at[:, 128:]
+    g2 = g_ref[...]
+    seq = k2.shape[0]
+    lane = lanes(seq)
+    l64 = lane % 64
+    zero = jnp.zeros_like(k2)
+    one = jnp.ones_like(k2)
+    scale = jnp.asarray(HD**-0.5, bf16)
+    prod = c_ref[...].astype(f32) * g2.astype(f32)
+    d0 = jnp.sum(jnp.where(lane < 64, prod, 0.0), axis=1, keepdims=True)
+    d1 = jnp.sum(jnp.where(lane < 64, 0.0, prod), axis=1, keepdims=True)
+    qs[:, :128] = q2 * scale
+    aug = lse_ref[...]
+    if not causal:
+        aug = jnp.where(l64 == 3, one, aug)
+        pos = lax.broadcasted_iota(jnp.int32, (seq, 128), 0)
+        bias = jnp.where(pos >= len_ref[0], -1e30, 0.0).astype(bf16)
+    qs[:, 128:] = aug
+    gs[:, :128] = g2
+    gs[:, 128:] = place3(-jnp.where(lane < 64, d0, d1), seq)
+    for h in range(2):
+        own = (lane // 64) == h
+        sel = own & (l64 < 3)
+        qm[h] = jnp.where(own, q2 * scale, zero)
+        gm[h] = jnp.where(own, g2, zero)
+        ka[h, :, :128] = jnp.where(own, k2, zero)
+        ko = jnp.where(sel, one, zero)
+        if not causal:
+            ko = jnp.where(own & (l64 == 3), bias, ko)
+        ka[h, :, 128:] = ko
+        va[h, :, :128] = jnp.where(own, v2, zero)
+        va[h, :, 128:] = jnp.where(sel, one, zero)
+    dqa[...] = jnp.zeros_like(dqa)
+
+    def block(j):
+        rows = slice(j * BLK, (j + 1) * BLK)
+        q0 = j * BLK if causal else 0
+        dk = None
+        dv = None
+        for h in range(2):
+            p = jnp.exp(dot(ka[h, rows, :], qs[q0:, :], NT))
+            if causal:
+                a = lax.broadcasted_iota(jnp.int32, (BLK, BLK), 0)
+                b = lax.broadcasted_iota(jnp.int32, (BLK, BLK), 1)
+                d = jnp.where(a <= b, p[:, :BLK], 0.0)
+                p = d if q0 + BLK == seq else jnp.concatenate([d, p[:, BLK:]], axis=1)
+            dp = dot(va[h, rows, :], gs[q0:, :], NT)
+            ds = (p * dp).astype(bf16)
+            p = p.astype(bf16)
+            a = dot(p, gm[h, q0:, :])
+            b = dot(ds, qm[h, q0:, :])
+            dv = a if dv is None else dv + a
+            dk = b if dk is None else dk + b
+            dqa[q0:, :] += dot(ds, ka[h, rows, :128], TN)
+        dk_ref[rows, :] = dk.astype(bf16)
+        dv_ref[rows, :] = dv.astype(bf16)
+
+    for j in range(seq // BLK):
+        if causal:
+            block(j)
+        else:
+            pl.when(j * BLK < len_ref[0])(functools.partial(block, j))
+
+            def clear(j=j):
+                rows = slice(j * BLK, (j + 1) * BLK)
+                dk_ref[rows, :] = jnp.zeros((BLK, 128), bf16)
+                dv_ref[rows, :] = jnp.zeros((BLK, 128), bf16)
+
+            pl.when(j * BLK >= len_ref[0])(clear)
+    dq_ref[...] = (dqa[...] * HD**-0.5).astype(bf16)
+
+
+def attend_bwd(arrays, context, lse, grad, length, causal, first, blocks):
+    seq = grad.shape[0]
+    widths = (384,) if causal else (128, 256)
+    vmem = pltpu.VMEM
+    return pl.pallas_call(
+        functools.partial(bwd_kernel, causal),
+        grid=(blocks,),
+        in_specs=[pl.BlockSpec(memory_space=pltpu.SMEM)]
+        + [columns(seq, w, first) for w in widths + (128, 128, 128)],
+        out_specs=[columns(seq, w) for w in widths],
+        out_shape=[jax.ShapeDtypeStruct((seq, w * blocks), bf16) for w in widths],
+        scratch_shapes=[
+            vmem((seq, 256), bf16),
+            vmem((2, seq, 128), bf16),
+            vmem((2, seq, 256), bf16),
+            vmem((seq, 256), bf16),
+            vmem((2, seq, 128), bf16),
+            vmem((2, seq, 256), bf16),
+            vmem((seq, 128), f32),
+        ],
+        compiler_params=pltpu.CompilerParams(vmem_limit_bytes=48 * 2**20),
+        cost_estimate=cost(5, blocks, seq, causal),
+        name="attend_causal_back" if causal else "attend_memory_back",
+    )(length, *arrays, context, lse, grad)
+
+
+def partner(bit):
+    d = lax.axis_index("dp")
+    t = lax.axis_index("tensor")
+    if bit == 0:
+        return (d, 1 - t)
+    size = 2 ** (bit - 1)
+    return (d + size * (1 - 2 * ((d // size) % 2)), t)
+
+
+X, CORE, Y, Z1, Z2 = range(5)
+STAGES = 7
+LINKS = (X, Y, Z1, Z2, Y, CORE, CORE)
+DELAY = 2
+SLOTS = 2 * DELAY
+
+
+def greet():
+    barrier = pltpu.get_barrier_semaphore()
+    for bit in range(5):
+        pl.semaphore_signal(barrier, inc=1, device_id=partner(bit), device_id_type=pl.DeviceIdType.MESH)
+    pl.semaphore_wait(barrier, 5)
+
+
+def sum_scratch(widths, chunk):
+    shapes = []
+    for w in widths:
+        shapes += [
+            pltpu.VMEM((2, SLOTS, chunk, 2 * w), bf16),
+            pltpu.VMEM((8, SLOTS, chunk, w), bf16),
+            pltpu.SemaphoreType.DMA((STAGES, SLOTS)),
+            pltpu.SemaphoreType.DMA((STAGES, SLOTS)),
+            pltpu.SemaphoreType.DMA((2, SLOTS)),
+        ]
+    return shapes
+
+
+def sum_step(t, chunks, chunk, tensors):
+    for stage in range(STAGES - 1, -1, -1):
+        c = t - DELAY * stage
+        pl.when((c >= 0) & (c < chunks))(functools.partial(sum_stage, stage, c, chunk, tensors))
+
+
+def sum_stage(stage, c, chunk, tensors):
+    slot = lax.rem(c, SLOTS)
+    rows = pl.ds(pl.multiple_of(c * chunk, chunk), chunk)
+    for oth, own, out, wide, narrow, send, recv, local in tensors:
+        w = narrow.shape[-1]
+        came, mine = wide.at[0, slot], wide.at[1, slot]
+        side, kept, got_y, s3, got_z, s4, got_zz, s5 = [narrow.at[i, slot] for i in range(8)]
+
+        def remote(k):
+            src, dst = (
+                (oth.at[rows], came),
+                (side, got_y),
+                (s3, got_z),
+                (s4, got_zz),
+                (s5, out.at[1, rows]),
+                (s5, out.at[2, rows]),
+                (out.at[1, rows], out.at[3, rows]),
+            )[k]
+            return pltpu.make_async_remote_copy(
+                src_ref=src,
+                dst_ref=dst,
+                send_sem=send.at[k, slot],
+                recv_sem=recv.at[k, slot],
+                device_id=partner(LINKS[k]),
+                device_id_type=pl.DeviceIdType.MESH,
+            )
+
+        def load():
+            return pltpu.make_async_copy(own.at[rows], mine, local.at[0, slot])
+
+        def keep():
+            return pltpu.make_async_copy(s5, out.at[0, rows], local.at[1, slot])
+
+        if stage == 0:
+            remote(0).start()
+            load().start()
+        elif stage == 1:
+            remote(0).wait()
+            load().wait()
+            v = came[...] + mine[...]
+            side[...] = v[:, w:]
+            kept[...] = v[:, :w]
+            remote(1).start()
+        elif stage == 2:
+            remote(1).wait()
+            s3[...] = kept[...] + got_y[...]
+            remote(2).start()
+        elif stage == 3:
+            remote(2).wait()
+            s4[...] = s3[...] + got_z[...]
+            remote(3).start()
+        elif stage == 4:
+            remote(3).wait()
+            s5[...] = s4[...] + got_zz[...]
+            remote(4).start()
+            remote(5).start()
+            keep().start()
+        elif stage == 5:
+            remote(4).wait()
+            remote(5).wait()
+            keep().wait()
+            remote(6).start()
+        else:
+            remote(6).wait()
+
+
+def sum_kernel(count, chunks, chunk, *refs):
+    ins, outs, scratch = refs[: 2 * count], refs[2 * count : 3 * count], refs[3 * count :]
+    tensors = [(ins[2 * i], ins[2 * i + 1], outs[i], *scratch[5 * i : 5 * i + 5]) for i in range(count)]
+    greet()
+
+    @pl.loop(0, chunks + DELAY * (STAGES - 1))
+    def _(t):
+        sum_step(t, chunks, chunk, tensors)
+
+
+def sum_all(pairs, ident, chunk=32):
+    rows = pairs[0][0].shape[0]
+    widths = [p[0].shape[1] // 2 for p in pairs]
+    anywhere = pl.BlockSpec(memory_space=pl.ANY)
+    return pl.pallas_call(
+        functools.partial(sum_kernel, len(pairs), rows // chunk, chunk),
+        in_specs=[anywhere] * (2 * len(pairs)),
+        out_specs=[anywhere] * len(pairs),
+        out_shape=[jax.ShapeDtypeStruct((4, rows, w), bf16) for w in widths],
+        scratch_shapes=sum_scratch(widths, chunk),
+        compiler_params=pltpu.CompilerParams(
+            collective_id=ident, has_side_effects=True, vmem_limit_bytes=48 * 2**20
+        ),
+        cost_estimate=pl.CostEstimate(flops=0, bytes_accessed=sum(widths) * rows * 16, transcendentals=0),
+        name="sum_gradients",
+    )(*[x for p in pairs for x in p])
+
+
+ALL = ("dp", "tensor")
+DEVICES = 32
+BOTH = (0, 1)
+
+
+def swap(x, flip):
+    return lax.ppermute(x, ALL, [(i, i ^ flip) for i in range(DEVICES)])
+
+
+def swap_tensor(x):
+    return swap(x, 1)
+
+
+def swap_core(x):
+    return swap(x, 2)
+
+
+def swap_y(x):
+    return swap(x, 4)
+
+
+def my_block():
+    d = lax.axis_index("dp")
+    return 2 * (d % 2) + (d // 2) % 2
+
+
+def add_low(*terms):
+    return sum(t.astype(f32) for t in terms).astype(bf16)
+
+
+def blocks_of(own, axis):
+    size = own.shape[axis] // 4
+    return [lax.dynamic_slice_in_dim(own, (my_block() ^ j) * size, size, axis) for j in range(4)]
+
+
+def swap_pieces(x, move):
+    return [move(p) for p in x] if isinstance(x, (list, tuple)) else move(x)
+
+
+def tie(*xs):
+    return lax.optimization_barrier(xs)
+
+
+class Pipe:
+    def __init__(self):
+        self.live = []
+
+    def put(self, gen):
+        wait, arrays = next(gen)
+        self.live.append([gen, wait, arrays])
+
+    def step(self, due, landed):
+        done = 0
+        for item in due:
+            arrays = landed[done : done + len(item[2])]
+            done += len(item[2])
+            try:
+                item[1], item[2] = item[0].send(arrays)
+            except StopIteration:
+                self.live.remove(item)
+
+    def cut(self, *xs):
+        due = []
+        for item in self.live:
+            item[1] -= 1
+            if item[1] <= 0:
+                due.append(item)
+        tied = tie(*xs, *[a for item in due for a in item[2]])
+        self.step(due, tied[len(xs) :])
+        return tied[: len(xs)] if len(xs) > 1 else tied[0]
+
+    def drain(self):
+        while self.live:
+            self.step(list(self.live), [a for item in self.live for a in item[2]])
+
+
+def fetch(out, key, block, waits):
+    far = swap_tensor(block)
+    (far,) = yield waits[0], [far]
+    side = swap_y(far)
+    near = swap_core(far)
+    side, near = yield waits[1], [side, near]
+    out[key] = [far, side, near, swap_core(side)]
+    return
+
+
+def assemble_kernel(axis, me_ref, x_ref, out_ref):
+    x = x_ref[...].astype(f32)
+    out_ref[...] = x.T if axis == 0 else x
+
+
+def assemble(blocks, axis, members=1):
+    _, rows, width = blocks.shape
+    tiles = 2
+    high = rows // tiles
+    narrow = width // members
+    if axis == 0:
+        out_spec = pl.BlockSpec((narrow, high), lambda b, m, t, me: (b ^ me[0], t))
+        shape = (4 * width, rows)
+    else:
+        out_spec = pl.BlockSpec((None, high, narrow), lambda b, m, t, me: (m, t, b ^ me[0]))
+        shape = (members, rows, narrow * 4)
+    return pl.pallas_call(
+        functools.partial(assemble_kernel, axis),
+        grid_spec=pltpu.PrefetchScalarGridSpec(
+            num_scalar_prefetch=1,
+            grid=(4, members, tiles),
+            in_specs=[pl.BlockSpec((None, high, narrow), lambda b, m, t, me: (b, t, m))],
+            out_specs=out_spec,
+        ),
+        out_shape=jax.ShapeDtypeStruct(shape, f32),
+        compiler_params=pltpu.CompilerParams(vmem_limit_bytes=40 * 2**20),
+        cost_estimate=pl.CostEstimate(flops=0, bytes_accessed=24 * rows * width, transcendentals=0),
+        name="assemble",
+    )(my_block().reshape(1), blocks)
+
+
+def core_sum(part):
+    send = [part(i, 2).astype(bf16) for i in BOTH]
+    got = [swap_core(x) for x in send]
+    keep = [add_low(part(i, 0), got[i]) for i in BOTH]
+    return keep[1], keep[0]
+
+
+def sum_small(out, x):
+    for flip in (1, 2, 4, 8, 16):
+        (other,) = yield 1, [swap(x, flip)]
+        x = x + other
+    out["small"] = x
+
+
+def ffn_kernel(h_ref, *refs):
+    ups, downs = refs[:4], refs[4:8]
+    a_ref, d_ref, b_ref = refs[8:]
+    h = h_ref[...]
+    size = ups[0].shape[1]
+    total = None
+    for j in range(4):
+        u = dot(h, ups[j][...])
+        cdf = 0.5 + 0.5 * lax.erf(u * (0.5**0.5))
+        slope = cdf + u * (jnp.exp(-0.5 * u * u) * 0.3989422804014327)
+        act = (u * cdf).astype(bf16)
+        cols = slice(j * size, (j + 1) * size)
+        a_ref[:, cols] = act
+        d_ref[:, cols] = slope.astype(bf16)
+        term = dot(act, downs[j][...])
+        total = term if total is None else total + term
+    b_ref[...] = total
+
+
+def whole(x):
+    return pl.BlockSpec(x.shape, lambda r: (0, 0))
+
+
+ROWS = 256
+
+
+def ffn_forward(h, ups, downs):
+    seq, width = h.shape
+    units = 4 * ups[0].shape[1]
+    rows = lambda w: pl.BlockSpec((ROWS, w), lambda r: (r, 0))
+    return pl.pallas_call(
+        ffn_kernel,
+        grid=(seq // ROWS,),
+        in_specs=[rows(width)] + [whole(x) for x in ups + downs],
+        out_specs=[rows(units), rows(units), rows(width)],
+        out_shape=[jax.ShapeDtypeStruct((seq, units), bf16)] * 2 + [jax.ShapeDtypeStruct((seq, width), f32)],
+        compiler_params=pltpu.CompilerParams(vmem_limit_bytes=50 * 2**20),
+        cost_estimate=pl.CostEstimate(flops=4 * seq * width * units, bytes_accessed=22 * 2**20, transcendentals=2 * seq * units),
+        name="feed_forward",
+    )(h, *ups, *downs)
+
+
+def ffn_back_kernel(g_ref, d_ref, *refs):
+    ups, downs = refs[:4], refs[4:8]
+    du_ref, dh_ref = refs[-2:]
+    g = g_ref[...]
+    size = ups[0].shape[1]
+    total = refs[8][...] if len(refs) > 10 else None
+    for j in range(4):
+        cols = slice(j * size, (j + 1) * size)
+        du = (dot(g, downs[j][...], NT) * d_ref[:, cols].astype(f32)).astype(bf16)
+        du_ref[:, cols] = du
+        term = dot(du, ups[j][...], NT)
+        total = term if total is None else total + term
+    dh_ref[...] = total
+
+
+def ffn_backward(g, slope, ups, downs, before=None):
+    seq, width = g.shape
+    units = slope.shape[1]
+    rows = lambda w: pl.BlockSpec((ROWS, w), lambda r: (r, 0))
+    extra = [] if before is None else [before]
+    return pl.pallas_call(
+        ffn_back_kernel,
+        grid=(seq // ROWS,),
+        in_specs=[rows(width), rows(units)] + [whole(x) for x in ups + downs] + [rows(width)] * len(extra),
+        out_specs=[rows(units), rows(width)],
+        out_shape=[jax.ShapeDtypeStruct((seq, units), bf16), jax.ShapeDtypeStruct((seq, width), f32)],
+        compiler_params=pltpu.CompilerParams(vmem_limit_bytes=50 * 2**20),
+        cost_estimate=pl.CostEstimate(flops=4 * seq * width * units, bytes_accessed=22 * 2**20, transcendentals=0),
+        name="feed_forward_back",
+    )(g, slope, *ups, *downs, *extra)
+
+
+def side_by_side(parts):
+    return jnp.concatenate(parts, axis=1)
+
+
+def cols(x, first, last, of=4):
+    size = x.shape[1] // of
+    return x[:, first * size : last * size]
+
+
+def one_pair_each(
+    target,
+    memory,
+    mem_len,
+    grad_out,
+    self_qkv,
+    self_out,
+    cross_query,
+    cross_kv,
+    cross_out,
+    ffn_up,
+    ffn_down,
+    ln_gain,
+    ln_bias,
+):
+    length = lax.dynamic_slice_in_dim(mem_len, lax.axis_index("tensor"), 1)
+    pipe = Pipe()
+    got = {}
+
+    qkv_b = [side_by_side(list(b)) for b in blocks_of(self_qkv, 2)]
+    pipe.put(fetch(got, "qkv", qkv_b[0], (1, 1)))
+    qkv_w = [side_by_side(qkv_b), None]
+    qkv = [dot(target, qkv_w[0]).astype(bf16), None]
+    at1 = [attend_fwd((qkv[0],), length, True), None]
+    so_b = blocks_of(self_out, 0)
+    kv_b = [side_by_side(list(b)) for b in blocks_of(cross_kv, 2)]
+    cq_b = blocks_of(cross_query, 1)
+    co_b = blocks_of(cross_out, 0)
+    kv_w = [side_by_side(kv_b), None]
+    mem, so_b[0], cq_b[0], co_b[0], _ = pipe.cut(memory, so_b[0], cq_b[0], co_b[0], at1[0][0])
+    kv = [dot(mem, kv_w[0]).astype(bf16), None]
+    pipe.put(fetch(got, "so", so_b[0], (2, 1)))
+    pipe.put(fetch(got, "cq", cq_b[0], (2, 1)))
+    tar, kv[0], kv_b[0] = pipe.cut(target, kv[0], kv_b[0])
+    qkv_w[1] = side_by_side(got["qkv"])
+    qkv[1] = dot(tar, qkv_w[1]).astype(bf16)
+    pipe.put(fetch(got, "kv", kv_b[0], (1, 1)))
+    pipe.put(fetch(got, "co", co_b[0], (2, 1)))
+    qkv[1], = tie(qkv[1])
+    at1[1] = attend_fwd((qkv[1],), length, True)
+    c1 = [at1[i][0] for i in BOTH]
+    up_b = blocks_of(ffn_up, 1)
+    down_b = blocks_of(ffn_down, 0)
+    c1[1], up_b[0] = pipe.cut(c1[1], up_b[0])
+    pipe.put(fetch(got, "up", up_b[0], (1, 1)))
+    c1[1] = pipe.cut(c1[1]) if False else c1[1]
+    so_w = [jnp.concatenate(so_b, axis=0), jnp.concatenate(got["so"], axis=0)] if "so" in got else None
+    if so_w is None:
+        c1[1] = pipe.cut(c1[1])
+        so_w = [jnp.concatenate(so_b, axis=0), jnp.concatenate(got["so"], axis=0)]
+    b1 = dot(c1[0], so_w[0]) + dot(c1[1], so_w[1])
+    h1, back1 = jax.vjp(norm_rows, alpha_res * target.astype(f32) + b1, ln_gain[0], ln_bias[0])
+    h1_low = h1.astype(bf16)
+    cq_w = [side_by_side(cq_b), side_by_side(got["cq"])]
+    q2 = [dot(h1_low, cq_w[i]).astype(bf16) for i in BOTH]
+    q2[0], down_b[0] = pipe.cut(q2[0], down_b[0])
+    pipe.put(fetch(got, "down", down_b[0], (1, 1)))
+    at2 = [attend_fwd((q2[0], kv[0]), length, False), None]
+    if "kv" not in got:
+        at2[0] = pipe.cut(*at2[0])
+    kv_w[1] = side_by_side(got["kv"])
+    kv[1] = dot(memory, kv_w[1]).astype(bf16)
+    at2[1] = attend_fwd((q2[1], kv[1]), length, False)
+    at2[1] = pipe.cut(*at2[1])
+    c2 = [at2[i][0] for i in BOTH]
+    co_w = [jnp.concatenate(co_b, axis=0), jnp.concatenate(got["co"], axis=0)]
+    b2 = dot(c2[0], co_w[0]) + dot(c2[1], co_w[1])
+    h2, back2 = jax.vjp(norm_rows, alpha_res * h1 + b2, ln_gain[1], ln_bias[1])
+    h2_low = h2.astype(bf16)
+    act0, slope0, b3 = ffn_forward(h2_low, up_b, down_b)
+    while "up" not in got or "down" not in got:
+        act0 = pipe.cut(act0)
+    h2_again, _ = tie(h2_low, act0)
+    act1, slope1, b3b = ffn_forward(h2_again, got["up"], got["down"])
+    act, slope = (act0, act1), (slope0, slope1)
+    result, back3 = jax.vjp(norm_rows, alpha_res * h2 + b3 + b3b, ln_gain[2], ln_bias[2])
+
+    dz3, gain3, bias3 = back3(grad_out.astype(f32))
+    g3 = dz3.astype(bf16)
+    out = {}
+    du1, dh2 = ffn_backward(g3, slope[1], got["up"], got["down"])
+    du0, dh2 = ffn_backward(g3, slope[0], up_b, down_b, dh2)
+    du = (du0, du1)
+    down_pair = core_sum(lambda i, f: dot(g3, cols(act[i], f, f + 2), TN))
+    up_pair = core_sum(lambda i, f: dot(h2_low, cols(du[i], f, f + 2), TN))
+    dz2, gain2, bias2 = back2(alpha_res * dz3 + dh2)
+    g2 = dz2.astype(bf16)
+    co_pair = core_sum(lambda i, f: dot(g2, cols(c2[i], f, f + 2), TN))
+    dc2 = [dot(g2, co_w[i], NT).astype(bf16) for i in BOTH]
+    p2 = {
+        (i, f): attend_bwd((q2[i], kv[i]), *at2[i], dc2[i], length, False, f, 2) for f in (2, 0) for i in (1, 0)
+    }
+    cq_pair = core_sum(lambda i, f: dot(h1_low, p2[i, f][0], TN))
+    kv_pair = core_sum(lambda i, f: dot(memory, p2[i, f][1], TN))
+    dq_terms = [(p2[i, f][0], cols(cq_w[i], f, f + 2)) for i in BOTH for f in (0, 2)]
+    dh1 = alpha_res * dz2 + sum(dot(x, w, NT) for x, w in dq_terms)
+    dz1, gain1, bias1 = back1(dh1)
+    g1 = dz1.astype(bf16)
+    pipe.put(sum_small(out, jnp.stack([gain1, gain2, gain3, bias1, bias2, bias3])))
+    so_pair = core_sum(lambda i, f: dot(g1, cols(c1[i], f, f + 2), TN))
+    dc1 = [dot(g1, so_w[i], NT).astype(bf16) for i in BOTH]
+    p1 = {}
+    for f in (2, 0):
+        for i in (1, 0):
+            dc1[i] = pipe.cut(dc1[i])
+            p1[i, f] = attend_bwd((qkv[i],), *at1[i], dc1[i], length, True, f, 2)
+            p1[i, f] = tie(*p1[i, f])
+    tar = pipe.cut(target)
+    qkv_pair = core_sum(lambda i, f: dot(tar, p1[i, f][0], TN))
+    dmem = sum(dot(p2[i, f][1], cols(kv_w[i], f, f + 2), NT) for i in BOTH for f in (0, 2)).astype(bf16)
+    dtar = alpha_res * dz1 + sum(dot(p1[i, f][0], cols(qkv_w[i], f, f + 2), NT) for i in BOTH for f in (0, 2))
+    dtar = dtar.astype(bf16)
+    pipe.drain()
+    qkv_t, so_t, cq_t, kv_t, co_t, up_t, down_t = sum_all(
+        [qkv_pair, so_pair, cq_pair, kv_pair, co_pair, up_pair, down_pair], 1
+    )
+    small = out["small"]
+    return (
+        result.astype(bf16),
+        dtar,
+        dmem,
+        assemble(qkv_t, 1, 3),
+        assemble(so_t, 0),
+        assemble(cq_t, 1)[0],
+        assemble(kv_t, 1, 2),
+        assemble(co_t, 0),
+        assemble(up_t, 1)[0],
+        assemble(down_t, 0),
+        small[:3],
+        small[3:],
+    )
+
+
 def solution(mesh):
     placed = (
         P(("dp", "tensor"), None),
@@ -355,8 +1047,9 @@
         P(),
         P(),
     )
+    body = one_pair_each if mesh.shape["tensor"] == 2 and mesh.shape["dp"] == 16 else on_device
     return jax.shard_map(
-        on_device,
+        body,
         mesh=mesh,
         in_specs=placed,
         out_specs=(

time: 2080 us -> 830 us (0.40)
  waiting for transfers between devices: 1040 us -> 45 us
  Pallas kernels: 0 us -> 491 us
  matrix products: 504 us -> 162 us
  local copies, waits for them, and re-layouts: 261 us -> 67.7 us
  other arithmetic: 209 us -> 29 us
  blocking collectives: 41.3 us -> 0 us
  starting transfers between devices: 1.27 us -> 27.2 us
    pallas_call x0 -> x24, Pallas kernels: none -> 491 us  [the longest x1 217 us: sum_all(): pl.pallas_call(functools.partial(sum_kernel, len(pairs), rows // chunk, c...]
    reduce_scatter x7 -> x0, waiting for transfers between devices: 471 us -> none  [the longest x3 296 us: scatter_branch(): lax.psum_scatter(partial_term(jnp.int32(0), row_count * lax.axis_size('te...]
    dot_general x80 -> x54, matrix products: 504 us -> 162 us  [dot(): return lax.dot_general(a, b, dims, preferred_element_type=f32)]
    all_gather x7 -> x0, waiting for transfers between devices: 336 us -> none  [the longest x4 208 us: gather_rows(): return lax.all_gather(local_rows, 'tensor', axis=0, tiled=True)]
    psum x1 -> x0, waiting for transfers between devices: 231 us -> none  [on_device(): lax.psum(self_qkv_grad.astype(jnp.bfloat16), 'dp').astype(jnp.float32)]
    convert_element_type x19 -> x5, other arithmetic: 108 us -> 5.22 us  [the longest x1 2.04 us: one_pair_each(): h2_low = h2.astype(bf16)]
    another operation x20 -> x1, local copies, waits for them, and re-layouts: 53 us -> 0.05 us  [one_pair_each(): jnp.stack([gain1, gain2, gain3, bias1, bias2, bias3])]
    while x224 -> x0, local copies, waits for them, and re-layouts: 50.1 us -> none
  transfers between devices with their start and end apart: 15 -> 47, of which waited for: 15 -> 8; matrix products, arithmetic and copies ran while one was open for 7% -> 20% of each run, Pallas kernels for 0% -> 14%
where the time goes in v1:
time: 830 us; the launch traced here: 824 us
  Pallas kernels  491 us (59%)
  matrix products  162 us (20%)
  local copies, waits for them, and re-layouts  67.7 us (8%)
  waiting for transfers between devices  45 us (5%)
  other arithmetic  29 us (3%)
  starting transfers between devices  27.2 us (3%)
    pallas_call x1, Pallas kernels, sum_all(): pl.pallas_call(functools.partial(sum_kernel, len(pairs), rows // chunk, c...  217 us
    dot_general x54, matrix products, dot(): return lax.dot_general(a, b, dims, preferred_element_type=f32)  162 us
    pallas_call x8, Pallas kernels, attend_bwd(): pl.pallas_call(functools.partial(bwd_kernel, causal), grid=(blocks,), in_...  120 us
    pallas_call x4, Pallas kernels, attend_fwd(): pl.pallas_call(functools.partial(fwd_kernel, causal), grid=(blocks,), in_...  56.9 us
    unnamed x292, local copies, waits for them, and re-layouts  55.2 us
    ppermute x47, waiting for transfers between devices, swap(): return lax.ppermute(x, ALL, [(i, i ^ flip) for i in range(DEVICES)])  45 us
    pallas_call x7, Pallas kernels, assemble(): pl.pallas_call(functools.partial(assemble_kernel, axis), grid_spec=pltpu....  34.4 us
    pallas_call x2, Pallas kernels, ffn_forward(): pl.pallas_call(ffn_kernel, grid=(seq // ROWS,), in_specs=[rows(width)] +...  32.3 us
  transfers between devices with their start and end apart: 47, of which 8 were waited for; matrix products, arithmetic and copies ran while one was open for 20% of the time, Pallas kernels for 14%

profile of v1, /device:TPU:0, one launch (start us, length us, event | category | flops | bytes accessed | tf_op | source)
XLA Modules:
  0.0 824.3 jit_solution(15912021530740964302)
XLA Ops:
  7.0 2.9 collective-permute-start
  32.9 6.1 fusion.6.refs_0_
  42.4 13.0 %attend_causal.2 = (bf16[1024,512]{1,0:T(8,128)(2,1)S(1)}, bf16[1024,512]{1,0:T(8,128)(2,1)S(1)}) custom-call(s32[1]{0:T(128)} %dynamic_slice.87.len_ref, bf16[1024,1536]{1,0:T(8,128)(2,1)S(1)} %fusion.6.refs_0_), custom_call_target="tpu_custom_call" | custom-call | flops 5368709120 | bytes 8388608 | tf_op jit(solution)/shard_map/attend_causal/pallas_call | solution.py:432
  59.7 5.2 convolution_convert_fusion.2.refs_1_
  65.8 9.9 %collective-permute-done.1 = bf16[1024,384]{1,0:T(8,128)(2,1)} collective-permute-done((bf16[1024,384]{1,0:T(8,128)(2,1)}, bf16[1024,384]{1,0:T(8,128)(2,1)}, u32[]{:S(2)}, u32[]{:S(2)}) %collective-permute-start.1) | collective-permute-done | bytes 786464 | tf_op jit(solution)/shard_map/ppermute | solution.py:693
  75.8 3.6 constant_dynamic-slice_fusion.3
  83.4 5.0 convolution_convert_fusion.1.refs_0_
  88.5 13.1 %attend_causal.3 = (bf16[1024,512]{1,0:T(8,128)(2,1)S(1)}, bf16[1024,512]{1,0:T(8,128)(2,1)S(1)}) custom-call(s32[1]{0:T(128)} %dynamic_slice.87.len_ref, bf16[1024,1536]{1,0:T(8,128)(2,1)S(1)} %convolution_convert_fusion.1.refs_0_), custom_call_target="tpu_custom_call" | custom-call | flops 5368709120 | bytes 8388608 | tf_op jit(solution)/shard_map/attend_causal/pallas_call | solution.py:432
  102.7 8.2 collective-permute-done.6
  115.8 4.6 collective-permute-done.7
  124.5 12.4 %collective-permute-done.9 = bf16[1024,128]{1,0:T(8,128)(2,1)S(1)} collective-permute-done((bf16[1024,128]{1,0:T(8,128)(2,1)S(1)}, bf16[1024,128]{1,0:T(8,128)(2,1)S(1)}, u32[]{:S(2)}, u32[]{:S(2)}) %collective-permute-start.9) | collective-permute-done | bytes 262176 | tf_op jit(solution)/shard_map/ppermute | solution.py:693
  151.1 3.4 convert_bitcast_fusion.refs_1_
  154.5 15.6 %attend_memory.3 = (bf16[1024,512]{1,0:T(8,128)(2,1)S(1)}, bf16[1024,512]{1,0:T(8,128)(2,1)S(1)}) custom-call(s32[1]{0:T(128)} %dynamic_slice.87.len_ref, bf16[1024,512]{1,0:T(8,128)(2,1)S(1)} %convolution_convert_fusion.11.refs_0_, bf16[1024,1024]{1,0:T(8,128)(2,1)S(1)} %convert_bitcast_fusion.refs_1_), custom_call_target="tpu_custom_call" | custom-call | flops 8589934592 | bytes 8388608 | tf_op jit(solution)/shard_map/attend_memory/pallas_call | solution.py:432
  179.8 15.2 %attend_memory.2 = (bf16[1024,512]{1,0:T(8,128)(2,1)S(1)}, bf16[1024,512]{1,0:T(8,128)(2,1)S(1)}) custom-call(s32[1]{0:T(128)} %dynamic_slice.87.len_ref, bf16[1024,512]{1,0:T(8,128)(2,1)S(1)} %copy-done.27, bf16[1024,1024]{1,0:T(8,128)(2,1)S(1)} %copy-done.30), custom_call_target="tpu_custom_call" | custom-call | flops 8589934592 | bytes 8388608 | tf_op jit(solution)/shard_map/attend_memory/pallas_call | solution.py:432
  200.7 3.0 fusion.188
  207.9 16.2 %feed_forward.2 = (bf16[1024,2048]{1,0:T(8,128)(2,1)}, bf16[1024,2048]{1,0:T(8,128)(2,1)}, f32[1024,1024]{1,0:T(8,128)}) custom-call(bf16[1024,1024]{1,0:T(8,128)(2,1)} %fusion.5.h_ref, bf16[1024,512]{1,0:T(8,128)(2,1)S(1)} %get-tuple-element.107.refs_0_, bf16[1024,512]{1,0:T(8,128)(2,1)S(1)} %get-tuple-element.218.refs_1_, ...), custom_call_target="tpu_custom_call" | custom-call | flops 8589934592 | bytes 23068672 | tf_op jit(solution)/shard_map/feed_forward/pallas_call | solution.py:848
  226.3 3.0 collective-permute-done.27.refs_7_
  229.3 16.1 %feed_forward.3 = (bf16[1024,2048]{1,0:T(8,128)(2,1)}, bf16[1024,2048]{1,0:T(8,128)(2,1)}, f32[1024,1024]{1,0:T(8,128)}) custom-call(bf16[1024,1024]{1,0:T(8,128)(2,1)} %fusion.5.h_ref, bf16[1024,512]{1,0:T(8,128)(2,1)S(1)} %collective-permute-done.14.refs_0_, bf16[1024,512]{1,0:T(8,128)(2,1)S(1)} %collective-permute-done.18.refs_1_, ...), custom_call_target="tpu_custom_call" | custom-call | flops 8589934592 | bytes 23068672 | tf_op jit(solution)/shard_map/feed_forward/pallas_call | solution.py:848
  245.4 5.5 fusion.183
  254.5 3.2 fusion.182
  260.4 14.5 %feed_forward_back.2 = (bf16[1024,2048]{1,0:T(8,128)(2,1)}, f32[1024,1024]{1,0:T(8,128)}) custom-call(bf16[1024,1024]{1,0:T(8,128)(2,1)} %add_convert_fusion.9.g_ref, bf16[1024,2048]{1,0:T(8,128)(2,1)} %get-tuple-element.137.d_ref, bf16[1024,512]{1,0:T(8,128)(2,1)S(1)} %collective-permute-done.14.refs_0_, ...), custom_call_target="tpu_custom_call" | custom-call | flops 8589934592 | bytes 23068672 | tf_op jit(solution)/shard_map/feed_forward_back/pallas_call | solution.py:880
  274.9 15.7 %feed_forward_back.3 = (bf16[1024,2048]{1,0:T(8,128)(2,1)}, f32[1024,1024]{1,0:T(8,128)}) custom-call(bf16[1024,1024]{1,0:T(8,128)(2,1)} %add_convert_fusion.9.g_ref, bf16[1024,2048]{1,0:T(8,128)(2,1)} %get-tuple-element.136.d_ref, bf16[1024,512]{1,0:T(8,128)(2,1)S(1)} %get-tuple-element.107.refs_0_, bf16[1024,512]{1,0:T(8,128)(2,1)S(1)} %get-tuple-element.218.refs_1_, ...), custom_call_target="tpu_custom_call" | custom-call | flops 8589934592 | bytes 23068672 | tf_op jit(solution)/shard_map/feed_forward_back/pallas_call | solution.py:880
  290.6 5.9 multiply_reduce_fusion
  300.4 3.3 convolution_convert_fusion.9.refs_4_
  309.1 18.9 %attend_memory_back.5 = (bf16[1024,256]{1,0:T(8,128)(2,1)S(1)}, bf16[1024,512]{1,0:T(8,128)(2,1)S(1)}) custom-call(s32[1]{0:T(128)} %dynamic_slice.87.len_ref, bf16[1024,512]{1,0:T(8,128)(2,1)S(1)} %copy-done.27, bf16[1024,1024]{1,0:T(8,128)(2,1)} %convolution_convert_fusion.2.refs_1_, bf16[1024,512]{1,0:T(8,128)(2,1)S(1)} %get-tuple-element.115.refs_2_, ...), custom_call_target="tpu_custom_call" | custom-call | flops 10737418240 | bytes 4194304 | tf_op jit(solution)/shard_map/attend_memory_back/pallas_call | solution.py:529
  328.1 19.3 %attend_memory_back.4 = (bf16[1024,256]{1,0:T(8,128)(2,1)S(1)}, bf16[1024,512]{1,0:T(8,128)(2,1)S(1)}) custom-call(s32[1]{0:T(128)} %dynamic_slice.87.len_ref, bf16[1024,512]{1,0:T(8,128)(2,1)S(1)} %copy-done.27, bf16[1024,1024]{1,0:T(8,128)(2,1)} %convolution_convert_fusion.2.refs_1_, bf16[1024,512]{1,0:T(8,128)(2,1)S(1)} %get-tuple-element.115.refs_2_, ...), custom_call_target="tpu_custom_call" | custom-call | flops 10737418240 | bytes 4194304 | tf_op jit(solution)/shard_map/attend_memory_back/pallas_call | solution.py:529
  348.3 18.9 %attend_memory_back.7 = (bf16[1024,256]{1,0:T(8,128)(2,1)S(1)}, bf16[1024,512]{1,0:T(8,128)(2,1)S(1)}) custom-call(s32[1]{0:T(128)} %dynamic_slice.87.len_ref, bf16[1024,512]{1,0:T(8,128)(2,1)S(1)} %convolution_convert_fusion.11.refs_0_, bf16[1024,1024]{1,0:T(8,128)(2,1)} %copy-done.31, bf16[1024,512]{1,0:T(8,128)(2,1)S(1)} %get-tuple-element.123.refs_2_, ...), custom_call_target="tpu_custom_call" | custom-call | flops 10737418240 | bytes 4194304 | tf_op jit(solution)/shard_map/attend_memory_back/pallas_call | solution.py:529
  368.5 19.5 %attend_memory_back.6 = (bf16[1024,256]{1,0:T(8,128)(2,1)S(1)}, bf16[1024,512]{1,0:T(8,128)(2,1)S(1)}) custom-call(s32[1]{0:T(128)} %dynamic_slice.87.len_ref, bf16[1024,512]{1,0:T(8,128)(2,1)S(1)} %copy-done.26, bf16[1024,1024]{1,0:T(8,128)(2,1)} %copy-done.31, bf16[1024,512]{1,0:T(8,128)(2,1)S(1)} %get-tuple-element.123.refs_2_, ...), custom_call_target="tpu_custom_call" | custom-call | flops 10737418240 | bytes 4194304 | tf_op jit(solution)/shard_map/attend_memory_back/pallas_call | solution.py:529
  388.0 5.6 fusion.49
  395.2 2.8 fusion.114
  399.6 2.9 fusion.118
  402.5 2.8 fusion.110
  406.4 6.0 multiply_reduce_fusion.1
  418.7 3.3 convolution_convert_fusion.8.refs_3_
  429.2 4.5 fusion.103
  433.7 3.7 fusion.43
  437.5 3.8 fusion.40
  441.2 4.2 fusion.46
  447.1 2.8 fusion.87
  452.7 2.8 add_convert_fusion.4
  457.6 10.9 %attend_causal_back.7 = bf16[1024,768]{1,0:T(8,128)(2,1)S(1)} custom-call(s32[1]{0:T(128)} %dynamic_slice.87.len_ref, bf16[1024,1536]{1,0:T(8,128)(2,1)} %copy-done.33, bf16[1024,512]{1,0:T(8,128)(2,1)S(1)} %copy-done.7, bf16[1024,512]{1,0:T(8,128)(2,1)S(1)} %copy-done.37, bf16[1024,512]{1,0:T(8,128)(2,1)S(1)} %copy-done.28), custom_call_target="tpu_custom_call" | custom-call | flops 6710886400 | bytes 4194304 | tf_op jit(solution)/shard_map/attend_causal_back/pallas_call | solution.py:529
  469.1 10.9 %attend_causal_back.5 = bf16[1024,768]{1,0:T(8,128)(2,1)S(1)} custom-call(s32[1]{0:T(128)} %dynamic_slice.87.len_ref, bf16[1024,1536]{1,0:T(8,128)(2,1)} %copy-done.32, bf16[1024,512]{1,0:T(8,128)(2,1)S(1)} %copy-done.18, bf16[1024,512]{1,0:T(8,128)(2,1)S(1)} %copy-done.35, bf16[1024,512]{1,0:T(8,128)(2,1)S(1)} %copy-done.29), custom_call_target="tpu_custom_call" | custom-call | flops 6710886400 | bytes 4194304 | tf_op jit(solution)/shard_map/attend_causal_back/pallas_call | solution.py:529
  480.0 5.3 fusion.190
  487.0 10.7 %attend_causal_back.6 = bf16[1024,768]{1,0:T(8,128)(2,1)S(1)} custom-call(s32[1]{0:T(128)} %dynamic_slice.87.len_ref, bf16[1024,1536]{1,0:T(8,128)(2,1)} %copy-done.33, bf16[1024,512]{1,0:T(8,128)(2,1)S(1)} %copy-done.7, bf16[1024,512]{1,0:T(8,128)(2,1)S(1)} %copy-done.37, bf16[1024,512]{1,0:T(8,128)(2,1)S(1)} %copy-done.28), custom_call_target="tpu_custom_call" | custom-call | flops 6710886400 | bytes 4194304 | tf_op jit(solution)/shard_map/attend_causal_back/pallas_call | solution.py:529
  497.7 5.2 fusion.62
  504.7 11.1 %attend_causal_back.4 = bf16[1024,768]{1,0:T(8,128)(2,1)S(1)} custom-call(s32[1]{0:T(128)} %dynamic_slice.87.len_ref, bf16[1024,1536]{1,0:T(8,128)(2,1)} %copy-done.32, bf16[1024,512]{1,0:T(8,128)(2,1)S(1)} %copy-done.18, bf16[1024,512]{1,0:T(8,128)(2,1)S(1)} %copy-done.35, bf16[1024,512]{1,0:T(8,128)(2,1)S(1)} %copy-done.29), custom_call_target="tpu_custom_call" | custom-call | flops 6710886400 | bytes 4194304 | tf_op jit(solution)/shard_map/attend_causal_back/pallas_call | solution.py:529
  515.9 3.4 fusion.189
  519.8 6.2 add_convert_fusion.5
  526.0 3.6 convolution_convert_fusion.3
  544.1 3.7 fusion.22.refs_7_
  550.7 3.1 add_convert_fusion.11.refs_0_
  553.8 3.1 add_convert_fusion.10.refs_1_
  556.9 3.8 add_convert_fusion.1.refs_12_
  560.7 3.8 add_convert_fusion.refs_13_
  564.5 4.0 add_convert_fusion.3.refs_10_
  568.5 3.8 add_convert_fusion.2.refs_11_
  572.3 216.7 %sum_gradients.1 = (bf16[4,1024,384]{2,1,0:T(8,128)(2,1)}, bf16[4,1024,128]{2,1,0:T(8,128)(2,1)S(1)}, bf16[4,1024,128]{2,1,0:T(8,128)(2,1)S(1)}, bf16[4,1024,256...) custom-call(bf16[1024,768]{1,0:T(8,128)(2,1)} %add_convert_fusion.11, ...), custom_call_target="tpu_custom_call" | custom-call | bytes 33554432 | tf_op jit(solution)/shard_map/sum_gradients/pallas_call | solution.py:673
  789.0 3.4 assemble.8
  792.4 3.0 assemble.9
  795.4 3.3 assemble.11
  798.8 9.0 %assemble.7 = f32[3,1024,512]{2,1,0:T(8,128)} custom-call(s32[1]{0:T(128)} %bitcast.34.me_ref, bf16[4,1024,384]{2,1,0:T(8,128)(2,1)S(1)} %copy-done.3), custom_call_target="tpu_custom_call" | custom-call | bytes 9437184 | tf_op jit(solution)/shard_map/assemble/pallas_call | solution.py:789
  807.8 6.1 assemble.10
  813.9 4.5 assemble.12
  818.9 5.1 assemble.13
  (446 shorter events, 151.5 us)
Async XLA Ops:
  0.6 59.1 %copy-start = (bf16[1024,1024]{1,0:T(8,128)(2,1)S(1)}, bf16[1024,1024]{1,0:T(8,128)(2,1)}, u32[]{:S(2)}) copy-start(bf16[1024,1024]{1,0:T(8,128)(2,1)} %param.14) | copy-start | bytes 6291460
  7.0 48.4 %collective-permute-start = (bf16[1024,384]{1,0:T(8,128)(2,1)}, bf16[1024,384]{1,0:T(8,128)(2,1)}, u32[]{:S(2)}, u32[]{:S(2)}) collective-permute-start(bf16[1024,384]{1,0:T(8,128)(2,1)} %pad_maximum_fusion.2), channel_id=1, source_target_pairs={{0,1},{1,0},{2,3},{3,2},{4,5},{5,4},{6,7},{7,6},{8,9},{9,8},{10,11... | collective-permute-start | bytes 2359304 | tf_op jit(solution)/shard_map/ppermute | solution.py:693
  14.2 44.7 %copy-start.72 = (bf16[1024,128]{1,0:T(8,128)(2,1)}, bf16[1024,128]{1,0:T(8,128)(2,1)S(1)}, u32[]{:S(2)}) copy-start(bf16[1024,128]{1,0:T(8,128)(2,1)S(1)} %get-tuple-element.209) | copy-start | bytes 786436
  55.4 66.8 %copy-start.17 = (bf16[1024,512]{1,0:T(8,128)(2,1)}, bf16[1024,512]{1,0:T(8,128)(2,1)S(1)}, u32[]{:S(2)}) copy-start(bf16[1024,512]{1,0:T(8,128)(2,1)S(1)} %get-tuple-element.92.refs_1_) | copy-start | bytes 3145732
  55.4 9.6 %collective-permute-start.2 = (bf16[1024,384]{1,0:T(8,128)(2,1)}, bf16[1024,384]{1,0:T(8,128)(2,1)S(1)}, u32[]{:S(2)}, u32[]{:S(2)}) collective-permute-start(bf16[1024,384]{1,0:T(8,128)(2,1)} %collective-permute-done), channel_id=1, source_target_pairs={{0,2},{1,3},{2,0},{3,1},{4,6},{5,7},{6,4},{7,5},{8,10},{9,11},{10,... | collective-permute-start | bytes 2359304 | tf_op jit(solution)/shard_map/ppermute | solution.py:693
  55.5 20.3 %collective-permute-start.1 = (bf16[1024,384]{1,0:T(8,128)(2,1)}, bf16[1024,384]{1,0:T(8,128)(2,1)}, u32[]{:S(2)}, u32[]{:S(2)}) collective-permute-start(bf16[1024,384]{1,0:T(8,128)(2,1)} %collective-permute-done), channel_id=1, source_target_pairs={{0,4},{1,5},{2,6},{3,7},{4,0},{5,1},{6,2},{7,3},{8,12},{9,13},{10,... | collective-permute-start | bytes 2359304 | tf_op jit(solution)/shard_map/ppermute | solution.py:693
  75.7 7.7 collective-permute-start.3
  79.4 23.3 %collective-permute-start.4 = (bf16[128,1024]{1,0:T(8,128)(2,1)}, bf16[128,1024]{1,0:T(8,128)(2,1)S(1)}, u32[]{:S(2)}, u32[]{:S(2)}) collective-permute-start(bf16[128,1024]{1,0:T(8,128)(2,1)} %get-tuple-element.93), channel_id=1, source_target_pairs={{0,1},{1,0},{2,3},{3,2},{4,5},{5,4},{6,7},{7,6},{8,9},{9,8},{10,11... | collective-permute-start | bytes 786440 | tf_op jit(solution)/shard_map/ppermute | solution.py:693
  79.7 23.0 %collective-permute-start.5 = (bf16[1024,128]{1,0:T(8,128)(2,1)S(1)}, bf16[1024,128]{1,0:T(8,128)(2,1)S(1)}, u32[]{:S(2)}, u32[]{:S(2)}) collective-permute-start(bf16[1024,128]{1,0:T(8,128)(2,1)S(1)} %copy-done.77), channel_id=1, source_target_pairs={{0,1},{1,0},{2,3},{3,2},{4,5},{5,4},{6,7},{7,6},{8,9},{9,8},{10,11... | collective-permute-start | bytes 786440 | tf_op jit(solution)/shard_map/ppermute | solution.py:693
  81.4 32.0 %collective-permute-start.13 = (bf16[128,1024]{1,0:T(8,128)(2,1)}, bf16[128,1024]{1,0:T(8,128)(2,1)}, u32[]{:S(2)}, u32[]{:S(2)}) collective-permute-start(bf16[128,1024]{1,0:T(8,128)(2,1)} %get-tuple-element.106), channel_id=1, source_target_pairs={{0,1},{1,0},{2,3},{3,2},{4,5},{5,4},{6,7},{7,6},{8,9},{9,8},{10,11... | collective-permute-start | bytes 786440 | tf_op jit(solution)/shard_map/ppermute | solution.py:693
  81.7 29.2 %collective-permute-start.6 = (bf16[1024,256]{1,0:T(8,128)(2,1)}, bf16[1024,256]{1,0:T(8,128)(2,1)}, u32[]{:S(2)}, u32[]{:S(2)}) collective-permute-start(bf16[1024,256]{1,0:T(8,128)(2,1)} %pad_maximum_fusion.3), channel_id=1, source_target_pairs={{0,1},{1,0},{2,3},{3,2},{4,5},{5,4},{6,7},{7,6},{8,9},{9,8},{10,11... | collective-permute-start | bytes 1572872 | tf_op jit(solution)/shard_map/ppermute | solution.py:693
  88.5 22.7 %copy-start.116 = (f32[3,1024]{1,0:T(4,128)S(1)}, f32[3,1024]{1,0:T(4,128)}, u32[]{:S(2)}) copy-start(f32[3,1024]{1,0:T(4,128)} %param.24) | copy-start | bytes 36868
  88.5 24.6 %copy-start.117 = (f32[3,1024]{1,0:T(4,128)S(1)}, f32[3,1024]{1,0:T(4,128)}, u32[]{:S(2)}) copy-start(f32[3,1024]{1,0:T(4,128)} %param.25) | copy-start | bytes 36868
  88.5 25.1 %copy-start.53 = (bf16[2048,1024]{1,0:T(8,128)(2,1)S(1)}, bf16[2048,1024]{1,0:T(8,128)(2,1)}, u32[]{:S(2)}) copy-start(bf16[2048,1024]{1,0:T(8,128)(2,1)} %param.23) | copy-start | bytes 12582916
  102.6 39.0 %copy-start.5 = (bf16[1024,512]{1,0:T(8,128)(2,1)}, bf16[1024,512]{1,0:T(8,128)(2,1)S(1)}, u32[]{:S(2)}) copy-start(bf16[1024,512]{1,0:T(8,128)(2,1)S(1)} %get-tuple-element.108.refs_1_) | copy-start | bytes 3145732
  102.6 46.2 %copy-start.97 = (bf16[1024,128]{1,0:T(8,128)(2,1)}, bf16[1024,128]{1,0:T(8,128)(2,1)S(1)}, u32[]{:S(2)}) copy-start(bf16[1024,128]{1,0:T(8,128)(2,1)S(1)} %collective-permute-done.5) | copy-start | bytes 786436
  110.9 26.0 %collective-permute-start.14 = (bf16[1024,512]{1,0:T(8,128)(2,1)S(1)}, bf16[1024,512]{1,0:T(8,128)(2,1)S(1)}, u32[]{:S(2)}, u32[]{:S(2)}) collective-permute-start(bf16[1024,512]{1,0:T(8,128)(2,1)S(1)} %get-tuple-element.107.refs_0_), channel_id=1, source_target_pairs={{0,1},{1,0},{2,3},{3,2},{4,5},{5,4},{6,7},{7,6},{8,9},{9,8},{10,11... | collective-permute-start | bytes 3145736 | tf_op jit(solution)/shard_map/ppermute | solution.py:693
  111.2 4.5 collective-permute-start.8
  111.2 9.2 %collective-permute-start.7 = (bf16[128,1024]{1,0:T(8,128)(2,1)S(1)}, bf16[128,1024]{1,0:T(8,128)(2,1)S(1)}, u32[]{:S(2)}, u32[]{:S(2)}) collective-permute-start(bf16[128,1024]{1,0:T(8,128)(2,1)S(1)} %collective-permute-done.4), channel_id=1, source_target_pairs={{0,4},{1,5},{2,6},{3,7},{4,0},{5,1},{6,2},{7,3},{8,12},{9,13},{10,... | collective-permute-start | bytes 786440 | tf_op jit(solution)/shard_map/ppermute | solution.py:693
  113.1 23.7 %collective-permute-start.12 = (bf16[1024,256]{1,0:T(8,128)(2,1)}, bf16[1024,256]{1,0:T(8,128)(2,1)S(1)}, u32[]{:S(2)}, u32[]{:S(2)}) collective-permute-start(bf16[1024,256]{1,0:T(8,128)(2,1)} %collective-permute-done.6), channel_id=1, source_target_pairs={{0,2},{1,3},{2,0},{3,1},{4,6},{5,7},{6,4},{7,5},{8,10},{9,11},{10,... | collective-permute-start | bytes 1572872 | tf_op jit(solution)/shard_map/ppermute | solution.py:693
  113.3 23.5 %collective-permute-start.11 = (bf16[1024,256]{1,0:T(8,128)(2,1)}, bf16[1024,256]{1,0:T(8,128)(2,1)S(1)}, u32[]{:S(2)}, u32[]{:S(2)}) collective-permute-start(bf16[1024,256]{1,0:T(8,128)(2,1)} %collective-permute-done.6), channel_id=1, source_target_pairs={{0,4},{1,5},{2,6},{3,7},{4,0},{5,1},{6,2},{7,3},{8,12},{9,13},{10,... | collective-permute-start | bytes 1572872 | tf_op jit(solution)/shard_map/ppermute | solution.py:693
  115.7 8.7 %collective-permute-start.10 = (bf16[1024,128]{1,0:T(8,128)(2,1)S(1)}, bf16[1024,128]{1,0:T(8,128)(2,1)S(1)}, u32[]{:S(2)}, u32[]{:S(2)}) collective-permute-start(bf16[1024,128]{1,0:T(8,128)(2,1)S(1)} %collective-permute-done.5), channel_id=1, source_target_pairs={{0,2},{1,3},{2,0},{3,1},{4,6},{5,7},{6,4},{7,5},{8,10},{9,11},{10,... | collective-permute-start | bytes 786440 | tf_op jit(solution)/shard_map/ppermute | solution.py:693
  120.4 16.4 %collective-permute-start.9 = (bf16[1024,128]{1,0:T(8,128)(2,1)S(1)}, bf16[1024,128]{1,0:T(8,128)(2,1)S(1)}, u32[]{:S(2)}, u32[]{:S(2)}) collective-permute-start(bf16[1024,128]{1,0:T(8,128)(2,1)S(1)} %collective-permute-done.5), channel_id=1, source_target_pairs={{0,4},{1,5},{2,6},{3,7},{4,0},{5,1},{6,2},{7,3},{8,12},{9,13},{10,... | collective-permute-start | bytes 786440 | tf_op jit(solution)/shard_map/ppermute | solution.py:693
  124.4 24.4 %copy-start.93 = (bf16[1024,128]{1,0:T(8,128)(2,1)}, bf16[1024,128]{1,0:T(8,128)(2,1)S(1)}, u32[]{:S(2)}) copy-start(bf16[1024,128]{1,0:T(8,128)(2,1)S(1)} %collective-permute-done.10) | copy-start | bytes 786436
  136.9 34.2 %collective-permute-start.17 = (bf16[128,1024]{1,0:T(8,128)(2,1)}, bf16[128,1024]{1,0:T(8,128)(2,1)S(1)}, u32[]{:S(2)}, u32[]{:S(2)}) collective-permute-start(bf16[128,1024]{1,0:T(8,128)(2,1)} %collective-permute-done.13), channel_id=1, source_target_pairs={{0,2},{1,3},{2,0},{3,1},{4,6},{5,7},{6,4},{7,5},{8,10},{9,11},{10,... | collective-permute-start | bytes 786440 | tf_op jit(solution)/shard_map/ppermute | solution.py:693
  136.9 34.2 %collective-permute-start.16 = (bf16[128,1024]{1,0:T(8,128)(2,1)}, bf16[128,1024]{1,0:T(8,128)(2,1)S(1)}, u32[]{:S(2)}, u32[]{:S(2)}) collective-permute-start(bf16[128,1024]{1,0:T(8,128)(2,1)} %collective-permute-done.13), channel_id=1, source_target_pairs={{0,4},{1,5},{2,6},{3,7},{4,0},{5,1},{6,2},{7,3},{8,12},{9,13},{10,... | collective-permute-start | bytes 786440 | tf_op jit(solution)/shard_map/ppermute | solution.py:693
  138.8 2.4 collective-permute-start.15
  140.6 8.0 collective-permute-start.20
  140.9 9.2 %collective-permute-start.21 = (bf16[1024,256]{1,0:T(8,128)(2,1)S(1)}, bf16[1024,256]{1,0:T(8,128)(2,1)S(1)}, u32[]{:S(2)}, u32[]{:S(2)}) collective-permute-start(bf16[1024,256]{1,0:T(8,128)(2,1)S(1)} %collective-permute-done.11), channel_id=1, source_target_pairs={{0,2},{1,3},{2,0},{3,1},{4,6},{5,7},{6,4},{7,5},{8,10},{9,11},{10,... | collective-permute-start | bytes 1572872 | tf_op jit(solution)/shard_map/ppermute | solution.py:693
  141.2 29.9 %collective-permute-start.19 = (bf16[1024,512]{1,0:T(8,128)(2,1)S(1)}, bf16[1024,512]{1,0:T(8,128)(2,1)S(1)}, u32[]{:S(2)}, u32[]{:S(2)}) collective-permute-start(bf16[1024,512]{1,0:T(8,128)(2,1)S(1)} %collective-permute-done.14.refs_0_), channel_id=1, source_target_pairs={{0,2},{1,3},{2,0},{3,1},{4,6},{5,7},{6,4},{7,5},{8,10},{9,11},{10,... | collective-permute-start | bytes 3145736 | tf_op jit(solution)/shard_map/ppermute | solution.py:693
  148.6 25.2 %collective-permute-start.18 = (bf16[1024,512]{1,0:T(8,128)(2,1)S(1)}, bf16[1024,512]{1,0:T(8,128)(2,1)S(1)}, u32[]{:S(2)}, u32[]{:S(2)}) collective-permute-start(bf16[1024,512]{1,0:T(8,128)(2,1)S(1)} %collective-permute-done.14.refs_0_), channel_id=1, source_target_pairs={{0,4},{1,5},{2,6},{3,7},{4,0},{5,1},{6,2},{7,3},{8,12},{9,13},{10,... | collective-permute-start | bytes 3145736 | tf_op jit(solution)/shard_map/ppermute | solution.py:693
  150.1 197.2 %copy-start.25 = (bf16[1024,512]{1,0:T(8,128)(2,1)}, bf16[1024,512]{1,0:T(8,128)(2,1)S(1)}, u32[]{:S(2)}) copy-start(bf16[1024,512]{1,0:T(8,128)(2,1)S(1)} %convolution_convert_fusion.11.refs_0_) | copy-start | bytes 3145732
  171.1 196.1 %copy-start.8 = (bf16[1024,512]{1,0:T(8,128)(2,1)}, bf16[1024,512]{1,0:T(8,128)(2,1)S(1)}, u32[]{:S(2)}) copy-start(bf16[1024,512]{1,0:T(8,128)(2,1)S(1)} %get-tuple-element.123.refs_2_) | copy-start | bytes 3145732
  173.8 24.0 %collective-permute-start.23 = (bf16[128,1024]{1,0:T(8,128)(2,1)S(1)}, bf16[128,1024]{1,0:T(8,128)(2,1)S(1)}, u32[]{:S(2)}, u32[]{:S(2)}) collective-permute-start(bf16[128,1024]{1,0:T(8,128)(2,1)S(1)} %collective-permute-done.16), channel_id=1, source_target_pairs={{0,2},{1,3},{2,0},{3,1},{4,6},{5,7},{6,4},{7,5},{8,10},{9,11},{10,... | collective-permute-start | bytes 786440 | tf_op jit(solution)/shard_map/ppermute | solution.py:693
  174.6 25.9 %collective-permute-start.22 = (bf16[512,1024]{1,0:T(8,128)(2,1)}, bf16[512,1024]{1,0:T(8,128)(2,1)}, u32[]{:S(2)}, u32[]{:S(2)}) collective-permute-start(bf16[512,1024]{1,0:T(8,128)(2,1)} %get-tuple-element.122.refs_4_), channel_id=1, source_target_pairs={{0,1},{1,0},{2,3},{3,2},{4,5},{5,4},{6,7},{7,6},{8,9},{9,8},{10,11... | collective-permute-start | bytes 3145736 | tf_op jit(solution)/shard_map/ppermute | solution.py:693
  176.0 50.3 %collective-permute-start.26 = (bf16[1024,512]{1,0:T(8,128)(2,1)S(1)}, bf16[1024,512]{1,0:T(8,128)(2,1)}, u32[]{:S(2)}, u32[]{:S(2)}) collective-permute-start(bf16[1024,512]{1,0:T(8,128)(2,1)S(1)} %collective-permute-done.18.refs_1_), channel_id=1, source_target_pairs={{0,2},{1,3},{2,0},{3,1},{4,6},{5,7},{6,4},{7,5},{8,10},{9,11},{10,... | collective-permute-start | bytes 3145736 | tf_op jit(solution)/shard_map/ppermute | solution.py:693
  195.0 133.0 %copy-start.19 = (bf16[1024,512]{1,0:T(8,128)(2,1)}, bf16[1024,512]{1,0:T(8,128)(2,1)S(1)}, u32[]{:S(2)}) copy-start(bf16[1024,512]{1,0:T(8,128)(2,1)S(1)} %get-tuple-element.115.refs_2_) | copy-start | bytes 3145732
  200.4 23.6 %collective-permute-start.25 = (bf16[512,1024]{1,0:T(8,128)(2,1)}, bf16[512,1024]{1,0:T(8,128)(2,1)}, u32[]{:S(2)}, u32[]{:S(2)}) collective-permute-start(bf16[512,1024]{1,0:T(8,128)(2,1)} %collective-permute-done.22.refs_4_), channel_id=1, source_target_pairs={{0,2},{1,3},{2,0},{3,1},{4,6},{5,7},{6,4},{7,5},{8,10},{9,11},{10,... | collective-permute-start | bytes 3145736 | tf_op jit(solution)/shard_map/ppermute | solution.py:693
  200.4 25.9 %collective-permute-start.24 = (bf16[512,1024]{1,0:T(8,128)(2,1)}, bf16[512,1024]{1,0:T(8,128)(2,1)}, u32[]{:S(2)}, u32[]{:S(2)}) collective-permute-start(bf16[512,1024]{1,0:T(8,128)(2,1)} %collective-permute-done.22.refs_4_), channel_id=1, source_target_pairs={{0,4},{1,5},{2,6},{3,7},{4,0},{5,1},{6,2},{7,3},{8,12},{9,13},{10,... | collective-permute-start | bytes 3145736 | tf_op jit(solution)/shard_map/ppermute | solution.py:693
  226.3 3.0 collective-permute-start.27
  328.0 96.1 %copy-start.23 = (bf16[1024,512]{1,0:T(8,128)(2,1)}, bf16[1024,512]{1,0:T(8,128)(2,1)S(1)}, u32[]{:S(2)}) copy-start(bf16[1024,512]{1,0:T(8,128)(2,1)S(1)} %get-tuple-element.156) | copy-start | bytes 3145732
  328.0 20.3 %copy-start.39 = (bf16[1024,512]{1,0:T(8,128)(2,1)S(1)}, bf16[1024,512]{1,0:T(8,128)(2,1)}, u32[]{:S(2)}) copy-start(bf16[1024,512]{1,0:T(8,128)(2,1)} %copy-done.38) | copy-start | bytes 3145732
  348.3 54.1 %copy-start.15 = (bf16[1024,256]{1,0:T(8,128)(2,1)}, bf16[1024,256]{1,0:T(8,128)(2,1)S(1)}, u32[]{:S(2)}) copy-start(bf16[1024,256]{1,0:T(8,128)(2,1)S(1)} %get-tuple-element.141) | copy-start | bytes 1572868
  368.4 58.5 %copy-start.10 = (bf16[1024,512]{1,0:T(8,128)(2,1)}, bf16[1024,512]{1,0:T(8,128)(2,1)S(1)}, u32[]{:S(2)}) copy-start(bf16[1024,512]{1,0:T(8,128)(2,1)S(1)} %get-tuple-element.158) | copy-start | bytes 3145732
  368.4 19.5 %copy-start.63 = (bf16[1024,1024]{1,0:T(8,128)(2,1)S(1)}, bf16[1024,1024]{1,0:T(8,128)(2,1)}, u32[]{:S(2)}) copy-start(bf16[1024,1024]{1,0:T(8,128)(2,1)} %add_convert_fusion.9.g_ref) | copy-start | bytes 6291460
  423.6 108.5 %collective-permute-start.41 = (bf16[1024,256]{1,0:T(8,128)(2,1)}, bf16[1024,256]{1,0:T(8,128)(2,1)}, u32[]{:S(2)}, u32[]{:S(2)}) collective-permute-start(bf16[1024,256]{1,0:T(8,128)(2,1)} %convolution_convert_fusion.14), channel_id=1, source_target_pairs={{0,2},{1,3},{2,0},{3,1},{4,6},{5,7},{6,4},{7,5},{8,10},{9,11},{10,... | collective-permute-start | bytes 1572872 | tf_op jit(solution)/shard_map/ppermute | solution.py:693
  423.6 110.9 %collective-permute-start.42 = (bf16[1024,256]{1,0:T(8,128)(2,1)}, bf16[1024,256]{1,0:T(8,128)(2,1)}, u32[]{:S(2)}, u32[]{:S(2)}) collective-permute-start(bf16[1024,256]{1,0:T(8,128)(2,1)} %convolution_convert_fusion.13), channel_id=1, source_target_pairs={{0,2},{1,3},{2,0},{3,1},{4,6},{5,7},{6,4},{7,5},{8,10},{9,11},{10,... | collective-permute-start | bytes 1572872 | tf_op jit(solution)/shard_map/ppermute | solution.py:693
  424.1 114.9 %collective-permute-start.38 = (bf16[1024,256]{1,0:T(8,128)(2,1)}, bf16[1024,256]{1,0:T(8,128)(2,1)}, u32[]{:S(2)}, u32[]{:S(2)}) collective-permute-start(bf16[1024,256]{1,0:T(8,128)(2,1)} %convolution_convert_fusion.15), channel_id=1, source_target_pairs={{0,2},{1,3},{2,0},{3,1},{4,6},{5,7},{6,4},{7,5},{8,10},{9,11},{10,... | collective-permute-start | bytes 1572872 | tf_op jit(solution)/shard_map/ppermute | solution.py:693
  426.4 116.8 %collective-permute-start.40 = (bf16[1024,512]{1,0:T(8,128)(2,1)}, bf16[1024,512]{1,0:T(8,128)(2,1)}, u32[]{:S(2)}, u32[]{:S(2)}) collective-permute-start(bf16[1024,512]{1,0:T(8,128)(2,1)} %fusion.70), channel_id=1, source_target_pairs={{0,2},{1,3},{2,0},{3,1},{4,6},{5,7},{6,4},{7,5},{8,10},{9,11},{10,... | collective-permute-start | bytes 3145736 | tf_op jit(solution)/shard_map/ppermute | solution.py:693
  445.5 11.7 %collective-permute-start.28 = (f32[6,1024]{1,0:T(8,128)S(1)}, f32[6,1024]{1,0:T(8,128)S(1)}, u32[]{:S(2)}, u32[]{:S(2)}) collective-permute-start(f32[6,1024]{1,0:T(8,128)S(1)} %stack.2), channel_id=1, source_target_pairs={{0,1},{1,0},{2,3},{3,2},{4,5},{5,4},{6,7},{7,6},{8,9},{9,8},{10,11... | collective-permute-start | bytes 73736 | tf_op jit(solution)/shard_map/ppermute | solution.py:693
  457.2 11.3 %collective-permute-start.29 = (f32[6,1024]{1,0:T(8,128)S(1)}, f32[6,1024]{1,0:T(8,128)S(1)}, u32[]{:S(2)}, u32[]{:S(2)}) collective-permute-start(f32[6,1024]{1,0:T(8,128)S(1)} %add.366), channel_id=1, source_target_pairs={{0,2},{1,3},{2,0},{3,1},{4,6},{5,7},{6,4},{7,5},{8,10},{9,11},{10,... | collective-permute-start | bytes 73736 | tf_op jit(solution)/shard_map/ppermute | solution.py:693
  468.5 16.8 %collective-permute-start.30 = (f32[6,1024]{1,0:T(8,128)S(1)}, f32[6,1024]{1,0:T(8,128)S(1)}, u32[]{:S(2)}, u32[]{:S(2)}) collective-permute-start(f32[6,1024]{1,0:T(8,128)S(1)} %add.367), channel_id=1, source_target_pairs={{0,4},{1,5},{2,6},{3,7},{4,0},{5,1},{6,2},{7,3},{8,12},{9,13},{10,... | collective-permute-start | bytes 73736 | tf_op jit(solution)/shard_map/ppermute | solution.py:693
  485.3 17.6 %collective-permute-start.31 = (f32[6,1024]{1,0:T(8,128)S(1)}, f32[6,1024]{1,0:T(8,128)S(1)}, u32[]{:S(2)}, u32[]{:S(2)}) collective-permute-start(f32[6,1024]{1,0:T(8,128)S(1)} %add.368), channel_id=1, source_target_pairs={{0,8},{1,9},{2,10},{3,11},{4,12},{5,13},{6,14},{7,15},{8,0},{9,1},... | collective-permute-start | bytes 73736 | tf_op jit(solution)/shard_map/ppermute | solution.py:693
  502.9 23.1 %collective-permute-start.32 = (f32[6,1024]{1,0:T(8,128)S(1)}, f32[6,1024]{1,0:T(8,128)S(1)}, u32[]{:S(2)}, u32[]{:S(2)}) collective-permute-start(f32[6,1024]{1,0:T(8,128)S(1)} %add.376), channel_id=1, source_target_pairs={{0,16},{1,17},{2,18},{3,19},{4,20},{5,21},{6,22},{7,23},{8,24},{9,... | collective-permute-start | bytes 73736 | tf_op jit(solution)/shard_map/ppermute | solution.py:693
  526.0 16.3 %collective-permute-start.37 = (bf16[1024,256]{1,0:T(8,128)(2,1)S(1)}, bf16[1024,256]{1,0:T(8,128)(2,1)S(1)}, u32[]{:S(2)}, u32[]{:S(2)}) collective-permute-start(bf16[1024,256]{1,0:T(8,128)(2,1)S(1)} %copy-done.123), channel_id=1, source_target_pairs={{0,2},{1,3},{2,0},{3,1},{4,6},{5,7},{6,4},{7,5},{8,10},{9,11},{10,... | collective-permute-start | bytes 1572872 | tf_op jit(solution)/shard_map/ppermute | solution.py:693
  532.1 4.6 collective-permute-start.35
  534.5 3.5 collective-permute-start.36
  536.7 11.1 %collective-permute-start.39 = (bf16[1024,512]{1,0:T(8,128)(2,1)S(1)}, bf16[1024,512]{1,0:T(8,128)(2,1)S(1)}, u32[]{:S(2)}, u32[]{:S(2)}) collective-permute-start(bf16[1024,512]{1,0:T(8,128)(2,1)S(1)} %copy-done.122), channel_id=1, source_target_pairs={{0,2},{1,3},{2,0},{3,1},{4,6},{5,7},{6,4},{7,5},{8,10},{9,11},{10,... | collective-permute-start | bytes 3145736 | tf_op jit(solution)/shard_map/ppermute | solution.py:693
  538.1 12.3 %collective-permute-start.33 = (bf16[1024,768]{1,0:T(8,128)(2,1)S(1)}, bf16[1024,768]{1,0:T(8,128)(2,1)S(1)}, u32[]{:S(2)}, u32[]{:S(2)}) collective-permute-start(bf16[1024,768]{1,0:T(8,128)(2,1)S(1)} %convolution_convert_fusion.4), channel_id=1, source_target_pairs={{0,2},{1,3},{2,0},{3,1},{4,6},{5,7},{6,4},{7,5},{8,10},{9,11},{10,... | collective-permute-start | bytes 4718600 | tf_op jit(solution)/shard_map/ppermute | solution.py:693
  539.6 17.2 %collective-permute-start.45 = (bf16[1024,1024]{1,0:T(8,128)(2,1)S(1)}, bf16[1024,1024]{1,0:T(8,128)(2,1)S(1)}, u32[]{:S(2)}, u32[]{:S(2)}) collective-permute-start(bf16[1024,1024]{1,0:T(8,128)(2,1)S(1)} %copy-done.121), channel_id=1, source_target_pairs={{0,2},{1,3},{2,0},{3,1},{4,6},{5,7},{6,4},{7,5},{8,10},{9,11},{10,... | collective-permute-start | bytes 6291464 | tf_op jit(solution)/shard_map/ppermute | solution.py:693
  542.3 11.5 %collective-permute-start.34 = (bf16[1024,768]{1,0:T(8,128)(2,1)S(1)}, bf16[1024,768]{1,0:T(8,128)(2,1)S(1)}, u32[]{:S(2)}, u32[]{:S(2)}) collective-permute-start(bf16[1024,768]{1,0:T(8,128)(2,1)S(1)} %convolution_convert_fusion.3), channel_id=1, source_target_pairs={{0,2},{1,3},{2,0},{3,1},{4,6},{5,7},{6,4},{7,5},{8,10},{9,11},{10,... | collective-permute-start | bytes 4718600 | tf_op jit(solution)/shard_map/ppermute | solution.py:693
  543.8 16.8 %collective-permute-start.46 = (bf16[1024,1024]{1,0:T(8,128)(2,1)S(1)}, bf16[1024,1024]{1,0:T(8,128)(2,1)S(1)}, u32[]{:S(2)}, u32[]{:S(2)}) collective-permute-start(bf16[1024,1024]{1,0:T(8,128)(2,1)S(1)} %copy-done.118), channel_id=1, source_target_pairs={{0,2},{1,3},{2,0},{3,1},{4,6},{5,7},{6,4},{7,5},{8,10},{9,11},{10,... | collective-permute-start | bytes 6291464 | tf_op jit(solution)/shard_map/ppermute | solution.py:693
  547.8 16.6 %collective-permute-start.43 = (bf16[1024,1024]{1,0:T(8,128)(2,1)S(1)}, bf16[1024,1024]{1,0:T(8,128)(2,1)S(1)}, u32[]{:S(2)}, u32[]{:S(2)}) collective-permute-start(bf16[1024,1024]{1,0:T(8,128)(2,1)S(1)} %copy-done.120), channel_id=1, source_target_pairs={{0,2},{1,3},{2,0},{3,1},{4,6},{5,7},{6,4},{7,5},{8,10},{9,11},{10,... | collective-permute-start | bytes 6291464 | tf_op jit(solution)/shard_map/ppermute | solution.py:693
  550.4 18.1 %collective-permute-start.44 = (bf16[1024,1024]{1,0:T(8,128)(2,1)S(1)}, bf16[1024,1024]{1,0:T(8,128)(2,1)S(1)}, u32[]{:S(2)}, u32[]{:S(2)}) collective-permute-start(bf16[1024,1024]{1,0:T(8,128)(2,1)S(1)} %copy-done.119), channel_id=1, source_target_pairs={{0,2},{1,3},{2,0},{3,1},{4,6},{5,7},{6,4},{7,5},{8,10},{9,11},{10,... | collective-permute-start | bytes 6291464 | tf_op jit(solution)/shard_map/ppermute | solution.py:693
  (116 other events, 509.9 us)

commit v2 on v1

--- a/solution.py
+++ b/solution.py
@@ -368,13 +368,8 @@
     return jnp.where(at == 0, hi, jnp.where(at == 1, mid, jnp.where(at == 2, lo, jnp.zeros_like(hi))))
 
 
-def fwd_kernel(causal, len_ref, *refs):
-    if causal:
-        qkv_ref, c_ref, lse_ref, kaug, vaug = refs
-        q_ref, k2, v2 = qkv_ref.at[:, :128], qkv_ref[:, 128:256], qkv_ref[:, 256:]
-    else:
-        q_ref, kv_ref, c_ref, lse_ref, kaug, vaug = refs
-        k2, v2 = kv_ref[:, :128], kv_ref[:, 128:]
+def fwd_kernel(causal, len_ref, q_ref, k_ref, v_ref, c_ref, lse_ref, kaug, vaug):
+    k2, v2 = k_ref[...], v_ref[...]
     seq = k2.shape[0]
     lane = lanes(seq)
     zero = jnp.zeros_like(k2)
@@ -421,52 +416,51 @@
     )
 
 
-def columns(seq, width, first=0):
-    return pl.BlockSpec((seq, width), lambda i: (0, i + first))
-
-
-def attend_fwd(arrays, length, causal):
-    seq = arrays[0].shape[0]
-    widths = (384,) if causal else (128, 256)
-    blocks = arrays[0].shape[1] // widths[0]
+def attend_fwd(q, k, v, length, causal):
+    seq, width = q.shape
+    spec = pl.BlockSpec((seq, 128), lambda i: (0, i))
     return pl.pallas_call(
         functools.partial(fwd_kernel, causal),
-        grid=(blocks,),
-        in_specs=[pl.BlockSpec(memory_space=pltpu.SMEM)] + [columns(seq, w) for w in widths],
-        out_specs=[columns(seq, 128)] * 2,
-        out_shape=[jax.ShapeDtypeStruct((seq, 128 * blocks), bf16)] * 2,
+        grid=(width // 128,),
+        in_specs=[pl.BlockSpec(memory_space=pltpu.SMEM)] + [spec] * 3,
+        out_specs=[spec] * 2,
+        out_shape=[jax.ShapeDtypeStruct((seq, width), bf16)] * 2,
         scratch_shapes=[pltpu.VMEM((2, seq, 256), bf16)] * 2,
         compiler_params=pltpu.CompilerParams(vmem_limit_bytes=48 * 2**20),
-        cost_estimate=cost(2, blocks, seq, causal),
+        cost_estimate=cost(2, width // 128, seq, causal),
         name="attend_causal" if causal else "attend_memory",
-    )(length, *arrays)
-
-
-def bwd_kernel(causal, len_ref, *refs):
-    if causal:
-        qkv_ref, c_ref, lse_ref, g_ref, d_ref, qs, qm, ka, gs, gm, va, dqa = refs
-        q2, k2, v2 = qkv_ref[:, :128], qkv_ref[:, 128:256], qkv_ref[:, 256:]
-        dq_ref, dk_ref, dv_ref = d_ref.at[:, :128], d_ref.at[:, 128:256], d_ref.at[:, 256:]
-    else:
-        q_ref, kv_ref, c_ref, lse_ref, g_ref, dq_ref, dkv_ref, qs, qm, ka, gs, gm, va, dqa = refs
-        q2, k2, v2 = q_ref[...], kv_ref[:, :128], kv_ref[:, 128:]
-        dk_ref, dv_ref = dkv_ref.at[:, :128], dkv_ref.at[:, 128:]
-    g2 = g_ref[...]
+    )(length, q, k, v)
+
+
+def back_scratch(seq):
+    vmem = pltpu.VMEM
+    return [
+        vmem((seq, 256), bf16),
+        vmem((2, seq, 128), bf16),
+        vmem((2, seq, 256), bf16),
+        vmem((seq, 256), bf16),
+        vmem((2, seq, 128), bf16),
+        vmem((2, seq, 256), bf16),
+        vmem((seq, 128), f32),
+    ]
+
+
+def back_pair(causal, length, q2, k2, v2, c2, aug, g2, grads, scratch, tick):
+    qs, qm, ka, gs, gm, va, dqa = scratch
     seq = k2.shape[0]
     lane = lanes(seq)
     l64 = lane % 64
     zero = jnp.zeros_like(k2)
     one = jnp.ones_like(k2)
     scale = jnp.asarray(HD**-0.5, bf16)
-    prod = c_ref[...].astype(f32) * g2.astype(f32)
+    prod = c2.astype(f32) * g2.astype(f32)
     d0 = jnp.sum(jnp.where(lane < 64, prod, 0.0), axis=1, keepdims=True)
     d1 = jnp.sum(jnp.where(lane < 64, 0.0, prod), axis=1, keepdims=True)
     qs[:, :128] = q2 * scale
-    aug = lse_ref[...]
     if not causal:
         aug = jnp.where(l64 == 3, one, aug)
         pos = lax.broadcasted_iota(jnp.int32, (seq, 128), 0)
-        bias = jnp.where(pos >= len_ref[0], -1e30, 0.0).astype(bf16)
+        bias = jnp.where(pos >= length, -1e30, 0.0).astype(bf16)
     qs[:, 128:] = aug
     gs[:, :128] = g2
     gs[:, 128:] = place3(-jnp.where(lane < 64, d0, d1), seq)
@@ -483,8 +477,8 @@
         va[h, :, :128] = jnp.where(own, v2, zero)
         va[h, :, 128:] = jnp.where(sel, one, zero)
     dqa[...] = jnp.zeros_like(dqa)
-
-    def block(j):
+    grads[:, 384:] = c2
+    for j in range(seq // BLK):
         rows = slice(j * BLK, (j + 1) * BLK)
         q0 = j * BLK if causal else 0
         dk = None
@@ -504,48 +498,23 @@
             dv = a if dv is None else dv + a
             dk = b if dk is None else dk + b
             dqa[q0:, :] += dot(ds, ka[h, rows, :128], TN)
-        dk_ref[rows, :] = dk.astype(bf16)
-        dv_ref[rows, :] = dv.astype(bf16)
-
-    for j in range(seq // BLK):
-        if causal:
-            block(j)
-        else:
-            pl.when(j * BLK < len_ref[0])(functools.partial(block, j))
-
-            def clear(j=j):
-                rows = slice(j * BLK, (j + 1) * BLK)
-                dk_ref[rows, :] = jnp.zeros((BLK, 128), bf16)
-                dv_ref[rows, :] = jnp.zeros((BLK, 128), bf16)
-
-            pl.when(j * BLK >= len_ref[0])(clear)
-    dq_ref[...] = (dqa[...] * HD**-0.5).astype(bf16)
-
-
-def attend_bwd(arrays, context, lse, grad, length, causal, first, blocks):
-    seq = grad.shape[0]
-    widths = (384,) if causal else (128, 256)
-    vmem = pltpu.VMEM
-    return pl.pallas_call(
-        functools.partial(bwd_kernel, causal),
-        grid=(blocks,),
-        in_specs=[pl.BlockSpec(memory_space=pltpu.SMEM)]
-        + [columns(seq, w, first) for w in widths + (128, 128, 128)],
-        out_specs=[columns(seq, w) for w in widths],
-        out_shape=[jax.ShapeDtypeStruct((seq, w * blocks), bf16) for w in widths],
-        scratch_shapes=[
-            vmem((seq, 256), bf16),
-            vmem((2, seq, 128), bf16),
-            vmem((2, seq, 256), bf16),
-            vmem((seq, 256), bf16),
-            vmem((2, seq, 128), bf16),
-            vmem((2, seq, 256), bf16),
-            vmem((seq, 128), f32),
-        ],
-        compiler_params=pltpu.CompilerParams(vmem_limit_bytes=48 * 2**20),
-        cost_estimate=cost(5, blocks, seq, causal),
-        name="attend_causal_back" if causal else "attend_memory_back",
-    )(length, *arrays, context, lse, grad)
+        grads[rows, 128:256] = dk.astype(bf16)
+        grads[rows, 256:384] = dv.astype(bf16)
+        tick(j)
+    grads[:, :128] = (dqa[...] * HD**-0.5).astype(bf16)
+
+
+BOTH = (0, 1)
+X, CORE, Y, Z1, Z2 = range(5)
+DELAY = 2
+SLOTS = 2 * DELAY
+CHUNK = 32
+SUBS = 8
+PAIRS_HERE = 4
+LEAD = SUBS
+HBM_LINKS = (X, Y, Z1, Z2, Y, CORE, CORE)
+PAIR_LINKS = (CORE, X, Y, Z1, Z2, Y, CORE, CORE)
+dma_sem = pltpu.SemaphoreType.DMA
 
 
 def partner(bit):
@@ -557,13 +526,6 @@
     return (d + size * (1 - 2 * ((d // size) % 2)), t)
 
 
-X, CORE, Y, Z1, Z2 = range(5)
-STAGES = 7
-LINKS = (X, Y, Z1, Z2, Y, CORE, CORE)
-DELAY = 2
-SLOTS = 2 * DELAY
-
-
 def greet():
     barrier = pltpu.get_barrier_semaphore()
     for bit in range(5):
@@ -571,122 +533,360 @@
     pl.semaphore_wait(barrier, 5)
 
 
-def sum_scratch(widths, chunk):
-    shapes = []
-    for w in widths:
-        shapes += [
-            pltpu.VMEM((2, SLOTS, chunk, 2 * w), bf16),
-            pltpu.VMEM((8, SLOTS, chunk, w), bf16),
-            pltpu.SemaphoreType.DMA((STAGES, SLOTS)),
-            pltpu.SemaphoreType.DMA((STAGES, SLOTS)),
-            pltpu.SemaphoreType.DMA((2, SLOTS)),
+def remote_copy(src, dst, send, recv, bit):
+    return pltpu.make_async_remote_copy(
+        src_ref=src,
+        dst_ref=dst,
+        send_sem=send,
+        recv_sem=recv,
+        device_id=partner(bit),
+        device_id_type=pl.DeviceIdType.MESH,
+    )
+
+
+def whole_scratch(w):
+    return [
+        pltpu.VMEM((2, SLOTS, CHUNK, 2 * w), bf16),
+        pltpu.VMEM((8, SLOTS, CHUNK, w), bf16),
+        dma_sem((7, SLOTS)),
+        dma_sem((7, SLOTS)),
+        dma_sem((2, SLOTS)),
+    ]
+
+
+def whole_stage(stage, c, oth, own, out, wide, narrow, send, recv, local):
+    slot = lax.rem(c, SLOTS)
+    rows = pl.ds(pl.multiple_of(c * CHUNK, CHUNK), CHUNK)
+    w = narrow.shape[-1]
+    came, mine = wide.at[0, slot], wide.at[1, slot]
+    side, kept, got_y, s3, got_z, s4, got_zz, s5 = [narrow.at[i, slot] for i in range(8)]
+
+    def remote(k):
+        src, dst = (
+            (oth.at[rows], came),
+            (side, got_y),
+            (s3, got_z),
+            (s4, got_zz),
+            (s5, out.at[1, rows]),
+            (s5, out.at[2, rows]),
+            (out.at[1, rows], out.at[3, rows]),
+        )[k]
+        return remote_copy(src, dst, send.at[k, slot], recv.at[k, slot], HBM_LINKS[k])
+
+    def load():
+        return pltpu.make_async_copy(own.at[rows], mine, local.at[0, slot])
+
+    def keep():
+        return pltpu.make_async_copy(s5, out.at[0, rows], local.at[1, slot])
+
+    if stage == 0:
+        remote(0).start()
+        load().start()
+    elif stage == 1:
+        remote(0).wait()
+        load().wait()
+        v = came[...] + mine[...]
+        side[...] = v[:, w:]
+        kept[...] = v[:, :w]
+        remote(1).start()
+    elif stage == 2:
+        remote(1).wait()
+        s3[...] = kept[...] + got_y[...]
+        remote(2).start()
+    elif stage == 3:
+        remote(2).wait()
+        s4[...] = s3[...] + got_z[...]
+        remote(3).start()
+    elif stage == 4:
+        remote(3).wait()
+        s5[...] = s4[...] + got_zz[...]
+        remote(4).start()
+        remote(5).start()
+        keep().start()
+    elif stage == 5:
+        remote(4).wait()
+        remote(5).wait()
+        keep().wait()
+        remote(6).start()
+    else:
+        remote(6).wait()
+
+
+def pair_scratch(w):
+    return [
+        pltpu.VMEM((2, 2, 2, 2, SUBS, CHUNK, w), bf16),
+        pltpu.VMEM((SLOTS, 2, 2, CHUNK, w), bf16),
+        pltpu.VMEM((3, SLOTS, 2, CHUNK, w), bf16),
+        pltpu.VMEM((6, SLOTS, CHUNK, w), bf16),
+        dma_sem((8, SLOTS)),
+        dma_sem((8, SLOTS)),
+        dma_sem((SLOTS,)),
+    ]
+
+
+def pair_stage(stage, c, out, prod, near, wide, narrow, send, recv, local):
+    d = lax.axis_index("dp")
+    core = d % 2
+    y = (d // 2) % 2
+    slot = lax.rem(c, SLOTS)
+    pair = c // SUBS
+    place = pair - jnp.where(pair > PAIRS_HERE, 1, 0)
+    sub = lax.rem(c, SUBS)
+    par = lax.rem(pair, 2)
+    away, came, own = [wide.at[i, slot] for i in range(3)]
+    got_y, s3, got_z, s4, got_zz, s5 = [narrow.at[i, slot] for i in range(6)]
+
+    def remote(k):
+        src, dst = (
+            (prod.at[par, :, 1 - core, :, sub], near.at[slot]),
+            (away, came),
+            (own.at[1 - y], got_y),
+            (s3, got_z),
+            (s4, got_zz),
+            (s5, out.at[place, core, y, sub]),
+            (s5, out.at[place, core, y, sub]),
+            (out.at[place, core, 1 - y, sub], out.at[place, core, 1 - y, sub]),
+        )[k]
+        return remote_copy(src, dst, send.at[k, slot], recv.at[k, slot], PAIR_LINKS[k])
+
+    def keep():
+        return pltpu.make_async_copy(s5, out.at[place, core, y, sub], local.at[slot])
+
+    if stage == 0:
+        remote(0).start()
+    elif stage == 1:
+        remote(0).wait()
+        away[...] = prod[par, 1, core, :, sub] + near[slot, 1]
+        own[...] = prod[par, 0, core, :, sub] + near[slot, 0]
+        remote(1).start()
+    elif stage == 2:
+        remote(1).wait()
+        own[...] = own[...] + came[...]
+        remote(2).start()
+    elif stage == 3:
+        remote(2).wait()
+        s3[...] = wide[2, slot, y] + got_y[...]
+        remote(3).start()
+    elif stage == 4:
+        remote(3).wait()
+        s4[...] = s3[...] + got_z[...]
+        remote(4).start()
+    elif stage == 5:
+        remote(4).wait()
+        s5[...] = s4[...] + got_zz[...]
+        remote(5).start()
+        remote(6).start()
+        keep().start()
+    elif stage == 6:
+        remote(5).wait()
+        remote(6).wait()
+        keep().wait()
+        remote(7).start()
+    else:
+        remote(7).wait()
+
+
+def small_scratch(shape):
+    return [pltpu.VMEM((6,) + shape, f32), pltpu.VMEM((5,) + shape, f32), dma_sem((5,)), dma_sem((5,))]
+
+
+def small_stage(k, out, acc, got, send, recv):
+    def remote(i):
+        return remote_copy(acc.at[i], got.at[i], send.at[i], recv.at[i], i)
+
+    if k > 0:
+        remote(k - 1).wait()
+        acc[k] = acc[k - 1] + got[k - 1]
+    if k < 5:
+        remote(k).start()
+    else:
+        out[...] = acc[5]
+
+
+HALF_STEPS = 2 * PAIRS_HERE
+BETWEEN = 4 * HALF_STEPS
+AFTER = BETWEEN + SUBS
+CHUNKS = 2 * PAIRS_HERE * SUBS + SUBS
+WHOLE = 1024 // CHUNK
+TICKS = CHUNKS + LEAD + 7 * DELAY
+TILE = 256
+
+
+def between_step(dq2, cq, so, gain_ref, sum_ref, base_ref, dz_ref, dc1, g1_t, acc, zt, bt, sems, tick):
+    def fetch_tile(a):
+        rows = pl.ds(a * TILE, TILE)
+        return [
+            pltpu.make_async_copy(sum_ref.at[rows], zt.at[a % 2], sems.at[0, a % 2]),
+            pltpu.make_async_copy(base_ref.at[rows], bt.at[a % 2], sems.at[1, a % 2]),
         ]
-    return shapes
-
-
-def sum_step(t, chunks, chunk, tensors):
-    for stage in range(STAGES - 1, -1, -1):
-        c = t - DELAY * stage
-        pl.when((c >= 0) & (c < chunks))(functools.partial(sum_stage, stage, c, chunk, tensors))
-
-
-def sum_stage(stage, c, chunk, tensors):
-    slot = lax.rem(c, SLOTS)
-    rows = pl.ds(pl.multiple_of(c * chunk, chunk), chunk)
-    for oth, own, out, wide, narrow, send, recv, local in tensors:
-        w = narrow.shape[-1]
-        came, mine = wide.at[0, slot], wide.at[1, slot]
-        side, kept, got_y, s3, got_z, s4, got_zz, s5 = [narrow.at[i, slot] for i in range(8)]
-
-        def remote(k):
-            src, dst = (
-                (oth.at[rows], came),
-                (side, got_y),
-                (s3, got_z),
-                (s4, got_zz),
-                (s5, out.at[1, rows]),
-                (s5, out.at[2, rows]),
-                (out.at[1, rows], out.at[3, rows]),
-            )[k]
-            return pltpu.make_async_remote_copy(
-                src_ref=src,
-                dst_ref=dst,
-                send_sem=send.at[k, slot],
-                recv_sem=recv.at[k, slot],
-                device_id=partner(LINKS[k]),
-                device_id_type=pl.DeviceIdType.MESH,
-            )
-
-        def load():
-            return pltpu.make_async_copy(own.at[rows], mine, local.at[0, slot])
-
-        def keep():
-            return pltpu.make_async_copy(s5, out.at[0, rows], local.at[1, slot])
-
-        if stage == 0:
-            remote(0).start()
-            load().start()
-        elif stage == 1:
-            remote(0).wait()
-            load().wait()
-            v = came[...] + mine[...]
-            side[...] = v[:, w:]
-            kept[...] = v[:, :w]
-            remote(1).start()
-        elif stage == 2:
-            remote(1).wait()
-            s3[...] = kept[...] + got_y[...]
-            remote(2).start()
-        elif stage == 3:
-            remote(2).wait()
-            s4[...] = s3[...] + got_z[...]
-            remote(3).start()
-        elif stage == 4:
-            remote(3).wait()
-            s5[...] = s4[...] + got_zz[...]
-            remote(4).start()
-            remote(5).start()
-            keep().start()
-        elif stage == 5:
-            remote(4).wait()
-            remote(5).wait()
-            keep().wait()
-            remote(6).start()
-        else:
-            remote(6).wait()
-
-
-def sum_kernel(count, chunks, chunk, *refs):
-    ins, outs, scratch = refs[: 2 * count], refs[2 * count : 3 * count], refs[3 * count :]
-    tensors = [(ins[2 * i], ins[2 * i + 1], outs[i], *scratch[5 * i : 5 * i + 5]) for i in range(count)]
-    greet()
-
-    @pl.loop(0, chunks + DELAY * (STAGES - 1))
-    def _(t):
-        sum_step(t, chunks, chunk, tensors)
-
-
-def sum_all(pairs, ident, chunk=32):
-    rows = pairs[0][0].shape[0]
-    widths = [p[0].shape[1] // 2 for p in pairs]
+
+    def put_tile(a):
+        return pltpu.make_async_copy(bt.at[a % 2], dz_ref.at[pl.ds(a * TILE, TILE)], sems.at[2, a % 2])
+
+    tiles = dc1.shape[1] // TILE
+    for copy in fetch_tile(0):
+        copy.start()
+    for a in range(tiles):
+        rows = slice(a * TILE, (a + 1) * TILE)
+        for copy in fetch_tile(a):
+            copy.wait()
+        if a >= 1:
+            put_tile(a - 1).wait()
+        if a + 1 < tiles:
+            for copy in fetch_tile(a + 1):
+                copy.start()
+        z = zt[a % 2]
+        dh = bt[a % 2]
+        for i in BOTH:
+            dh = dh + dot(dq2[i, rows, :], cq[i][...], NT)
+        centered = z - jnp.mean(z, axis=1, keepdims=True)
+        r = lax.rsqrt(jnp.mean(centered * centered, axis=1, keepdims=True) + norm_eps)
+        n = centered * r
+        acc[0, 0:1, :] = acc[0, 0:1, :] + jnp.sum(dh * n, axis=0, keepdims=True)
+        acc[0, 3:4, :] = acc[0, 3:4, :] + jnp.sum(dh, axis=0, keepdims=True)
+        e = dh * gain_ref[0:1, :]
+        dz = r * (e - jnp.mean(e, axis=1, keepdims=True) - n * jnp.mean(e * n, axis=1, keepdims=True))
+        bt[a % 2] = dz
+        put_tile(a).start()
+        g = dz.astype(bf16)
+        g1_t[:, rows] = g.T
+        for i in BOTH:
+            dc1[i, rows, :] = dot(g, so[i][...], NT).astype(bf16)
+        tick(BETWEEN + 2 * a)
+        tick(BETWEEN + 2 * a + 1)
+    put_tile(tiles - 1).wait()
+
+
+def back_kernel(*refs):
+    refs = list(refs)
+    take = lambda n: [refs.pop(0) for _ in range(n)]
+    (len_ref,) = take(1)
+    cross_in = [take(6) for _ in BOTH]
+    self_in = [take(5) for _ in BOTH]
+    h1_t, mem_t, g2_t, tar_t = take(4)
+    cq, so = take(2), take(2)
+    gain_ref, small_ref, sum_ref, base_ref = take(4)
+    down_in, up_in = take(2), take(2)
+    dk2_ref, dv2_ref, dq1_ref, dk1_ref, dv1_ref, dz_ref, pair_out, down_out, up_out, small_out = take(10)
+    grads, *scratch = take(8)
+    pair_refs = [pair_out] + take(7)
+    down_refs = down_in + [down_out] + take(5)
+    up_refs = up_in + [up_out] + take(5)
+    small_refs = [small_out] + take(4)
+    acc = small_refs[1]
+    dq2, dc1, g1_t, zt, bt, sems = take(6)
+    step = pl.program_id(0)
+    prod = pair_refs[1]
+
+    def tick(t):
+        for stage in range(7, -1, -1):
+            c = t - LEAD - DELAY * stage
+            real = (c >= 0) & (c < CHUNKS) & ((c < PAIRS_HERE * SUBS) | (c >= (PAIRS_HERE + 1) * SUBS))
+            pl.when(real)(functools.partial(pair_stage, stage, c, *pair_refs))
+        for first, whole_refs in ((0, down_refs), (WHOLE, up_refs)):
+            for stage in range(6, -1, -1):
+                c = t - first - DELAY * stage
+                pl.when((c >= 0) & (c < WHOLE))(functools.partial(whole_stage, stage, c, *whole_refs))
+        for k in range(5, -1, -1):
+            pl.when(t == AFTER + 2 * k)(functools.partial(small_stage, k, *small_refs))
+
+    half = lax.rem(step, 2)
+
+    def products(pair, spans):
+        par = lax.rem(pair, 2)
+        for a in range(4):
+            rows = slice(a * TILE, (a + 1) * TILE)
+            at = prod.at[par, half, a // 2, a % 2]
+            for left, lo, hi in spans:
+                at[:, :, lo:hi] = dot(left[rows, :], grads[:, lo:hi]).astype(bf16).reshape(SUBS, CHUNK, hi - lo)
+
+    @pl.when(step == 0)
+    def _():
+        greet()
+        acc[0] = small_ref[...]
+
+    @pl.when(step < HALF_STEPS)
+    def _():
+        pair = step // 2
+        q2, k2, v2, c2, aug, g2 = [jnp.where(half == 0, a[...], b[...]) for a, b in zip(*cross_in)]
+        back_pair(False, len_ref[0], q2, k2, v2, c2, aug, g2, grads, scratch, lambda j: tick(4 * step + j))
+        dq2[half, :, pl.ds(pl.multiple_of(pair * 128, 128), 128)] = grads[:, :128]
+        dk2_ref[...] = grads[:, 128:256]
+        dv2_ref[...] = grads[:, 256:384]
+        products(pair, ((h1_t, 0, 128), (mem_t, 128, 384), (g2_t, 384, 512)))
+
+    @pl.when(step == HALF_STEPS)
+    def _():
+        between_step(dq2, cq, so, gain_ref, sum_ref, base_ref, dz_ref, dc1, g1_t, acc, zt, bt, sems, tick)
+
+    @pl.when(step >= HALF_STEPS)
+    def _():
+        pair = step // 2 - PAIRS_HERE
+        q2, k2, v2, c2, aug = [jnp.where(half == 0, a[...], b[...]) for a, b in zip(*self_in)]
+        g2 = dc1[half, :, pl.ds(pl.multiple_of(pair * 128, 128), 128)]
+        back_pair(True, 0, q2, k2, v2, c2, aug, g2, grads, scratch, lambda j: tick(4 * step + SUBS + j))
+        dq1_ref[...] = grads[:, :128]
+        dk1_ref[...] = grads[:, 128:256]
+        dv1_ref[...] = grads[:, 256:384]
+        products(pair + PAIRS_HERE + 1, ((tar_t, 0, 384), (g1_t, 384, 512)))
+
+    @pl.when(step == 2 * HALF_STEPS - 1)
+    def _():
+        pl.loop(4 * 2 * HALF_STEPS + SUBS, TICKS)(tick)
+
+
+def attention_back(length, cross_in, self_in, lefts, cq, so, gain, small, sums, base, down, up):
+    seq, width = cross_in[0][0].shape
+    w = down[0].shape[1] // 2
+    low = lambda s: jnp.minimum(s, HALF_STEPS - 1)
+    high = lambda s: jnp.maximum(s - HALF_STEPS, 0)
+    cross_spec = pl.BlockSpec((seq, 128), lambda s: (0, low(s) // 2))
+    self_spec = pl.BlockSpec((seq, 128), lambda s: (0, high(s) // 2))
+    cross_out = pl.BlockSpec((None, seq, 128), lambda s: (low(s) % 2, 0, low(s) // 2))
+    self_out = pl.BlockSpec((None, seq, 128), lambda s: (high(s) % 2, 0, high(s) // 2))
     anywhere = pl.BlockSpec(memory_space=pl.ANY)
+    full = lambda x: pl.BlockSpec(x.shape, lambda s: (0, 0), pipeline_mode=pl.Buffered(1))
+    shape = jax.ShapeDtypeStruct
     return pl.pallas_call(
-        functools.partial(sum_kernel, len(pairs), rows // chunk, chunk),
-        in_specs=[anywhere] * (2 * len(pairs)),
-        out_specs=[anywhere] * len(pairs),
-        out_shape=[jax.ShapeDtypeStruct((4, rows, w), bf16) for w in widths],
-        scratch_shapes=sum_scratch(widths, chunk),
+        back_kernel,
+        grid=(2 * HALF_STEPS,),
+        in_specs=[pl.BlockSpec(memory_space=pltpu.SMEM)]
+        + [cross_spec] * 12
+        + [self_spec] * 10
+        + [full(x) for x in (*lefts, *cq, *so, gain, small)]
+        + [anywhere] * 6,
+        out_specs=[cross_out] * 2 + [self_out] * 3 + [anywhere] * 4 + [full(small)],
+        out_shape=[shape((2, seq, width), bf16)] * 5
+        + [
+            shape((seq, sums.shape[1]), f32),
+            shape((2 * PAIRS_HERE, 2, 2, SUBS, CHUNK, 512), bf16),
+            shape((4, seq, w), bf16),
+            shape((4, seq, w), bf16),
+            shape(small.shape, f32),
+        ],
+        scratch_shapes=[pltpu.VMEM((seq, 512), bf16)]
+        + back_scratch(seq)
+        + pair_scratch(512)
+        + whole_scratch(w) * 2
+        + small_scratch(small.shape)
+        + [
+            pltpu.VMEM((2, seq, width), bf16),
+            pltpu.VMEM((2, seq, width), bf16),
+            pltpu.VMEM((sums.shape[1], seq), bf16),
+            pltpu.VMEM((2, TILE, sums.shape[1]), f32),
+            pltpu.VMEM((2, TILE, sums.shape[1]), f32),
+            dma_sem((3, 2)),
+        ],
         compiler_params=pltpu.CompilerParams(
-            collective_id=ident, has_side_effects=True, vmem_limit_bytes=48 * 2**20
+            collective_id=1, has_side_effects=True, vmem_limit_bytes=60 * 2**20
         ),
-        cost_estimate=pl.CostEstimate(flops=0, bytes_accessed=sum(widths) * rows * 16, transcendentals=0),
-        name="sum_gradients",
-    )(*[x for p in pairs for x in p])
+        cost_estimate=cost(12, 8, seq, False),
+        name="attention_back",
+    )(length, *cross_in[0], *cross_in[1], *self_in[0], *self_in[1], *lefts, *cq, *so, gain, small, sums, base, *down, *up)
 
 
 ALL = ("dp", "tensor")
 DEVICES = 32
-BOTH = (0, 1)
 
 
 def swap(x, flip):
@@ -808,13 +1008,6 @@
     return keep[1], keep[0]
 
 
-def sum_small(out, x):
-    for flip in (1, 2, 4, 8, 16):
-        (other,) = yield 1, [swap(x, flip)]
-        x = x + other
-    out["small"] = x
-
-
 def ffn_kernel(h_ref, *refs):
     ups, downs = refs[:4], refs[4:8]
     a_ref, d_ref, b_ref = refs[8:]
@@ -896,6 +1089,86 @@
 def cols(x, first, last, of=4):
     size = x.shape[1] // of
     return x[:, first * size : last * size]
+
+
+def arrange_kernel(me_ref, *refs):
+    for j in range(4):
+
+        @pl.when(pl.program_id(0) == j)
+        def _(j=j):
+            refs[4][...] = refs[j][...]
+
+
+def arrange(slabs):
+    members, rows, width = slabs[0].shape
+    return pl.pallas_call(
+        arrange_kernel,
+        grid_spec=pltpu.PrefetchScalarGridSpec(
+            num_scalar_prefetch=1,
+            grid=(4,),
+            in_specs=[pl.BlockSpec((members, rows, width), lambda j, me: (0, 0, 0))] * 4,
+            out_specs=pl.BlockSpec((members, rows, width), lambda j, me: (0, j ^ me[0], 0)),
+        ),
+        out_shape=jax.ShapeDtypeStruct((members, 4 * rows, width), bf16),
+        compiler_params=pltpu.CompilerParams(vmem_limit_bytes=40 * 2**20),
+        cost_estimate=pl.CostEstimate(flops=0, bytes_accessed=16 * members * rows * width, transcendentals=0),
+        name="arrange",
+    )(my_block().reshape(1), *slabs)
+
+
+def slab_of(own):
+    rows = own.shape[1] // 4
+    return lax.dynamic_slice_in_dim(own, my_block() * rows, rows, 1)
+
+
+def spread_kernel(spans, x_ref, *out_refs):
+    for lo, hi, k, m in spans:
+        x = x_ref[:, lo:hi].astype(f32)
+        if m is None:
+            out_refs[k][...] = x.T
+        else:
+            out_refs[k][m] = x
+
+
+def spread(pairs, first, spans, outs):
+    _, rows, width = pairs.shape
+    tile = 512
+    specs = []
+    shapes = []
+    for members in outs:
+        if members is None:
+            specs.append(pl.BlockSpec((128, tile), lambda p, t: (p, t)))
+            shapes.append(jax.ShapeDtypeStruct((512, rows), f32))
+        else:
+            specs.append(pl.BlockSpec((members, tile, 128), lambda p, t: (0, t, p)))
+            shapes.append(jax.ShapeDtypeStruct((members, rows, 512), f32))
+    return pl.pallas_call(
+        functools.partial(spread_kernel, spans),
+        grid=(4, rows // tile),
+        in_specs=[pl.BlockSpec((None, tile, width), lambda p, t: (p + first, t, 0))],
+        out_specs=specs,
+        out_shape=shapes,
+        compiler_params=pltpu.CompilerParams(vmem_limit_bytes=40 * 2**20),
+        cost_estimate=pl.CostEstimate(flops=0, bytes_accessed=24 * rows * width, transcendentals=0),
+        name="spread",
+    )(pairs)
+
+
+def flip_kernel(x_ref, out_ref):
+    out_ref[...] = x_ref[...].T
+
+
+def flip(x):
+    rows, width = x.shape
+    return pl.pallas_call(
+        flip_kernel,
+        grid=(4,),
+        in_specs=[pl.BlockSpec((rows // 4, width), lambda i: (i, 0))],
+        out_specs=pl.BlockSpec((width, rows // 4), lambda i: (0, i)),
+        out_shape=jax.ShapeDtypeStruct((width, rows), x.dtype),
+        cost_estimate=pl.CostEstimate(flops=0, bytes_accessed=4 * rows * width, transcendentals=0),
+        name="flip",
+    )(x)
 
 
 def one_pair_each(
@@ -916,58 +1189,53 @@
     length = lax.dynamic_slice_in_dim(mem_len, lax.axis_index("tensor"), 1)
     pipe = Pipe()
     got = {}
-
-    qkv_b = [side_by_side(list(b)) for b in blocks_of(self_qkv, 2)]
-    pipe.put(fetch(got, "qkv", qkv_b[0], (1, 1)))
-    qkv_w = [side_by_side(qkv_b), None]
-    qkv = [dot(target, qkv_w[0]).astype(bf16), None]
-    at1 = [attend_fwd((qkv[0],), length, True), None]
-    so_b = blocks_of(self_out, 0)
-    kv_b = [side_by_side(list(b)) for b in blocks_of(cross_kv, 2)]
-    cq_b = blocks_of(cross_query, 1)
-    co_b = blocks_of(cross_out, 0)
-    kv_w = [side_by_side(kv_b), None]
-    mem, so_b[0], cq_b[0], co_b[0], _ = pipe.cut(memory, so_b[0], cq_b[0], co_b[0], at1[0][0])
-    kv = [dot(mem, kv_w[0]).astype(bf16), None]
-    pipe.put(fetch(got, "so", so_b[0], (2, 1)))
-    pipe.put(fetch(got, "cq", cq_b[0], (2, 1)))
-    tar, kv[0], kv_b[0] = pipe.cut(target, kv[0], kv_b[0])
-    qkv_w[1] = side_by_side(got["qkv"])
-    qkv[1] = dot(tar, qkv_w[1]).astype(bf16)
-    pipe.put(fetch(got, "kv", kv_b[0], (1, 1)))
-    pipe.put(fetch(got, "co", co_b[0], (2, 1)))
-    qkv[1], = tie(qkv[1])
-    at1[1] = attend_fwd((qkv[1],), length, True)
-    c1 = [at1[i][0] for i in BOTH]
+    so3, cq3, co3 = self_out[None], cross_query[None], cross_out[None]
+
+    pipe.put(fetch(got, "qkv", slab_of(self_qkv), (1, 1)))
+    q1 = [[dot(target, self_qkv[m]).astype(bf16) for m in range(3)], None]
+    at1 = [attend_fwd(*q1[0], length, True), None]
+    so_s, cq_s, kv_s, co_s = [slab_of(x) for x in (so3, cq3, cross_kv, co3)]
+    mem, so_s, cq_s, kv_s, _ = pipe.cut(memory, so_s, cq_s, kv_s, at1[0][0])
+    pipe.put(fetch(got, "so", so_s, (1, 1)))
+    pipe.put(fetch(got, "cq", cq_s, (1, 1)))
+    pipe.put(fetch(got, "kv", kv_s, (1, 1)))
+    kv = [[dot(mem, cross_kv[m]).astype(bf16) for m in range(2)], None]
     up_b = blocks_of(ffn_up, 1)
     down_b = blocks_of(ffn_down, 0)
-    c1[1], up_b[0] = pipe.cut(c1[1], up_b[0])
-    pipe.put(fetch(got, "up", up_b[0], (1, 1)))
-    c1[1] = pipe.cut(c1[1]) if False else c1[1]
-    so_w = [jnp.concatenate(so_b, axis=0), jnp.concatenate(got["so"], axis=0)] if "so" in got else None
-    if so_w is None:
-        c1[1] = pipe.cut(c1[1])
-        so_w = [jnp.concatenate(so_b, axis=0), jnp.concatenate(got["so"], axis=0)]
-    b1 = dot(c1[0], so_w[0]) + dot(c1[1], so_w[1])
-    h1, back1 = jax.vjp(norm_rows, alpha_res * target.astype(f32) + b1, ln_gain[0], ln_bias[0])
+    target_t = flip(target)
+    memory_t = flip(mem)
+    *_, up_b[0], co_s, target_t, memory_t = tie(*kv[0], *up_b[1:], *down_b, up_b[0], co_s, target_t, memory_t)
+    tar = pipe.cut(target)
+    qkv_oth = arrange(got["qkv"])
+    q1[1] = [dot(tar, qkv_oth[m]).astype(bf16) for m in range(3)]
+    pipe.put(fetch(got, "co", co_s, (1, 1)))
+    q1[1][0], up_b[0] = tie(q1[1][0], up_b[0])
+    pipe.put(fetch(got, "up", up_b[0], (2, 1)))
+    at1[1] = attend_fwd(*q1[1], length, True)
+    at1[1], _ = tie(at1[1], at1[1][0])
+    c1_oth = pipe.cut(at1[1][0])
+    c1 = [at1[0][0], c1_oth]
+    so_oth = arrange(got["so"])[0]
+    b1 = dot(c1[0], self_out) + dot(c1[1], so_oth)
+    h1 = norm_rows(alpha_res * target.astype(f32) + b1, ln_gain[0], ln_bias[0])
     h1_low = h1.astype(bf16)
-    cq_w = [side_by_side(cq_b), side_by_side(got["cq"])]
-    q2 = [dot(h1_low, cq_w[i]).astype(bf16) for i in BOTH]
-    q2[0], down_b[0] = pipe.cut(q2[0], down_b[0])
+    cq_oth = arrange(got["cq"])[0]
+    kv_oth = arrange(got["kv"])
+    q2 = [dot(h1_low, cross_query).astype(bf16), dot(h1_low, cq_oth).astype(bf16)]
+    kv[1] = [dot(memory, kv_oth[m]).astype(bf16) for m in range(2)]
+    q2[0], kv[1][0], down_b[0] = pipe.cut(q2[0], kv[1][0], down_b[0])
     pipe.put(fetch(got, "down", down_b[0], (1, 1)))
-    at2 = [attend_fwd((q2[0], kv[0]), length, False), None]
-    if "kv" not in got:
-        at2[0] = pipe.cut(*at2[0])
-    kv_w[1] = side_by_side(got["kv"])
-    kv[1] = dot(memory, kv_w[1]).astype(bf16)
-    at2[1] = attend_fwd((q2[1], kv[1]), length, False)
-    at2[1] = pipe.cut(*at2[1])
-    c2 = [at2[i][0] for i in BOTH]
-    co_w = [jnp.concatenate(co_b, axis=0), jnp.concatenate(got["co"], axis=0)]
-    b2 = dot(c2[0], co_w[0]) + dot(c2[1], co_w[1])
+    at2 = [attend_fwd(q2[0], *kv[0], length, False), None]
+    q2[1], _ = pipe.cut(q2[1], at2[0][0])
+    at2[1] = attend_fwd(q2[1], *kv[1], length, False)
+    co_oth = arrange(got["co"])[0]
+    c2 = [at2[0][0], at2[1][0]]
+    c2[1] = pipe.cut(c2[1])
+    b2 = dot(c2[0], cross_out) + dot(c2[1], co_oth)
     h2, back2 = jax.vjp(norm_rows, alpha_res * h1 + b2, ln_gain[1], ln_bias[1])
     h2_low = h2.astype(bf16)
     act0, slope0, b3 = ffn_forward(h2_low, up_b, down_b)
+    h1_t = flip(h1_low)
     while "up" not in got or "down" not in got:
         act0 = pipe.cut(act0)
     h2_again, _ = tie(h2_low, act0)
@@ -977,57 +1245,78 @@
 
     dz3, gain3, bias3 = back3(grad_out.astype(f32))
     g3 = dz3.astype(bf16)
-    out = {}
+
+    def down_part(i, f):
+        return dot(g3, cols(act[i], f, f + 2), TN)
+
+    down_send = [down_part(i, 2).astype(bf16) for i in BOTH]
+    g3, *down_send = tie(g3, *down_send)
+    down_got = [swap_core(x) for x in down_send]
     du1, dh2 = ffn_backward(g3, slope[1], got["up"], got["down"])
+    g3, dh2, *down_got = tie(g3, dh2, *down_got)
+    down_pair = (add_low(down_part(1, 0), down_got[1]), add_low(down_part(0, 0), down_got[0]))
     du0, dh2 = ffn_backward(g3, slope[0], up_b, down_b, dh2)
     du = (du0, du1)
-    down_pair = core_sum(lambda i, f: dot(g3, cols(act[i], f, f + 2), TN))
-    up_pair = core_sum(lambda i, f: dot(h2_low, cols(du[i], f, f + 2), TN))
+
+    def up_part(i, f):
+        return dot(h2_low, cols(du[i], f, f + 2), TN)
+
+    up_send = [up_part(i, 2).astype(bf16) for i in BOTH]
+    dh2, *up_send = tie(dh2, *up_send)
+    up_got = [swap_core(x) for x in up_send]
     dz2, gain2, bias2 = back2(alpha_res * dz3 + dh2)
     g2 = dz2.astype(bf16)
-    co_pair = core_sum(lambda i, f: dot(g2, cols(c2[i], f, f + 2), TN))
-    dc2 = [dot(g2, co_w[i], NT).astype(bf16) for i in BOTH]
-    p2 = {
-        (i, f): attend_bwd((q2[i], kv[i]), *at2[i], dc2[i], length, False, f, 2) for f in (2, 0) for i in (1, 0)
-    }
-    cq_pair = core_sum(lambda i, f: dot(h1_low, p2[i, f][0], TN))
-    kv_pair = core_sum(lambda i, f: dot(memory, p2[i, f][1], TN))
-    dq_terms = [(p2[i, f][0], cols(cq_w[i], f, f + 2)) for i in BOTH for f in (0, 2)]
-    dh1 = alpha_res * dz2 + sum(dot(x, w, NT) for x, w in dq_terms)
-    dz1, gain1, bias1 = back1(dh1)
-    g1 = dz1.astype(bf16)
-    pipe.put(sum_small(out, jnp.stack([gain1, gain2, gain3, bias1, bias2, bias3])))
-    so_pair = core_sum(lambda i, f: dot(g1, cols(c1[i], f, f + 2), TN))
-    dc1 = [dot(g1, so_w[i], NT).astype(bf16) for i in BOTH]
-    p1 = {}
-    for f in (2, 0):
-        for i in (1, 0):
-            dc1[i] = pipe.cut(dc1[i])
-            p1[i, f] = attend_bwd((qkv[i],), *at1[i], dc1[i], length, True, f, 2)
-            p1[i, f] = tie(*p1[i, f])
-    tar = pipe.cut(target)
-    qkv_pair = core_sum(lambda i, f: dot(tar, p1[i, f][0], TN))
-    dmem = sum(dot(p2[i, f][1], cols(kv_w[i], f, f + 2), NT) for i in BOTH for f in (0, 2)).astype(bf16)
-    dtar = alpha_res * dz1 + sum(dot(p1[i, f][0], cols(qkv_w[i], f, f + 2), NT) for i in BOTH for f in (0, 2))
-    dtar = dtar.astype(bf16)
-    pipe.drain()
-    qkv_t, so_t, cq_t, kv_t, co_t, up_t, down_t = sum_all(
-        [qkv_pair, so_pair, cq_pair, kv_pair, co_pair, up_pair, down_pair], 1
-    )
-    small = out["small"]
+    dc2 = [dot(g2, w, NT).astype(bf16) for w in (cross_out, co_oth)]
+    g2_t = flip(g2)
+    dc2[0], dc2[1], g2_t, *up_got = tie(*dc2, g2_t, *up_got)
+    up_pair = (add_low(up_part(1, 0), up_got[1]), add_low(up_part(0, 0), up_got[0]))
+    halves2 = [[q2[i], *kv[i], c2[i], at2[i][1], dc2[i]] for i in BOTH]
+    halves1 = [[*q1[i], c1[i], at1[i][1]] for i in BOTH]
+    none = jnp.zeros_like(gain2)
+    small = jnp.stack([none, gain2, gain3, none, bias2, bias3, none, none])
+    dk2, dv2, dq1, dk1, dv1, dz1, pairs, down_t, up_t, small = attention_back(
+        length,
+        halves2,
+        halves1,
+        [h1_t, memory_t, g2_t, target_t],
+        (cross_query, cq_oth),
+        (self_out, so_oth),
+        ln_gain,
+        small,
+        alpha_res * target.astype(f32) + b1,
+        alpha_res * dz2,
+        down_pair,
+        up_pair,
+    )
+    pairs = pairs.reshape(8, 1024, 512)
+    cross_pairs, self_pairs = (pairs, 0), (pairs, 4)
+    kv_both = (cross_kv, kv_oth)
+    dmem = sum(dot(d[i], kv_both[i][m], NT) for i in BOTH for m, d in enumerate((dk2, dv2)))
+    qkv_both = (self_qkv, qkv_oth)
+    dtar = alpha_res * dz1 + sum(dot(d[i], qkv_both[i][m], NT) for i in BOTH for m, d in enumerate((dq1, dk1, dv1)))
+    cq_total, kv_total, co_total = spread(
+        *cross_pairs,
+        ((0, 128, 0, 0), (128, 256, 1, 0), (256, 384, 1, 1), (384, 512, 2, None)),
+        (1, 2, None),
+    )
+    qkv_total, so_total = spread(
+        *self_pairs,
+        ((0, 128, 0, 0), (128, 256, 0, 1), (256, 384, 0, 2), (384, 512, 1, None)),
+        (3, None),
+    )
     return (
         result.astype(bf16),
-        dtar,
-        dmem,
-        assemble(qkv_t, 1, 3),
-        assemble(so_t, 0),
-        assemble(cq_t, 1)[0],
-        assemble(kv_t, 1, 2),
-        assemble(co_t, 0),
+        dtar.astype(bf16),
+        dmem.astype(bf16),
+        qkv_total,
+        so_total,
+        cq_total[0],
+        kv_total,
+        co_total,
         assemble(up_t, 1)[0],
         assemble(down_t, 0),
         small[:3],
-        small[3:],
+        small[3:6],
     )
 
 

time: 830 us -> 710 us (0.86)
  matrix products: 162 us -> 125 us
  local copies, waits for them, and re-layouts: 67.7 us -> 31 us
  Pallas kernels: 491 us -> 465 us
  starting transfers between devices: 27.2 us -> 18.4 us
    unnamed x292 -> x182, local copies, waits for them, and re-layouts: 55.2 us -> 14.9 us
    dot_general x54 -> x36, matrix products: 162 us -> 125 us  [dot(): return lax.dot_general(a, b, dims, preferred_element_type=f32)]
    pallas_call x7 -> x2, Pallas kernels: 34.4 us -> 9.62 us  [assemble(): pl.pallas_call(functools.partial(assemble_kernel, axis), grid_spec=pltpu....]
    ppermute x47 -> x32, starting transfers between devices: 27.2 us -> 18.4 us  [swap(): return lax.ppermute(x, ALL, [(i, i ^ flip) for i in range(DEVICES)])]
    ppermute x47 -> x32, waiting for transfers between devices: 45 us -> 39 us  [swap(): return lax.ppermute(x, ALL, [(i, i ^ flip) for i in range(DEVICES)])]
    pallas_call x13 -> x16, Pallas kernels: 394 us -> 393 us  [the longest x1 305 us: attention_back(): pl.pallas_call(back_kernel, grid=(2 * HALF_STEPS,), in_specs=[pl.BlockSpe...]
  transfers between devices with their start and end apart: 47 -> 32, of which waited for: 8 -> 8; matrix products, arithmetic and copies ran while one was open for 20% -> 11% of each run, Pallas kernels for 14% -> 16%
where the time goes in v2:
time: 710 us; the launch traced here: 707 us
  Pallas kernels  465 us (65%)
  matrix products  125 us (18%)
  waiting for transfers between devices  39 us (5%)
  local copies, waits for them, and re-layouts  31 us (4%)
  other arithmetic  26 us (4%)
  starting transfers between devices  18.4 us (3%)
    pallas_call x1, Pallas kernels, attention_back(): pl.pallas_call(back_kernel, grid=(2 * HALF_STEPS,), in_specs=[pl.BlockSpe...  305 us
    dot_general x36, matrix products, dot(): return lax.dot_general(a, b, dims, preferred_element_type=f32)  125 us
    pallas_call x4, Pallas kernels, attend_fwd(): pl.pallas_call(functools.partial(fwd_kernel, causal), grid=(width // 128,...  57.5 us
    ppermute x32, waiting for transfers between devices, swap(): return lax.ppermute(x, ALL, [(i, i ^ flip) for i in range(DEVICES)])  39 us
    pallas_call x2, Pallas kernels, ffn_forward(): pl.pallas_call(ffn_kernel, grid=(seq // ROWS,), in_specs=[rows(width)] +...  32.5 us
    pallas_call x2, Pallas kernels, ffn_backward(): pl.pallas_call(ffn_back_kernel, grid=(seq // ROWS,), in_specs=[rows(width...  30.3 us
    ppermute x32, starting transfers between devices, swap(): return lax.ppermute(x, ALL, [(i, i ^ flip) for i in range(DEVICES)])  18.4 us
    pallas_call x4, Pallas kernels, flip(): pl.pallas_call(flip_kernel, grid=(4,), in_specs=[pl.BlockSpec((rows // 4,...  16.9 us
  transfers between devices with their start and end apart: 32, of which 8 were waited for; matrix products, arithmetic and copies ran while one was open for 11% of the time, Pallas kernels for 16%

profile of v2, /device:TPU:0, one launch (start us, length us, event | category | flops | bytes accessed | tf_op | source)
XLA Modules:
  0.0 706.7 jit_solution(13386709489207726741)
XLA Ops:
  0.7 2.1 constant_dynamic-slice_fusion.8
  2.9 2.9 collective-permute-start
  5.8 3.2 convolution_convert_fusion.13.q_ref.refs_13_
  9.1 3.8 convolution_convert_fusion.12.k_ref.refs_14_
  18.7 3.2 convolution_convert_fusion.11.v_ref.refs_15_
  22.0 13.4 %attend_causal.2 = (bf16[1024,512]{1,0:T(8,128)(2,1)S(1)}, bf16[1024,512]{1,0:T(8,128)(2,1)S(1)}) custom-call(s32[1]{0:T(128)} %dynamic_slice.42.len_ref.refs_0_, bf16[1024,512]{1,0:T(8,128)(2,1)S(1)} %convolution_convert_fusion.13.q_ref.refs_13_, bf16[1024,512]{1,0:T(8,128)(2,1)S(1)} %copy-done.27, ...), custom_call_target="tpu_custom_call" | custom-call | flops 5368709120 | bytes 8388608 | tf_op jit(solution)/shard_map/attend_causal/pallas_call | solution.py:422
  38.4 3.3 fusion.110
  43.7 4.0 constant_dynamic-slice_fusion
  47.7 2.1 constant_dynamic-slice_fusion.1
  49.9 8.5 %collective-permute-done.3.refs_0_ = bf16[1,128,1024]{2,1,0:T(8,128)(2,1)S(1)} collective-permute-done((bf16[1,128,1024]{2,1,0:T(8,128)(2,1)}, bf16[1,128,1024]{2,1,0:T(8,128)(2,1)S(1)}, u32[]{:S(2)}, u32[]{:S(2)}) %collective-permute-start.3) | collective-permute-done | bytes 262176 | tf_op jit(solution)/shard_map/ppermute | solution.py:893
  58.4 5.2 collective-permute-done.4.refs_0_
  64.4 4.1 flip.4.refs_26_
  68.6 4.1 flip.5.refs_24_
  72.7 3.2 convolution_convert_fusion.9.k_ref.refs_2_
  80.2 2.2 arrange.5
  87.0 13.5 %attend_causal.3 = (bf16[1024,512]{1,0:T(8,128)(2,1)S(1)}, bf16[1024,512]{1,0:T(8,128)(2,1)S(1)}) custom-call(s32[1]{0:T(128)} %dynamic_slice.42.len_ref.refs_0_, bf16[1024,512]{1,0:T(8,128)(2,1)S(1)} %convolution_convert_fusion.10.q_ref.refs_18_, bf16[1024,512]{1,0:T(8,128)(2,1)S(1)} %convolution_convert_fusion.7.k_ref.refs_19_, ...), custom_call_target="tpu_custom_call" | custom-call | flops 5368709120 | bytes 8388608 | tf_op jit(solution)/shard_map/attend_causal/pallas_call | solution.py:422
  100.6 2.6 collective-permute-done.9.refs_1_
  106.1 4.8 fusion.108
  119.7 9.8 %collective-permute-done.18.refs_0_ = bf16[1024,512]{1,0:T(8,128)(2,1)S(1)} collective-permute-done((bf16[1024,512]{1,0:T(8,128)(2,1)S(1)}, bf16[1024,512]{1,0:T(8,128)(2,1)S(1)}, u32[]{:S(2)}, u32[]{:S(2)}) %collective-permute-start.18) | collective-permute-done | bytes 1048608 | tf_op jit(solution)/shard_map/ppermute | solution.py:893
  134.2 15.5 %attend_memory.2 = (bf16[1024,512]{1,0:T(8,128)(2,1)S(1)}, bf16[1024,512]{1,0:T(8,128)(2,1)S(1)}) custom-call(s32[1]{0:T(128)} %dynamic_slice.42.len_ref.refs_0_, bf16[1024,512]{1,0:T(8,128)(2,1)S(1)} %convolution_convert_fusion.5.q_ref.refs_1_, bf16[1024,512]{1,0:T(8,128)(2,1)S(1)} %convolution_convert_fusion.9.k_ref.refs_2_, ...), custom_call_target="tpu_custom_call" | custom-call | flops 8589934592 | bytes 8388608 | tf_op jit(solution)/shard_map/attend_memory/pallas_call | solution.py:422
  149.7 4.3 collective-permute-done.20.refs_1_
  154.0 2.8 collective-permute-done.22.refs_4_
  157.2 3.3 fusion.111
  161.3 15.3 %attend_memory.3 = (bf16[1024,512]{1,0:T(8,128)(2,1)S(1)}, bf16[1024,512]{1,0:T(8,128)(2,1)S(1)}) custom-call(s32[1]{0:T(128)} %dynamic_slice.42.len_ref.refs_0_, bf16[1024,512]{1,0:T(8,128)(2,1)S(1)} %convolution_convert_fusion.4.q_ref.refs_7_, bf16[1024,512]{1,0:T(8,128)(2,1)S(1)} %fusion.40.k_ref.refs_8_, bf16[1024,512]{1,0:T(8,128)(2,1)S(1)} %fusion.41.v_ref.refs_9_), custom_call_target="tpu_custom_call" | custom-call | flops 8589934592 | bytes 8388608 | tf_op jit(solution)/shard_map/attend_memory/pallas_call | solution.py:422
  176.6 5.3 collective-permute-done.23.refs_5_
  181.9 5.3 fusion.109
  189.2 2.0 fusion.4.h_ref
  191.3 16.3 %feed_forward.2 = (bf16[1024,2048]{1,0:T(8,128)(2,1)}, bf16[1024,2048]{1,0:T(8,128)(2,1)}, f32[1024,1024]{1,0:T(8,128)}) custom-call(bf16[1024,1024]{1,0:T(8,128)(2,1)} %fusion.4.h_ref, bf16[1024,512]{1,0:T(8,128)(2,1)S(1)} %get-tuple-element.121.refs_0_, bf16[1024,512]{1,0:T(8,128)(2,1)S(1)} %copy-done.12, bf16[1024,512]{1,0:T(8,128)(2,1)S(1)} %copy-done.10, ...), custom_call_target="tpu_custom_call" | custom-call | flops 8589934592 | bytes 23068672 | tf_op jit(solution)/shard_map/feed_forward/pallas_call | solution.py:1041
  209.6 16.2 %feed_forward.3 = (bf16[1024,2048]{1,0:T(8,128)(2,1)}, bf16[1024,2048]{1,0:T(8,128)(2,1)}, f32[1024,1024]{1,0:T(8,128)}) custom-call(bf16[1024,1024]{1,0:T(8,128)(2,1)} %fusion.4.h_ref, bf16[1024,512]{1,0:T(8,128)(2,1)S(1)} %collective-permute-done.18.refs_0_, bf16[1024,512]{1,0:T(8,128)(2,1)S(1)} %collective-permute-done.20.refs_1_, ...), custom_call_target="tpu_custom_call" | custom-call | flops 8589934592 | bytes 23068672 | tf_op jit(solution)/shard_map/feed_forward/pallas_call | solution.py:1041
  225.8 5.5 fusion.104
  234.9 3.6 fusion.103
  238.8 3.4 copy-done.84
  242.2 3.7 fusion.22
  245.9 3.7 fusion.25
  250.1 4.1 flip.7.refs_23_
  257.9 14.7 %feed_forward_back.2 = (bf16[1024,2048]{1,0:T(8,128)(2,1)}, f32[1024,1024]{1,0:T(8,128)}) custom-call(bf16[1024,1024]{1,0:T(8,128)(2,1)} %copy-done.61, bf16[1024,2048]{1,0:T(8,128)(2,1)} %get-tuple-element.146.d_ref, bf16[1024,512]{1,0:T(8,128)(2,1)S(1)} %copy-done.19, bf16[1024,512]{1,0:T(8,128)(2,1)S(1)} %copy-done.21, bf16[1024,512]{1,0:T(8,128)(2,1)S(1)} %copy-done.23, ...), custom_call_target="tpu_custom_call" | custom-call | flops 8589934592 | bytes 23068672 | tf_op jit(solution)/shard_map/feed_forward_back/pallas_call | solution.py:1073
  272.6 5.5 fusion.31
  278.1 15.6 %feed_forward_back.3 = (bf16[1024,2048]{1,0:T(8,128)(2,1)}, f32[1024,1024]{1,0:T(8,128)}) custom-call(bf16[1024,1024]{1,0:T(8,128)(2,1)} %copy-done.61, bf16[1024,2048]{1,0:T(8,128)(2,1)} %get-tuple-element.151.d_ref, bf16[1024,512]{1,0:T(8,128)(2,1)S(1)} %get-tuple-element.121.refs_0_, bf16[1024,512]{1,0:T(8,128)(2,1)S(1)} %copy-done.13, ...), custom_call_target="tpu_custom_call" | custom-call | flops 8589934592 | bytes 23068672 | tf_op jit(solution)/shard_map/feed_forward_back/pallas_call | solution.py:1073
  293.8 5.5 fusion.28
  299.3 2.3 multiply_reduce_fusion
  303.3 2.4 add_multiply_fusion
  305.7 2.3 convolution_convert_fusion.3.refs_6_
  308.5 2.3 convolution_convert_fusion.2.refs_12_
  310.8 4.6 flip.6.refs_25_
  316.2 4.2 fusion.6
  320.4 5.5 add_convert_fusion.5.refs_35_
  325.9 5.5 add_convert_fusion.4.refs_36_
  331.4 5.4 add_convert_fusion.3.refs_37_
  336.8 3.8 add_convert_fusion.2.refs_38_
  340.6 304.7 %attention_back.1 = (bf16[2,1024,512]{2,1,0:T(8,128)(2,1)}, bf16[2,1024,512]{2,1,0:T(8,128)(2,1)}, bf16[2,1024,512]{2,1,0:T(8,128)(2,1)}, bf16[2,1024,512]{2,1,0...) custom-call(s32[1]{0:T(128)} %dynamic_slice.42.len_ref.refs_0_, ...), custom_call_target="tpu_custom_call" | custom-call | flops 103079215104 | bytes 16777216 | tf_op jit(solution)/shard_map/attention_back/pallas_call | solution.py:850
  645.3 2.7 fusion.58
  648.2 3.3 fusion.64
  651.5 3.2 fusion.56
  654.8 3.3 fusion.62
  658.0 3.3 fusion.46
  661.4 3.2 fusion.50
  664.6 4.6 spread.2
  669.2 4.4 spread.3
  673.6 3.3 fusion.60
  676.9 3.3 fusion.48
  680.2 4.5 assemble.2
  685.2 5.1 assemble.3
  691.0 6.8 add_convert_fusion
  697.8 8.7 %add_convert_fusion.1 = bf16[1024,1024]{1,0:T(8,128)(2,1)} fusion(f32[1024,1024]{1,0:T(8,128)} %fusion.56, f32[1024,1024]{1,0:T(8,128)S(1)} %fusion.58, f32[1024,1024]{1,0:T(8,128)} %fusion.60, f32[1024,1024]{1,0:T(8,128)S(1)} %copy-done.53, f32[1024,1024]{1,0:T(8,128)} %fusion.62, f32[1024,1024]{1,0:T(8,128)S(1)} %copy-done.52, ...), kind=kOutput, calls=%fused_computation.10 | convolution fusion | flops 1082130432 | bytes 29360128 | tf_op jit(solution)/shard_map/dot_general | solution.py:355
  (278 shorter events, 54.2 us)
Async XLA Ops:
  0.6 63.1 %copy-start = (bf16[512,1024]{1,0:T(8,128)(2,1)S(1)}, bf16[512,1024]{1,0:T(8,128)(2,1)}, u32[]{:S(2)}) copy-start(bf16[512,1024]{1,0:T(8,128)(2,1)} %param.21) | copy-start | bytes 3145732
  2.9 33.5 %collective-permute-start = (bf16[3,256,512]{2,1,0:T(8,128)(2,1)}, bf16[3,256,512]{2,1,0:T(8,128)(2,1)S(1)}, u32[]{:S(2)}, u32[]{:S(2)}) collective-permute-start(bf16[3,256,512]{2,1,0:T(8,128)(2,1)} %constant_dynamic-slice_fusion.8), channel_id=1, source_target_pairs={{0,1},{1,0},{2,3},{3,2},{4,5},{5,4},{6,7},{7,6},{8,9},{9,8},{10,11... | collective-permute-start | bytes 2359304 | tf_op jit(solution)/shard_map/ppermute | solution.py:893
  9.1 12.9 %copy-start.26 = (bf16[1024,512]{1,0:T(8,128)(2,1)}, bf16[1024,512]{1,0:T(8,128)(2,1)S(1)}, u32[]{:S(2)}) copy-start(bf16[1024,512]{1,0:T(8,128)(2,1)S(1)} %convolution_convert_fusion.13.q_ref.refs_13_) | copy-start | bytes 3145732
  9.1 7.4 %copy-start.80 = (s32[2]{0:T(128)S(1)}, s32[2]{0:T(128)}, u32[]{:S(2)}) copy-start(s32[2]{0:T(128)} %param.15) | copy-start | bytes 28
  21.9 13.4 %copy-start.28 = (bf16[1024,512]{1,0:T(8,128)(2,1)}, bf16[1024,512]{1,0:T(8,128)(2,1)S(1)}, u32[]{:S(2)}) copy-start(bf16[1024,512]{1,0:T(8,128)(2,1)S(1)} %convolution_convert_fusion.11.v_ref.refs_15_) | copy-start | bytes 3145732
  21.9 16.5 %copy-start.71 = (bf16[512,1024]{1,0:T(8,128)(2,1)S(1)}, bf16[512,1024]{1,0:T(8,128)(2,1)}, u32[]{:S(2)}) copy-start(bf16[512,1024]{1,0:T(8,128)(2,1)} %refs_29_.1) | copy-start | bytes 3145732
  36.3 27.3 %collective-permute-start.1 = (bf16[3,256,512]{2,1,0:T(8,128)(2,1)S(1)}, bf16[3,256,512]{2,1,0:T(8,128)(2,1)}, u32[]{:S(2)}, u32[]{:S(2)}) collective-permute-start(bf16[3,256,512]{2,1,0:T(8,128)(2,1)S(1)} %collective-permute-done.refs_0_), channel_id=1, source_target_pairs={{0,4},{1,5},{2,6},{3,7},{4,0},{5,1},{6,2},{7,3},{8,12},{9,13},{10,... | collective-permute-start | bytes 2359304 | tf_op jit(solution)/shard_map/ppermute | solution.py:893
  37.8 25.8 %collective-permute-start.2 = (bf16[3,256,512]{2,1,0:T(8,128)(2,1)S(1)}, bf16[3,256,512]{2,1,0:T(8,128)(2,1)}, u32[]{:S(2)}, u32[]{:S(2)}) collective-permute-start(bf16[3,256,512]{2,1,0:T(8,128)(2,1)S(1)} %collective-permute-done.refs_0_), channel_id=1, source_target_pairs={{0,2},{1,3},{2,0},{3,1},{4,6},{5,7},{6,4},{7,5},{8,10},{9,11},{10,... | collective-permute-start | bytes 2359304 | tf_op jit(solution)/shard_map/ppermute | solution.py:893
  37.8 25.8 %collective-permute-start.5 = (bf16[2,256,512]{2,1,0:T(8,128)(2,1)}, bf16[2,256,512]{2,1,0:T(8,128)(2,1)}, u32[]{:S(2)}, u32[]{:S(2)}) collective-permute-start(bf16[2,256,512]{2,1,0:T(8,128)(2,1)} %constant_dynamic-slice_fusion.9), channel_id=1, source_target_pairs={{0,1},{1,0},{2,3},{3,2},{4,5},{5,4},{6,7},{7,6},{8,9},{9,8},{10,11... | collective-permute-start | bytes 1572872 | tf_op jit(solution)/shard_map/ppermute | solution.py:893
  41.7 16.7 %collective-permute-start.3 = (bf16[1,128,1024]{2,1,0:T(8,128)(2,1)}, bf16[1,128,1024]{2,1,0:T(8,128)(2,1)S(1)}, u32[]{:S(2)}, u32[]{:S(2)}) collective-permute-start(bf16[1,128,1024]{2,1,0:T(8,128)(2,1)} %dynamic-slice_bitcast_fusion.2), channel_id=1, source_target_pairs={{0,1},{1,0},{2,3},{3,2},{4,5},{5,4},{6,7},{7,6},{8,9},{9,8},{10,11... | collective-permute-start | bytes 786440 | tf_op jit(solution)/shard_map/ppermute | solution.py:893
  43.1 20.5 %collective-permute-start.4 = (bf16[1,256,512]{2,1,0:T(8,128)(2,1)}, bf16[1,256,512]{2,1,0:T(8,128)(2,1)S(1)}, u32[]{:S(2)}, u32[]{:S(2)}) collective-permute-start(bf16[1,256,512]{2,1,0:T(8,128)(2,1)} %dynamic-slice_bitcast_fusion.1), channel_id=1, source_target_pairs={{0,1},{1,0},{2,3},{3,2},{4,5},{5,4},{6,7},{7,6},{8,9},{9,8},{10,11... | collective-permute-start | bytes 786440 | tf_op jit(solution)/shard_map/ppermute | solution.py:893
  58.4 19.7 %copy-start.16 = (bf16[1,128,1024]{2,1,0:T(8,128)(2,1)}, bf16[1,128,1024]{2,1,0:T(8,128)(2,1)S(1)}, u32[]{:S(2)}) copy-start(bf16[1,128,1024]{2,1,0:T(8,128)(2,1)S(1)} %collective-permute-done.3.refs_0_) | copy-start | bytes 786436
  63.6 16.3 %collective-permute-start.6 = (bf16[3,256,512]{2,1,0:T(8,128)(2,1)}, bf16[3,256,512]{2,1,0:T(8,128)(2,1)}, u32[]{:S(2)}, u32[]{:S(2)}) collective-permute-start(bf16[3,256,512]{2,1,0:T(8,128)(2,1)} %collective-permute-done.1.refs_1_), channel_id=1, source_target_pairs={{0,2},{1,3},{2,0},{3,1},{4,6},{5,7},{6,4},{7,5},{8,10},{9,11},{10,... | collective-permute-start | bytes 2359304 | tf_op jit(solution)/shard_map/ppermute | solution.py:893
  76.0 58.2 %copy-start.29 = (bf16[1024,512]{1,0:T(8,128)(2,1)}, bf16[1024,512]{1,0:T(8,128)(2,1)S(1)}, u32[]{:S(2)}) copy-start(bf16[1024,512]{1,0:T(8,128)(2,1)S(1)} %convolution_convert_fusion.9.k_ref.refs_2_) | copy-start | bytes 3145732
  77.2 57.0 %copy-start.30 = (bf16[1024,512]{1,0:T(8,128)(2,1)}, bf16[1024,512]{1,0:T(8,128)(2,1)S(1)}, u32[]{:S(2)}) copy-start(bf16[1024,512]{1,0:T(8,128)(2,1)S(1)} %convolution_convert_fusion.8.v_ref.refs_3_) | copy-start | bytes 3145732
  77.3 8.9 %collective-permute-start.13 = (bf16[1,128,1024]{2,1,0:T(8,128)(2,1)S(1)}, bf16[1,128,1024]{2,1,0:T(8,128)(2,1)S(1)}, u32[]{:S(2)}, u32[]{:S(2)}) collective-permute-start(bf16[1,128,1024]{2,1,0:T(8,128)(2,1)S(1)} %copy-done.66), channel_id=1, source_target_pairs={{0,1},{1,0},{2,3},{3,2},{4,5},{5,4},{6,7},{7,6},{8,9},{9,8},{10,11... | collective-permute-start | bytes 786440 | tf_op jit(solution)/shard_map/ppermute | solution.py:893
  77.9 9.1 %collective-permute-start.7 = (bf16[1,128,1024]{2,1,0:T(8,128)(2,1)S(1)}, bf16[1,128,1024]{2,1,0:T(8,128)(2,1)S(1)}, u32[]{:S(2)}, u32[]{:S(2)}) collective-permute-start(bf16[1,128,1024]{2,1,0:T(8,128)(2,1)S(1)} %collective-permute-done.3.refs_0_), channel_id=1, source_target_pairs={{0,4},{1,5},{2,6},{3,7},{4,0},{5,1},{6,2},{7,3},{8,12},{9,13},{10,... | collective-permute-start | bytes 786440 | tf_op jit(solution)/shard_map/ppermute | solution.py:893
  78.1 22.4 %collective-permute-start.8 = (bf16[1,128,1024]{2,1,0:T(8,128)(2,1)S(1)}, bf16[1,128,1024]{2,1,0:T(8,128)(2,1)S(1)}, u32[]{:S(2)}, u32[]{:S(2)}) collective-permute-start(bf16[1,128,1024]{2,1,0:T(8,128)(2,1)S(1)} %collective-permute-done.3.refs_0_), channel_id=1, source_target_pairs={{0,2},{1,3},{2,0},{3,1},{4,6},{5,7},{6,4},{7,5},{8,10},{9,11},{10,... | collective-permute-start | bytes 786440 | tf_op jit(solution)/shard_map/ppermute | solution.py:893
  78.1 25.0 %collective-permute-start.11 = (bf16[2,256,512]{2,1,0:T(8,128)(2,1)}, bf16[2,256,512]{2,1,0:T(8,128)(2,1)S(1)}, u32[]{:S(2)}, u32[]{:S(2)}) collective-permute-start(bf16[2,256,512]{2,1,0:T(8,128)(2,1)} %collective-permute-done.5.refs_0_), channel_id=1, source_target_pairs={{0,4},{1,5},{2,6},{3,7},{4,0},{5,1},{6,2},{7,3},{8,12},{9,13},{10,... | collective-permute-start | bytes 1572872 | tf_op jit(solution)/shard_map/ppermute | solution.py:893
  79.9 23.2 %collective-permute-start.12 = (bf16[2,256,512]{2,1,0:T(8,128)(2,1)}, bf16[2,256,512]{2,1,0:T(8,128)(2,1)S(1)}, u32[]{:S(2)}, u32[]{:S(2)}) collective-permute-start(bf16[2,256,512]{2,1,0:T(8,128)(2,1)} %collective-permute-done.5.refs_0_), channel_id=1, source_target_pairs={{0,2},{1,3},{2,0},{3,1},{4,6},{5,7},{6,4},{7,5},{8,10},{9,11},{10,... | collective-permute-start | bytes 1572872 | tf_op jit(solution)/shard_map/ppermute | solution.py:893
  86.1 14.4 %copy-start.33 = (bf16[1024,512]{1,0:T(8,128)(2,1)}, bf16[1024,512]{1,0:T(8,128)(2,1)S(1)}, u32[]{:S(2)}) copy-start(bf16[1024,512]{1,0:T(8,128)(2,1)S(1)} %convolution_convert_fusion.6.v_ref.refs_20_) | copy-start | bytes 3145732
  86.1 17.1 %copy-start.74 = (f32[3,1024]{1,0:T(4,128)S(1)}, f32[3,1024]{1,0:T(4,128)}, u32[]{:S(2)}) copy-start(f32[3,1024]{1,0:T(4,128)} %param.25) | copy-start | bytes 36868
  86.2 17.1 %copy-start.75 = (f32[3,1024]{1,0:T(4,128)S(1)}, f32[3,1024]{1,0:T(4,128)}, u32[]{:S(2)}) copy-start(f32[3,1024]{1,0:T(4,128)} %refs_31_.1) | copy-start | bytes 36868
  86.2 19.7 %copy-start.17 = (bf16[1,128,1024]{2,1,0:T(8,128)(2,1)S(1)}, bf16[1,128,1024]{2,1,0:T(8,128)(2,1)}, u32[]{:S(2)}) copy-start(bf16[1,128,1024]{2,1,0:T(8,128)(2,1)} %copy-done.16) | copy-start | bytes 786436
  86.2 17.0 %collective-permute-start.9 = (bf16[1,256,512]{2,1,0:T(8,128)(2,1)S(1)}, bf16[1,256,512]{2,1,0:T(8,128)(2,1)S(1)}, u32[]{:S(2)}, u32[]{:S(2)}) collective-permute-start(bf16[1,256,512]{2,1,0:T(8,128)(2,1)S(1)} %collective-permute-done.4.refs_0_), channel_id=1, source_target_pairs={{0,4},{1,5},{2,6},{3,7},{4,0},{5,1},{6,2},{7,3},{8,12},{9,13},{10,... | collective-permute-start | bytes 786440 | tf_op jit(solution)/shard_map/ppermute | solution.py:893
  87.0 16.1 %collective-permute-start.10 = (bf16[1,256,512]{2,1,0:T(8,128)(2,1)S(1)}, bf16[1,256,512]{2,1,0:T(8,128)(2,1)S(1)}, u32[]{:S(2)}, u32[]{:S(2)}) collective-permute-start(bf16[1,256,512]{2,1,0:T(8,128)(2,1)S(1)} %collective-permute-done.4.refs_0_), channel_id=1, source_target_pairs={{0,2},{1,3},{2,0},{3,1},{4,6},{5,7},{6,4},{7,5},{8,10},{9,11},{10,... | collective-permute-start | bytes 786440 | tf_op jit(solution)/shard_map/ppermute | solution.py:893
  100.5 10.4 %copy-start.9 = (bf16[1024,512]{1,0:T(8,128)(2,1)}, bf16[1024,512]{1,0:T(8,128)(2,1)S(1)}, u32[]{:S(2)}) copy-start(bf16[1024,512]{1,0:T(8,128)(2,1)S(1)} %get-tuple-element.115.refs_21_) | copy-start | bytes 3145732
  100.5 10.4 %copy-start.39 = (bf16[1024,512]{1,0:T(8,128)(2,1)}, bf16[1024,512]{1,0:T(8,128)(2,1)S(1)}, u32[]{:S(2)}) copy-start(bf16[1024,512]{1,0:T(8,128)(2,1)S(1)} %get-tuple-element.163.refs_22_) | copy-start | bytes 3145732
  103.2 2.7 collective-permute-start.14
  103.3 16.4 %collective-permute-start.16 = (bf16[1,128,1024]{2,1,0:T(8,128)(2,1)S(1)}, bf16[1,128,1024]{2,1,0:T(8,128)(2,1)S(1)}, u32[]{:S(2)}, u32[]{:S(2)}) collective-permute-start(bf16[1,128,1024]{2,1,0:T(8,128)(2,1)S(1)} %collective-permute-done.13.refs_0_), channel_id=1, source_target_pairs={{0,4},{1,5},{2,6},{3,7},{4,0},{5,1},{6,2},{7,3},{8,12},{9,13},{10,... | collective-permute-start | bytes 786440 | tf_op jit(solution)/shard_map/ppermute | solution.py:893
  103.7 16.1 %collective-permute-start.17 = (bf16[1,128,1024]{2,1,0:T(8,128)(2,1)S(1)}, bf16[1,128,1024]{2,1,0:T(8,128)(2,1)S(1)}, u32[]{:S(2)}, u32[]{:S(2)}) collective-permute-start(bf16[1,128,1024]{2,1,0:T(8,128)(2,1)S(1)} %collective-permute-done.13.refs_0_), channel_id=1, source_target_pairs={{0,2},{1,3},{2,0},{3,1},{4,6},{5,7},{6,4},{7,5},{8,10},{9,11},{10,... | collective-permute-start | bytes 786440 | tf_op jit(solution)/shard_map/ppermute | solution.py:893
  103.9 12.4 %collective-permute-start.15 = (bf16[2,256,512]{2,1,0:T(8,128)(2,1)S(1)}, bf16[2,256,512]{2,1,0:T(8,128)(2,1)S(1)}, u32[]{:S(2)}, u32[]{:S(2)}) collective-permute-start(bf16[2,256,512]{2,1,0:T(8,128)(2,1)S(1)} %collective-permute-done.11.refs_1_), channel_id=1, source_target_pairs={{0,2},{1,3},{2,0},{3,1},{4,6},{5,7},{6,4},{7,5},{8,10},{9,11},{10,... | collective-permute-start | bytes 1572872 | tf_op jit(solution)/shard_map/ppermute | solution.py:893
  104.2 25.3 %collective-permute-start.18 = (bf16[1024,512]{1,0:T(8,128)(2,1)S(1)}, bf16[1024,512]{1,0:T(8,128)(2,1)S(1)}, u32[]{:S(2)}, u32[]{:S(2)}) collective-permute-start(bf16[1024,512]{1,0:T(8,128)(2,1)S(1)} %get-tuple-element.121.refs_0_), channel_id=1, source_target_pairs={{0,1},{1,0},{2,3},{3,2},{4,5},{5,4},{6,7},{7,6},{8,9},{9,8},{10,11... | collective-permute-start | bytes 3145736 | tf_op jit(solution)/shard_map/ppermute | solution.py:893
  105.9 9.0 %collective-permute-start.19 = (bf16[1,256,512]{2,1,0:T(8,128)(2,1)S(1)}, bf16[1,256,512]{2,1,0:T(8,128)(2,1)S(1)}, u32[]{:S(2)}, u32[]{:S(2)}) collective-permute-start(bf16[1,256,512]{2,1,0:T(8,128)(2,1)S(1)} %collective-permute-done.9.refs_1_), channel_id=1, source_target_pairs={{0,2},{1,3},{2,0},{3,1},{4,6},{5,7},{6,4},{7,5},{8,10},{9,11},{10,... | collective-permute-start | bytes 786440 | tf_op jit(solution)/shard_map/ppermute | solution.py:893
  114.8 19.4 %copy-start.34 = (bf16[1024,512]{1,0:T(8,128)(2,1)}, bf16[1024,512]{1,0:T(8,128)(2,1)S(1)}, u32[]{:S(2)}) copy-start(bf16[1024,512]{1,0:T(8,128)(2,1)S(1)} %convolution_convert_fusion.5.q_ref.refs_1_) | copy-start | bytes 3145732
  116.3 45.0 %copy-start.35 = (bf16[1024,512]{1,0:T(8,128)(2,1)}, bf16[1024,512]{1,0:T(8,128)(2,1)S(1)}, u32[]{:S(2)}) copy-start(bf16[1024,512]{1,0:T(8,128)(2,1)S(1)} %convolution_convert_fusion.4.q_ref.refs_7_) | copy-start | bytes 3145732
  118.5 14.2 %copy-start.4 = (bf16[2,1024,512]{2,1,0:T(8,128)(2,1)}, bf16[2,1024,512]{2,1,0:T(8,128)(2,1)S(1)}, u32[]{:S(2)}) copy-start(bf16[2,1024,512]{2,1,0:T(8,128)(2,1)S(1)} %arrange.7) | copy-start | bytes 6291460
  118.5 12.7 %copy-start.63 = (bf16[512,1024]{1,0:T(8,128)(2,1)S(1)}, bf16[512,1024]{1,0:T(8,128)(2,1)}, u32[]{:S(2)}) copy-start(bf16[512,1024]{1,0:T(8,128)(2,1)} %get-tuple-element.127.refs_4_) | copy-start | bytes 3145732
  119.7 41.6 %copy-start.36 = (bf16[1024,512]{1,0:T(8,128)(2,1)}, bf16[1024,512]{1,0:T(8,128)(2,1)S(1)}, u32[]{:S(2)}) copy-start(bf16[1024,512]{1,0:T(8,128)(2,1)S(1)} %fusion.40.k_ref.refs_8_) | copy-start | bytes 3145732
  129.5 78.1 %copy-start.18 = (bf16[1024,512]{1,0:T(8,128)(2,1)}, bf16[1024,512]{1,0:T(8,128)(2,1)S(1)}, u32[]{:S(2)}) copy-start(bf16[1024,512]{1,0:T(8,128)(2,1)S(1)} %collective-permute-done.18.refs_0_) | copy-start | bytes 3145732
  129.5 24.5 %collective-permute-start.20 = (bf16[1024,512]{1,0:T(8,128)(2,1)S(1)}, bf16[1024,512]{1,0:T(8,128)(2,1)S(1)}, u32[]{:S(2)}, u32[]{:S(2)}) collective-permute-start(bf16[1024,512]{1,0:T(8,128)(2,1)S(1)} %collective-permute-done.18.refs_0_), channel_id=1, source_target_pairs={{0,4},{1,5},{2,6},{3,7},{4,0},{5,1},{6,2},{7,3},{8,12},{9,13},{10,... | collective-permute-start | bytes 3145736 | tf_op jit(solution)/shard_map/ppermute | solution.py:893
  131.2 22.8 %collective-permute-start.21 = (bf16[1024,512]{1,0:T(8,128)(2,1)S(1)}, bf16[1024,512]{1,0:T(8,128)(2,1)S(1)}, u32[]{:S(2)}, u32[]{:S(2)}) collective-permute-start(bf16[1024,512]{1,0:T(8,128)(2,1)S(1)} %collective-permute-done.18.refs_0_), channel_id=1, source_target_pairs={{0,2},{1,3},{2,0},{3,1},{4,6},{5,7},{6,4},{7,5},{8,10},{9,11},{10,... | collective-permute-start | bytes 3145736 | tf_op jit(solution)/shard_map/ppermute | solution.py:893
  131.2 25.7 %collective-permute-start.22 = (bf16[512,1024]{1,0:T(8,128)(2,1)S(1)}, bf16[512,1024]{1,0:T(8,128)(2,1)}, u32[]{:S(2)}, u32[]{:S(2)}) collective-permute-start(bf16[512,1024]{1,0:T(8,128)(2,1)S(1)} %copy-done.63), channel_id=1, source_target_pairs={{0,1},{1,0},{2,3},{3,2},{4,5},{5,4},{6,7},{7,6},{8,9},{9,8},{10,11... | collective-permute-start | bytes 3145736 | tf_op jit(solution)/shard_map/ppermute | solution.py:893
  133.9 27.4 %copy-start.37 = (bf16[1024,512]{1,0:T(8,128)(2,1)}, bf16[1024,512]{1,0:T(8,128)(2,1)S(1)}, u32[]{:S(2)}) copy-start(bf16[1024,512]{1,0:T(8,128)(2,1)S(1)} %fusion.41.v_ref.refs_9_) | copy-start | bytes 3145732
  133.9 26.6 %collective-permute-start.25 = (bf16[1,128,1024]{2,1,0:T(8,128)(2,1)S(1)}, bf16[1,128,1024]{2,1,0:T(8,128)(2,1)S(1)}, u32[]{:S(2)}, u32[]{:S(2)}) collective-permute-start(bf16[1,128,1024]{2,1,0:T(8,128)(2,1)S(1)} %collective-permute-done.16.refs_1_), channel_id=1, source_target_pairs={{0,2},{1,3},{2,0},{3,1},{4,6},{5,7},{6,4},{7,5},{8,10},{9,11},{10,... | collective-permute-start | bytes 786440 | tf_op jit(solution)/shard_map/ppermute | solution.py:893
  149.7 10.8 %copy-start.25 = (bf16[1024,512]{1,0:T(8,128)(2,1)}, bf16[1024,512]{1,0:T(8,128)(2,1)S(1)}, u32[]{:S(2)}) copy-start(bf16[1024,512]{1,0:T(8,128)(2,1)S(1)} %get-tuple-element.123.refs_4_) | copy-start | bytes 3145732
  149.7 10.8 %copy-start.40 = (bf16[1024,512]{1,0:T(8,128)(2,1)}, bf16[1024,512]{1,0:T(8,128)(2,1)S(1)}, u32[]{:S(2)}) copy-start(bf16[1024,512]{1,0:T(8,128)(2,1)S(1)} %get-tuple-element.143.refs_5_) | copy-start | bytes 3145732
  154.0 53.6 %copy-start.20 = (bf16[1024,512]{1,0:T(8,128)(2,1)}, bf16[1024,512]{1,0:T(8,128)(2,1)S(1)}, u32[]{:S(2)}) copy-start(bf16[1024,512]{1,0:T(8,128)(2,1)S(1)} %collective-permute-done.20.refs_1_) | copy-start | bytes 3145732
  154.0 53.6 %copy-start.22 = (bf16[1024,512]{1,0:T(8,128)(2,1)}, bf16[1024,512]{1,0:T(8,128)(2,1)S(1)}, u32[]{:S(2)}) copy-start(bf16[1024,512]{1,0:T(8,128)(2,1)S(1)} %collective-permute-done.21.refs_2_) | copy-start | bytes 3145732
  156.8 25.0 %collective-permute-start.23 = (bf16[512,1024]{1,0:T(8,128)(2,1)}, bf16[512,1024]{1,0:T(8,128)(2,1)S(1)}, u32[]{:S(2)}, u32[]{:S(2)}) collective-permute-start(bf16[512,1024]{1,0:T(8,128)(2,1)} %collective-permute-done.22.refs_4_), channel_id=1, source_target_pairs={{0,4},{1,5},{2,6},{3,7},{4,0},{5,1},{6,2},{7,3},{8,12},{9,13},{10,... | collective-permute-start | bytes 3145736 | tf_op jit(solution)/shard_map/ppermute | solution.py:893
  157.2 24.6 %collective-permute-start.24 = (bf16[512,1024]{1,0:T(8,128)(2,1)}, bf16[512,1024]{1,0:T(8,128)(2,1)S(1)}, u32[]{:S(2)}, u32[]{:S(2)}) collective-permute-start(bf16[512,1024]{1,0:T(8,128)(2,1)} %collective-permute-done.22.refs_4_), channel_id=1, source_target_pairs={{0,2},{1,3},{2,0},{3,1},{4,6},{5,7},{6,4},{7,5},{8,10},{9,11},{10,... | collective-permute-start | bytes 3145736 | tf_op jit(solution)/shard_map/ppermute | solution.py:893
  160.7 46.8 %collective-permute-start.26 = (bf16[1024,512]{1,0:T(8,128)(2,1)S(1)}, bf16[1024,512]{1,0:T(8,128)(2,1)S(1)}, u32[]{:S(2)}, u32[]{:S(2)}) collective-permute-start(bf16[1024,512]{1,0:T(8,128)(2,1)S(1)} %collective-permute-done.20.refs_1_), channel_id=1, source_target_pairs={{0,2},{1,3},{2,0},{3,1},{4,6},{5,7},{6,4},{7,5},{8,10},{9,11},{10,... | collective-permute-start | bytes 3145736 | tf_op jit(solution)/shard_map/ppermute | solution.py:893
  176.6 10.6 %copy-start.14 = (bf16[1024,512]{1,0:T(8,128)(2,1)}, bf16[1024,512]{1,0:T(8,128)(2,1)S(1)}, u32[]{:S(2)}) copy-start(bf16[1024,512]{1,0:T(8,128)(2,1)S(1)} %get-tuple-element.132.refs_10_) | copy-start | bytes 3145732
  176.6 10.6 %copy-start.41 = (bf16[1024,512]{1,0:T(8,128)(2,1)}, bf16[1024,512]{1,0:T(8,128)(2,1)S(1)}, u32[]{:S(2)}) copy-start(bf16[1024,512]{1,0:T(8,128)(2,1)S(1)} %get-tuple-element.160.refs_11_) | copy-start | bytes 3145732
  187.8 19.7 %collective-permute-start.27 = (bf16[512,1024]{1,0:T(8,128)(2,1)S(1)}, bf16[512,1024]{1,0:T(8,128)(2,1)S(1)}, u32[]{:S(2)}, u32[]{:S(2)}) collective-permute-start(bf16[512,1024]{1,0:T(8,128)(2,1)S(1)} %collective-permute-done.23.refs_5_), channel_id=1, source_target_pairs={{0,2},{1,3},{2,0},{3,1},{4,6},{5,7},{6,4},{7,5},{8,10},{9,11},{10,... | collective-permute-start | bytes 3145736 | tf_op jit(solution)/shard_map/ppermute | solution.py:893
  238.5 7.4 %copy-start.45 = (f32[1024,1024]{1,0:T(8,128)}, f32[1024,1024]{1,0:T(8,128)S(1)}, u32[]{:S(2)}) copy-start(f32[1024,1024]{1,0:T(8,128)S(1)} %get-tuple-element.196) | copy-start | bytes 12582916
  249.6 28.5 %collective-permute-start.28 = (bf16[1024,1024]{1,0:T(8,128)(2,1)}, bf16[1024,1024]{1,0:T(8,128)(2,1)}, u32[]{:S(2)}, u32[]{:S(2)}) collective-permute-start(bf16[1024,1024]{1,0:T(8,128)(2,1)} %fusion.22), channel_id=1, source_target_pairs={{0,2},{1,3},{2,0},{3,1},{4,6},{5,7},{6,4},{7,5},{8,10},{9,11},{10,... | collective-permute-start | bytes 6291464 | tf_op jit(solution)/shard_map/ppermute | solution.py:893
  249.6 28.5 %collective-permute-start.29 = (bf16[1024,1024]{1,0:T(8,128)(2,1)}, bf16[1024,1024]{1,0:T(8,128)(2,1)}, u32[]{:S(2)}, u32[]{:S(2)}) collective-permute-start(bf16[1024,1024]{1,0:T(8,128)(2,1)} %fusion.25), channel_id=1, source_target_pairs={{0,2},{1,3},{2,0},{3,1},{4,6},{5,7},{6,4},{7,5},{8,10},{9,11},{10,... | collective-permute-start | bytes 6291464 | tf_op jit(solution)/shard_map/ppermute | solution.py:893
  257.9 14.7 %copy-start.57 = (bf16[1024,1024]{1,0:T(8,128)(2,1)S(1)}, bf16[1024,1024]{1,0:T(8,128)(2,1)}, u32[]{:S(2)}) copy-start(bf16[1024,1024]{1,0:T(8,128)(2,1)} %fusion.4.h_ref) | copy-start | bytes 6291460
  308.0 23.4 %collective-permute-start.30 = (bf16[1024,1024]{1,0:T(8,128)(2,1)}, bf16[1024,1024]{1,0:T(8,128)(2,1)}, u32[]{:S(2)}, u32[]{:S(2)}) collective-permute-start(bf16[1024,1024]{1,0:T(8,128)(2,1)} %fusion.28), channel_id=1, source_target_pairs={{0,2},{1,3},{2,0},{3,1},{4,6},{5,7},{6,4},{7,5},{8,10},{9,11},{10,... | collective-permute-start | bytes 6291464 | tf_op jit(solution)/shard_map/ppermute | solution.py:893
  308.0 23.4 %collective-permute-start.31 = (bf16[1024,1024]{1,0:T(8,128)(2,1)}, bf16[1024,1024]{1,0:T(8,128)(2,1)}, u32[]{:S(2)}, u32[]{:S(2)}) collective-permute-start(bf16[1024,1024]{1,0:T(8,128)(2,1)} %fusion.31), channel_id=1, source_target_pairs={{0,2},{1,3},{2,0},{3,1},{4,6},{5,7},{6,4},{7,5},{8,10},{9,11},{10,... | collective-permute-start | bytes 6291464 | tf_op jit(solution)/shard_map/ppermute | solution.py:893
  340.6 304.7 %copy-start.3 = (bf16[3,1024,512]{2,1,0:T(8,128)(2,1)S(1)}, bf16[3,1024,512]{2,1,0:T(8,128)(2,1)}, u32[]{:S(2)}) copy-start(bf16[3,1024,512]{2,1,0:T(8,128)(2,1)} %copy-done.2) | copy-start | bytes 9437188
  691.0 6.8 copy-start.53
  697.8 8.7 %copy-start.1 = (bf16[512,1024]{1,0:T(8,128)(2,1)S(1)}, bf16[512,1024]{1,0:T(8,128)(2,1)}, u32[]{:S(2)}) copy-start(bf16[512,1024]{1,0:T(8,128)(2,1)} %param.21) | copy-start | bytes 3145732
  (59 other events, 213.1 us)

commit v3 on v2

--- a/solution.py
+++ b/solution.py
@@ -441,12 +441,13 @@
         vmem((seq, 256), bf16),
         vmem((2, seq, 128), bf16),
         vmem((2, seq, 256), bf16),
-        vmem((seq, 128), f32),
+        vmem((128, seq), f32),
+        vmem((2, 128, seq), bf16),
     ]
 
 
 def back_pair(causal, length, q2, k2, v2, c2, aug, g2, grads, scratch, tick):
-    qs, qm, ka, gs, gm, va, dqa = scratch
+    qs, qm, ka, gs, gm, va, dqa, kt = scratch
     seq = k2.shape[0]
     lane = lanes(seq)
     l64 = lane % 64
@@ -476,6 +477,7 @@
         ka[h, :, 128:] = ko
         va[h, :, :128] = jnp.where(own, v2, zero)
         va[h, :, 128:] = jnp.where(sel, one, zero)
+        kt[h] = ka[h, :, :128].T
     dqa[...] = jnp.zeros_like(dqa)
     grads[:, 384:] = c2
     for j in range(seq // BLK):
@@ -483,6 +485,7 @@
         q0 = j * BLK if causal else 0
         dk = None
         dv = None
+        dq = None
         for h in range(2):
             p = jnp.exp(dot(ka[h, rows, :], qs[q0:, :], NT))
             if causal:
@@ -495,25 +498,35 @@
             p = p.astype(bf16)
             a = dot(p, gm[h, q0:, :])
             b = dot(ds, qm[h, q0:, :])
+            c = dot(kt[h, :, rows], ds)
             dv = a if dv is None else dv + a
             dk = b if dk is None else dk + b
-            dqa[q0:, :] += dot(ds, ka[h, rows, :128], TN)
+            dq = c if dq is None else dq + c
+        dqa[:, q0:] += dq
         grads[rows, 128:256] = dk.astype(bf16)
         grads[rows, 256:384] = dv.astype(bf16)
         tick(j)
-    grads[:, :128] = (dqa[...] * HD**-0.5).astype(bf16)
+    grads[:, :128] = (dqa[...] * HD**-0.5).T.astype(bf16)
 
 
 BOTH = (0, 1)
 X, CORE, Y, Z1, Z2 = range(5)
 DELAY = 2
 SLOTS = 2 * DELAY
-CHUNK = 32
-SUBS = 8
-PAIRS_HERE = 4
-LEAD = SUBS
-HBM_LINKS = (X, Y, Z1, Z2, Y, CORE, CORE)
-PAIR_LINKS = (CORE, X, Y, Z1, Z2, Y, CORE, CORE)
+CHUNK = 64
+SUBS = 4
+QUADS = 4
+WIDTH = 512
+LEAD = 5
+LINKS = (CORE, X, Y, Z1, Z2, Y, CORE, CORE)
+CHUNKS = 4 * QUADS * SUBS
+TICKS = CHUNKS + LEAD + 7 * DELAY
+STEPS = 2 * QUADS
+FEED_TICKS, CROSS_TICKS, SELF_TICKS, NORM_TICKS = 2, 3, 2, 4
+CROSS_AT = STEPS * FEED_TICKS + NORM_TICKS
+SELF_AT = CROSS_AT + STEPS * CROSS_TICKS + NORM_TICKS
+DRAIN_AT = SELF_AT + STEPS * SELF_TICKS
+TILE = 256
 dma_sem = pltpu.SemaphoreType.DMA
 
 
@@ -544,40 +557,45 @@
     )
 
 
-def whole_scratch(w):
+def stream_scratch():
     return [
-        pltpu.VMEM((2, SLOTS, CHUNK, 2 * w), bf16),
-        pltpu.VMEM((8, SLOTS, CHUNK, w), bf16),
-        dma_sem((7, SLOTS)),
-        dma_sem((7, SLOTS)),
+        pltpu.VMEM((2, SLOTS, 2, 2, CHUNK, WIDTH), bf16),
+        pltpu.VMEM((3, SLOTS, 2, CHUNK, WIDTH), bf16),
+        pltpu.VMEM((6, SLOTS, CHUNK, WIDTH), bf16),
+        dma_sem((8, SLOTS)),
+        dma_sem((8, SLOTS)),
         dma_sem((2, SLOTS)),
     ]
 
 
-def whole_stage(stage, c, oth, own, out, wide, narrow, send, recv, local):
+def stream_stage(stage, c, queue, out, pairs, wide, narrow, send, recv, local):
+    d = lax.axis_index("dp")
+    core = d % 2
+    y = (d // 2) % 2
     slot = lax.rem(c, SLOTS)
-    rows = pl.ds(pl.multiple_of(c * CHUNK, CHUNK), CHUNK)
-    w = narrow.shape[-1]
-    came, mine = wide.at[0, slot], wide.at[1, slot]
-    side, kept, got_y, s3, got_z, s4, got_zz, s5 = [narrow.at[i, slot] for i in range(8)]
+    block = c // SUBS
+    sub = lax.rem(c, SUBS)
+    away, came, own = [wide.at[i, slot] for i in range(3)]
+    got_y, s3, got_z, s4, got_zz, s5 = [narrow.at[i, slot] for i in range(6)]
 
     def remote(k):
         src, dst = (
-            (oth.at[rows], came),
-            (side, got_y),
+            (queue.at[block, :, 1 - core, :, sub], pairs.at[0, slot]),
+            (away, came),
+            (own.at[1 - y], got_y),
             (s3, got_z),
             (s4, got_zz),
-            (s5, out.at[1, rows]),
-            (s5, out.at[2, rows]),
-            (out.at[1, rows], out.at[3, rows]),
+            (s5, out.at[block, core, y, sub]),
+            (s5, out.at[block, core, y, sub]),
+            (out.at[block, core, 1 - y, sub], out.at[block, core, 1 - y, sub]),
         )[k]
-        return remote_copy(src, dst, send.at[k, slot], recv.at[k, slot], HBM_LINKS[k])
+        return remote_copy(src, dst, send.at[k, slot], recv.at[k, slot], LINKS[k])
 
     def load():
-        return pltpu.make_async_copy(own.at[rows], mine, local.at[0, slot])
+        return pltpu.make_async_copy(queue.at[block, :, core, :, sub], pairs.at[1, slot], local.at[0, slot])
 
     def keep():
-        return pltpu.make_async_copy(s5, out.at[0, rows], local.at[1, slot])
+        return pltpu.make_async_copy(s5, out.at[block, core, y, sub], local.at[1, slot])
 
     if stage == 0:
         remote(0).start()
@@ -585,80 +603,9 @@
     elif stage == 1:
         remote(0).wait()
         load().wait()
-        v = came[...] + mine[...]
-        side[...] = v[:, w:]
-        kept[...] = v[:, :w]
+        away[...] = pairs[1, slot, 1] + pairs[0, slot, 1]
         remote(1).start()
-    elif stage == 2:
-        remote(1).wait()
-        s3[...] = kept[...] + got_y[...]
-        remote(2).start()
-    elif stage == 3:
-        remote(2).wait()
-        s4[...] = s3[...] + got_z[...]
-        remote(3).start()
-    elif stage == 4:
-        remote(3).wait()
-        s5[...] = s4[...] + got_zz[...]
-        remote(4).start()
-        remote(5).start()
-        keep().start()
-    elif stage == 5:
-        remote(4).wait()
-        remote(5).wait()
-        keep().wait()
-        remote(6).start()
-    else:
-        remote(6).wait()
-
-
-def pair_scratch(w):
-    return [
-        pltpu.VMEM((2, 2, 2, 2, SUBS, CHUNK, w), bf16),
-        pltpu.VMEM((SLOTS, 2, 2, CHUNK, w), bf16),
-        pltpu.VMEM((3, SLOTS, 2, CHUNK, w), bf16),
-        pltpu.VMEM((6, SLOTS, CHUNK, w), bf16),
-        dma_sem((8, SLOTS)),
-        dma_sem((8, SLOTS)),
-        dma_sem((SLOTS,)),
-    ]
-
-
-def pair_stage(stage, c, out, prod, near, wide, narrow, send, recv, local):
-    d = lax.axis_index("dp")
-    core = d % 2
-    y = (d // 2) % 2
-    slot = lax.rem(c, SLOTS)
-    pair = c // SUBS
-    place = pair - jnp.where(pair > PAIRS_HERE, 1, 0)
-    sub = lax.rem(c, SUBS)
-    par = lax.rem(pair, 2)
-    away, came, own = [wide.at[i, slot] for i in range(3)]
-    got_y, s3, got_z, s4, got_zz, s5 = [narrow.at[i, slot] for i in range(6)]
-
-    def remote(k):
-        src, dst = (
-            (prod.at[par, :, 1 - core, :, sub], near.at[slot]),
-            (away, came),
-            (own.at[1 - y], got_y),
-            (s3, got_z),
-            (s4, got_zz),
-            (s5, out.at[place, core, y, sub]),
-            (s5, out.at[place, core, y, sub]),
-            (out.at[place, core, 1 - y, sub], out.at[place, core, 1 - y, sub]),
-        )[k]
-        return remote_copy(src, dst, send.at[k, slot], recv.at[k, slot], PAIR_LINKS[k])
-
-    def keep():
-        return pltpu.make_async_copy(s5, out.at[place, core, y, sub], local.at[slot])
-
-    if stage == 0:
-        remote(0).start()
-    elif stage == 1:
-        remote(0).wait()
-        away[...] = prod[par, 1, core, :, sub] + near[slot, 1]
-        own[...] = prod[par, 0, core, :, sub] + near[slot, 0]
-        remote(1).start()
+        own[...] = pairs[1, slot, 0] + pairs[0, slot, 0]
     elif stage == 2:
         remote(1).wait()
         own[...] = own[...] + came[...]
@@ -703,186 +650,262 @@
         out[...] = acc[5]
 
 
-HALF_STEPS = 2 * PAIRS_HERE
-BETWEEN = 4 * HALF_STEPS
-AFTER = BETWEEN + SUBS
-CHUNKS = 2 * PAIRS_HERE * SUBS + SUBS
-WHOLE = 1024 // CHUNK
-TICKS = CHUNKS + LEAD + 7 * DELAY
-TILE = 256
-
-
-def between_step(dq2, cq, so, gain_ref, sum_ref, base_ref, dz_ref, dc1, g1_t, acc, zt, bt, sems, tick):
+def norm_step(index, more, weights, gain_ref, sum_ref, total, dc, left, acc, zt, sems, tick):
     def fetch_tile(a):
-        rows = pl.ds(a * TILE, TILE)
-        return [
-            pltpu.make_async_copy(sum_ref.at[rows], zt.at[a % 2], sems.at[0, a % 2]),
-            pltpu.make_async_copy(base_ref.at[rows], bt.at[a % 2], sems.at[1, a % 2]),
-        ]
-
-    def put_tile(a):
-        return pltpu.make_async_copy(bt.at[a % 2], dz_ref.at[pl.ds(a * TILE, TILE)], sems.at[2, a % 2])
-
-    tiles = dc1.shape[1] // TILE
-    for copy in fetch_tile(0):
-        copy.start()
-    for a in range(tiles):
-        rows = slice(a * TILE, (a + 1) * TILE)
-        for copy in fetch_tile(a):
-            copy.wait()
-        if a >= 1:
-            put_tile(a - 1).wait()
-        if a + 1 < tiles:
-            for copy in fetch_tile(a + 1):
-                copy.start()
-        z = zt[a % 2]
-        dh = bt[a % 2]
-        for i in BOTH:
-            dh = dh + dot(dq2[i, rows, :], cq[i][...], NT)
+        slot = lax.rem(a, 2)
+        rows = pl.ds(pl.multiple_of(a * TILE, TILE), TILE)
+        return pltpu.make_async_copy(sum_ref.at[rows], zt.at[slot], sems.at[slot])
+
+    tiles = total.shape[0] // TILE
+    fetch_tile(0).start()
+
+    @pl.loop(0, tiles)
+    def _(a):
+        rows = pl.ds(pl.multiple_of(a * TILE, TILE), TILE)
+        fetch_tile(a).wait()
+
+        @pl.when(a + 1 < tiles)
+        def _():
+            fetch_tile(a + 1).start()
+
+        z = zt[lax.rem(a, 2)]
+        dh = total[rows, :]
+        for x, w in more:
+            dh = dh + dot(x[rows, :], w[...], NT)
         centered = z - jnp.mean(z, axis=1, keepdims=True)
         r = lax.rsqrt(jnp.mean(centered * centered, axis=1, keepdims=True) + norm_eps)
         n = centered * r
-        acc[0, 0:1, :] = acc[0, 0:1, :] + jnp.sum(dh * n, axis=0, keepdims=True)
-        acc[0, 3:4, :] = acc[0, 3:4, :] + jnp.sum(dh, axis=0, keepdims=True)
-        e = dh * gain_ref[0:1, :]
+        acc[0, index : index + 1, :] = acc[0, index : index + 1, :] + jnp.sum(dh * n, axis=0, keepdims=True)
+        acc[0, 3 + index : 4 + index, :] = acc[0, 3 + index : 4 + index, :] + jnp.sum(dh, axis=0, keepdims=True)
+        e = dh * gain_ref[index : index + 1, :]
         dz = r * (e - jnp.mean(e, axis=1, keepdims=True) - n * jnp.mean(e * n, axis=1, keepdims=True))
-        bt[a % 2] = dz
-        put_tile(a).start()
+        total[rows, :] = alpha_res * dz
         g = dz.astype(bf16)
-        g1_t[:, rows] = g.T
+        left[:, rows] = g.T
         for i in BOTH:
-            dc1[i, rows, :] = dot(g, so[i][...], NT).astype(bf16)
-        tick(BETWEEN + 2 * a)
-        tick(BETWEEN + 2 * a + 1)
-    put_tile(tiles - 1).wait()
+            dc[i, rows, :] = dot(g, weights[i][...], NT).astype(bf16)
+        tick(a)
 
 
 def back_kernel(*refs):
     refs = list(refs)
     take = lambda n: [refs.pop(0) for _ in range(n)]
     (len_ref,) = take(1)
-    cross_in = [take(6) for _ in BOTH]
+    cross_in = [take(5) for _ in BOTH]
     self_in = [take(5) for _ in BOTH]
-    h1_t, mem_t, g2_t, tar_t = take(4)
-    cq, so = take(2), take(2)
-    gain_ref, small_ref, sum_ref, base_ref = take(4)
-    down_in, up_in = take(2), take(2)
-    dk2_ref, dv2_ref, dq1_ref, dk1_ref, dv1_ref, dz_ref, pair_out, down_out, up_out, small_out = take(10)
-    grads, *scratch = take(8)
-    pair_refs = [pair_out] + take(7)
-    down_refs = down_in + [down_out] + take(5)
-    up_refs = up_in + [up_out] + take(5)
+    co, cq, so = take(2), take(2), take(2)
+    gain_ref, small_ref = take(2)
+    feed_in = [take(4) for _ in BOTH]
+    g3_ref, g3t_ref, h2t_ref, h1t_ref, memt_ref, tart_ref, base_ref, sum2_ref, sum1_ref = take(9)
+    dk2_ref, dv2_ref, dq1_ref, dk1_ref, dv1_ref, dz_ref, out, queue, small_out = take(9)
+    grads, *scratch = take(9)
+    stream = [queue, out] + take(6)
     small_refs = [small_out] + take(4)
     acc = small_refs[1]
-    dq2, dc1, g1_t, zt, bt, sems = take(6)
+    lefts, tall, flat, total, dq2, dc, zt, staged = take(8)
+    left_sems, feed_sems, zt_sems, staged_sems, base_sem = take(5)
     step = pl.program_id(0)
-    prod = pair_refs[1]
+    half = lax.rem(step, 2)
+    pair = lax.rem(step // 2, QUADS)
 
     def tick(t):
         for stage in range(7, -1, -1):
             c = t - LEAD - DELAY * stage
-            real = (c >= 0) & (c < CHUNKS) & ((c < PAIRS_HERE * SUBS) | (c >= (PAIRS_HERE + 1) * SUBS))
-            pl.when(real)(functools.partial(pair_stage, stage, c, *pair_refs))
-        for first, whole_refs in ((0, down_refs), (WHOLE, up_refs)):
-            for stage in range(6, -1, -1):
-                c = t - first - DELAY * stage
-                pl.when((c >= 0) & (c < WHOLE))(functools.partial(whole_stage, stage, c, *whole_refs))
-        for k in range(5, -1, -1):
-            pl.when(t == AFTER + 2 * k)(functools.partial(small_stage, k, *small_refs))
-
-    half = lax.rem(step, 2)
-
-    def products(pair, spans):
-        par = lax.rem(pair, 2)
-        for a in range(4):
-            rows = slice(a * TILE, (a + 1) * TILE)
-            at = prod.at[par, half, a // 2, a % 2]
-            for left, lo, hi in spans:
-                at[:, :, lo:hi] = dot(left[rows, :], grads[:, lo:hi]).astype(bf16).reshape(SUBS, CHUNK, hi - lo)
+            pl.when((c >= 0) & (c < CHUNKS))(functools.partial(stream_stage, stage, c, *stream))
+
+    def load_left(i, ref):
+        return pltpu.make_async_copy(ref, lefts.at[i], left_sems.at[i])
+
+    def load_feed(i, j):
+        cols_j = pl.ds(pl.multiple_of(j * WIDTH, WIDTH), WIDTH)
+        act, slope, up, down = feed_in[i]
+        return [
+            pltpu.make_async_copy(act.at[:, cols_j], tall.at[0, i], feed_sems.at[0, i]),
+            pltpu.make_async_copy(slope.at[:, cols_j], tall.at[1, i], feed_sems.at[1, i]),
+            pltpu.make_async_copy(up.at[:, cols_j], tall.at[2, i], feed_sems.at[2, i]),
+            pltpu.make_async_copy(down.at[cols_j], flat.at[i], feed_sems.at[3, i]),
+        ]
+
+    def post(slot, block):
+        return pltpu.make_async_copy(staged.at[slot], queue.at[block, half], staged_sems.at[slot])
+
+    def products(slot, block, spans, ticks):
+        for a in range(2):
+            rows = slice(2 * a * TILE, 2 * (a + 1) * TILE)
+            for left, right, lo, hi in spans:
+                result = dot(lefts[left, rows, :], right[:, lo:hi]).astype(bf16)
+                staged[slot, a, :, :, :, lo:hi] = result.reshape(2, SUBS, CHUNK, hi - lo)
+            if a in ticks:
+                tick(ticks[a])
+        post(slot, block).start()
 
     @pl.when(step == 0)
     def _():
+        for copy in load_feed(0, 0) + [load_left(i, r) for i, r in enumerate((g3t_ref, h2t_ref, g3_ref))]:
+            copy.start()
+        base = pltpu.make_async_copy(base_ref, total, base_sem)
+        base.start()
+        acc[0] = small_ref[...]
         greet()
-        acc[0] = small_ref[...]
-
-    @pl.when(step < HALF_STEPS)
+        for copy in [load_left(i, r) for i, r in enumerate((g3t_ref, h2t_ref, g3_ref))]:
+            copy.wait()
+        base.wait()
+
+    @pl.when(step < STEPS)
     def _():
-        pair = step // 2
-        q2, k2, v2, c2, aug, g2 = [jnp.where(half == 0, a[...], b[...]) for a, b in zip(*cross_in)]
-        back_pair(False, len_ref[0], q2, k2, v2, c2, aug, g2, grads, scratch, lambda j: tick(4 * step + j))
-        dq2[half, :, pl.ds(pl.multiple_of(pair * 128, 128), 128)] = grads[:, :128]
+        t = step * FEED_TICKS
+        for i in BOTH:
+
+            @pl.when(half == i)
+            def _(i=i):
+                for copy in load_feed(i, pair):
+                    copy.wait()
+
+                @pl.when(step < STEPS - 1)
+                def _():
+                    for copy in load_feed(1 - i, pair + i):
+                        copy.start()
+
+        for a in range(2):
+            rows = slice(2 * a * TILE, 2 * (a + 1) * TILE)
+            du = dot(lefts[2, rows, :], flat[half], NT) * tall[1, half, rows, :].astype(f32)
+            grads[rows, :] = du.astype(bf16)
+        @pl.when(step > 0)
+        def _():
+            post(0, 0).wait()
+
+        products(0, 2 * pair, ((0, tall.at[0, half], 0, WIDTH),), {1: t})
+        for a in range(2):
+            rows = slice(2 * a * TILE, 2 * (a + 1) * TILE)
+            total[rows, :] += dot(grads[rows, :], tall[2, half], NT)
+
+        @pl.when(step > 0)
+        def _():
+            post(1, 0).wait()
+
+        products(1, 2 * pair + 1, ((1, grads, 0, WIDTH),), {1: t + 1})
+
+    @pl.when(step == STEPS)
+    def _():
+        fetch = [load_left(0, h1t_ref), load_left(1, memt_ref)]
+        for copy in fetch:
+            copy.start()
+        norm_step(
+            1, [], co, gain_ref, sum2_ref, total, dc, lefts.at[2], acc, zt, zt_sems, lambda k: tick(STEPS * FEED_TICKS + k)
+        )
+        for copy in fetch:
+            copy.wait()
+        post(1, 0).wait()
+
+    at = pl.ds(pl.multiple_of(pair * 128, 128), 128)
+
+    @pl.when((step >= STEPS) & (step < 2 * STEPS))
+    def _():
+        t = CROSS_AT + (step - STEPS) * CROSS_TICKS
+        q2, k2, v2, c2, aug = [jnp.where(half == 0, a[...], b[...]) for a, b in zip(*cross_in)]
+
+        def ticks(j):
+            if j % 2 == 1:
+                tick(t + j // 2)
+
+        back_pair(False, len_ref[0], q2, k2, v2, c2, aug, dc[half, :, at], grads, scratch, ticks)
+        dq2[half, :, at] = grads[:, :128]
         dk2_ref[...] = grads[:, 128:256]
         dv2_ref[...] = grads[:, 256:384]
-        products(pair, ((h1_t, 0, 128), (mem_t, 128, 384), (g2_t, 384, 512)))
-
-    @pl.when(step == HALF_STEPS)
+        post(0, 0).wait()
+        spans = ((0, grads, 0, 128), (1, grads, 128, 384), (2, grads, 384, 512))
+        products(0, 2 * QUADS + pair, spans, {1: t + 2})
+
+    @pl.when(step == 2 * STEPS)
     def _():
-        between_step(dq2, cq, so, gain_ref, sum_ref, base_ref, dz_ref, dc1, g1_t, acc, zt, bt, sems, tick)
-
-    @pl.when(step >= HALF_STEPS)
+        fetch = load_left(0, tart_ref)
+        fetch.start()
+        more = [(dq2.at[i], cq[i]) for i in BOTH]
+        norm_step(
+            0, more, so, gain_ref, sum1_ref, total, dc, lefts.at[2], acc, zt, zt_sems, lambda k: tick(SELF_AT - NORM_TICKS + k)
+        )
+        fetch.wait()
+        pltpu.make_async_copy(total, dz_ref, base_sem).start()
+
+    @pl.when(step >= 2 * STEPS)
     def _():
-        pair = step // 2 - PAIRS_HERE
+        t = SELF_AT + (step - 2 * STEPS) * SELF_TICKS
         q2, k2, v2, c2, aug = [jnp.where(half == 0, a[...], b[...]) for a, b in zip(*self_in)]
-        g2 = dc1[half, :, pl.ds(pl.multiple_of(pair * 128, 128), 128)]
-        back_pair(True, 0, q2, k2, v2, c2, aug, g2, grads, scratch, lambda j: tick(4 * step + SUBS + j))
+        def ticks(j):
+            if j == 0:
+                tick(t)
+
+        back_pair(True, 0, q2, k2, v2, c2, aug, dc[half, :, at], grads, scratch, ticks)
         dq1_ref[...] = grads[:, :128]
         dk1_ref[...] = grads[:, 128:256]
         dv1_ref[...] = grads[:, 256:384]
-        products(pair + PAIRS_HERE + 1, ((tar_t, 0, 384), (g1_t, 384, 512)))
-
-    @pl.when(step == 2 * HALF_STEPS - 1)
+        post(0, 0).wait()
+        products(0, 3 * QUADS + pair, ((0, grads, 0, 384), (2, grads, 384, 512)), {0: t + 1})
+        for k in range(5, -1, -1):
+            pl.when(step == 2 * STEPS + 1 + k)(functools.partial(small_stage, k, *small_refs))
+
+    @pl.when(step == 3 * STEPS - 1)
     def _():
-        pl.loop(4 * 2 * HALF_STEPS + SUBS, TICKS)(tick)
-
-
-def attention_back(length, cross_in, self_in, lefts, cq, so, gain, small, sums, base, down, up):
+        post(0, 0).wait()
+        pltpu.make_async_copy(total, dz_ref, base_sem).wait()
+        pl.loop(DRAIN_AT, TICKS)(tick)
+
+
+def layer_back(length, cross_in, self_in, weights, gain, small, feed_in, rest):
     seq, width = cross_in[0][0].shape
-    w = down[0].shape[1] // 2
-    low = lambda s: jnp.minimum(s, HALF_STEPS - 1)
-    high = lambda s: jnp.maximum(s - HALF_STEPS, 0)
-    cross_spec = pl.BlockSpec((seq, 128), lambda s: (0, low(s) // 2))
-    self_spec = pl.BlockSpec((seq, 128), lambda s: (0, high(s) // 2))
-    cross_out = pl.BlockSpec((None, seq, 128), lambda s: (low(s) % 2, 0, low(s) // 2))
-    self_out = pl.BlockSpec((None, seq, 128), lambda s: (high(s) % 2, 0, high(s) // 2))
+    model = gain.shape[1]
+    early = lambda s: jnp.clip(s - STEPS, 0, STEPS - 1)
+    late = lambda s: jnp.clip(s - 2 * STEPS, 0, STEPS - 1)
+    cross_spec = pl.BlockSpec((seq, 128), lambda s: (0, early(s) // 2))
+    self_spec = pl.BlockSpec((seq, 128), lambda s: (0, late(s) // 2))
+    cross_out = pl.BlockSpec((None, seq, 128), lambda s: (early(s) % 2, 0, early(s) // 2))
+    self_out = pl.BlockSpec((None, seq, 128), lambda s: (late(s) % 2, 0, late(s) // 2))
     anywhere = pl.BlockSpec(memory_space=pl.ANY)
     full = lambda x: pl.BlockSpec(x.shape, lambda s: (0, 0), pipeline_mode=pl.Buffered(1))
     shape = jax.ShapeDtypeStruct
+    vmem = pltpu.VMEM
+    blocks = 4 * QUADS
     return pl.pallas_call(
         back_kernel,
-        grid=(2 * HALF_STEPS,),
+        grid=(3 * STEPS,),
         in_specs=[pl.BlockSpec(memory_space=pltpu.SMEM)]
-        + [cross_spec] * 12
+        + [cross_spec] * 10
         + [self_spec] * 10
-        + [full(x) for x in (*lefts, *cq, *so, gain, small)]
-        + [anywhere] * 6,
-        out_specs=[cross_out] * 2 + [self_out] * 3 + [anywhere] * 4 + [full(small)],
+        + [full(x) for x in (*weights, gain, small)]
+        + [anywhere] * 17,
+        out_specs=[cross_out] * 2 + [self_out] * 3 + [anywhere] * 3 + [full(small)],
         out_shape=[shape((2, seq, width), bf16)] * 5
         + [
-            shape((seq, sums.shape[1]), f32),
-            shape((2 * PAIRS_HERE, 2, 2, SUBS, CHUNK, 512), bf16),
-            shape((4, seq, w), bf16),
-            shape((4, seq, w), bf16),
+            shape((seq, model), f32),
+            shape((blocks, 2, 2, SUBS, CHUNK, WIDTH), bf16),
+            shape((blocks, 2, 2, 2, SUBS, CHUNK, WIDTH), bf16),
             shape(small.shape, f32),
         ],
-        scratch_shapes=[pltpu.VMEM((seq, 512), bf16)]
+        scratch_shapes=[vmem((seq, WIDTH), bf16)]
         + back_scratch(seq)
-        + pair_scratch(512)
-        + whole_scratch(w) * 2
+        + stream_scratch()
         + small_scratch(small.shape)
         + [
-            pltpu.VMEM((2, seq, width), bf16),
-            pltpu.VMEM((2, seq, width), bf16),
-            pltpu.VMEM((sums.shape[1], seq), bf16),
-            pltpu.VMEM((2, TILE, sums.shape[1]), f32),
-            pltpu.VMEM((2, TILE, sums.shape[1]), f32),
-            dma_sem((3, 2)),
+            vmem((3, model, seq), bf16),
+            vmem((3, 2, seq, WIDTH), bf16),
+            vmem((2, WIDTH, model), bf16),
+            vmem((seq, model), f32),
+            vmem((2, seq, width), bf16),
+            vmem((2, seq, width), bf16),
+            vmem((2, TILE, model), f32),
+            vmem((2, 2, 2, SUBS, CHUNK, WIDTH), bf16),
+            dma_sem((3,)),
+            dma_sem((4, 2)),
+            dma_sem((2,)),
+            dma_sem((2,)),
+            dma_sem,
         ],
         compiler_params=pltpu.CompilerParams(
             collective_id=1, has_side_effects=True, vmem_limit_bytes=60 * 2**20
         ),
-        cost_estimate=cost(12, 8, seq, False),
-        name="attention_back",
-    )(length, *cross_in[0], *cross_in[1], *self_in[0], *self_in[1], *lefts, *cq, *so, gain, small, sums, base, *down, *up)
+        cost_estimate=cost(16, 8, seq, False),
+        name="layer_back",
+    )(length, *cross_in[0], *cross_in[1], *self_in[0], *self_in[1], *weights, gain, small, *feed_in[0], *feed_in[1], *rest)
 
 
 ALL = ("dp", "tensor")
@@ -970,59 +993,19 @@
     return
 
 
-def assemble_kernel(axis, me_ref, x_ref, out_ref):
-    x = x_ref[...].astype(f32)
-    out_ref[...] = x.T if axis == 0 else x
-
-
-def assemble(blocks, axis, members=1):
-    _, rows, width = blocks.shape
-    tiles = 2
-    high = rows // tiles
-    narrow = width // members
-    if axis == 0:
-        out_spec = pl.BlockSpec((narrow, high), lambda b, m, t, me: (b ^ me[0], t))
-        shape = (4 * width, rows)
-    else:
-        out_spec = pl.BlockSpec((None, high, narrow), lambda b, m, t, me: (m, t, b ^ me[0]))
-        shape = (members, rows, narrow * 4)
-    return pl.pallas_call(
-        functools.partial(assemble_kernel, axis),
-        grid_spec=pltpu.PrefetchScalarGridSpec(
-            num_scalar_prefetch=1,
-            grid=(4, members, tiles),
-            in_specs=[pl.BlockSpec((None, high, narrow), lambda b, m, t, me: (b, t, m))],
-            out_specs=out_spec,
-        ),
-        out_shape=jax.ShapeDtypeStruct(shape, f32),
-        compiler_params=pltpu.CompilerParams(vmem_limit_bytes=40 * 2**20),
-        cost_estimate=pl.CostEstimate(flops=0, bytes_accessed=24 * rows * width, transcendentals=0),
-        name="assemble",
-    )(my_block().reshape(1), blocks)
-
-
-def core_sum(part):
-    send = [part(i, 2).astype(bf16) for i in BOTH]
-    got = [swap_core(x) for x in send]
-    keep = [add_low(part(i, 0), got[i]) for i in BOTH]
-    return keep[1], keep[0]
-
-
-def ffn_kernel(h_ref, *refs):
-    ups, downs = refs[:4], refs[4:8]
-    a_ref, d_ref, b_ref = refs[8:]
+def ffn_kernel(h_ref, up_ref, down_ref, a_ref, d_ref, b_ref):
     h = h_ref[...]
-    size = ups[0].shape[1]
+    size = 512
     total = None
     for j in range(4):
-        u = dot(h, ups[j][...])
+        cols = slice(j * size, (j + 1) * size)
+        u = dot(h, up_ref[:, cols])
         cdf = 0.5 + 0.5 * lax.erf(u * (0.5**0.5))
         slope = cdf + u * (jnp.exp(-0.5 * u * u) * 0.3989422804014327)
         act = (u * cdf).astype(bf16)
-        cols = slice(j * size, (j + 1) * size)
         a_ref[:, cols] = act
         d_ref[:, cols] = slope.astype(bf16)
-        term = dot(act, downs[j][...])
+        term = dot(act, down_ref[cols, :])
         total = term if total is None else total + term
     b_ref[...] = total
 
@@ -1031,64 +1014,23 @@
     return pl.BlockSpec(x.shape, lambda r: (0, 0))
 
 
-ROWS = 256
-
-
-def ffn_forward(h, ups, downs):
+ROWS = 512
+
+
+def ffn_forward(h, up, down):
     seq, width = h.shape
-    units = 4 * ups[0].shape[1]
+    units = up.shape[1]
     rows = lambda w: pl.BlockSpec((ROWS, w), lambda r: (r, 0))
     return pl.pallas_call(
         ffn_kernel,
         grid=(seq // ROWS,),
-        in_specs=[rows(width)] + [whole(x) for x in ups + downs],
+        in_specs=[rows(width)] + [whole(up), whole(down)],
         out_specs=[rows(units), rows(units), rows(width)],
         out_shape=[jax.ShapeDtypeStruct((seq, units), bf16)] * 2 + [jax.ShapeDtypeStruct((seq, width), f32)],
         compiler_params=pltpu.CompilerParams(vmem_limit_bytes=50 * 2**20),
         cost_estimate=pl.CostEstimate(flops=4 * seq * width * units, bytes_accessed=22 * 2**20, transcendentals=2 * seq * units),
         name="feed_forward",
-    )(h, *ups, *downs)
-
-
-def ffn_back_kernel(g_ref, d_ref, *refs):
-    ups, downs = refs[:4], refs[4:8]
-    du_ref, dh_ref = refs[-2:]
-    g = g_ref[...]
-    size = ups[0].shape[1]
-    total = refs[8][...] if len(refs) > 10 else None
-    for j in range(4):
-        cols = slice(j * size, (j + 1) * size)
-        du = (dot(g, downs[j][...], NT) * d_ref[:, cols].astype(f32)).astype(bf16)
-        du_ref[:, cols] = du
-        term = dot(du, ups[j][...], NT)
-        total = term if total is None else total + term
-    dh_ref[...] = total
-
-
-def ffn_backward(g, slope, ups, downs, before=None):
-    seq, width = g.shape
-    units = slope.shape[1]
-    rows = lambda w: pl.BlockSpec((ROWS, w), lambda r: (r, 0))
-    extra = [] if before is None else [before]
-    return pl.pallas_call(
-        ffn_back_kernel,
-        grid=(seq // ROWS,),
-        in_specs=[rows(width), rows(units)] + [whole(x) for x in ups + downs] + [rows(width)] * len(extra),
-        out_specs=[rows(units), rows(width)],
-        out_shape=[jax.ShapeDtypeStruct((seq, units), bf16), jax.ShapeDtypeStruct((seq, width), f32)],
-        compiler_params=pltpu.CompilerParams(vmem_limit_bytes=50 * 2**20),
-        cost_estimate=pl.CostEstimate(flops=4 * seq * width * units, bytes_accessed=22 * 2**20, transcendentals=0),
-        name="feed_forward_back",
-    )(g, slope, *ups, *downs, *extra)
-
-
-def side_by_side(parts):
-    return jnp.concatenate(parts, axis=1)
-
-
-def cols(x, first, last, of=4):
-    size = x.shape[1] // of
-    return x[:, first * size : last * size]
+    )(h, up, down)
 
 
 def arrange_kernel(me_ref, *refs):
@@ -1171,6 +1113,35 @@
     )(x)
 
 
+def spread_feed_kernel(x_ref, down_ref, up_ref):
+    even = lax.rem(pl.program_id(0), 2) == 0
+
+    @pl.when(even)
+    def _():
+        down_ref[...] = x_ref[...].astype(f32).T
+
+    @pl.when(jnp.logical_not(even))
+    def _():
+        up_ref[...] = x_ref[...].astype(f32)
+
+
+def spread_feed(blocks):
+    _, rows, width = blocks.shape
+    return pl.pallas_call(
+        spread_feed_kernel,
+        grid=(8,),
+        in_specs=[pl.BlockSpec((None, rows, width), lambda b: (b, 0, 0))],
+        out_specs=[
+            pl.BlockSpec((width, rows), lambda b: (b // 2, 0)),
+            pl.BlockSpec((rows, width), lambda b: (0, b // 2)),
+        ],
+        out_shape=[jax.ShapeDtypeStruct((4 * width, rows), f32), jax.ShapeDtypeStruct((rows, 4 * width), f32)],
+        compiler_params=pltpu.CompilerParams(vmem_limit_bytes=40 * 2**20),
+        cost_estimate=pl.CostEstimate(flops=0, bytes_accessed=48 * rows * width, transcendentals=0),
+        name="spread_feed",
+    )(blocks)
+
+
 def one_pair_each(
     target,
     memory,
@@ -1200,31 +1171,31 @@
     pipe.put(fetch(got, "cq", cq_s, (1, 1)))
     pipe.put(fetch(got, "kv", kv_s, (1, 1)))
     kv = [[dot(mem, cross_kv[m]).astype(bf16) for m in range(2)], None]
-    up_b = blocks_of(ffn_up, 1)
-    down_b = blocks_of(ffn_down, 0)
+    up_s, down_s = slab_of(ffn_up[None]), slab_of(ffn_down[None])
     target_t = flip(target)
     memory_t = flip(mem)
-    *_, up_b[0], co_s, target_t, memory_t = tie(*kv[0], *up_b[1:], *down_b, up_b[0], co_s, target_t, memory_t)
+    kv[0][0], up_s, co_s, target_t, memory_t = tie(kv[0][0], up_s, co_s, target_t, memory_t)
     tar = pipe.cut(target)
     qkv_oth = arrange(got["qkv"])
     q1[1] = [dot(tar, qkv_oth[m]).astype(bf16) for m in range(3)]
     pipe.put(fetch(got, "co", co_s, (1, 1)))
-    q1[1][0], up_b[0] = tie(q1[1][0], up_b[0])
-    pipe.put(fetch(got, "up", up_b[0], (2, 1)))
+    q1[1][0], up_s = tie(q1[1][0], up_s)
+    pipe.put(fetch(got, "up", up_s, (2, 1)))
     at1[1] = attend_fwd(*q1[1], length, True)
     at1[1], _ = tie(at1[1], at1[1][0])
     c1_oth = pipe.cut(at1[1][0])
     c1 = [at1[0][0], c1_oth]
     so_oth = arrange(got["so"])[0]
     b1 = dot(c1[0], self_out) + dot(c1[1], so_oth)
-    h1 = norm_rows(alpha_res * target.astype(f32) + b1, ln_gain[0], ln_bias[0])
+    sum1 = alpha_res * target.astype(f32) + b1
+    h1 = norm_rows(sum1, ln_gain[0], ln_bias[0])
     h1_low = h1.astype(bf16)
     cq_oth = arrange(got["cq"])[0]
     kv_oth = arrange(got["kv"])
     q2 = [dot(h1_low, cross_query).astype(bf16), dot(h1_low, cq_oth).astype(bf16)]
     kv[1] = [dot(memory, kv_oth[m]).astype(bf16) for m in range(2)]
-    q2[0], kv[1][0], down_b[0] = pipe.cut(q2[0], kv[1][0], down_b[0])
-    pipe.put(fetch(got, "down", down_b[0], (1, 1)))
+    q2[0], kv[1][0], down_s = pipe.cut(q2[0], kv[1][0], down_s)
+    pipe.put(fetch(got, "down", down_s, (1, 1)))
     at2 = [attend_fwd(q2[0], *kv[0], length, False), None]
     q2[1], _ = pipe.cut(q2[1], at2[0][0])
     at2[1] = attend_fwd(q2[1], *kv[1], length, False)
@@ -1232,78 +1203,49 @@
     c2 = [at2[0][0], at2[1][0]]
     c2[1] = pipe.cut(c2[1])
     b2 = dot(c2[0], cross_out) + dot(c2[1], co_oth)
-    h2, back2 = jax.vjp(norm_rows, alpha_res * h1 + b2, ln_gain[1], ln_bias[1])
+    sum2 = alpha_res * h1 + b2
+    h2 = norm_rows(sum2, ln_gain[1], ln_bias[1])
     h2_low = h2.astype(bf16)
-    act0, slope0, b3 = ffn_forward(h2_low, up_b, down_b)
-    h1_t = flip(h1_low)
+    act0, slope0, b3 = ffn_forward(h2_low, ffn_up, ffn_down)
+    h1_t, h2_t = flip(h1_low), flip(h2_low)
     while "up" not in got or "down" not in got:
         act0 = pipe.cut(act0)
-    h2_again, _ = tie(h2_low, act0)
-    act1, slope1, b3b = ffn_forward(h2_again, got["up"], got["down"])
-    act, slope = (act0, act1), (slope0, slope1)
+    h2_again, h1_t, h2_t, _ = tie(h2_low, h1_t, h2_t, act0)
+    up_oth, down_oth = arrange(got["up"])[0], arrange(got["down"])[0]
+    act1, slope1, b3b = ffn_forward(h2_again, up_oth, down_oth)
     result, back3 = jax.vjp(norm_rows, alpha_res * h2 + b3 + b3b, ln_gain[2], ln_bias[2])
-
     dz3, gain3, bias3 = back3(grad_out.astype(f32))
     g3 = dz3.astype(bf16)
-
-    def down_part(i, f):
-        return dot(g3, cols(act[i], f, f + 2), TN)
-
-    down_send = [down_part(i, 2).astype(bf16) for i in BOTH]
-    g3, *down_send = tie(g3, *down_send)
-    down_got = [swap_core(x) for x in down_send]
-    du1, dh2 = ffn_backward(g3, slope[1], got["up"], got["down"])
-    g3, dh2, *down_got = tie(g3, dh2, *down_got)
-    down_pair = (add_low(down_part(1, 0), down_got[1]), add_low(down_part(0, 0), down_got[0]))
-    du0, dh2 = ffn_backward(g3, slope[0], up_b, down_b, dh2)
-    du = (du0, du1)
-
-    def up_part(i, f):
-        return dot(h2_low, cols(du[i], f, f + 2), TN)
-
-    up_send = [up_part(i, 2).astype(bf16) for i in BOTH]
-    dh2, *up_send = tie(dh2, *up_send)
-    up_got = [swap_core(x) for x in up_send]
-    dz2, gain2, bias2 = back2(alpha_res * dz3 + dh2)
-    g2 = dz2.astype(bf16)
-    dc2 = [dot(g2, w, NT).astype(bf16) for w in (cross_out, co_oth)]
-    g2_t = flip(g2)
-    dc2[0], dc2[1], g2_t, *up_got = tie(*dc2, g2_t, *up_got)
-    up_pair = (add_low(up_part(1, 0), up_got[1]), add_low(up_part(0, 0), up_got[0]))
-    halves2 = [[q2[i], *kv[i], c2[i], at2[i][1], dc2[i]] for i in BOTH]
-    halves1 = [[*q1[i], c1[i], at1[i][1]] for i in BOTH]
-    none = jnp.zeros_like(gain2)
-    small = jnp.stack([none, gain2, gain3, none, bias2, bias3, none, none])
-    dk2, dv2, dq1, dk1, dv1, dz1, pairs, down_t, up_t, small = attention_back(
+    none = jnp.zeros_like(gain3)
+    small = jnp.stack([none, none, gain3, none, none, bias3, none, none])
+    dk2, dv2, dq1, dk1, dv1, dz1, blocks, _, small = layer_back(
         length,
-        halves2,
-        halves1,
-        [h1_t, memory_t, g2_t, target_t],
-        (cross_query, cq_oth),
-        (self_out, so_oth),
+        [[q2[i], *kv[i], c2[i], at2[i][1]] for i in BOTH],
+        [[*q1[i], c1[i], at1[i][1]] for i in BOTH],
+        (cross_out, co_oth, cross_query, cq_oth, self_out, so_oth),
         ln_gain,
         small,
-        alpha_res * target.astype(f32) + b1,
-        alpha_res * dz2,
-        down_pair,
-        up_pair,
-    )
-    pairs = pairs.reshape(8, 1024, 512)
-    cross_pairs, self_pairs = (pairs, 0), (pairs, 4)
+        [(act0, slope0, ffn_up, ffn_down), (act1, slope1, up_oth, down_oth)],
+        (g3, flip(g3), h2_t, h1_t, memory_t, target_t, alpha_res * dz3, sum2, sum1),
+    )
+    blocks = blocks.reshape(16, 1024, 512)
     kv_both = (cross_kv, kv_oth)
     dmem = sum(dot(d[i], kv_both[i][m], NT) for i in BOTH for m, d in enumerate((dk2, dv2)))
     qkv_both = (self_qkv, qkv_oth)
-    dtar = alpha_res * dz1 + sum(dot(d[i], qkv_both[i][m], NT) for i in BOTH for m, d in enumerate((dq1, dk1, dv1)))
+    dtar = dz1 + sum(dot(d[i], qkv_both[i][m], NT) for i in BOTH for m, d in enumerate((dq1, dk1, dv1)))
     cq_total, kv_total, co_total = spread(
-        *cross_pairs,
+        blocks,
+        8,
         ((0, 128, 0, 0), (128, 256, 1, 0), (256, 384, 1, 1), (384, 512, 2, None)),
         (1, 2, None),
     )
     qkv_total, so_total = spread(
-        *self_pairs,
+        blocks,
+        12,
         ((0, 128, 0, 0), (128, 256, 0, 1), (256, 384, 0, 2), (384, 512, 1, None)),
         (3, None),
     )
+    down_total, up_total = spread_feed(blocks)
     return (
         result.astype(bf16),
         dtar.astype(bf16),
@@ -1313,8 +1255,8 @@
         cq_total[0],
         kv_total,
         co_total,
-        assemble(up_t, 1)[0],
-        assemble(down_t, 0),
+        up_total,
+        down_total,
         small[:3],
         small[3:6],
     )

time: 710 us -> 615 us (0.87)
  matrix products: 125 us -> 72.1 us
  Pallas kernels: 465 us -> 434 us
    dot_general x36 -> x26, matrix products: 125 us -> 72.1 us  [dot(): return lax.dot_general(a, b, dims, preferred_element_type=f32)]
    pallas_call x5 -> x2, Pallas kernels: 345 us -> 298 us  [the longest x1 286 us: layer_back(): pl.pallas_call(back_kernel, grid=(3 * STEPS,), in_specs=[pl.BlockSpec(mem...]
    ppermute x32 -> x28, waiting for transfers between devices: 39 us -> 34.4 us  [swap(): return lax.ppermute(x, ALL, [(i, i ^ flip) for i in range(DEVICES)])]
    pallas_call x4 -> x5, Pallas kernels: 16.9 us -> 20.7 us  [flip(): pl.pallas_call(flip_kernel, grid=(4,), in_specs=[pl.BlockSpec((rows // 4,...]
    ppermute x32 -> x28, starting transfers between devices: 18.4 us -> 17.7 us  [swap(): return lax.ppermute(x, ALL, [(i, i ^ flip) for i in range(DEVICES)])]
    unnamed x182 -> x168, local copies, waits for them, and re-layouts: 14.9 us -> 14.5 us
  transfers between devices with their start and end apart: 32 -> 28, of which waited for: 8 -> 7; matrix products, arithmetic and copies ran while one was open for 11% -> 9% of each run, Pallas kernels for 16% -> 16%
where the time goes in v3:
time: 615 us; the launch traced here: 611 us
  Pallas kernels  434 us (71%)
  matrix products  72.1 us (12%)
  waiting for transfers between devices  34.4 us (6%)
  local copies, waits for them, and re-layouts  28.7 us (5%)
  other arithmetic  22.3 us (4%)
  starting transfers between devices  17.7 us (3%)
    pallas_call x1, Pallas kernels, layer_back(): pl.pallas_call(back_kernel, grid=(3 * STEPS,), in_specs=[pl.BlockSpec(mem...  286 us
    dot_general x26, matrix products, dot(): return lax.dot_general(a, b, dims, preferred_element_type=f32)  72.1 us
    pallas_call x4, Pallas kernels, attend_fwd(): pl.pallas_call(functools.partial(fwd_kernel, causal), grid=(width // 128,...  58.5 us
    ppermute x28, waiting for transfers between devices, swap(): return lax.ppermute(x, ALL, [(i, i ^ flip) for i in range(DEVICES)])  34.4 us
    pallas_call x2, Pallas kernels, ffn_forward(): pl.pallas_call(ffn_kernel, grid=(seq // ROWS,), in_specs=[rows(width)] +...  33.1 us
    pallas_call x5, Pallas kernels, flip(): pl.pallas_call(flip_kernel, grid=(4,), in_specs=[pl.BlockSpec((rows // 4,...  20.7 us
    ppermute x28, starting transfers between devices, swap(): return lax.ppermute(x, ALL, [(i, i ^ flip) for i in range(DEVICES)])  17.7 us
    pallas_call x2, Pallas kernels, spread(): pl.pallas_call(functools.partial(spread_kernel, spans), grid=(4, rows //...  14.7 us
  transfers between devices with their start and end apart: 28, of which 7 were waited for; matrix products, arithmetic and copies ran while one was open for 9% of the time, Pallas kernels for 16%

profile of v3, /device:TPU:0, one launch (start us, length us, event | category | flops | bytes accessed | tf_op | source)
XLA Modules:
  0.0 610.9 jit_solution(17296139741752450136)
XLA Ops:
  0.7 2.1 constant_dynamic-slice_fusion
  2.8 2.9 collective-permute-start
  5.7 3.2 convolution_convert_fusion.9.v_ref.refs_13_
  9.0 2.9 convolution_convert_fusion.10.k_ref.refs_12_
  13.0 1.9 constant_dynamic-slice_fusion.1
  16.5 3.1 convolution_convert_fusion.11.q_ref.refs_11_
  19.6 13.3 %attend_causal.2 = (bf16[1024,512]{1,0:T(8,128)(2,1)S(1)}, bf16[1024,512]{1,0:T(8,128)(2,1)S(1)}) custom-call(s32[1]{0:T(128)} %dynamic_slice.24.len_ref.refs_0_, bf16[1024,512]{1,0:T(8,128)(2,1)S(1)} %convolution_convert_fusion.11.q_ref.refs_11_, bf16[1024,512]{1,0:T(8,128)(2,1)S(1)} %convolution_convert_fusion.10.k_ref.refs_12_, ...), custom_call_target="tpu_custom_call" | custom-call | flops 5368709120 | bytes 8388608 | tf_op jit(solution)/shard_map/attend_causal/pallas_call | solution.py:422
  33.1 1.6 collective-permute-start.1
  35.4 1.5 collective-permute-start.3
  37.5 2.3 dynamic-slice_bitcast_fusion
  39.7 2.3 dynamic-slice_bitcast_fusion.1
  42.0 13.2 %collective-permute-done.3.refs_0_ = bf16[1,128,1024]{2,1,0:T(8,128)(2,1)S(1)} collective-permute-done((bf16[1,128,1024]{2,1,0:T(8,128)(2,1)S(1)}, bf16[1,128,1024]{2,1,0:T(8,128)(2,1)S(1)}, u32[]{:S(2)}, u32[]{:S(2)}) %collective-permute-start.3) | collective-permute-done | bytes 262176 | tf_op jit(solution)/shard_map/ppermute | solution.py:916
  55.2 4.8 collective-permute-done.4.refs_0_
  60.9 1.7 dynamic-slice_bitcast_fusion.2
  62.6 4.2 flip.5.refs_42_
  66.7 4.8 fusion.71
  71.5 4.1 flip.6.refs_41_
  75.6 4.2 convolution_convert_fusion.7.k_ref.refs_2_
  80.9 1.8 collective-permute-start.11
  87.1 1.4 collective-permute-done.13.refs_0_
  89.1 13.2 %attend_causal.3 = (bf16[1024,512]{1,0:T(8,128)(2,1)S(1)}, bf16[1024,512]{1,0:T(8,128)(2,1)S(1)}) custom-call(s32[1]{0:T(128)} %dynamic_slice.24.len_ref.refs_0_, bf16[1024,512]{1,0:T(8,128)(2,1)S(1)} %convolution_convert_fusion.8.q_ref.refs_16_, bf16[1024,512]{1,0:T(8,128)(2,1)S(1)} %convolution_convert_fusion.6.k_ref.refs_17_, ...), custom_call_target="tpu_custom_call" | custom-call | flops 5368709120 | bytes 8388608 | tf_op jit(solution)/shard_map/attend_causal/pallas_call | solution.py:422
  104.1 2.0 collective-permute-done.9.refs_1_
  106.2 2.2 convolution_convert_fusion.3.v_ref.refs_3_
  109.2 1.7 collective-permute-start.18
  111.6 1.5 fusion.69
  116.5 2.2 convolution_convert_fusion.4.q_ref.refs_1_
  118.7 4.1 flip.7.refs_40_
  124.1 3.2 convolution_convert_fusion.2.q_ref.refs_6_
  127.4 1.9 arrange.9
  131.5 2.8 collective-permute-done.18.refs_0_
  134.3 1.7 collective-permute-start.20
  136.0 1.5 collective-permute-start.22
  138.8 16.2 %attend_memory.2 = (bf16[1024,512]{1,0:T(8,128)(2,1)S(1)}, bf16[1024,512]{1,0:T(8,128)(2,1)S(1)}) custom-call(s32[1]{0:T(128)} %dynamic_slice.24.len_ref.refs_0_, bf16[1024,512]{1,0:T(8,128)(2,1)S(1)} %copy-done.43, bf16[1024,512]{1,0:T(8,128)(2,1)S(1)} %copy-done.38, bf16[1024,512]{1,0:T(8,128)(2,1)S(1)} %copy-done.42), custom_call_target="tpu_custom_call" | custom-call | flops 8589934592 | bytes 8388608 | tf_op jit(solution)/shard_map/attend_memory/pallas_call | solution.py:422
  155.0 6.2 %collective-permute-done.22.refs_0_ = bf16[1,512,1024]{2,1,0:T(8,128)(2,1)S(1)} collective-permute-done((bf16[1,512,1024]{2,1,0:T(8,128)(2,1)S(1)}, bf16[1,512,1024]{2,1,0:T(8,128)(2,1)S(1)}, u32[]{:S(2)}, u32[]{:S(2)}) %collective-permute-start.22) | collective-permute-done | bytes 1048608 | tf_op jit(solution)/shard_map/ppermute | solution.py:916
  161.8 3.3 fusion.72
  166.5 15.8 %attend_memory.3 = (bf16[1024,512]{1,0:T(8,128)(2,1)S(1)}, bf16[1024,512]{1,0:T(8,128)(2,1)S(1)}) custom-call(s32[1]{0:T(128)} %dynamic_slice.24.len_ref.refs_0_, bf16[1024,512]{1,0:T(8,128)(2,1)S(1)} %convolution_convert_fusion.2.q_ref.refs_6_, bf16[1024,512]{1,0:T(8,128)(2,1)S(1)} %fusion.6.k_ref.refs_7_, bf16[1024,512]{1,0:T(8,128)(2,1)S(1)} %fusion.7.v_ref.refs_8_), custom_call_target="tpu_custom_call" | custom-call | flops 8589934592 | bytes 8388608 | tf_op jit(solution)/shard_map/attend_memory/pallas_call | solution.py:422
  183.2 3.8 collective-permute-done.23.refs_1_
  187.1 3.8 fusion.70
  192.8 2.0 fusion.5.h_ref.x_ref
  194.9 4.2 flip.8.refs_39_
  199.1 16.6 %feed_forward.2 = (bf16[1024,2048]{1,0:T(8,128)(2,1)}, bf16[1024,2048]{1,0:T(8,128)(2,1)}, f32[1024,1024]{1,0:T(8,128)}) custom-call(bf16[1024,1024]{1,0:T(8,128)(2,1)S(1)} %copy-done, bf16[1024,2048]{1,0:T(8,128)(2,1)} %refs_31_.1, bf16[2048,1024]{1,0:T(8,128)(2,1)} %refs_32_.1), custom_call_target="tpu_custom_call" | custom-call | flops 8589934592 | bytes 23068672 | tf_op jit(solution)/shard_map/feed_forward/pallas_call | solution.py:1024
  215.8 2.1 arrange.12
  217.9 2.0 copy-done.5
  219.9 2.0 arrange.13
  221.9 2.0 copy-done.6
  223.9 16.4 %feed_forward.3 = (bf16[1024,2048]{1,0:T(8,128)(2,1)}, bf16[1024,2048]{1,0:T(8,128)(2,1)}, f32[1024,1024]{1,0:T(8,128)}) custom-call(bf16[1024,1024]{1,0:T(8,128)(2,1)S(1)} %copy-done, bf16[1024,2048]{1,0:T(8,128)(2,1)} %bitcast.138, bf16[2048,1024]{1,0:T(8,128)(2,1)} %bitcast.140), custom_call_target="tpu_custom_call" | custom-call | flops 8589934592 | bytes 23068672 | tf_op jit(solution)/shard_map/feed_forward/pallas_call | solution.py:1024
  240.4 3.3 fusion.65
  245.3 2.0 fusion.2
  247.2 3.2 fusion.64
  250.4 3.2 add_multiply_fusion
  253.6 4.1 flip.9.refs_38_
  258.3 286.4 %layer_back.1 = (bf16[2,1024,512]{2,1,0:T(8,128)(2,1)}, bf16[2,1024,512]{2,1,0:T(8,128)(2,1)}, bf16[2,1024,512]{2,1,0:T(8,128)(2,1)}, bf16[2,1024,512]{2,1,0:T(8...) custom-call(s32[1]{0:T(128)} %dynamic_slice.24.len_ref.refs_0_, ...), custom_call_target="tpu_custom_call" | custom-call | flops 137438953472 | bytes 16777216 | tf_op jit(solution)/shard_map/layer_back/pallas_call | solution.py:868
  544.7 2.7 fusion.22
  550.5 3.3 fusion.24
  553.8 3.3 fusion.20
  557.1 3.4 fusion.26
  560.5 3.3 fusion.12
  563.8 3.2 fusion.16
  567.0 7.3 %spread.3 = (f32[1,1024,512]{2,1,0:T(8,128)}, f32[2,1024,512]{2,1,0:T(8,128)}, f32[512,1024]{1,0:T(8,128)}) custom-call(bf16[16,1024,512]{2,1,0:T(8,128)(2,1)} %bitcast.143), custom_call_target="tpu_custom_call" | custom-call | bytes 12582912 | tf_op jit(solution)/shard_map/spread/pallas_call | solution.py:1087
  574.3 7.4 %spread.2 = (f32[3,1024,512]{2,1,0:T(8,128)}, f32[512,1024]{1,0:T(8,128)}) custom-call(bf16[16,1024,512]{2,1,0:T(8,128)(2,1)} %bitcast.144), custom_call_target="tpu_custom_call" | custom-call | bytes 12582912 | tf_op jit(solution)/shard_map/spread/pallas_call | solution.py:1087
  581.8 11.2 %spread_feed.1 = (f32[2048,1024]{1,0:T(8,128)}, f32[1024,2048]{1,0:T(8,128)}) custom-call(bf16[16,1024,512]{2,1,0:T(8,128)(2,1)} %bitcast.145), custom_call_target="tpu_custom_call" | custom-call | bytes 25165824 | tf_op jit(solution)/shard_map/spread_feed/pallas_call | solution.py:1130
  593.6 3.4 fusion.14
  597.9 6.4 %add_convert_fusion = bf16[1024,1024]{1,0:T(8,128)(2,1)} fusion(f32[1024,1024]{1,0:T(8,128)S(1)} %copy-done.63, f32[1024,1024]{1,0:T(8,128)} %fusion.16, f32[1024,1024]{1,0:T(8,128)} %fusion.14, bf16[2,1024,512]{2,1,0:T(8,128)(2,1)S(1)} %copy-done.68, bf16[2,1024,512]{2,1,0:T(8,128)(2,1)S(1)} %copy-done.2), kind=kOutput, calls=%fused_computation.8 | convolution fusion | flops 1077936128 | bytes 16777216 | tf_op jit(solution)/shard_map/dot_general | solution.py:355
  604.3 6.3 %add_convert_fusion.1 = bf16[1024,1024]{1,0:T(8,128)(2,1)} fusion(f32[1024,1024]{1,0:T(8,128)S(1)} %copy-done.59, f32[1024,1024]{1,0:T(8,128)S(1)} %fusion.18, f32[1024,1024]{1,0:T(8,128)} %fusion.20, f32[1024,1024]{1,0:T(8,128)S(1)} %fusion.22, f32[1024,1024]{1,0:T(8,128)S(1)} %copy-done.60, f32[1024,1024]{1,0:T(8,128)S(1)} %fusion.28, f32[1024,1024]{1,0:T(8,128)} %fusion.26), kind=kLoop, calls=%fused_computation.9 | loop fusion | flops 7340032 | bytes 31457280 | tf_op jit(solution)/shard_map/convert_element_type | solution.py:1251
  (239 shorter events, 33.8 us)
Async XLA Ops:
  2.8 30.3 %collective-permute-start = (bf16[3,256,512]{2,1,0:T(8,128)(2,1)}, bf16[3,256,512]{2,1,0:T(8,128)(2,1)S(1)}, u32[]{:S(2)}, u32[]{:S(2)}) collective-permute-start(bf16[3,256,512]{2,1,0:T(8,128)(2,1)} %constant_dynamic-slice_fusion), channel_id=1, source_target_pairs={{0,1},{1,0},{2,3},{3,2},{4,5},{5,4},{6,7},{7,6},{8,9},{9,8},{10,11... | collective-permute-start | bytes 2359304 | tf_op jit(solution)/shard_map/ppermute | solution.py:916
  9.0 10.6 %copy-start.35 = (bf16[1024,512]{1,0:T(8,128)(2,1)}, bf16[1024,512]{1,0:T(8,128)(2,1)S(1)}, u32[]{:S(2)}) copy-start(bf16[1024,512]{1,0:T(8,128)(2,1)S(1)} %convolution_convert_fusion.9.v_ref.refs_13_) | copy-start | bytes 3145732
  11.8 7.8 %copy-start.36 = (bf16[1024,512]{1,0:T(8,128)(2,1)}, bf16[1024,512]{1,0:T(8,128)(2,1)S(1)}, u32[]{:S(2)}) copy-start(bf16[1024,512]{1,0:T(8,128)(2,1)S(1)} %convolution_convert_fusion.10.k_ref.refs_12_) | copy-start | bytes 3145732
  19.6 13.4 %copy-start.37 = (bf16[1024,512]{1,0:T(8,128)(2,1)}, bf16[1024,512]{1,0:T(8,128)(2,1)S(1)}, u32[]{:S(2)}) copy-start(bf16[1024,512]{1,0:T(8,128)(2,1)S(1)} %convolution_convert_fusion.11.q_ref.refs_11_) | copy-start | bytes 3145732
  19.6 15.1 %copy-start.77 = (f32[3,1024]{1,0:T(4,128)S(1)}, f32[3,1024]{1,0:T(4,128)}, u32[]{:S(2)}) copy-start(f32[3,1024]{1,0:T(4,128)} %param.25) | copy-start | bytes 36868
  19.6 15.1 %copy-start.69 = (bf16[2,256,512]{2,1,0:T(8,128)(2,1)S(1)}, bf16[2,256,512]{2,1,0:T(8,128)(2,1)}, u32[]{:S(2)}) copy-start(bf16[2,256,512]{2,1,0:T(8,128)(2,1)} %constant_dynamic-slice_fusion.1) | copy-start | bytes 1572868
  19.6 15.7 %copy-start.78 = (f32[3,1024]{1,0:T(4,128)S(1)}, f32[3,1024]{1,0:T(4,128)}, u32[]{:S(2)}) copy-start(f32[3,1024]{1,0:T(4,128)} %refs_27_.1) | copy-start | bytes 36868
  33.0 27.9 %copy-start.33 = (bf16[1024,512]{1,0:T(8,128)(2,1)}, bf16[1024,512]{1,0:T(8,128)(2,1)S(1)}, u32[]{:S(2)}) copy-start(bf16[1024,512]{1,0:T(8,128)(2,1)S(1)} %get-tuple-element.83.refs_14_) | copy-start | bytes 3145732
  33.0 27.9 %copy-start.47 = (bf16[1024,512]{1,0:T(8,128)(2,1)}, bf16[1024,512]{1,0:T(8,128)(2,1)S(1)}, u32[]{:S(2)}) copy-start(bf16[1024,512]{1,0:T(8,128)(2,1)S(1)} %get-tuple-element.130.refs_15_) | copy-start | bytes 3145732
  33.0 27.0 %collective-permute-start.2 = (bf16[3,256,512]{2,1,0:T(8,128)(2,1)S(1)}, bf16[3,256,512]{2,1,0:T(8,128)(2,1)S(1)}, u32[]{:S(2)}, u32[]{:S(2)}) collective-permute-start(bf16[3,256,512]{2,1,0:T(8,128)(2,1)S(1)} %collective-permute-done.refs_0_), channel_id=1, source_target_pairs={{0,2},{1,3},{2,0},{3,1},{4,6},{5,7},{6,4},{7,5},{8,10},{9,11},{10,... | collective-permute-start | bytes 2359304 | tf_op jit(solution)/shard_map/ppermute | solution.py:916
  33.1 26.9 %collective-permute-start.1 = (bf16[3,256,512]{2,1,0:T(8,128)(2,1)S(1)}, bf16[3,256,512]{2,1,0:T(8,128)(2,1)S(1)}, u32[]{:S(2)}, u32[]{:S(2)}) collective-permute-start(bf16[3,256,512]{2,1,0:T(8,128)(2,1)S(1)} %collective-permute-done.refs_0_), channel_id=1, source_target_pairs={{0,4},{1,5},{2,6},{3,7},{4,0},{5,1},{6,2},{7,3},{8,12},{9,13},{10,... | collective-permute-start | bytes 2359304 | tf_op jit(solution)/shard_map/ppermute | solution.py:916
  34.7 25.3 %collective-permute-start.5 = (bf16[2,256,512]{2,1,0:T(8,128)(2,1)S(1)}, bf16[2,256,512]{2,1,0:T(8,128)(2,1)S(1)}, u32[]{:S(2)}, u32[]{:S(2)}) collective-permute-start(bf16[2,256,512]{2,1,0:T(8,128)(2,1)S(1)} %copy-done.69), channel_id=1, source_target_pairs={{0,1},{1,0},{2,3},{3,2},{4,5},{5,4},{6,7},{7,6},{8,9},{9,8},{10,11... | collective-permute-start | bytes 1572872 | tf_op jit(solution)/shard_map/ppermute | solution.py:916
  35.4 19.8 %collective-permute-start.3 = (bf16[1,128,1024]{2,1,0:T(8,128)(2,1)S(1)}, bf16[1,128,1024]{2,1,0:T(8,128)(2,1)S(1)}, u32[]{:S(2)}, u32[]{:S(2)}) collective-permute-start(bf16[1,128,1024]{2,1,0:T(8,128)(2,1)S(1)} %dynamic-slice_bitcast_fusion.4), channel_id=1, source_target_pairs={{0,1},{1,0},{2,3},{3,2},{4,5},{5,4},{6,7},{7,6},{8,9},{9,8},{10,11... | collective-permute-start | bytes 786440 | tf_op jit(solution)/shard_map/ppermute | solution.py:916
  36.9 23.1 %collective-permute-start.4 = (bf16[1,256,512]{2,1,0:T(8,128)(2,1)S(1)}, bf16[1,256,512]{2,1,0:T(8,128)(2,1)S(1)}, u32[]{:S(2)}, u32[]{:S(2)}) collective-permute-start(bf16[1,256,512]{2,1,0:T(8,128)(2,1)S(1)} %dynamic-slice_bitcast_fusion.3), channel_id=1, source_target_pairs={{0,1},{1,0},{2,3},{3,2},{4,5},{5,4},{6,7},{7,6},{8,9},{9,8},{10,11... | collective-permute-start | bytes 786440 | tf_op jit(solution)/shard_map/ppermute | solution.py:916
  60.9 20.1 %collective-permute-start.6 = (bf16[3,256,512]{2,1,0:T(8,128)(2,1)S(1)}, bf16[3,256,512]{2,1,0:T(8,128)(2,1)S(1)}, u32[]{:S(2)}, u32[]{:S(2)}) collective-permute-start(bf16[3,256,512]{2,1,0:T(8,128)(2,1)S(1)} %collective-permute-done.1.refs_1_), channel_id=1, source_target_pairs={{0,2},{1,3},{2,0},{3,1},{4,6},{5,7},{6,4},{7,5},{8,10},{9,11},{10,... | collective-permute-start | bytes 2359304 | tf_op jit(solution)/shard_map/ppermute | solution.py:916
  79.8 8.7 %collective-permute-start.13 = (bf16[1,128,1024]{2,1,0:T(8,128)(2,1)S(1)}, bf16[1,128,1024]{2,1,0:T(8,128)(2,1)S(1)}, u32[]{:S(2)}, u32[]{:S(2)}) collective-permute-start(bf16[1,128,1024]{2,1,0:T(8,128)(2,1)S(1)} %copy-done.70), channel_id=1, source_target_pairs={{0,1},{1,0},{2,3},{3,2},{4,5},{5,4},{6,7},{7,6},{8,9},{9,8},{10,11... | collective-permute-start | bytes 786440 | tf_op jit(solution)/shard_map/ppermute | solution.py:916
  80.4 8.2 %collective-permute-start.8 = (bf16[1,128,1024]{2,1,0:T(8,128)(2,1)S(1)}, bf16[1,128,1024]{2,1,0:T(8,128)(2,1)S(1)}, u32[]{:S(2)}, u32[]{:S(2)}) collective-permute-start(bf16[1,128,1024]{2,1,0:T(8,128)(2,1)S(1)} %copy-done.28), channel_id=1, source_target_pairs={{0,2},{1,3},{2,0},{3,1},{4,6},{5,7},{6,4},{7,5},{8,10},{9,11},{10,... | collective-permute-start | bytes 786440 | tf_op jit(solution)/shard_map/ppermute | solution.py:916
  80.6 22.7 %collective-permute-start.7 = (bf16[1,128,1024]{2,1,0:T(8,128)(2,1)S(1)}, bf16[1,128,1024]{2,1,0:T(8,128)(2,1)S(1)}, u32[]{:S(2)}, u32[]{:S(2)}) collective-permute-start(bf16[1,128,1024]{2,1,0:T(8,128)(2,1)S(1)} %copy-done.28), channel_id=1, source_target_pairs={{0,4},{1,5},{2,6},{3,7},{4,0},{5,1},{6,2},{7,3},{8,12},{9,13},{10,... | collective-permute-start | bytes 786440 | tf_op jit(solution)/shard_map/ppermute | solution.py:916
  80.9 25.1 %collective-permute-start.12 = (bf16[2,256,512]{2,1,0:T(8,128)(2,1)S(1)}, bf16[2,256,512]{2,1,0:T(8,128)(2,1)S(1)}, u32[]{:S(2)}, u32[]{:S(2)}) collective-permute-start(bf16[2,256,512]{2,1,0:T(8,128)(2,1)S(1)} %copy-done.21), channel_id=1, source_target_pairs={{0,2},{1,3},{2,0},{3,1},{4,6},{5,7},{6,4},{7,5},{8,10},{9,11},{10,... | collective-permute-start | bytes 1572872 | tf_op jit(solution)/shard_map/ppermute | solution.py:916
  80.9 25.1 %collective-permute-start.11 = (bf16[2,256,512]{2,1,0:T(8,128)(2,1)S(1)}, bf16[2,256,512]{2,1,0:T(8,128)(2,1)}, u32[]{:S(2)}, u32[]{:S(2)}) collective-permute-start(bf16[2,256,512]{2,1,0:T(8,128)(2,1)S(1)} %copy-done.21), channel_id=1, source_target_pairs={{0,4},{1,5},{2,6},{3,7},{4,0},{5,1},{6,2},{7,3},{8,12},{9,13},{10,... | collective-permute-start | bytes 1572872 | tf_op jit(solution)/shard_map/ppermute | solution.py:916
  87.1 15.3 %copy-start.41 = (bf16[1024,512]{1,0:T(8,128)(2,1)}, bf16[1024,512]{1,0:T(8,128)(2,1)S(1)}, u32[]{:S(2)}) copy-start(bf16[1024,512]{1,0:T(8,128)(2,1)S(1)} %convolution_convert_fusion.8.q_ref.refs_16_) | copy-start | bytes 3145732
  87.1 19.1 %copy-start.64 = (bf16[1024,1024]{1,0:T(8,128)(2,1)S(1)}, bf16[1024,1024]{1,0:T(8,128)(2,1)}, u32[]{:S(2)}) copy-start(bf16[1024,1024]{1,0:T(8,128)(2,1)} %x_ref.2) | copy-start | bytes 6291460
  87.1 19.1 %copy-start.72 = (bf16[2,1024,512]{2,1,0:T(8,128)(2,1)S(1)}, bf16[2,1024,512]{2,1,0:T(8,128)(2,1)}, u32[]{:S(2)}) copy-start(bf16[2,1024,512]{2,1,0:T(8,128)(2,1)} %param.20) | copy-start | bytes 6291460
  88.5 14.8 %collective-permute-start.10 = (bf16[1,256,512]{2,1,0:T(8,128)(2,1)S(1)}, bf16[1,256,512]{2,1,0:T(8,128)(2,1)S(1)}, u32[]{:S(2)}, u32[]{:S(2)}) collective-permute-start(bf16[1,256,512]{2,1,0:T(8,128)(2,1)S(1)} %copy-done.26), channel_id=1, source_target_pairs={{0,2},{1,3},{2,0},{3,1},{4,6},{5,7},{6,4},{7,5},{8,10},{9,11},{10,... | collective-permute-start | bytes 786440 | tf_op jit(solution)/shard_map/ppermute | solution.py:916
  88.6 17.5 %collective-permute-start.9 = (bf16[1,256,512]{2,1,0:T(8,128)(2,1)S(1)}, bf16[1,256,512]{2,1,0:T(8,128)(2,1)}, u32[]{:S(2)}, u32[]{:S(2)}) collective-permute-start(bf16[1,256,512]{2,1,0:T(8,128)(2,1)S(1)} %copy-done.26), channel_id=1, source_target_pairs={{0,4},{1,5},{2,6},{3,7},{4,0},{5,1},{6,2},{7,3},{8,12},{9,13},{10,... | collective-permute-start | bytes 786440 | tf_op jit(solution)/shard_map/ppermute | solution.py:916
  103.3 8.3 %copy-start.9 = (bf16[1024,512]{1,0:T(8,128)(2,1)}, bf16[1024,512]{1,0:T(8,128)(2,1)S(1)}, u32[]{:S(2)}) copy-start(bf16[1024,512]{1,0:T(8,128)(2,1)S(1)} %get-tuple-element.99.refs_19_) | copy-start | bytes 3145732
  106.1 4.8 collective-permute-start.14
  108.4 22.3 %collective-permute-start.17 = (bf16[1,128,1024]{2,1,0:T(8,128)(2,1)S(1)}, bf16[1,128,1024]{2,1,0:T(8,128)(2,1)S(1)}, u32[]{:S(2)}, u32[]{:S(2)}) collective-permute-start(bf16[1,128,1024]{2,1,0:T(8,128)(2,1)S(1)} %collective-permute-done.13.refs_0_), channel_id=1, source_target_pairs={{0,2},{1,3},{2,0},{3,1},{4,6},{5,7},{6,4},{7,5},{8,10},{9,11},{10,... | collective-permute-start | bytes 786440 | tf_op jit(solution)/shard_map/ppermute | solution.py:916
  108.9 22.6 %collective-permute-start.16 = (bf16[1,128,1024]{2,1,0:T(8,128)(2,1)S(1)}, bf16[1,128,1024]{2,1,0:T(8,128)(2,1)}, u32[]{:S(2)}, u32[]{:S(2)}) collective-permute-start(bf16[1,128,1024]{2,1,0:T(8,128)(2,1)S(1)} %collective-permute-done.13.refs_0_), channel_id=1, source_target_pairs={{0,4},{1,5},{2,6},{3,7},{4,0},{5,1},{6,2},{7,3},{8,12},{9,13},{10,... | collective-permute-start | bytes 786440 | tf_op jit(solution)/shard_map/ppermute | solution.py:916
  109.2 25.1 %collective-permute-start.18 = (bf16[1,256,2048]{2,1,0:T(8,128)(2,1)}, bf16[1,256,2048]{2,1,0:T(8,128)(2,1)S(1)}, u32[]{:S(2)}, u32[]{:S(2)}) collective-permute-start(bf16[1,256,2048]{2,1,0:T(8,128)(2,1)} %dynamic-slice_bitcast_fusion.1), channel_id=1, source_target_pairs={{0,1},{1,0},{2,3},{3,2},{4,5},{5,4},{6,7},{7,6},{8,9},{9,8},{10,11... | collective-permute-start | bytes 3145736 | tf_op jit(solution)/shard_map/ppermute | solution.py:916
  110.9 11.9 %collective-permute-start.19 = (bf16[1,256,512]{2,1,0:T(8,128)(2,1)}, bf16[1,256,512]{2,1,0:T(8,128)(2,1)}, u32[]{:S(2)}, u32[]{:S(2)}) collective-permute-start(bf16[1,256,512]{2,1,0:T(8,128)(2,1)} %collective-permute-done.9.refs_1_), channel_id=1, source_target_pairs={{0,2},{1,3},{2,0},{3,1},{4,6},{5,7},{6,4},{7,5},{8,10},{9,11},{10,... | collective-permute-start | bytes 786440 | tf_op jit(solution)/shard_map/ppermute | solution.py:916
  110.9 16.4 %collective-permute-start.15 = (bf16[2,256,512]{2,1,0:T(8,128)(2,1)}, bf16[2,256,512]{2,1,0:T(8,128)(2,1)S(1)}, u32[]{:S(2)}, u32[]{:S(2)}) collective-permute-start(bf16[2,256,512]{2,1,0:T(8,128)(2,1)} %collective-permute-done.11.refs_1_), channel_id=1, source_target_pairs={{0,2},{1,3},{2,0},{3,1},{4,6},{5,7},{6,4},{7,5},{8,10},{9,11},{10,... | collective-permute-start | bytes 1572872 | tf_op jit(solution)/shard_map/ppermute | solution.py:916
  127.3 39.2 %copy-start.44 = (bf16[1024,512]{1,0:T(8,128)(2,1)}, bf16[1024,512]{1,0:T(8,128)(2,1)S(1)}, u32[]{:S(2)}) copy-start(bf16[1024,512]{1,0:T(8,128)(2,1)S(1)} %convolution_convert_fusion.2.q_ref.refs_6_) | copy-start | bytes 3145732
  129.5 8.0 %copy-start.1 = (bf16[2,1024,512]{2,1,0:T(8,128)(2,1)}, bf16[2,1024,512]{2,1,0:T(8,128)(2,1)S(1)}, u32[]{:S(2)}) copy-start(bf16[2,1024,512]{2,1,0:T(8,128)(2,1)S(1)} %arrange.9) | copy-start | bytes 6291460
  129.5 6.5 %copy-start.66 = (bf16[1,512,1024]{2,1,0:T(8,128)(2,1)S(1)}, bf16[1,512,1024]{2,1,0:T(8,128)(2,1)}, u32[]{:S(2)}) copy-start(bf16[1,512,1024]{2,1,0:T(8,128)(2,1)} %dynamic-slice_bitcast_fusion) | copy-start | bytes 3145732
  130.7 8.1 %copy-start.38 = (bf16[1024,512]{1,0:T(8,128)(2,1)S(1)}, bf16[1024,512]{1,0:T(8,128)(2,1)}, u32[]{:S(2)}) copy-start(bf16[1024,512]{1,0:T(8,128)(2,1)} %convolution_convert_fusion.7.k_ref.refs_2_) | copy-start | bytes 3145732
  130.7 8.1 %copy-start.42 = (bf16[1024,512]{1,0:T(8,128)(2,1)S(1)}, bf16[1024,512]{1,0:T(8,128)(2,1)}, u32[]{:S(2)}) copy-start(bf16[1024,512]{1,0:T(8,128)(2,1)} %convolution_convert_fusion.3.v_ref.refs_3_) | copy-start | bytes 3145732
  130.7 8.1 %copy-start.43 = (bf16[1024,512]{1,0:T(8,128)(2,1)S(1)}, bf16[1024,512]{1,0:T(8,128)(2,1)}, u32[]{:S(2)}) copy-start(bf16[1024,512]{1,0:T(8,128)(2,1)} %convolution_convert_fusion.4.q_ref.refs_1_) | copy-start | bytes 3145732
  134.3 27.0 %collective-permute-start.21 = (bf16[1,256,2048]{2,1,0:T(8,128)(2,1)S(1)}, bf16[1,256,2048]{2,1,0:T(8,128)(2,1)S(1)}, u32[]{:S(2)}, u32[]{:S(2)}) collective-permute-start(bf16[1,256,2048]{2,1,0:T(8,128)(2,1)S(1)} %collective-permute-done.18.refs_0_), channel_id=1, source_target_pairs={{0,2},{1,3},{2,0},{3,1},{4,6},{5,7},{6,4},{7,5},{8,10},{9,11},{10,... | collective-permute-start | bytes 3145736 | tf_op jit(solution)/shard_map/ppermute | solution.py:916
  134.3 27.0 %collective-permute-start.20 = (bf16[1,256,2048]{2,1,0:T(8,128)(2,1)S(1)}, bf16[1,256,2048]{2,1,0:T(8,128)(2,1)}, u32[]{:S(2)}, u32[]{:S(2)}) collective-permute-start(bf16[1,256,2048]{2,1,0:T(8,128)(2,1)S(1)} %collective-permute-done.18.refs_0_), channel_id=1, source_target_pairs={{0,4},{1,5},{2,6},{3,7},{4,0},{5,1},{6,2},{7,3},{8,12},{9,13},{10,... | collective-permute-start | bytes 3145736 | tf_op jit(solution)/shard_map/ppermute | solution.py:916
  136.0 25.3 %collective-permute-start.22 = (bf16[1,512,1024]{2,1,0:T(8,128)(2,1)S(1)}, bf16[1,512,1024]{2,1,0:T(8,128)(2,1)S(1)}, u32[]{:S(2)}, u32[]{:S(2)}) collective-permute-start(bf16[1,512,1024]{2,1,0:T(8,128)(2,1)S(1)} %copy-done.66), channel_id=1, source_target_pairs={{0,1},{1,0},{2,3},{3,2},{4,5},{5,4},{6,7},{7,6},{8,9},{9,8},{10,11... | collective-permute-start | bytes 3145736 | tf_op jit(solution)/shard_map/ppermute | solution.py:916
  138.7 27.8 %copy-start.46 = (bf16[1024,512]{1,0:T(8,128)(2,1)}, bf16[1024,512]{1,0:T(8,128)(2,1)S(1)}, u32[]{:S(2)}) copy-start(bf16[1024,512]{1,0:T(8,128)(2,1)S(1)} %fusion.7.v_ref.refs_8_) | copy-start | bytes 3145732
  138.7 23.0 %copy-start.75 = (bf16[512,1024]{1,0:T(8,128)(2,1)S(1)}, bf16[512,1024]{1,0:T(8,128)(2,1)}, u32[]{:S(2)}) copy-start(bf16[512,1024]{1,0:T(8,128)(2,1)} %refs_21_.1) | copy-start | bytes 3145732
  138.7 26.3 %collective-permute-start.25 = (bf16[1,128,1024]{2,1,0:T(8,128)(2,1)}, bf16[1,128,1024]{2,1,0:T(8,128)(2,1)S(1)}, u32[]{:S(2)}, u32[]{:S(2)}) collective-permute-start(bf16[1,128,1024]{2,1,0:T(8,128)(2,1)} %collective-permute-done.16.refs_1_), channel_id=1, source_target_pairs={{0,2},{1,3},{2,0},{3,1},{4,6},{5,7},{6,4},{7,5},{8,10},{9,11},{10,... | collective-permute-start | bytes 786440 | tf_op jit(solution)/shard_map/ppermute | solution.py:916
  155.0 10.0 %copy-start.34 = (bf16[1024,512]{1,0:T(8,128)(2,1)}, bf16[1024,512]{1,0:T(8,128)(2,1)S(1)}, u32[]{:S(2)}) copy-start(bf16[1024,512]{1,0:T(8,128)(2,1)S(1)} %get-tuple-element.108.refs_4_) | copy-start | bytes 3145732
  155.0 10.0 %copy-start.49 = (bf16[1024,512]{1,0:T(8,128)(2,1)}, bf16[1024,512]{1,0:T(8,128)(2,1)S(1)}, u32[]{:S(2)}) copy-start(bf16[1024,512]{1,0:T(8,128)(2,1)S(1)} %get-tuple-element.128.refs_5_) | copy-start | bytes 3145732
  161.3 21.9 %collective-permute-start.24 = (bf16[1,512,1024]{2,1,0:T(8,128)(2,1)S(1)}, bf16[1,512,1024]{2,1,0:T(8,128)(2,1)S(1)}, u32[]{:S(2)}, u32[]{:S(2)}) collective-permute-start(bf16[1,512,1024]{2,1,0:T(8,128)(2,1)S(1)} %collective-permute-done.22.refs_0_), channel_id=1, source_target_pairs={{0,2},{1,3},{2,0},{3,1},{4,6},{5,7},{6,4},{7,5},{8,10},{9,11},{10,... | collective-permute-start | bytes 3145736 | tf_op jit(solution)/shard_map/ppermute | solution.py:916
  161.4 25.7 %collective-permute-start.23 = (bf16[1,512,1024]{2,1,0:T(8,128)(2,1)S(1)}, bf16[1,512,1024]{2,1,0:T(8,128)(2,1)}, u32[]{:S(2)}, u32[]{:S(2)}) collective-permute-start(bf16[1,512,1024]{2,1,0:T(8,128)(2,1)S(1)} %collective-permute-done.22.refs_0_), channel_id=1, source_target_pairs={{0,4},{1,5},{2,6},{3,7},{4,0},{5,1},{6,2},{7,3},{8,12},{9,13},{10,... | collective-permute-start | bytes 3145736 | tf_op jit(solution)/shard_map/ppermute | solution.py:916
  166.2 20.8 %copy-start.4 = (bf16[1,512,1024]{2,1,0:T(8,128)(2,1)}, bf16[1,512,1024]{2,1,0:T(8,128)(2,1)S(1)}, u32[]{:S(2)}) copy-start(bf16[1,512,1024]{2,1,0:T(8,128)(2,1)S(1)} %arrange.11) | copy-start | bytes 3145732
  166.2 20.8 %copy-start.52 = (f32[1024,1024]{1,0:T(8,128)S(1)}, f32[1024,1024]{1,0:T(8,128)}, u32[]{:S(2)}) copy-start(f32[1024,1024]{1,0:T(8,128)} %copy-done.51) | copy-start | bytes 12582916
  166.2 49.5 %collective-permute-start.26 = (bf16[1,256,2048]{2,1,0:T(8,128)(2,1)}, bf16[1,256,2048]{2,1,0:T(8,128)(2,1)}, u32[]{:S(2)}, u32[]{:S(2)}) collective-permute-start(bf16[1,256,2048]{2,1,0:T(8,128)(2,1)} %collective-permute-done.20.refs_1_), channel_id=1, source_target_pairs={{0,2},{1,3},{2,0},{3,1},{4,6},{5,7},{6,4},{7,5},{8,10},{9,11},{10,... | collective-permute-start | bytes 3145736 | tf_op jit(solution)/shard_map/ppermute | solution.py:916
  183.2 7.6 %copy-start.12 = (bf16[1024,512]{1,0:T(8,128)(2,1)}, bf16[1024,512]{1,0:T(8,128)(2,1)S(1)}, u32[]{:S(2)}) copy-start(bf16[1024,512]{1,0:T(8,128)(2,1)S(1)} %get-tuple-element.117.refs_9_) | copy-start | bytes 3145732
  183.2 7.6 %copy-start.50 = (bf16[1024,512]{1,0:T(8,128)(2,1)}, bf16[1024,512]{1,0:T(8,128)(2,1)S(1)}, u32[]{:S(2)}) copy-start(bf16[1024,512]{1,0:T(8,128)(2,1)S(1)} %get-tuple-element.129.refs_10_) | copy-start | bytes 3145732
  183.2 7.6 %copy-start.17 = (bf16[1,512,1024]{2,1,0:T(8,128)(2,1)}, bf16[1,512,1024]{2,1,0:T(8,128)(2,1)S(1)}, u32[]{:S(2)}) copy-start(bf16[1,512,1024]{2,1,0:T(8,128)(2,1)S(1)} %collective-permute-done.24.refs_2_) | copy-start | bytes 3145732
  187.0 32.9 %collective-permute-start.27 = (bf16[1,512,1024]{2,1,0:T(8,128)(2,1)}, bf16[1,512,1024]{2,1,0:T(8,128)(2,1)}, u32[]{:S(2)}, u32[]{:S(2)}) collective-permute-start(bf16[1,512,1024]{2,1,0:T(8,128)(2,1)} %collective-permute-done.23.refs_1_), channel_id=1, source_target_pairs={{0,2},{1,3},{2,0},{3,1},{4,6},{5,7},{6,4},{7,5},{8,10},{9,11},{10,... | collective-permute-start | bytes 3145736 | tf_op jit(solution)/shard_map/ppermute | solution.py:916
  199.1 16.7 %copy-start.11 = (bf16[1,256,2048]{2,1,0:T(8,128)(2,1)S(1)}, bf16[1,256,2048]{2,1,0:T(8,128)(2,1)}, u32[]{:S(2)}) copy-start(bf16[1,256,2048]{2,1,0:T(8,128)(2,1)} %copy-done.10) | copy-start | bytes 3145732
  199.1 16.7 %copy-start.14 = (bf16[1,256,2048]{2,1,0:T(8,128)(2,1)S(1)}, bf16[1,256,2048]{2,1,0:T(8,128)(2,1)}, u32[]{:S(2)}) copy-start(bf16[1,256,2048]{2,1,0:T(8,128)(2,1)} %copy-done.13) | copy-start | bytes 3145732
  223.9 16.4 %copy-start.54 = (f32[1024,1024]{1,0:T(8,128)S(1)}, f32[1024,1024]{1,0:T(8,128)}, u32[]{:S(2)}) copy-start(f32[1024,1024]{1,0:T(8,128)} %copy-done.53) | copy-start | bytes 12582916
  223.9 16.4 %copy-start.62 = (f32[1024,1024]{1,0:T(8,128)S(1)}, f32[1024,1024]{1,0:T(8,128)}, u32[]{:S(2)}) copy-start(f32[1024,1024]{1,0:T(8,128)} %get-tuple-element.120) | copy-start | bytes 12582916
  258.3 286.4 %copy-start.8 = (bf16[3,1024,512]{2,1,0:T(8,128)(2,1)S(1)}, bf16[3,1024,512]{2,1,0:T(8,128)(2,1)}, u32[]{:S(2)}) copy-start(bf16[3,1024,512]{2,1,0:T(8,128)(2,1)} %copy-done.7) | copy-start | bytes 9437188
  581.8 11.2 %copy-start.76 = (f32[8,1024]{1,0:T(8,128)S(1)}, f32[8,1024]{1,0:T(8,128)}, u32[]{:S(2)}) copy-start(f32[8,1024]{1,0:T(8,128)} %get-tuple-element.153) | copy-start | bytes 98308
  581.8 11.9 %copy-start.67 = (bf16[2,1024,512]{2,1,0:T(8,128)(2,1)S(1)}, bf16[2,1024,512]{2,1,0:T(8,128)(2,1)}, u32[]{:S(2)}) copy-start(bf16[2,1024,512]{2,1,0:T(8,128)(2,1)} %get-tuple-element.144) | copy-start | bytes 6291460
  597.9 6.4 %copy-start.59 = (f32[1024,1024]{1,0:T(8,128)S(1)}, f32[1024,1024]{1,0:T(8,128)}, u32[]{:S(2)}) copy-start(f32[1024,1024]{1,0:T(8,128)} %get-tuple-element.139) | copy-start | bytes 12582916
  597.9 6.4 %copy-start.60 = (f32[1024,1024]{1,0:T(8,128)S(1)}, f32[1024,1024]{1,0:T(8,128)}, u32[]{:S(2)}) copy-start(f32[1024,1024]{1,0:T(8,128)} %fusion.24) | copy-start | bytes 12582916
  (48 other events, 146.6 us)

commit v4 on v3

--- a/solution.py
+++ b/solution.py
@@ -511,7 +511,7 @@
 
 BOTH = (0, 1)
 X, CORE, Y, Z1, Z2 = range(5)
-DELAY = 2
+DELAY = 3
 SLOTS = 2 * DELAY
 CHUNK = 64
 SUBS = 4
@@ -693,16 +693,17 @@
     (len_ref,) = take(1)
     cross_in = [take(5) for _ in BOTH]
     self_in = [take(5) for _ in BOTH]
-    co, cq, so = take(2), take(2), take(2)
+    co = take(2)
     gain_ref, small_ref = take(2)
     feed_in = [take(4) for _ in BOTH]
     g3_ref, g3t_ref, h2t_ref, h1t_ref, memt_ref, tart_ref, base_ref, sum2_ref, sum1_ref = take(9)
-    dk2_ref, dv2_ref, dq1_ref, dk1_ref, dv1_ref, dz_ref, out, queue, small_out = take(9)
+    cq_in, so_in, kv_in, qkv_in = take(2), take(2), take(2), take(2)
+    dmem_ref, dtar_ref, out, queue, small_out = take(5)
     grads, *scratch = take(9)
     stream = [queue, out] + take(6)
     small_refs = [small_out] + take(4)
     acc = small_refs[1]
-    lefts, tall, flat, total, dq2, dc, zt, staged = take(8)
+    lefts, tall, flat, total, ends, dc, zt, staged = take(8)
     left_sems, feed_sems, zt_sems, staged_sems, base_sem = take(5)
     step = pl.program_id(0)
     half = lax.rem(step, 2)
@@ -725,6 +726,31 @@
             pltpu.make_async_copy(up.at[:, cols_j], tall.at[2, i], feed_sems.at[2, i]),
             pltpu.make_async_copy(down.at[cols_j], flat.at[i], feed_sems.at[3, i]),
         ]
+
+    def load_late():
+        return [
+            copy
+            for i in BOTH
+            for copy in (
+                pltpu.make_async_copy(kv_in[i].at[0], tall.at[0, i], feed_sems.at[0, i]),
+                pltpu.make_async_copy(kv_in[i].at[1], tall.at[1, i], feed_sems.at[1, i]),
+                pltpu.make_async_copy(cq_in[i], tall.at[2, i], feed_sems.at[2, i]),
+                pltpu.make_async_copy(so_in[i], flat.at[i], feed_sems.at[3, i]),
+            )
+        ]
+
+    def load_last():
+        return [pltpu.make_async_copy(qkv_in[i].at[m], tall.at[m, i], feed_sems.at[m, i]) for i in BOTH for m in range(3)]
+
+    def input_grad(rows, members, start):
+        for m in range(members):
+            for i in BOTH:
+                term = dot(ends[m, i, rows, :], tall[m, i], NT)
+                start = term if start is None else start + term
+        lefts[1, rows, :] = start.astype(bf16)
+
+    def send_grad(ref):
+        return pltpu.make_async_copy(lefts.at[1], ref, base_sem)
 
     def post(slot, block):
         return pltpu.make_async_copy(staged.at[slot], queue.at[block, half], staged_sems.at[slot])
@@ -788,7 +814,7 @@
     @pl.when(step == STEPS)
     def _():
         fetch = [load_left(0, h1t_ref), load_left(1, memt_ref)]
-        for copy in fetch:
+        for copy in fetch + load_late():
             copy.start()
         norm_step(
             1, [], co, gain_ref, sum2_ref, total, dc, lefts.at[2], acc, zt, zt_sems, lambda k: tick(STEPS * FEED_TICKS + k)
@@ -809,9 +835,9 @@
                 tick(t + j // 2)
 
         back_pair(False, len_ref[0], q2, k2, v2, c2, aug, dc[half, :, at], grads, scratch, ticks)
-        dq2[half, :, at] = grads[:, :128]
-        dk2_ref[...] = grads[:, 128:256]
-        dv2_ref[...] = grads[:, 256:384]
+        ends[2, half, :, at] = grads[:, :128]
+        ends[0, half, :, at] = grads[:, 128:256]
+        ends[1, half, :, at] = grads[:, 256:384]
         post(0, 0).wait()
         spans = ((0, grads, 0, 128), (1, grads, 128, 384), (2, grads, 384, 512))
         products(0, 2 * QUADS + pair, spans, {1: t + 2})
@@ -820,12 +846,22 @@
     def _():
         fetch = load_left(0, tart_ref)
         fetch.start()
-        more = [(dq2.at[i], cq[i]) for i in BOTH]
+        for copy in load_late():
+            copy.wait()
+        more = [(ends.at[2, i], tall.at[2, i]) for i in BOTH]
+        so = [flat.at[i] for i in BOTH]
         norm_step(
             0, more, so, gain_ref, sum1_ref, total, dc, lefts.at[2], acc, zt, zt_sems, lambda k: tick(SELF_AT - NORM_TICKS + k)
         )
         fetch.wait()
-        pltpu.make_async_copy(total, dz_ref, base_sem).start()
+
+        @pl.loop(0, 4)
+        def _(a):
+            input_grad(pl.ds(pl.multiple_of(a * TILE, TILE), TILE), 2, None)
+
+        send_grad(dmem_ref).start()
+        for copy in load_last():
+            copy.start()
 
     @pl.when(step >= 2 * STEPS)
     def _():
@@ -836,9 +872,9 @@
                 tick(t)
 
         back_pair(True, 0, q2, k2, v2, c2, aug, dc[half, :, at], grads, scratch, ticks)
-        dq1_ref[...] = grads[:, :128]
-        dk1_ref[...] = grads[:, 128:256]
-        dv1_ref[...] = grads[:, 256:384]
+        ends[0, half, :, at] = grads[:, :128]
+        ends[1, half, :, at] = grads[:, 128:256]
+        ends[2, half, :, at] = grads[:, 256:384]
         post(0, 0).wait()
         products(0, 3 * QUADS + pair, ((0, grads, 0, 384), (2, grads, 384, 512)), {0: t + 1})
         for k in range(5, -1, -1):
@@ -847,8 +883,19 @@
     @pl.when(step == 3 * STEPS - 1)
     def _():
         post(0, 0).wait()
-        pltpu.make_async_copy(total, dz_ref, base_sem).wait()
-        pl.loop(DRAIN_AT, TICKS)(tick)
+        send_grad(dmem_ref).wait()
+        for copy in load_last():
+            copy.wait()
+
+        @pl.loop(0, 4)
+        def _(a):
+            tick(DRAIN_AT + a)
+            rows = pl.ds(pl.multiple_of(a * TILE, TILE), TILE)
+            input_grad(rows, 3, total[rows, :])
+
+        send_grad(dtar_ref).start()
+        pl.loop(DRAIN_AT + 4, TICKS)(tick)
+        send_grad(dtar_ref).wait()
 
 
 def layer_back(length, cross_in, self_in, weights, gain, small, feed_in, rest):
@@ -858,8 +905,6 @@
     late = lambda s: jnp.clip(s - 2 * STEPS, 0, STEPS - 1)
     cross_spec = pl.BlockSpec((seq, 128), lambda s: (0, early(s) // 2))
     self_spec = pl.BlockSpec((seq, 128), lambda s: (0, late(s) // 2))
-    cross_out = pl.BlockSpec((None, seq, 128), lambda s: (early(s) % 2, 0, early(s) // 2))
-    self_out = pl.BlockSpec((None, seq, 128), lambda s: (late(s) % 2, 0, late(s) // 2))
     anywhere = pl.BlockSpec(memory_space=pl.ANY)
     full = lambda x: pl.BlockSpec(x.shape, lambda s: (0, 0), pipeline_mode=pl.Buffered(1))
     shape = jax.ShapeDtypeStruct
@@ -872,11 +917,10 @@
         + [cross_spec] * 10
         + [self_spec] * 10
         + [full(x) for x in (*weights, gain, small)]
-        + [anywhere] * 17,
-        out_specs=[cross_out] * 2 + [self_out] * 3 + [anywhere] * 3 + [full(small)],
-        out_shape=[shape((2, seq, width), bf16)] * 5
+        + [anywhere] * 25,
+        out_specs=[anywhere] * 4 + [full(small)],
+        out_shape=[shape((seq, model), bf16)] * 2
         + [
-            shape((seq, model), f32),
             shape((blocks, 2, 2, SUBS, CHUNK, WIDTH), bf16),
             shape((blocks, 2, 2, 2, SUBS, CHUNK, WIDTH), bf16),
             shape(small.shape, f32),
@@ -890,7 +934,7 @@
             vmem((3, 2, seq, WIDTH), bf16),
             vmem((2, WIDTH, model), bf16),
             vmem((seq, model), f32),
-            vmem((2, seq, width), bf16),
+            vmem((3, 2, seq, width), bf16),
             vmem((2, seq, width), bf16),
             vmem((2, TILE, model), f32),
             vmem((2, 2, 2, SUBS, CHUNK, WIDTH), bf16),
@@ -1175,7 +1219,7 @@
     target_t = flip(target)
     memory_t = flip(mem)
     kv[0][0], up_s, co_s, target_t, memory_t = tie(kv[0][0], up_s, co_s, target_t, memory_t)
-    tar = pipe.cut(target)
+    tar, kv[0][0], kv[0][1], target_t, memory_t = pipe.cut(target, *kv[0], target_t, memory_t)
     qkv_oth = arrange(got["qkv"])
     q1[1] = [dot(tar, qkv_oth[m]).astype(bf16) for m in range(3)]
     pipe.put(fetch(got, "co", co_s, (1, 1)))
@@ -1197,7 +1241,9 @@
     q2[0], kv[1][0], down_s = pipe.cut(q2[0], kv[1][0], down_s)
     pipe.put(fetch(got, "down", down_s, (1, 1)))
     at2 = [attend_fwd(q2[0], *kv[0], length, False), None]
-    q2[1], _ = pipe.cut(q2[1], at2[0][0])
+    h1_again, _ = tie(h1_low, at2[0][0])
+    h1_t = flip(h1_again)
+    q2[1], h1_t, _ = pipe.cut(q2[1], h1_t, at2[0][0])
     at2[1] = attend_fwd(q2[1], *kv[1], length, False)
     co_oth = arrange(got["co"])[0]
     c2 = [at2[0][0], at2[1][0]]
@@ -1207,7 +1253,7 @@
     h2 = norm_rows(sum2, ln_gain[1], ln_bias[1])
     h2_low = h2.astype(bf16)
     act0, slope0, b3 = ffn_forward(h2_low, ffn_up, ffn_down)
-    h1_t, h2_t = flip(h1_low), flip(h2_low)
+    h2_t = flip(h2_low)
     while "up" not in got or "down" not in got:
         act0 = pipe.cut(act0)
     h2_again, h1_t, h2_t, _ = tie(h2_low, h1_t, h2_t, act0)
@@ -1218,21 +1264,18 @@
     g3 = dz3.astype(bf16)
     none = jnp.zeros_like(gain3)
     small = jnp.stack([none, none, gain3, none, none, bias3, none, none])
-    dk2, dv2, dq1, dk1, dv1, dz1, blocks, _, small = layer_back(
+    dmem, dtar, blocks, _, small = layer_back(
         length,
         [[q2[i], *kv[i], c2[i], at2[i][1]] for i in BOTH],
         [[*q1[i], c1[i], at1[i][1]] for i in BOTH],
-        (cross_out, co_oth, cross_query, cq_oth, self_out, so_oth),
+        (cross_out, co_oth),
         ln_gain,
         small,
         [(act0, slope0, ffn_up, ffn_down), (act1, slope1, up_oth, down_oth)],
-        (g3, flip(g3), h2_t, h1_t, memory_t, target_t, alpha_res * dz3, sum2, sum1),
+        (g3, flip(g3), h2_t, h1_t, memory_t, target_t, alpha_res * dz3, sum2, sum1)
+        + (cross_query, cq_oth, self_out, so_oth, cross_kv, kv_oth, self_qkv, qkv_oth),
     )
     blocks = blocks.reshape(16, 1024, 512)
-    kv_both = (cross_kv, kv_oth)
-    dmem = sum(dot(d[i], kv_both[i][m], NT) for i in BOTH for m, d in enumerate((dk2, dv2)))
-    qkv_both = (self_qkv, qkv_oth)
-    dtar = dz1 + sum(dot(d[i], qkv_both[i][m], NT) for i in BOTH for m, d in enumerate((dq1, dk1, dv1)))
     cq_total, kv_total, co_total = spread(
         blocks,
         8,
@@ -1248,8 +1291,8 @@
     down_total, up_total = spread_feed(blocks)
     return (
         result.astype(bf16),
-        dtar.astype(bf16),
-        dmem.astype(bf16),
+        dtar,
+        dmem,
         qkv_total,
         so_total,
         cq_total[0],

time: 615 us -> 584 us (0.950)
  matrix products: 72.1 us -> 44.5 us
  waiting for transfers between devices: 34.4 us -> 26.7 us
  Pallas kernels: 434 us -> 441 us
  other arithmetic: 22.3 us -> 16.1 us
    dot_general x26 -> x16, matrix products: 72.1 us -> 44.5 us  [dot(): return lax.dot_general(a, b, dims, preferred_element_type=f32)]
    pallas_call x1, Pallas kernels: 286 us -> 297 us  [layer_back(): pl.pallas_call(back_kernel, grid=(3 * STEPS,), in_specs=[pl.BlockSpec(mem...]
    ppermute x28, waiting for transfers between devices: 34.4 us -> 26.7 us  [swap(): return lax.ppermute(x, ALL, [(i, i ^ flip) for i in range(DEVICES)])]
    convert_element_type x1 -> x0, other arithmetic: 6.29 us -> none  [one_pair_each(): dtar.astype(bf16)]
    unnamed x168 -> x126, local copies, waits for them, and re-layouts: 14.5 us -> 17.8 us
  transfers between devices with their start and end apart: 28 -> 28, of which waited for: 7 -> 7; matrix products, arithmetic and copies ran while one was open for 9% -> 10% of each run, Pallas kernels for 16% -> 16%
where the time goes in v4:
time: 584 us; the launch traced here: 580 us
  Pallas kernels  441 us (76%)
  matrix products  44.5 us (8%)
  local copies, waits for them, and re-layouts  32.4 us (6%)
  waiting for transfers between devices  26.7 us (5%)
  starting transfers between devices  17.7 us (3%)
  other arithmetic  16.1 us (3%)
    pallas_call x1, Pallas kernels, layer_back(): pl.pallas_call(back_kernel, grid=(3 * STEPS,), in_specs=[pl.BlockSpec(mem...  297 us
    pallas_call x4, Pallas kernels, attend_fwd(): pl.pallas_call(functools.partial(fwd_kernel, causal), grid=(width // 128,...  57.7 us
    dot_general x16, matrix products, dot(): return lax.dot_general(a, b, dims, preferred_element_type=f32)  44.5 us
    pallas_call x2, Pallas kernels, ffn_forward(): pl.pallas_call(ffn_kernel, grid=(seq // ROWS,), in_specs=[rows(width)] +...  32.9 us
    ppermute x28, waiting for transfers between devices, swap(): return lax.ppermute(x, ALL, [(i, i ^ flip) for i in range(DEVICES)])  26.7 us
    pallas_call x5, Pallas kernels, flip(): pl.pallas_call(flip_kernel, grid=(4,), in_specs=[pl.BlockSpec((rows // 4,...  20.7 us
    unnamed x126, local copies, waits for them, and re-layouts  17.8 us
    ppermute x28, starting transfers between devices, swap(): return lax.ppermute(x, ALL, [(i, i ^ flip) for i in range(DEVICES)])  17.7 us
  transfers between devices with their start and end apart: 28, of which 7 were waited for; matrix products, arithmetic and copies ran while one was open for 10% of the time, Pallas kernels for 16%

profile of v4, /device:TPU:0, one launch (start us, length us, event | category | flops | bytes accessed | tf_op | source)
XLA Modules:
  0.0 580.0 jit_solution(8496709413644308259)
XLA Ops:
  0.7 2.1 constant_dynamic-slice_fusion
  2.8 2.9 collective-permute-start
  5.7 3.1 convolution_convert_fusion.9.v_ref.refs_13_
  8.8 1.2 convolution_convert_fusion.10.k_ref.refs_12_
  10.1 2.2 convolution_convert_fusion.11.q_ref.refs_11_
  12.3 1.7 dynamic-slice_bitcast_fusion.3
  15.1 1.7 dynamic-slice_bitcast_fusion.4
  17.3 2.3 dynamic-slice_bitcast_fusion.1
  19.6 1.2 copy-done.28
  20.9 13.1 %attend_causal.2 = (bf16[1024,512]{1,0:T(8,128)(2,1)S(1)}, bf16[1024,512]{1,0:T(8,128)(2,1)S(1)}) custom-call(s32[1]{0:T(128)} %dynamic_slice.24.len_ref.refs_0_, bf16[1024,512]{1,0:T(8,128)(2,1)S(1)} %copy-done.28, bf16[1024,512]{1,0:T(8,128)(2,1)S(1)} %convolution_convert_fusion.10.k_ref.refs_12_, ...), custom_call_target="tpu_custom_call" | custom-call | flops 5368709120 | bytes 8388608 | tf_op jit(solution)/shard_map/attend_causal/pallas_call | solution.py:422
  36.0 1.6 collective-permute-start.1
  37.6 1.7 dynamic-slice_bitcast_fusion.2
  39.2 4.2 flip.5.refs_38_
  44.2 4.1 convolution_convert_fusion.8.k_ref.refs_2_
  48.3 4.1 flip.6.refs_37_
  52.4 1.3 collective-permute-start.3
  54.4 4.1 convolution_convert_fusion.7.v_ref.refs_3_
  58.5 5.3 collective-permute-done.3.refs_0_
  63.8 4.9 collective-permute-done.4.refs_0_
  69.8 4.9 fusion.29
  75.9 1.8 collective-permute-start.11
  78.2 1.2 convolution_convert_fusion.4.v_ref.refs_18_
  79.5 1.2 convolution_convert_fusion.5.k_ref.refs_17_
  80.8 1.3 convolution_convert_fusion.6.q_ref.refs_16_
  82.1 1.3 collective-permute-done.13.refs_0_
  83.9 13.2 %attend_causal.3 = (bf16[1024,512]{1,0:T(8,128)(2,1)S(1)}, bf16[1024,512]{1,0:T(8,128)(2,1)S(1)}) custom-call(s32[1]{0:T(128)} %dynamic_slice.24.len_ref.refs_0_, bf16[1024,512]{1,0:T(8,128)(2,1)S(1)} %convolution_convert_fusion.6.q_ref.refs_16_, bf16[1024,512]{1,0:T(8,128)(2,1)S(1)} %convolution_convert_fusion.5.k_ref.refs_17_, ...), custom_call_target="tpu_custom_call" | custom-call | flops 5368709120 | bytes 8388608 | tf_op jit(solution)/shard_map/attend_causal/pallas_call | solution.py:422
  97.1 3.9 collective-permute-done.9.refs_1_
  101.0 2.3 dynamic-slice_bitcast_fusion
  104.1 1.5 collective-permute-start.18
  106.3 4.2 fusion.27
  113.1 1.2 convolution_convert_fusion.3.q_ref.refs_1_
  114.6 2.3 convolution_convert_fusion.2.q_ref.refs_6_
  118.5 2.2 fusion.6.k_ref.refs_7_
  120.7 8.3 %collective-permute-done.18.refs_0_ = bf16[1,256,2048]{2,1,0:T(8,128)(2,1)S(1)} collective-permute-done((bf16[1,256,2048]{2,1,0:T(8,128)(2,1)S(1)}, bf16[1,256,2048]{2,1,0:T(8,128)(2,1)S(1)}, u32[]{:S(2)}, u32[]{:S(2)}) %collective-permute-start.18) | collective-permute-done | bytes 1048608 | tf_op jit(solution)/shard_map/ppermute | solution.py:960
  129.1 1.7 collective-permute-start.20
  130.7 1.3 collective-permute-start.22
  132.0 2.2 fusion.7.v_ref.refs_8_
  134.2 15.7 %attend_memory.2 = (bf16[1024,512]{1,0:T(8,128)(2,1)S(1)}, bf16[1024,512]{1,0:T(8,128)(2,1)S(1)}) custom-call(s32[1]{0:T(128)} %dynamic_slice.24.len_ref.refs_0_, bf16[1024,512]{1,0:T(8,128)(2,1)S(1)} %convolution_convert_fusion.3.q_ref.refs_1_, bf16[1024,512]{1,0:T(8,128)(2,1)S(1)} %copy-done.29, bf16[1024,512]{1,0:T(8,128)(2,1)S(1)} %copy-done.30), custom_call_target="tpu_custom_call" | custom-call | flops 8589934592 | bytes 8388608 | tf_op jit(solution)/shard_map/attend_memory/pallas_call | solution.py:422
  151.9 4.1 flip.7.refs_36_
  157.0 5.2 fusion.30
  162.2 1.2 arrange.11
  163.8 15.8 %attend_memory.3 = (bf16[1024,512]{1,0:T(8,128)(2,1)S(1)}, bf16[1024,512]{1,0:T(8,128)(2,1)S(1)}) custom-call(s32[1]{0:T(128)} %dynamic_slice.24.len_ref.refs_0_, bf16[1024,512]{1,0:T(8,128)(2,1)S(1)} %copy-done.35, bf16[1024,512]{1,0:T(8,128)(2,1)S(1)} %copy-done.36, bf16[1024,512]{1,0:T(8,128)(2,1)S(1)} %copy-done.37), custom_call_target="tpu_custom_call" | custom-call | flops 8589934592 | bytes 8388608 | tf_op jit(solution)/shard_map/attend_memory/pallas_call | solution.py:422
  179.7 2.6 collective-permute-done.23.refs_1_
  182.3 3.9 fusion.28
  186.8 1.5 copy-done.44
  188.3 2.0 fusion.5.h_ref.x_ref
  190.3 4.2 flip.8.refs_35_
  194.5 16.5 %feed_forward.2 = (bf16[1024,2048]{1,0:T(8,128)(2,1)}, bf16[1024,2048]{1,0:T(8,128)(2,1)}, f32[1024,1024]{1,0:T(8,128)}) custom-call(bf16[1024,1024]{1,0:T(8,128)(2,1)S(1)} %copy-done, bf16[1024,2048]{1,0:T(8,128)(2,1)} %refs_27_.1, bf16[2048,1024]{1,0:T(8,128)(2,1)} %refs_28_.1), custom_call_target="tpu_custom_call" | custom-call | flops 8589934592 | bytes 23068672 | tf_op jit(solution)/shard_map/feed_forward/pallas_call | solution.py:1068
  211.1 1.7 arrange.12
  212.8 2.0 copy-done.3
  214.8 2.3 arrange.13
  217.1 2.0 copy-done.4
  219.1 16.4 %feed_forward.3 = (bf16[1024,2048]{1,0:T(8,128)(2,1)}, bf16[1024,2048]{1,0:T(8,128)(2,1)}, f32[1024,1024]{1,0:T(8,128)}) custom-call(bf16[1024,1024]{1,0:T(8,128)(2,1)S(1)} %copy-done, bf16[1024,2048]{1,0:T(8,128)(2,1)} %bitcast.91, bf16[2048,1024]{1,0:T(8,128)(2,1)} %bitcast.93), custom_call_target="tpu_custom_call" | custom-call | flops 8589934592 | bytes 23068672 | tf_op jit(solution)/shard_map/feed_forward/pallas_call | solution.py:1068
  235.5 3.3 fusion.23
  240.5 2.0 fusion.2
  242.5 3.2 fusion.22
  245.7 3.2 add_multiply_fusion
  248.8 4.1 flip.9.refs_34_
  253.6 297.0 %layer_back.1 = (bf16[1024,1024]{1,0:T(8,128)(2,1)}, bf16[1024,1024]{1,0:T(8,128)(2,1)}, bf16[16,2,2,4,64,512]{5,4,3,2,1,0:T(8,128)(2,1)}, bf16[16,2,2,2,4,64,512]{6,5,4,3,2,1,0:T(8,128)(2,1)}, f32[8,1024]{1,0:T(8,128)}) custom-call(s32[1]{0:T(128)} %dynamic_slice.24.len_ref.refs_0_, bf16[1024,512]{1,0:T(8,128)(2,1)} %copy-done.34, ...), custom_call_target="tpu_custom_call" | custom-call | flops 137438953472 | bytes 16777216 | tf_op jit(solution)/shard_map/layer_back/pallas_call | solution.py:913
  550.6 7.3 %spread.3 = (f32[1,1024,512]{2,1,0:T(8,128)}, f32[2,1024,512]{2,1,0:T(8,128)}, f32[512,1024]{1,0:T(8,128)}) custom-call(bf16[16,1024,512]{2,1,0:T(8,128)(2,1)} %bitcast.96), custom_call_target="tpu_custom_call" | custom-call | bytes 12582912 | tf_op jit(solution)/shard_map/spread/pallas_call | solution.py:1131
  557.9 7.4 %spread.2 = (f32[3,1024,512]{2,1,0:T(8,128)}, f32[512,1024]{1,0:T(8,128)}) custom-call(bf16[16,1024,512]{2,1,0:T(8,128)(2,1)} %bitcast.97), custom_call_target="tpu_custom_call" | custom-call | bytes 12582912 | tf_op jit(solution)/shard_map/spread/pallas_call | solution.py:1131
  565.4 11.2 %spread_feed.1 = (f32[2048,1024]{1,0:T(8,128)}, f32[1024,2048]{1,0:T(8,128)}) custom-call(bf16[16,1024,512]{2,1,0:T(8,128)(2,1)} %bitcast.98), custom_call_target="tpu_custom_call" | custom-call | bytes 25165824 | tf_op jit(solution)/shard_map/spread_feed/pallas_call | solution.py:1174
  577.2 1.3 copy.39
  578.5 1.3 copy.40
  (186 shorter events, 21.1 us)
Async XLA Ops:
  2.8 6.0 %copy-start.47 = (bf16[1024,1024]{1,0:T(8,128)(2,1)S(1)}, bf16[1024,1024]{1,0:T(8,128)(2,1)}, u32[]{:S(2)}) copy-start(bf16[1024,1024]{1,0:T(8,128)(2,1)} %x_ref.1) | copy-start | bytes 6291460
  2.8 6.1 %copy-start.56 = (bf16[3,1024,512]{2,1,0:T(8,128)(2,1)S(1)}, bf16[3,1024,512]{2,1,0:T(8,128)(2,1)}, u32[]{:S(2)}) copy-start(bf16[3,1024,512]{2,1,0:T(8,128)(2,1)} %refs_48_.1) | copy-start | bytes 9437188
  2.8 32.2 %collective-permute-start = (bf16[3,256,512]{2,1,0:T(8,128)(2,1)}, bf16[3,256,512]{2,1,0:T(8,128)(2,1)S(1)}, u32[]{:S(2)}, u32[]{:S(2)}) collective-permute-start(bf16[3,256,512]{2,1,0:T(8,128)(2,1)} %constant_dynamic-slice_fusion), channel_id=1, source_target_pairs={{0,1},{1,0},{2,3},{3,2},{4,5},{5,4},{6,7},{7,6},{8,9},{9,8},{10,11... | collective-permute-start | bytes 2359304 | tf_op jit(solution)/shard_map/ppermute | solution.py:960
  8.8 10.8 %copy-start.26 = (bf16[1024,512]{1,0:T(8,128)(2,1)}, bf16[1024,512]{1,0:T(8,128)(2,1)S(1)}, u32[]{:S(2)}) copy-start(bf16[1024,512]{1,0:T(8,128)(2,1)S(1)} %convolution_convert_fusion.9.v_ref.refs_13_) | copy-start | bytes 3145732
  10.1 9.6 %copy-start.27 = (bf16[1024,512]{1,0:T(8,128)(2,1)}, bf16[1024,512]{1,0:T(8,128)(2,1)S(1)}, u32[]{:S(2)}) copy-start(bf16[1024,512]{1,0:T(8,128)(2,1)S(1)} %convolution_convert_fusion.10.k_ref.refs_12_) | copy-start | bytes 3145732
  10.1 6.7 %copy-start.61 = (s32[2]{0:T(128)S(1)}, s32[2]{0:T(128)}, u32[]{:S(2)}) copy-start(s32[2]{0:T(128)} %param.15) | copy-start | bytes 28
  36.0 32.8 %collective-permute-start.2 = (bf16[3,256,512]{2,1,0:T(8,128)(2,1)S(1)}, bf16[3,256,512]{2,1,0:T(8,128)(2,1)S(1)}, u32[]{:S(2)}, u32[]{:S(2)}) collective-permute-start(bf16[3,256,512]{2,1,0:T(8,128)(2,1)S(1)} %collective-permute-done.refs_0_), channel_id=1, source_target_pairs={{0,2},{1,3},{2,0},{3,1},{4,6},{5,7},{6,4},{7,5},{8,10},{9,11},{10,... | collective-permute-start | bytes 2359304 | tf_op jit(solution)/shard_map/ppermute | solution.py:960
  36.0 33.6 %collective-permute-start.1 = (bf16[3,256,512]{2,1,0:T(8,128)(2,1)S(1)}, bf16[3,256,512]{2,1,0:T(8,128)(2,1)S(1)}, u32[]{:S(2)}, u32[]{:S(2)}) collective-permute-start(bf16[3,256,512]{2,1,0:T(8,128)(2,1)S(1)} %collective-permute-done.refs_0_), channel_id=1, source_target_pairs={{0,4},{1,5},{2,6},{3,7},{4,0},{5,1},{6,2},{7,3},{8,12},{9,13},{10,... | collective-permute-start | bytes 2359304 | tf_op jit(solution)/shard_map/ppermute | solution.py:960
  43.4 25.3 %collective-permute-start.5 = (bf16[2,256,512]{2,1,0:T(8,128)(2,1)S(1)}, bf16[2,256,512]{2,1,0:T(8,128)(2,1)S(1)}, u32[]{:S(2)}, u32[]{:S(2)}) collective-permute-start(bf16[2,256,512]{2,1,0:T(8,128)(2,1)S(1)} %constant_dynamic-slice_fusion.1), channel_id=1, source_target_pairs={{0,1},{1,0},{2,3},{3,2},{4,5},{5,4},{6,7},{7,6},{8,9},{9,8},{10,11... | collective-permute-start | bytes 1572872 | tf_op jit(solution)/shard_map/ppermute | solution.py:960
  52.4 17.3 %copy-start.59 = (f32[3,1024]{1,0:T(4,128)S(1)}, f32[3,1024]{1,0:T(4,128)}, u32[]{:S(2)}) copy-start(f32[3,1024]{1,0:T(4,128)} %param.25) | copy-start | bytes 36868
  52.4 11.5 %collective-permute-start.3 = (bf16[1,128,1024]{2,1,0:T(8,128)(2,1)}, bf16[1,128,1024]{2,1,0:T(8,128)(2,1)S(1)}, u32[]{:S(2)}, u32[]{:S(2)}) collective-permute-start(bf16[1,128,1024]{2,1,0:T(8,128)(2,1)} %dynamic-slice_bitcast_fusion.4), channel_id=1, source_target_pairs={{0,1},{1,0},{2,3},{3,2},{4,5},{5,4},{6,7},{7,6},{8,9},{9,8},{10,11... | collective-permute-start | bytes 786440 | tf_op jit(solution)/shard_map/ppermute | solution.py:960
  53.7 15.0 %collective-permute-start.4 = (bf16[1,256,512]{2,1,0:T(8,128)(2,1)}, bf16[1,256,512]{2,1,0:T(8,128)(2,1)S(1)}, u32[]{:S(2)}, u32[]{:S(2)}) collective-permute-start(bf16[1,256,512]{2,1,0:T(8,128)(2,1)} %dynamic-slice_bitcast_fusion.3), channel_id=1, source_target_pairs={{0,1},{1,0},{2,3},{3,2},{4,5},{5,4},{6,7},{7,6},{8,9},{9,8},{10,11... | collective-permute-start | bytes 786440 | tf_op jit(solution)/shard_map/ppermute | solution.py:960
  63.8 5.8 copy-start.20
  69.6 6.3 %collective-permute-start.6 = (bf16[3,256,512]{2,1,0:T(8,128)(2,1)S(1)}, bf16[3,256,512]{2,1,0:T(8,128)(2,1)S(1)}, u32[]{:S(2)}, u32[]{:S(2)}) collective-permute-start(bf16[3,256,512]{2,1,0:T(8,128)(2,1)S(1)} %collective-permute-done.1.refs_1_), channel_id=1, source_target_pairs={{0,2},{1,3},{2,0},{3,1},{4,6},{5,7},{6,4},{7,5},{8,10},{9,11},{10,... | collective-permute-start | bytes 2359304 | tf_op jit(solution)/shard_map/ppermute | solution.py:960
  69.7 5.6 copy-start.21
  69.7 6.1 %copy-start.17 = (bf16[2,256,512]{2,1,0:T(8,128)(2,1)S(1)}, bf16[2,256,512]{2,1,0:T(8,128)(2,1)}, u32[]{:S(2)}) copy-start(bf16[2,256,512]{2,1,0:T(8,128)(2,1)} %copy-done.16) | copy-start | bytes 1572868
  74.6 8.7 %collective-permute-start.13 = (bf16[1,128,1024]{2,1,0:T(8,128)(2,1)S(1)}, bf16[1,128,1024]{2,1,0:T(8,128)(2,1)S(1)}, u32[]{:S(2)}, u32[]{:S(2)}) collective-permute-start(bf16[1,128,1024]{2,1,0:T(8,128)(2,1)S(1)} %copy-done.55), channel_id=1, source_target_pairs={{0,1},{1,0},{2,3},{3,2},{4,5},{5,4},{6,7},{7,6},{8,9},{9,8},{10,11... | collective-permute-start | bytes 786440 | tf_op jit(solution)/shard_map/ppermute | solution.py:960
  75.4 8.0 %collective-permute-start.8 = (bf16[1,128,1024]{2,1,0:T(8,128)(2,1)S(1)}, bf16[1,128,1024]{2,1,0:T(8,128)(2,1)S(1)}, u32[]{:S(2)}, u32[]{:S(2)}) collective-permute-start(bf16[1,128,1024]{2,1,0:T(8,128)(2,1)S(1)} %copy-done.21), channel_id=1, source_target_pairs={{0,2},{1,3},{2,0},{3,1},{4,6},{5,7},{6,4},{7,5},{8,10},{9,11},{10,... | collective-permute-start | bytes 786440 | tf_op jit(solution)/shard_map/ppermute | solution.py:960
  75.6 21.5 %collective-permute-start.7 = (bf16[1,128,1024]{2,1,0:T(8,128)(2,1)S(1)}, bf16[1,128,1024]{2,1,0:T(8,128)(2,1)S(1)}, u32[]{:S(2)}, u32[]{:S(2)}) collective-permute-start(bf16[1,128,1024]{2,1,0:T(8,128)(2,1)S(1)} %copy-done.21), channel_id=1, source_target_pairs={{0,4},{1,5},{2,6},{3,7},{4,0},{5,1},{6,2},{7,3},{8,12},{9,13},{10,... | collective-permute-start | bytes 786440 | tf_op jit(solution)/shard_map/ppermute | solution.py:960
  75.9 25.1 %collective-permute-start.12 = (bf16[2,256,512]{2,1,0:T(8,128)(2,1)S(1)}, bf16[2,256,512]{2,1,0:T(8,128)(2,1)S(1)}, u32[]{:S(2)}, u32[]{:S(2)}) collective-permute-start(bf16[2,256,512]{2,1,0:T(8,128)(2,1)S(1)} %copy-done.17), channel_id=1, source_target_pairs={{0,2},{1,3},{2,0},{3,1},{4,6},{5,7},{6,4},{7,5},{8,10},{9,11},{10,... | collective-permute-start | bytes 1572872 | tf_op jit(solution)/shard_map/ppermute | solution.py:960
  75.9 25.1 %collective-permute-start.11 = (bf16[2,256,512]{2,1,0:T(8,128)(2,1)S(1)}, bf16[2,256,512]{2,1,0:T(8,128)(2,1)S(1)}, u32[]{:S(2)}, u32[]{:S(2)}) collective-permute-start(bf16[2,256,512]{2,1,0:T(8,128)(2,1)S(1)} %copy-done.17), channel_id=1, source_target_pairs={{0,4},{1,5},{2,6},{3,7},{4,0},{5,1},{6,2},{7,3},{8,12},{9,13},{10,... | collective-permute-start | bytes 1572872 | tf_op jit(solution)/shard_map/ppermute | solution.py:960
  82.0 15.0 %copy-start.33 = (bf16[1024,512]{1,0:T(8,128)(2,1)}, bf16[1024,512]{1,0:T(8,128)(2,1)S(1)}, u32[]{:S(2)}) copy-start(bf16[1024,512]{1,0:T(8,128)(2,1)S(1)} %convolution_convert_fusion.6.q_ref.refs_16_) | copy-start | bytes 3145732
  82.0 21.2 %copy-start.60 = (f32[3,1024]{1,0:T(4,128)S(1)}, f32[3,1024]{1,0:T(4,128)}, u32[]{:S(2)}) copy-start(f32[3,1024]{1,0:T(4,128)} %refs_23_.1) | copy-start | bytes 36868
  82.1 22.0 %copy-start.54 = (bf16[1,256,2048]{2,1,0:T(8,128)(2,1)S(1)}, bf16[1,256,2048]{2,1,0:T(8,128)(2,1)}, u32[]{:S(2)}) copy-start(bf16[1,256,2048]{2,1,0:T(8,128)(2,1)} %dynamic-slice_bitcast_fusion.1) | copy-start | bytes 3145732
  83.3 13.7 %collective-permute-start.10 = (bf16[1,256,512]{2,1,0:T(8,128)(2,1)S(1)}, bf16[1,256,512]{2,1,0:T(8,128)(2,1)S(1)}, u32[]{:S(2)}, u32[]{:S(2)}) collective-permute-start(bf16[1,256,512]{2,1,0:T(8,128)(2,1)S(1)} %copy-done.19), channel_id=1, source_target_pairs={{0,2},{1,3},{2,0},{3,1},{4,6},{5,7},{6,4},{7,5},{8,10},{9,11},{10,... | collective-permute-start | bytes 786440 | tf_op jit(solution)/shard_map/ppermute | solution.py:960
  83.3 17.6 %collective-permute-start.9 = (bf16[1,256,512]{2,1,0:T(8,128)(2,1)S(1)}, bf16[1,256,512]{2,1,0:T(8,128)(2,1)S(1)}, u32[]{:S(2)}, u32[]{:S(2)}) collective-permute-start(bf16[1,256,512]{2,1,0:T(8,128)(2,1)S(1)} %copy-done.19), channel_id=1, source_target_pairs={{0,4},{1,5},{2,6},{3,7},{4,0},{5,1},{6,2},{7,3},{8,12},{9,13},{10,... | collective-permute-start | bytes 786440 | tf_op jit(solution)/shard_map/ppermute | solution.py:960
  97.0 13.4 %copy-start.7 = (bf16[1024,512]{1,0:T(8,128)(2,1)}, bf16[1024,512]{1,0:T(8,128)(2,1)S(1)}, u32[]{:S(2)}) copy-start(bf16[1024,512]{1,0:T(8,128)(2,1)S(1)} %get-tuple-element.104.refs_19_) | copy-start | bytes 3145732
  97.0 13.4 %copy-start.39 = (bf16[1024,512]{1,0:T(8,128)(2,1)}, bf16[1024,512]{1,0:T(8,128)(2,1)S(1)}, u32[]{:S(2)}) copy-start(bf16[1024,512]{1,0:T(8,128)(2,1)S(1)} %get-tuple-element.139.refs_20_) | copy-start | bytes 3145732
  101.0 4.6 collective-permute-start.14
  103.2 17.5 %collective-permute-start.17 = (bf16[1,128,1024]{2,1,0:T(8,128)(2,1)S(1)}, bf16[1,128,1024]{2,1,0:T(8,128)(2,1)S(1)}, u32[]{:S(2)}, u32[]{:S(2)}) collective-permute-start(bf16[1,128,1024]{2,1,0:T(8,128)(2,1)S(1)} %collective-permute-done.13.refs_0_), channel_id=1, source_target_pairs={{0,2},{1,3},{2,0},{3,1},{4,6},{5,7},{6,4},{7,5},{8,10},{9,11},{10,... | collective-permute-start | bytes 786440 | tf_op jit(solution)/shard_map/ppermute | solution.py:960
  103.8 16.9 %collective-permute-start.16 = (bf16[1,128,1024]{2,1,0:T(8,128)(2,1)S(1)}, bf16[1,128,1024]{2,1,0:T(8,128)(2,1)}, u32[]{:S(2)}, u32[]{:S(2)}) collective-permute-start(bf16[1,128,1024]{2,1,0:T(8,128)(2,1)S(1)} %collective-permute-done.13.refs_0_), channel_id=1, source_target_pairs={{0,4},{1,5},{2,6},{3,7},{4,0},{5,1},{6,2},{7,3},{8,12},{9,13},{10,... | collective-permute-start | bytes 786440 | tf_op jit(solution)/shard_map/ppermute | solution.py:960
  104.1 24.9 %collective-permute-start.18 = (bf16[1,256,2048]{2,1,0:T(8,128)(2,1)S(1)}, bf16[1,256,2048]{2,1,0:T(8,128)(2,1)S(1)}, u32[]{:S(2)}, u32[]{:S(2)}) collective-permute-start(bf16[1,256,2048]{2,1,0:T(8,128)(2,1)S(1)} %copy-done.54), channel_id=1, source_target_pairs={{0,1},{1,0},{2,3},{3,2},{4,5},{5,4},{6,7},{7,6},{8,9},{9,8},{10,11... | collective-permute-start | bytes 3145736 | tf_op jit(solution)/shard_map/ppermute | solution.py:960
  105.6 8.8 %collective-permute-start.19 = (bf16[1,256,512]{2,1,0:T(8,128)(2,1)S(1)}, bf16[1,256,512]{2,1,0:T(8,128)(2,1)S(1)}, u32[]{:S(2)}, u32[]{:S(2)}) collective-permute-start(bf16[1,256,512]{2,1,0:T(8,128)(2,1)S(1)} %collective-permute-done.9.refs_1_), channel_id=1, source_target_pairs={{0,2},{1,3},{2,0},{3,1},{4,6},{5,7},{6,4},{7,5},{8,10},{9,11},{10,... | collective-permute-start | bytes 786440 | tf_op jit(solution)/shard_map/ppermute | solution.py:960
  105.6 11.3 %collective-permute-start.15 = (bf16[2,256,512]{2,1,0:T(8,128)(2,1)S(1)}, bf16[2,256,512]{2,1,0:T(8,128)(2,1)S(1)}, u32[]{:S(2)}, u32[]{:S(2)}) collective-permute-start(bf16[2,256,512]{2,1,0:T(8,128)(2,1)S(1)} %collective-permute-done.11.refs_1_), channel_id=1, source_target_pairs={{0,2},{1,3},{2,0},{3,1},{4,6},{5,7},{6,4},{7,5},{8,10},{9,11},{10,... | collective-permute-start | bytes 1572872 | tf_op jit(solution)/shard_map/ppermute | solution.py:960
  114.3 19.9 %copy-start.34 = (bf16[1024,512]{1,0:T(8,128)(2,1)}, bf16[1024,512]{1,0:T(8,128)(2,1)S(1)}, u32[]{:S(2)}) copy-start(bf16[1024,512]{1,0:T(8,128)(2,1)S(1)} %convolution_convert_fusion.3.q_ref.refs_1_) | copy-start | bytes 3145732
  118.5 13.5 %copy-start.6 = (bf16[2,1024,512]{2,1,0:T(8,128)(2,1)}, bf16[2,1024,512]{2,1,0:T(8,128)(2,1)S(1)}, u32[]{:S(2)}) copy-start(bf16[2,1024,512]{2,1,0:T(8,128)(2,1)S(1)} %arrange.9.refs_47_) | copy-start | bytes 6291460
  120.7 13.5 %copy-start.29 = (bf16[1024,512]{1,0:T(8,128)(2,1)S(1)}, bf16[1024,512]{1,0:T(8,128)(2,1)}, u32[]{:S(2)}) copy-start(bf16[1024,512]{1,0:T(8,128)(2,1)} %convolution_convert_fusion.8.k_ref.refs_2_) | copy-start | bytes 3145732
  120.7 13.5 %copy-start.30 = (bf16[1024,512]{1,0:T(8,128)(2,1)S(1)}, bf16[1024,512]{1,0:T(8,128)(2,1)}, u32[]{:S(2)}) copy-start(bf16[1024,512]{1,0:T(8,128)(2,1)} %convolution_convert_fusion.7.v_ref.refs_3_) | copy-start | bytes 3145732
  120.7 13.5 %copy-start.22 = (bf16[1,128,1024]{2,1,0:T(8,128)(2,1)}, bf16[1,128,1024]{2,1,0:T(8,128)(2,1)S(1)}, u32[]{:S(2)}) copy-start(bf16[1,128,1024]{2,1,0:T(8,128)(2,1)S(1)} %collective-permute-done.17.refs_2_) | copy-start | bytes 786436
  129.0 5.2 copy-start.8
  129.0 27.3 %collective-permute-start.21 = (bf16[1,256,2048]{2,1,0:T(8,128)(2,1)S(1)}, bf16[1,256,2048]{2,1,0:T(8,128)(2,1)S(1)}, u32[]{:S(2)}, u32[]{:S(2)}) collective-permute-start(bf16[1,256,2048]{2,1,0:T(8,128)(2,1)S(1)} %collective-permute-done.18.refs_0_), channel_id=1, source_target_pairs={{0,2},{1,3},{2,0},{3,1},{4,6},{5,7},{6,4},{7,5},{8,10},{9,11},{10,... | collective-permute-start | bytes 3145736 | tf_op jit(solution)/shard_map/ppermute | solution.py:960
  129.1 27.3 %collective-permute-start.20 = (bf16[1,256,2048]{2,1,0:T(8,128)(2,1)S(1)}, bf16[1,256,2048]{2,1,0:T(8,128)(2,1)S(1)}, u32[]{:S(2)}, u32[]{:S(2)}) collective-permute-start(bf16[1,256,2048]{2,1,0:T(8,128)(2,1)S(1)} %collective-permute-done.18.refs_0_), channel_id=1, source_target_pairs={{0,4},{1,5},{2,6},{3,7},{4,0},{5,1},{6,2},{7,3},{8,12},{9,13},{10,... | collective-permute-start | bytes 3145736 | tf_op jit(solution)/shard_map/ppermute | solution.py:960
  130.7 25.6 %collective-permute-start.22 = (bf16[1,512,1024]{2,1,0:T(8,128)(2,1)}, bf16[1,512,1024]{2,1,0:T(8,128)(2,1)}, u32[]{:S(2)}, u32[]{:S(2)}) collective-permute-start(bf16[1,512,1024]{2,1,0:T(8,128)(2,1)} %dynamic-slice_bitcast_fusion), channel_id=1, source_target_pairs={{0,1},{1,0},{2,3},{3,2},{4,5},{5,4},{6,7},{7,6},{8,9},{9,8},{10,11... | collective-permute-start | bytes 3145736 | tf_op jit(solution)/shard_map/ppermute | solution.py:960
  134.2 28.0 %collective-permute-start.25 = (bf16[1,128,1024]{2,1,0:T(8,128)(2,1)}, bf16[1,128,1024]{2,1,0:T(8,128)(2,1)}, u32[]{:S(2)}, u32[]{:S(2)}) collective-permute-start(bf16[1,128,1024]{2,1,0:T(8,128)(2,1)} %collective-permute-done.16.refs_1_), channel_id=1, source_target_pairs={{0,2},{1,3},{2,0},{3,1},{4,6},{5,7},{6,4},{7,5},{8,10},{9,11},{10,... | collective-permute-start | bytes 786440 | tf_op jit(solution)/shard_map/ppermute | solution.py:960
  156.0 6.2 %copy-start.23 = (bf16[1,128,1024]{2,1,0:T(8,128)(2,1)S(1)}, bf16[1,128,1024]{2,1,0:T(8,128)(2,1)}, u32[]{:S(2)}) copy-start(bf16[1,128,1024]{2,1,0:T(8,128)(2,1)} %copy-done.22) | copy-start | bytes 786436
  156.0 7.8 %copy-start.35 = (bf16[1024,512]{1,0:T(8,128)(2,1)S(1)}, bf16[1024,512]{1,0:T(8,128)(2,1)}, u32[]{:S(2)}) copy-start(bf16[1024,512]{1,0:T(8,128)(2,1)} %convolution_convert_fusion.2.q_ref.refs_6_) | copy-start | bytes 3145732
  156.0 7.8 %copy-start.36 = (bf16[1024,512]{1,0:T(8,128)(2,1)S(1)}, bf16[1024,512]{1,0:T(8,128)(2,1)}, u32[]{:S(2)}) copy-start(bf16[1024,512]{1,0:T(8,128)(2,1)} %fusion.6.k_ref.refs_7_) | copy-start | bytes 3145732
  156.0 7.8 %copy-start.37 = (bf16[1024,512]{1,0:T(8,128)(2,1)S(1)}, bf16[1024,512]{1,0:T(8,128)(2,1)}, u32[]{:S(2)}) copy-start(bf16[1024,512]{1,0:T(8,128)(2,1)} %fusion.7.v_ref.refs_8_) | copy-start | bytes 3145732
  156.3 5.9 %copy-start.11 = (bf16[1,256,2048]{2,1,0:T(8,128)(2,1)}, bf16[1,256,2048]{2,1,0:T(8,128)(2,1)S(1)}, u32[]{:S(2)}) copy-start(bf16[1,256,2048]{2,1,0:T(8,128)(2,1)S(1)} %collective-permute-done.21.refs_2_) | copy-start | bytes 3145732
  156.3 23.3 %collective-permute-start.24 = (bf16[1,512,1024]{2,1,0:T(8,128)(2,1)}, bf16[1,512,1024]{2,1,0:T(8,128)(2,1)S(1)}, u32[]{:S(2)}, u32[]{:S(2)}) collective-permute-start(bf16[1,512,1024]{2,1,0:T(8,128)(2,1)} %collective-permute-done.22.refs_0_), channel_id=1, source_target_pairs={{0,2},{1,3},{2,0},{3,1},{4,6},{5,7},{6,4},{7,5},{8,10},{9,11},{10,... | collective-permute-start | bytes 3145736 | tf_op jit(solution)/shard_map/ppermute | solution.py:960
  156.6 25.7 %collective-permute-start.23 = (bf16[1,512,1024]{2,1,0:T(8,128)(2,1)}, bf16[1,512,1024]{2,1,0:T(8,128)(2,1)}, u32[]{:S(2)}, u32[]{:S(2)}) collective-permute-start(bf16[1,512,1024]{2,1,0:T(8,128)(2,1)} %collective-permute-done.22.refs_0_), channel_id=1, source_target_pairs={{0,4},{1,5},{2,6},{3,7},{4,0},{5,1},{6,2},{7,3},{8,12},{9,13},{10,... | collective-permute-start | bytes 3145736 | tf_op jit(solution)/shard_map/ppermute | solution.py:960
  163.4 18.8 %copy-start.2 = (bf16[1,512,1024]{2,1,0:T(8,128)(2,1)}, bf16[1,512,1024]{2,1,0:T(8,128)(2,1)S(1)}, u32[]{:S(2)}) copy-start(bf16[1,512,1024]{2,1,0:T(8,128)(2,1)S(1)} %arrange.11) | copy-start | bytes 3145732
  163.5 18.8 %copy-start.43 = (f32[1024,1024]{1,0:T(8,128)S(1)}, f32[1024,1024]{1,0:T(8,128)}, u32[]{:S(2)}) copy-start(f32[1024,1024]{1,0:T(8,128)} %copy-done.42) | copy-start | bytes 12582916
  163.5 47.6 %collective-permute-start.26 = (bf16[1,256,2048]{2,1,0:T(8,128)(2,1)S(1)}, bf16[1,256,2048]{2,1,0:T(8,128)(2,1)}, u32[]{:S(2)}, u32[]{:S(2)}) collective-permute-start(bf16[1,256,2048]{2,1,0:T(8,128)(2,1)S(1)} %collective-permute-done.20.refs_1_), channel_id=1, source_target_pairs={{0,2},{1,3},{2,0},{3,1},{4,6},{5,7},{6,4},{7,5},{8,10},{9,11},{10,... | collective-permute-start | bytes 3145736 | tf_op jit(solution)/shard_map/ppermute | solution.py:960
  179.6 6.5 %copy-start.10 = (bf16[1024,512]{1,0:T(8,128)(2,1)}, bf16[1024,512]{1,0:T(8,128)(2,1)S(1)}, u32[]{:S(2)}) copy-start(bf16[1024,512]{1,0:T(8,128)(2,1)S(1)} %get-tuple-element.124.refs_9_) | copy-start | bytes 3145732
  179.6 6.5 %copy-start.41 = (bf16[1024,512]{1,0:T(8,128)(2,1)}, bf16[1024,512]{1,0:T(8,128)(2,1)S(1)}, u32[]{:S(2)}) copy-start(bf16[1024,512]{1,0:T(8,128)(2,1)S(1)} %get-tuple-element.137.refs_10_) | copy-start | bytes 3145732
  179.6 6.5 %copy-start.13 = (bf16[1,512,1024]{2,1,0:T(8,128)(2,1)}, bf16[1,512,1024]{2,1,0:T(8,128)(2,1)S(1)}, u32[]{:S(2)}) copy-start(bf16[1,512,1024]{2,1,0:T(8,128)(2,1)S(1)} %collective-permute-done.24.refs_2_) | copy-start | bytes 3145732
  182.3 32.5 %collective-permute-start.27 = (bf16[1,512,1024]{2,1,0:T(8,128)(2,1)}, bf16[1,512,1024]{2,1,0:T(8,128)(2,1)}, u32[]{:S(2)}, u32[]{:S(2)}) collective-permute-start(bf16[1,512,1024]{2,1,0:T(8,128)(2,1)} %collective-permute-done.23.refs_1_), channel_id=1, source_target_pairs={{0,2},{1,3},{2,0},{3,1},{4,6},{5,7},{6,4},{7,5},{8,10},{9,11},{10,... | collective-permute-start | bytes 3145736 | tf_op jit(solution)/shard_map/ppermute | solution.py:960
  194.5 16.5 %copy-start.9 = (bf16[1,256,2048]{2,1,0:T(8,128)(2,1)S(1)}, bf16[1,256,2048]{2,1,0:T(8,128)(2,1)}, u32[]{:S(2)}) copy-start(bf16[1,256,2048]{2,1,0:T(8,128)(2,1)} %copy-done.8) | copy-start | bytes 3145732
  194.5 16.5 %copy-start.12 = (bf16[1,256,2048]{2,1,0:T(8,128)(2,1)S(1)}, bf16[1,256,2048]{2,1,0:T(8,128)(2,1)}, u32[]{:S(2)}) copy-start(bf16[1,256,2048]{2,1,0:T(8,128)(2,1)} %copy-done.11) | copy-start | bytes 3145732
  219.1 16.4 %copy-start.45 = (f32[1024,1024]{1,0:T(8,128)S(1)}, f32[1024,1024]{1,0:T(8,128)}, u32[]{:S(2)}) copy-start(f32[1024,1024]{1,0:T(8,128)} %copy-done.44) | copy-start | bytes 12582916
  219.1 16.4 %copy-start.50 = (f32[1024,1024]{1,0:T(8,128)S(1)}, f32[1024,1024]{1,0:T(8,128)}, u32[]{:S(2)}) copy-start(f32[1024,1024]{1,0:T(8,128)} %get-tuple-element.127) | copy-start | bytes 12582916
  565.3 11.2 %copy-start.58 = (f32[8,1024]{1,0:T(8,128)S(1)}, f32[8,1024]{1,0:T(8,128)}, u32[]{:S(2)}) copy-start(f32[8,1024]{1,0:T(8,128)} %get-tuple-element.157) | copy-start | bytes 98308
  565.4 11.9 %copy-start.53 = (bf16[1024,1024]{1,0:T(8,128)(2,1)S(1)}, bf16[1024,1024]{1,0:T(8,128)(2,1)}, u32[]{:S(2)}) copy-start(bf16[1024,1024]{1,0:T(8,128)(2,1)} %get-tuple-element.193) | copy-start | bytes 6291460
  (26 other events, 59.3 us)

commit v5 on v4

--- a/solution.py
+++ b/solution.py
@@ -446,7 +446,7 @@
     ]
 
 
-def back_pair(causal, length, q2, k2, v2, c2, aug, g2, grads, scratch, tick):
+def back_pair(causal, length, q2, k2, v2, c2, aug, g2, grads, member, scratch, tick):
     qs, qm, ka, gs, gm, va, dqa, kt = scratch
     seq = k2.shape[0]
     lane = lanes(seq)
@@ -479,7 +479,7 @@
         va[h, :, 128:] = jnp.where(sel, one, zero)
         kt[h] = ka[h, :, :128].T
     dqa[...] = jnp.zeros_like(dqa)
-    grads[:, 384:] = c2
+    grads[:, member(3)] = c2
     for j in range(seq // BLK):
         rows = slice(j * BLK, (j + 1) * BLK)
         q0 = j * BLK if causal else 0
@@ -503,15 +503,15 @@
             dk = b if dk is None else dk + b
             dq = c if dq is None else dq + c
         dqa[:, q0:] += dq
-        grads[rows, 128:256] = dk.astype(bf16)
-        grads[rows, 256:384] = dv.astype(bf16)
+        grads[rows, member(1)] = dk.astype(bf16)
+        grads[rows, member(2)] = dv.astype(bf16)
         tick(j)
-    grads[:, :128] = (dqa[...] * HD**-0.5).T.astype(bf16)
+    grads[:, member(0)] = (dqa[...] * HD**-0.5).T.astype(bf16)
 
 
 BOTH = (0, 1)
 X, CORE, Y, Z1, Z2 = range(5)
-DELAY = 3
+DELAY = 2
 SLOTS = 2 * DELAY
 CHUNK = 64
 SUBS = 4
@@ -527,6 +527,7 @@
 SELF_AT = CROSS_AT + STEPS * CROSS_TICKS + NORM_TICKS
 DRAIN_AT = SELF_AT + STEPS * SELF_TICKS
 TILE = 256
+NORM_TILE = 128
 dma_sem = pltpu.SemaphoreType.DMA
 
 
@@ -653,15 +654,15 @@
 def norm_step(index, more, weights, gain_ref, sum_ref, total, dc, left, acc, zt, sems, tick):
     def fetch_tile(a):
         slot = lax.rem(a, 2)
-        rows = pl.ds(pl.multiple_of(a * TILE, TILE), TILE)
+        rows = pl.ds(pl.multiple_of(a * NORM_TILE, NORM_TILE), NORM_TILE)
         return pltpu.make_async_copy(sum_ref.at[rows], zt.at[slot], sems.at[slot])
 
-    tiles = total.shape[0] // TILE
+    tiles = total.shape[0] // NORM_TILE
     fetch_tile(0).start()
 
     @pl.loop(0, tiles)
     def _(a):
-        rows = pl.ds(pl.multiple_of(a * TILE, TILE), TILE)
+        rows = pl.ds(pl.multiple_of(a * NORM_TILE, NORM_TILE), NORM_TILE)
         fetch_tile(a).wait()
 
         @pl.when(a + 1 < tiles)
@@ -684,7 +685,7 @@
         left[:, rows] = g.T
         for i in BOTH:
             dc[i, rows, :] = dot(g, weights[i][...], NT).astype(bf16)
-        tick(a)
+        pl.when(lax.rem(a, 2) == 1)(lambda: tick(a // 2))
 
 
 def back_kernel(*refs):
@@ -752,18 +753,28 @@
     def send_grad(ref):
         return pltpu.make_async_copy(lefts.at[1], ref, base_sem)
 
-    def post(slot, block):
-        return pltpu.make_async_copy(staged.at[slot], queue.at[block, half], staged_sems.at[slot])
-
-    def products(slot, block, spans, ticks):
-        for a in range(2):
-            rows = slice(2 * a * TILE, 2 * (a + 1) * TILE)
-            for left, right, lo, hi in spans:
-                result = dot(lefts[left, rows, :], right[:, lo:hi]).astype(bf16)
-                staged[slot, a, :, :, :, lo:hi] = result.reshape(2, SUBS, CHUNK, hi - lo)
-            if a in ticks:
-                tick(ticks[a])
-        post(slot, block).start()
+    def post(slot, block, i):
+        return pltpu.make_async_copy(staged.at[slot], queue.at[block, i], staged_sems.at[slot])
+
+    def posted():
+        for slot in range(2):
+            post(slot, 0, 0).wait()
+
+    def feed_product(slot, block, left, right):
+        result = dot(lefts[left], right[:, :WIDTH])
+        staged[slot] = result.astype(bf16).reshape(2, 2, SUBS, CHUNK, WIDTH)
+        post(slot, block, half).start()
+
+    def pair_products(block, spans):
+        for left, first, last in spans:
+            result = dot(lefts[left], grads[:, 256 * first : 256 * last]).astype(bf16)
+            for m in range(first, last):
+                for i in BOTH:
+                    at = 256 * (m - first) + 128 * i
+                    piece = result[:, at : at + 128].reshape(2, 2, SUBS, CHUNK, 128)
+                    staged[i, :, :, :, :, 128 * m : 128 * (m + 1)] = piece
+        for i in BOTH:
+            post(i, block, i).start()
 
     @pl.when(step == 0)
     def _():
@@ -792,24 +803,24 @@
                     for copy in load_feed(1 - i, pair + i):
                         copy.start()
 
+        du = dot(lefts[2], flat[half], NT) * tall[1, half].astype(f32)
+        grads[:, :WIDTH] = du.astype(bf16)
+        @pl.when(step > 0)
+        def _():
+            post(0, 0, 0).wait()
+
+        feed_product(0, 2 * pair, 0, tall.at[0, half])
+        tick(t)
         for a in range(2):
             rows = slice(2 * a * TILE, 2 * (a + 1) * TILE)
-            du = dot(lefts[2, rows, :], flat[half], NT) * tall[1, half, rows, :].astype(f32)
-            grads[rows, :] = du.astype(bf16)
+            total[rows, :] += dot(grads[rows, :WIDTH], tall[2, half], NT)
+
         @pl.when(step > 0)
         def _():
-            post(0, 0).wait()
-
-        products(0, 2 * pair, ((0, tall.at[0, half], 0, WIDTH),), {1: t})
-        for a in range(2):
-            rows = slice(2 * a * TILE, 2 * (a + 1) * TILE)
-            total[rows, :] += dot(grads[rows, :], tall[2, half], NT)
-
-        @pl.when(step > 0)
-        def _():
-            post(1, 0).wait()
-
-        products(1, 2 * pair + 1, ((1, grads, 0, WIDTH),), {1: t + 1})
+            post(1, 0, 0).wait()
+
+        feed_product(1, 2 * pair + 1, 1, grads)
+        tick(t + 1)
 
     @pl.when(step == STEPS)
     def _():
@@ -821,9 +832,13 @@
         )
         for copy in fetch:
             copy.wait()
-        post(1, 0).wait()
+        posted()
 
     at = pl.ds(pl.multiple_of(pair * 128, 128), 128)
+
+    def member(m):
+        return pl.ds(pl.multiple_of(256 * m + 128 * half, 128), 128)
+
 
     @pl.when((step >= STEPS) & (step < 2 * STEPS))
     def _():
@@ -834,13 +849,19 @@
             if j % 2 == 1:
                 tick(t + j // 2)
 
-        back_pair(False, len_ref[0], q2, k2, v2, c2, aug, dc[half, :, at], grads, scratch, ticks)
-        ends[2, half, :, at] = grads[:, :128]
-        ends[0, half, :, at] = grads[:, 128:256]
-        ends[1, half, :, at] = grads[:, 256:384]
-        post(0, 0).wait()
-        spans = ((0, grads, 0, 128), (1, grads, 128, 384), (2, grads, 384, 512))
-        products(0, 2 * QUADS + pair, spans, {1: t + 2})
+        back_pair(False, len_ref[0], q2, k2, v2, c2, aug, dc[half, :, at], grads, member, scratch, ticks)
+        for m, k in ((0, 2), (1, 0), (2, 1)):
+            ends[k, half, :, at] = grads[:, member(m)]
+
+        @pl.when((half == 0) & (step > STEPS))
+        def _():
+            posted()
+
+        @pl.when(half == 1)
+        def _():
+            pair_products(2 * QUADS + pair, ((0, 0, 1), (1, 1, 3), (2, 3, 4)))
+
+        tick(t + 2)
 
     @pl.when(step == 2 * STEPS)
     def _():
@@ -871,18 +892,25 @@
             if j == 0:
                 tick(t)
 
-        back_pair(True, 0, q2, k2, v2, c2, aug, dc[half, :, at], grads, scratch, ticks)
-        ends[0, half, :, at] = grads[:, :128]
-        ends[1, half, :, at] = grads[:, 128:256]
-        ends[2, half, :, at] = grads[:, 256:384]
-        post(0, 0).wait()
-        products(0, 3 * QUADS + pair, ((0, grads, 0, 384), (2, grads, 384, 512)), {0: t + 1})
+        back_pair(True, 0, q2, k2, v2, c2, aug, dc[half, :, at], grads, member, scratch, ticks)
+        for m in range(3):
+            ends[m, half, :, at] = grads[:, member(m)]
+
+        @pl.when(half == 0)
+        def _():
+            posted()
+
+        @pl.when(half == 1)
+        def _():
+            pair_products(3 * QUADS + pair, ((0, 0, 3), (2, 3, 4)))
+
+        tick(t + 1)
         for k in range(5, -1, -1):
             pl.when(step == 2 * STEPS + 1 + k)(functools.partial(small_stage, k, *small_refs))
 
     @pl.when(step == 3 * STEPS - 1)
     def _():
-        post(0, 0).wait()
+        posted()
         send_grad(dmem_ref).wait()
         for copy in load_last():
             copy.wait()
@@ -925,7 +953,7 @@
             shape((blocks, 2, 2, 2, SUBS, CHUNK, WIDTH), bf16),
             shape(small.shape, f32),
         ],
-        scratch_shapes=[vmem((seq, WIDTH), bf16)]
+        scratch_shapes=[vmem((seq, 2 * WIDTH), bf16)]
         + back_scratch(seq)
         + stream_scratch()
         + small_scratch(small.shape)
@@ -936,7 +964,7 @@
             vmem((seq, model), f32),
             vmem((3, 2, seq, width), bf16),
             vmem((2, seq, width), bf16),
-            vmem((2, TILE, model), f32),
+            vmem((2, NORM_TILE, model), f32),
             vmem((2, 2, 2, SUBS, CHUNK, WIDTH), bf16),
             dma_sem((3,)),
             dma_sem((4, 2)),
@@ -945,7 +973,7 @@
             dma_sem,
         ],
         compiler_params=pltpu.CompilerParams(
-            collective_id=1, has_side_effects=True, vmem_limit_bytes=60 * 2**20
+            collective_id=1, has_side_effects=True, vmem_limit_bytes=62 * 2**20
         ),
         cost_estimate=cost(16, 8, seq, False),
         name="layer_back",

time: 584 us -> 577 us (0.988)
  Pallas kernels: 441 us -> 433 us
    pallas_call x1, Pallas kernels: 297 us -> 289 us  [layer_back(): pl.pallas_call(back_kernel, grid=(3 * STEPS,), in_specs=[pl.BlockSpec(mem...]
  transfers between devices with their start and end apart: 28 -> 28, of which waited for: 7 -> 7; matrix products, arithmetic and copies ran while one was open for 10% -> 10% of each run, Pallas kernels for 16% -> 17%
where the time goes in v5:
time: 577 us; the launch traced here: 572 us
  Pallas kernels  433 us (75%)
  matrix products  44.5 us (8%)
  local copies, waits for them, and re-layouts  32.4 us (6%)
  waiting for transfers between devices  26.7 us (5%)
  starting transfers between devices  17.7 us (3%)
  other arithmetic  16.1 us (3%)
    pallas_call x1, Pallas kernels, layer_back(): pl.pallas_call(back_kernel, grid=(3 * STEPS,), in_specs=[pl.BlockSpec(mem...  289 us
    pallas_call x4, Pallas kernels, attend_fwd(): pl.pallas_call(functools.partial(fwd_kernel, causal), grid=(width // 128,...  57.7 us
    dot_general x16, matrix products, dot(): return lax.dot_general(a, b, dims, preferred_element_type=f32)  44.5 us
    pallas_call x2, Pallas kernels, ffn_forward(): pl.pallas_call(ffn_kernel, grid=(seq // ROWS,), in_specs=[rows(width)] +...  32.9 us
    ppermute x28, waiting for transfers between devices, swap(): return lax.ppermute(x, ALL, [(i, i ^ flip) for i in range(DEVICES)])  26.7 us
    pallas_call x5, Pallas kernels, flip(): pl.pallas_call(flip_kernel, grid=(4,), in_specs=[pl.BlockSpec((rows // 4,...  20.7 us
    unnamed x126, local copies, waits for them, and re-layouts  17.8 us
    ppermute x28, starting transfers between devices, swap(): return lax.ppermute(x, ALL, [(i, i ^ flip) for i in range(DEVICES)])  17.7 us
  transfers between devices with their start and end apart: 28, of which 7 were waited for; matrix products, arithmetic and copies ran while one was open for 10% of the time, Pallas kernels for 17%

profile of v5, /device:TPU:0, one launch (start us, length us, event | category | flops | bytes accessed | tf_op | source)
XLA Modules:
  0.0 572.1 jit_solution(3964363427824902493)
XLA Ops:
  0.7 2.1 constant_dynamic-slice_fusion
  2.8 2.9 collective-permute-start
  5.7 3.1 convolution_convert_fusion.9.v_ref.refs_13_
  8.8 1.2 convolution_convert_fusion.10.k_ref.refs_12_
  10.1 2.2 convolution_convert_fusion.11.q_ref.refs_11_
  12.3 1.7 dynamic-slice_bitcast_fusion.3
  15.1 1.7 dynamic-slice_bitcast_fusion.4
  17.3 2.3 dynamic-slice_bitcast_fusion.1
  19.6 1.2 copy-done.28
  20.9 13.1 %attend_causal.2 = (bf16[1024,512]{1,0:T(8,128)(2,1)S(1)}, bf16[1024,512]{1,0:T(8,128)(2,1)S(1)}) custom-call(s32[1]{0:T(128)} %dynamic_slice.24.len_ref.refs_0_, bf16[1024,512]{1,0:T(8,128)(2,1)S(1)} %copy-done.28, bf16[1024,512]{1,0:T(8,128)(2,1)S(1)} %convolution_convert_fusion.10.k_ref.refs_12_, ...), custom_call_target="tpu_custom_call" | custom-call | flops 5368709120 | bytes 8388608 | tf_op jit(solution)/shard_map/attend_causal/pallas_call | solution.py:422
  36.0 1.6 collective-permute-start.1
  37.6 1.7 dynamic-slice_bitcast_fusion.2
  39.2 4.2 flip.5.refs_38_
  44.2 4.1 convolution_convert_fusion.8.k_ref.refs_2_
  48.3 4.1 flip.6.refs_37_
  52.4 1.3 collective-permute-start.3
  54.4 4.1 convolution_convert_fusion.7.v_ref.refs_3_
  58.5 5.3 collective-permute-done.3.refs_0_
  63.8 4.9 collective-permute-done.4.refs_0_
  69.8 4.9 fusion.29
  75.9 1.8 collective-permute-start.11
  78.2 1.2 convolution_convert_fusion.4.v_ref.refs_18_
  79.5 1.2 convolution_convert_fusion.5.k_ref.refs_17_
  80.8 1.3 convolution_convert_fusion.6.q_ref.refs_16_
  82.1 1.3 collective-permute-done.13.refs_0_
  83.9 13.2 %attend_causal.3 = (bf16[1024,512]{1,0:T(8,128)(2,1)S(1)}, bf16[1024,512]{1,0:T(8,128)(2,1)S(1)}) custom-call(s32[1]{0:T(128)} %dynamic_slice.24.len_ref.refs_0_, bf16[1024,512]{1,0:T(8,128)(2,1)S(1)} %convolution_convert_fusion.6.q_ref.refs_16_, bf16[1024,512]{1,0:T(8,128)(2,1)S(1)} %convolution_convert_fusion.5.k_ref.refs_17_, ...), custom_call_target="tpu_custom_call" | custom-call | flops 5368709120 | bytes 8388608 | tf_op jit(solution)/shard_map/attend_causal/pallas_call | solution.py:422
  97.1 3.9 collective-permute-done.9.refs_1_
  101.0 2.3 dynamic-slice_bitcast_fusion
  104.1 1.5 collective-permute-start.18
  106.3 4.2 fusion.27
  113.1 1.2 convolution_convert_fusion.3.q_ref.refs_1_
  114.6 2.3 convolution_convert_fusion.2.q_ref.refs_6_
  118.5 2.2 fusion.6.k_ref.refs_7_
  120.7 8.3 %collective-permute-done.18.refs_0_ = bf16[1,256,2048]{2,1,0:T(8,128)(2,1)S(1)} collective-permute-done((bf16[1,256,2048]{2,1,0:T(8,128)(2,1)S(1)}, bf16[1,256,2048]{2,1,0:T(8,128)(2,1)S(1)}, u32[]{:S(2)}, u32[]{:S(2)}) %collective-permute-start.18) | collective-permute-done | bytes 1048608 | tf_op jit(solution)/shard_map/ppermute | solution.py:988
  129.1 1.7 collective-permute-start.20
  130.7 1.3 collective-permute-start.22
  132.0 2.2 fusion.7.v_ref.refs_8_
  134.2 15.7 %attend_memory.2 = (bf16[1024,512]{1,0:T(8,128)(2,1)S(1)}, bf16[1024,512]{1,0:T(8,128)(2,1)S(1)}) custom-call(s32[1]{0:T(128)} %dynamic_slice.24.len_ref.refs_0_, bf16[1024,512]{1,0:T(8,128)(2,1)S(1)} %convolution_convert_fusion.3.q_ref.refs_1_, bf16[1024,512]{1,0:T(8,128)(2,1)S(1)} %copy-done.29, bf16[1024,512]{1,0:T(8,128)(2,1)S(1)} %copy-done.30), custom_call_target="tpu_custom_call" | custom-call | flops 8589934592 | bytes 8388608 | tf_op jit(solution)/shard_map/attend_memory/pallas_call | solution.py:422
  151.9 4.1 flip.7.refs_36_
  157.0 5.2 fusion.30
  162.2 1.2 arrange.11
  163.8 15.8 %attend_memory.3 = (bf16[1024,512]{1,0:T(8,128)(2,1)S(1)}, bf16[1024,512]{1,0:T(8,128)(2,1)S(1)}) custom-call(s32[1]{0:T(128)} %dynamic_slice.24.len_ref.refs_0_, bf16[1024,512]{1,0:T(8,128)(2,1)S(1)} %copy-done.35, bf16[1024,512]{1,0:T(8,128)(2,1)S(1)} %copy-done.36, bf16[1024,512]{1,0:T(8,128)(2,1)S(1)} %copy-done.37), custom_call_target="tpu_custom_call" | custom-call | flops 8589934592 | bytes 8388608 | tf_op jit(solution)/shard_map/attend_memory/pallas_call | solution.py:422
  179.7 2.6 collective-permute-done.23.refs_1_
  182.3 3.9 fusion.28
  186.8 1.5 copy-done.44
  188.3 2.0 fusion.5.h_ref.x_ref
  190.3 4.2 flip.8.refs_35_
  194.5 16.5 %feed_forward.2 = (bf16[1024,2048]{1,0:T(8,128)(2,1)}, bf16[1024,2048]{1,0:T(8,128)(2,1)}, f32[1024,1024]{1,0:T(8,128)}) custom-call(bf16[1024,1024]{1,0:T(8,128)(2,1)S(1)} %copy-done, bf16[1024,2048]{1,0:T(8,128)(2,1)} %refs_27_.1, bf16[2048,1024]{1,0:T(8,128)(2,1)} %refs_28_.1), custom_call_target="tpu_custom_call" | custom-call | flops 8589934592 | bytes 23068672 | tf_op jit(solution)/shard_map/feed_forward/pallas_call | solution.py:1096
  211.1 1.7 arrange.12
  212.8 2.0 copy-done.3
  214.8 2.3 arrange.13
  217.1 2.0 copy-done.4
  219.1 16.4 %feed_forward.3 = (bf16[1024,2048]{1,0:T(8,128)(2,1)}, bf16[1024,2048]{1,0:T(8,128)(2,1)}, f32[1024,1024]{1,0:T(8,128)}) custom-call(bf16[1024,1024]{1,0:T(8,128)(2,1)S(1)} %copy-done, bf16[1024,2048]{1,0:T(8,128)(2,1)} %bitcast.91, bf16[2048,1024]{1,0:T(8,128)(2,1)} %bitcast.93), custom_call_target="tpu_custom_call" | custom-call | flops 8589934592 | bytes 23068672 | tf_op jit(solution)/shard_map/feed_forward/pallas_call | solution.py:1096
  235.5 3.3 fusion.23
  240.5 2.0 fusion.2
  242.5 3.2 fusion.22
  245.7 3.2 add_multiply_fusion
  248.8 4.1 flip.9.refs_34_
  253.6 289.1 %layer_back.1 = (bf16[1024,1024]{1,0:T(8,128)(2,1)}, bf16[1024,1024]{1,0:T(8,128)(2,1)}, bf16[16,2,2,4,64,512]{5,4,3,2,1,0:T(8,128)(2,1)}, bf16[16,2,2,2,4,64,512]{6,5,4,3,2,1,0:T(8,128)(2,1)}, f32[8,1024]{1,0:T(8,128)}) custom-call(s32[1]{0:T(128)} %dynamic_slice.24.len_ref.refs_0_, bf16[1024,512]{1,0:T(8,128)(2,1)} %copy-done.34, ...), custom_call_target="tpu_custom_call" | custom-call | flops 137438953472 | bytes 16777216 | tf_op jit(solution)/shard_map/layer_back/pallas_call | solution.py:941
  542.6 7.3 %spread.3 = (f32[1,1024,512]{2,1,0:T(8,128)}, f32[2,1024,512]{2,1,0:T(8,128)}, f32[512,1024]{1,0:T(8,128)}) custom-call(bf16[16,1024,512]{2,1,0:T(8,128)(2,1)} %bitcast.96), custom_call_target="tpu_custom_call" | custom-call | bytes 12582912 | tf_op jit(solution)/shard_map/spread/pallas_call | solution.py:1159
  550.0 7.4 %spread.2 = (f32[3,1024,512]{2,1,0:T(8,128)}, f32[512,1024]{1,0:T(8,128)}) custom-call(bf16[16,1024,512]{2,1,0:T(8,128)(2,1)} %bitcast.97), custom_call_target="tpu_custom_call" | custom-call | bytes 12582912 | tf_op jit(solution)/shard_map/spread/pallas_call | solution.py:1159
  557.4 11.2 %spread_feed.1 = (f32[2048,1024]{1,0:T(8,128)}, f32[1024,2048]{1,0:T(8,128)}) custom-call(bf16[16,1024,512]{2,1,0:T(8,128)(2,1)} %bitcast.98), custom_call_target="tpu_custom_call" | custom-call | bytes 25165824 | tf_op jit(solution)/shard_map/spread_feed/pallas_call | solution.py:1202
  569.2 1.3 copy.39
  570.5 1.3 copy.40
  (186 shorter events, 21.1 us)
Async XLA Ops:
  2.8 6.0 %copy-start.47 = (bf16[1024,1024]{1,0:T(8,128)(2,1)S(1)}, bf16[1024,1024]{1,0:T(8,128)(2,1)}, u32[]{:S(2)}) copy-start(bf16[1024,1024]{1,0:T(8,128)(2,1)} %x_ref.1) | copy-start | bytes 6291460
  2.8 6.1 %copy-start.56 = (bf16[3,1024,512]{2,1,0:T(8,128)(2,1)S(1)}, bf16[3,1024,512]{2,1,0:T(8,128)(2,1)}, u32[]{:S(2)}) copy-start(bf16[3,1024,512]{2,1,0:T(8,128)(2,1)} %refs_48_.1) | copy-start | bytes 9437188
  2.8 32.2 %collective-permute-start = (bf16[3,256,512]{2,1,0:T(8,128)(2,1)}, bf16[3,256,512]{2,1,0:T(8,128)(2,1)S(1)}, u32[]{:S(2)}, u32[]{:S(2)}) collective-permute-start(bf16[3,256,512]{2,1,0:T(8,128)(2,1)} %constant_dynamic-slice_fusion), channel_id=1, source_target_pairs={{0,1},{1,0},{2,3},{3,2},{4,5},{5,4},{6,7},{7,6},{8,9},{9,8},{10,11... | collective-permute-start | bytes 2359304 | tf_op jit(solution)/shard_map/ppermute | solution.py:988
  8.8 10.8 %copy-start.26 = (bf16[1024,512]{1,0:T(8,128)(2,1)}, bf16[1024,512]{1,0:T(8,128)(2,1)S(1)}, u32[]{:S(2)}) copy-start(bf16[1024,512]{1,0:T(8,128)(2,1)S(1)} %convolution_convert_fusion.9.v_ref.refs_13_) | copy-start | bytes 3145732
  10.1 9.6 %copy-start.27 = (bf16[1024,512]{1,0:T(8,128)(2,1)}, bf16[1024,512]{1,0:T(8,128)(2,1)S(1)}, u32[]{:S(2)}) copy-start(bf16[1024,512]{1,0:T(8,128)(2,1)S(1)} %convolution_convert_fusion.10.k_ref.refs_12_) | copy-start | bytes 3145732
  10.1 6.7 %copy-start.61 = (s32[2]{0:T(128)S(1)}, s32[2]{0:T(128)}, u32[]{:S(2)}) copy-start(s32[2]{0:T(128)} %param.15) | copy-start | bytes 28
  36.0 32.8 %collective-permute-start.2 = (bf16[3,256,512]{2,1,0:T(8,128)(2,1)S(1)}, bf16[3,256,512]{2,1,0:T(8,128)(2,1)S(1)}, u32[]{:S(2)}, u32[]{:S(2)}) collective-permute-start(bf16[3,256,512]{2,1,0:T(8,128)(2,1)S(1)} %collective-permute-done.refs_0_), channel_id=1, source_target_pairs={{0,2},{1,3},{2,0},{3,1},{4,6},{5,7},{6,4},{7,5},{8,10},{9,11},{10,... | collective-permute-start | bytes 2359304 | tf_op jit(solution)/shard_map/ppermute | solution.py:988
  36.0 33.6 %collective-permute-start.1 = (bf16[3,256,512]{2,1,0:T(8,128)(2,1)S(1)}, bf16[3,256,512]{2,1,0:T(8,128)(2,1)S(1)}, u32[]{:S(2)}, u32[]{:S(2)}) collective-permute-start(bf16[3,256,512]{2,1,0:T(8,128)(2,1)S(1)} %collective-permute-done.refs_0_), channel_id=1, source_target_pairs={{0,4},{1,5},{2,6},{3,7},{4,0},{5,1},{6,2},{7,3},{8,12},{9,13},{10,... | collective-permute-start | bytes 2359304 | tf_op jit(solution)/shard_map/ppermute | solution.py:988
  43.4 25.3 %collective-permute-start.5 = (bf16[2,256,512]{2,1,0:T(8,128)(2,1)S(1)}, bf16[2,256,512]{2,1,0:T(8,128)(2,1)S(1)}, u32[]{:S(2)}, u32[]{:S(2)}) collective-permute-start(bf16[2,256,512]{2,1,0:T(8,128)(2,1)S(1)} %constant_dynamic-slice_fusion.1), channel_id=1, source_target_pairs={{0,1},{1,0},{2,3},{3,2},{4,5},{5,4},{6,7},{7,6},{8,9},{9,8},{10,11... | collective-permute-start | bytes 1572872 | tf_op jit(solution)/shard_map/ppermute | solution.py:988
  52.4 17.3 %copy-start.59 = (f32[3,1024]{1,0:T(4,128)S(1)}, f32[3,1024]{1,0:T(4,128)}, u32[]{:S(2)}) copy-start(f32[3,1024]{1,0:T(4,128)} %param.25) | copy-start | bytes 36868
  52.4 11.5 %collective-permute-start.3 = (bf16[1,128,1024]{2,1,0:T(8,128)(2,1)}, bf16[1,128,1024]{2,1,0:T(8,128)(2,1)S(1)}, u32[]{:S(2)}, u32[]{:S(2)}) collective-permute-start(bf16[1,128,1024]{2,1,0:T(8,128)(2,1)} %dynamic-slice_bitcast_fusion.4), channel_id=1, source_target_pairs={{0,1},{1,0},{2,3},{3,2},{4,5},{5,4},{6,7},{7,6},{8,9},{9,8},{10,11... | collective-permute-start | bytes 786440 | tf_op jit(solution)/shard_map/ppermute | solution.py:988
  53.7 15.0 %collective-permute-start.4 = (bf16[1,256,512]{2,1,0:T(8,128)(2,1)}, bf16[1,256,512]{2,1,0:T(8,128)(2,1)S(1)}, u32[]{:S(2)}, u32[]{:S(2)}) collective-permute-start(bf16[1,256,512]{2,1,0:T(8,128)(2,1)} %dynamic-slice_bitcast_fusion.3), channel_id=1, source_target_pairs={{0,1},{1,0},{2,3},{3,2},{4,5},{5,4},{6,7},{7,6},{8,9},{9,8},{10,11... | collective-permute-start | bytes 786440 | tf_op jit(solution)/shard_map/ppermute | solution.py:988
  63.8 5.8 %copy-start.20 = (bf16[1,128,1024]{2,1,0:T(8,128)(2,1)}, bf16[1,128,1024]{2,1,0:T(8,128)(2,1)S(1)}, u32[]{:S(2)}) copy-start(bf16[1,128,1024]{2,1,0:T(8,128)(2,1)S(1)} %collective-permute-done.3.refs_0_) | copy-start | bytes 786436
  69.6 6.3 %collective-permute-start.6 = (bf16[3,256,512]{2,1,0:T(8,128)(2,1)S(1)}, bf16[3,256,512]{2,1,0:T(8,128)(2,1)S(1)}, u32[]{:S(2)}, u32[]{:S(2)}) collective-permute-start(bf16[3,256,512]{2,1,0:T(8,128)(2,1)S(1)} %collective-permute-done.1.refs_1_), channel_id=1, source_target_pairs={{0,2},{1,3},{2,0},{3,1},{4,6},{5,7},{6,4},{7,5},{8,10},{9,11},{10,... | collective-permute-start | bytes 2359304 | tf_op jit(solution)/shard_map/ppermute | solution.py:988
  69.7 5.6 copy-start.21
  69.7 6.1 %copy-start.17 = (bf16[2,256,512]{2,1,0:T(8,128)(2,1)S(1)}, bf16[2,256,512]{2,1,0:T(8,128)(2,1)}, u32[]{:S(2)}) copy-start(bf16[2,256,512]{2,1,0:T(8,128)(2,1)} %copy-done.16) | copy-start | bytes 1572868
  74.6 8.7 %collective-permute-start.13 = (bf16[1,128,1024]{2,1,0:T(8,128)(2,1)S(1)}, bf16[1,128,1024]{2,1,0:T(8,128)(2,1)S(1)}, u32[]{:S(2)}, u32[]{:S(2)}) collective-permute-start(bf16[1,128,1024]{2,1,0:T(8,128)(2,1)S(1)} %copy-done.55), channel_id=1, source_target_pairs={{0,1},{1,0},{2,3},{3,2},{4,5},{5,4},{6,7},{7,6},{8,9},{9,8},{10,11... | collective-permute-start | bytes 786440 | tf_op jit(solution)/shard_map/ppermute | solution.py:988
  75.4 8.0 %collective-permute-start.8 = (bf16[1,128,1024]{2,1,0:T(8,128)(2,1)S(1)}, bf16[1,128,1024]{2,1,0:T(8,128)(2,1)S(1)}, u32[]{:S(2)}, u32[]{:S(2)}) collective-permute-start(bf16[1,128,1024]{2,1,0:T(8,128)(2,1)S(1)} %copy-done.21), channel_id=1, source_target_pairs={{0,2},{1,3},{2,0},{3,1},{4,6},{5,7},{6,4},{7,5},{8,10},{9,11},{10,... | collective-permute-start | bytes 786440 | tf_op jit(solution)/shard_map/ppermute | solution.py:988
  75.6 21.5 %collective-permute-start.7 = (bf16[1,128,1024]{2,1,0:T(8,128)(2,1)S(1)}, bf16[1,128,1024]{2,1,0:T(8,128)(2,1)S(1)}, u32[]{:S(2)}, u32[]{:S(2)}) collective-permute-start(bf16[1,128,1024]{2,1,0:T(8,128)(2,1)S(1)} %copy-done.21), channel_id=1, source_target_pairs={{0,4},{1,5},{2,6},{3,7},{4,0},{5,1},{6,2},{7,3},{8,12},{9,13},{10,... | collective-permute-start | bytes 786440 | tf_op jit(solution)/shard_map/ppermute | solution.py:988
  75.9 25.1 %collective-permute-start.12 = (bf16[2,256,512]{2,1,0:T(8,128)(2,1)S(1)}, bf16[2,256,512]{2,1,0:T(8,128)(2,1)S(1)}, u32[]{:S(2)}, u32[]{:S(2)}) collective-permute-start(bf16[2,256,512]{2,1,0:T(8,128)(2,1)S(1)} %copy-done.17), channel_id=1, source_target_pairs={{0,2},{1,3},{2,0},{3,1},{4,6},{5,7},{6,4},{7,5},{8,10},{9,11},{10,... | collective-permute-start | bytes 1572872 | tf_op jit(solution)/shard_map/ppermute | solution.py:988
  75.9 25.1 %collective-permute-start.11 = (bf16[2,256,512]{2,1,0:T(8,128)(2,1)S(1)}, bf16[2,256,512]{2,1,0:T(8,128)(2,1)S(1)}, u32[]{:S(2)}, u32[]{:S(2)}) collective-permute-start(bf16[2,256,512]{2,1,0:T(8,128)(2,1)S(1)} %copy-done.17), channel_id=1, source_target_pairs={{0,4},{1,5},{2,6},{3,7},{4,0},{5,1},{6,2},{7,3},{8,12},{9,13},{10,... | collective-permute-start | bytes 1572872 | tf_op jit(solution)/shard_map/ppermute | solution.py:988
  82.0 15.0 %copy-start.33 = (bf16[1024,512]{1,0:T(8,128)(2,1)}, bf16[1024,512]{1,0:T(8,128)(2,1)S(1)}, u32[]{:S(2)}) copy-start(bf16[1024,512]{1,0:T(8,128)(2,1)S(1)} %convolution_convert_fusion.6.q_ref.refs_16_) | copy-start | bytes 3145732
  82.0 21.2 %copy-start.60 = (f32[3,1024]{1,0:T(4,128)S(1)}, f32[3,1024]{1,0:T(4,128)}, u32[]{:S(2)}) copy-start(f32[3,1024]{1,0:T(4,128)} %refs_23_.1) | copy-start | bytes 36868
  82.1 22.0 %copy-start.54 = (bf16[1,256,2048]{2,1,0:T(8,128)(2,1)S(1)}, bf16[1,256,2048]{2,1,0:T(8,128)(2,1)}, u32[]{:S(2)}) copy-start(bf16[1,256,2048]{2,1,0:T(8,128)(2,1)} %dynamic-slice_bitcast_fusion.1) | copy-start | bytes 3145732
  83.3 13.7 %collective-permute-start.10 = (bf16[1,256,512]{2,1,0:T(8,128)(2,1)S(1)}, bf16[1,256,512]{2,1,0:T(8,128)(2,1)S(1)}, u32[]{:S(2)}, u32[]{:S(2)}) collective-permute-start(bf16[1,256,512]{2,1,0:T(8,128)(2,1)S(1)} %copy-done.19), channel_id=1, source_target_pairs={{0,2},{1,3},{2,0},{3,1},{4,6},{5,7},{6,4},{7,5},{8,10},{9,11},{10,... | collective-permute-start | bytes 786440 | tf_op jit(solution)/shard_map/ppermute | solution.py:988
  83.3 17.6 %collective-permute-start.9 = (bf16[1,256,512]{2,1,0:T(8,128)(2,1)S(1)}, bf16[1,256,512]{2,1,0:T(8,128)(2,1)S(1)}, u32[]{:S(2)}, u32[]{:S(2)}) collective-permute-start(bf16[1,256,512]{2,1,0:T(8,128)(2,1)S(1)} %copy-done.19), channel_id=1, source_target_pairs={{0,4},{1,5},{2,6},{3,7},{4,0},{5,1},{6,2},{7,3},{8,12},{9,13},{10,... | collective-permute-start | bytes 786440 | tf_op jit(solution)/shard_map/ppermute | solution.py:988
  97.0 13.4 %copy-start.7 = (bf16[1024,512]{1,0:T(8,128)(2,1)}, bf16[1024,512]{1,0:T(8,128)(2,1)S(1)}, u32[]{:S(2)}) copy-start(bf16[1024,512]{1,0:T(8,128)(2,1)S(1)} %get-tuple-element.104.refs_19_) | copy-start | bytes 3145732
  97.0 13.4 %copy-start.39 = (bf16[1024,512]{1,0:T(8,128)(2,1)}, bf16[1024,512]{1,0:T(8,128)(2,1)S(1)}, u32[]{:S(2)}) copy-start(bf16[1024,512]{1,0:T(8,128)(2,1)S(1)} %get-tuple-element.139.refs_20_) | copy-start | bytes 3145732
  101.0 4.6 collective-permute-start.14
  103.2 17.5 %collective-permute-start.17 = (bf16[1,128,1024]{2,1,0:T(8,128)(2,1)S(1)}, bf16[1,128,1024]{2,1,0:T(8,128)(2,1)S(1)}, u32[]{:S(2)}, u32[]{:S(2)}) collective-permute-start(bf16[1,128,1024]{2,1,0:T(8,128)(2,1)S(1)} %collective-permute-done.13.refs_0_), channel_id=1, source_target_pairs={{0,2},{1,3},{2,0},{3,1},{4,6},{5,7},{6,4},{7,5},{8,10},{9,11},{10,... | collective-permute-start | bytes 786440 | tf_op jit(solution)/shard_map/ppermute | solution.py:988
  103.8 16.9 %collective-permute-start.16 = (bf16[1,128,1024]{2,1,0:T(8,128)(2,1)S(1)}, bf16[1,128,1024]{2,1,0:T(8,128)(2,1)}, u32[]{:S(2)}, u32[]{:S(2)}) collective-permute-start(bf16[1,128,1024]{2,1,0:T(8,128)(2,1)S(1)} %collective-permute-done.13.refs_0_), channel_id=1, source_target_pairs={{0,4},{1,5},{2,6},{3,7},{4,0},{5,1},{6,2},{7,3},{8,12},{9,13},{10,... | collective-permute-start | bytes 786440 | tf_op jit(solution)/shard_map/ppermute | solution.py:988
  104.1 24.9 %collective-permute-start.18 = (bf16[1,256,2048]{2,1,0:T(8,128)(2,1)S(1)}, bf16[1,256,2048]{2,1,0:T(8,128)(2,1)S(1)}, u32[]{:S(2)}, u32[]{:S(2)}) collective-permute-start(bf16[1,256,2048]{2,1,0:T(8,128)(2,1)S(1)} %copy-done.54), channel_id=1, source_target_pairs={{0,1},{1,0},{2,3},{3,2},{4,5},{5,4},{6,7},{7,6},{8,9},{9,8},{10,11... | collective-permute-start | bytes 3145736 | tf_op jit(solution)/shard_map/ppermute | solution.py:988
  105.6 8.8 %collective-permute-start.19 = (bf16[1,256,512]{2,1,0:T(8,128)(2,1)S(1)}, bf16[1,256,512]{2,1,0:T(8,128)(2,1)S(1)}, u32[]{:S(2)}, u32[]{:S(2)}) collective-permute-start(bf16[1,256,512]{2,1,0:T(8,128)(2,1)S(1)} %collective-permute-done.9.refs_1_), channel_id=1, source_target_pairs={{0,2},{1,3},{2,0},{3,1},{4,6},{5,7},{6,4},{7,5},{8,10},{9,11},{10,... | collective-permute-start | bytes 786440 | tf_op jit(solution)/shard_map/ppermute | solution.py:988
  105.6 11.3 %collective-permute-start.15 = (bf16[2,256,512]{2,1,0:T(8,128)(2,1)S(1)}, bf16[2,256,512]{2,1,0:T(8,128)(2,1)S(1)}, u32[]{:S(2)}, u32[]{:S(2)}) collective-permute-start(bf16[2,256,512]{2,1,0:T(8,128)(2,1)S(1)} %collective-permute-done.11.refs_1_), channel_id=1, source_target_pairs={{0,2},{1,3},{2,0},{3,1},{4,6},{5,7},{6,4},{7,5},{8,10},{9,11},{10,... | collective-permute-start | bytes 1572872 | tf_op jit(solution)/shard_map/ppermute | solution.py:988
  114.3 19.9 %copy-start.34 = (bf16[1024,512]{1,0:T(8,128)(2,1)}, bf16[1024,512]{1,0:T(8,128)(2,1)S(1)}, u32[]{:S(2)}) copy-start(bf16[1024,512]{1,0:T(8,128)(2,1)S(1)} %convolution_convert_fusion.3.q_ref.refs_1_) | copy-start | bytes 3145732
  118.5 13.5 %copy-start.6 = (bf16[2,1024,512]{2,1,0:T(8,128)(2,1)}, bf16[2,1024,512]{2,1,0:T(8,128)(2,1)S(1)}, u32[]{:S(2)}) copy-start(bf16[2,1024,512]{2,1,0:T(8,128)(2,1)S(1)} %arrange.9.refs_47_) | copy-start | bytes 6291460
  120.7 13.5 %copy-start.29 = (bf16[1024,512]{1,0:T(8,128)(2,1)S(1)}, bf16[1024,512]{1,0:T(8,128)(2,1)}, u32[]{:S(2)}) copy-start(bf16[1024,512]{1,0:T(8,128)(2,1)} %convolution_convert_fusion.8.k_ref.refs_2_) | copy-start | bytes 3145732
  120.7 13.5 %copy-start.30 = (bf16[1024,512]{1,0:T(8,128)(2,1)S(1)}, bf16[1024,512]{1,0:T(8,128)(2,1)}, u32[]{:S(2)}) copy-start(bf16[1024,512]{1,0:T(8,128)(2,1)} %convolution_convert_fusion.7.v_ref.refs_3_) | copy-start | bytes 3145732
  120.7 13.5 %copy-start.22 = (bf16[1,128,1024]{2,1,0:T(8,128)(2,1)}, bf16[1,128,1024]{2,1,0:T(8,128)(2,1)S(1)}, u32[]{:S(2)}) copy-start(bf16[1,128,1024]{2,1,0:T(8,128)(2,1)S(1)} %collective-permute-done.17.refs_2_) | copy-start | bytes 786436
  129.0 5.2 copy-start.8
  129.0 27.3 %collective-permute-start.21 = (bf16[1,256,2048]{2,1,0:T(8,128)(2,1)S(1)}, bf16[1,256,2048]{2,1,0:T(8,128)(2,1)S(1)}, u32[]{:S(2)}, u32[]{:S(2)}) collective-permute-start(bf16[1,256,2048]{2,1,0:T(8,128)(2,1)S(1)} %collective-permute-done.18.refs_0_), channel_id=1, source_target_pairs={{0,2},{1,3},{2,0},{3,1},{4,6},{5,7},{6,4},{7,5},{8,10},{9,11},{10,... | collective-permute-start | bytes 3145736 | tf_op jit(solution)/shard_map/ppermute | solution.py:988
  129.1 27.3 %collective-permute-start.20 = (bf16[1,256,2048]{2,1,0:T(8,128)(2,1)S(1)}, bf16[1,256,2048]{2,1,0:T(8,128)(2,1)S(1)}, u32[]{:S(2)}, u32[]{:S(2)}) collective-permute-start(bf16[1,256,2048]{2,1,0:T(8,128)(2,1)S(1)} %collective-permute-done.18.refs_0_), channel_id=1, source_target_pairs={{0,4},{1,5},{2,6},{3,7},{4,0},{5,1},{6,2},{7,3},{8,12},{9,13},{10,... | collective-permute-start | bytes 3145736 | tf_op jit(solution)/shard_map/ppermute | solution.py:988
  130.7 25.6 %collective-permute-start.22 = (bf16[1,512,1024]{2,1,0:T(8,128)(2,1)}, bf16[1,512,1024]{2,1,0:T(8,128)(2,1)}, u32[]{:S(2)}, u32[]{:S(2)}) collective-permute-start(bf16[1,512,1024]{2,1,0:T(8,128)(2,1)} %dynamic-slice_bitcast_fusion), channel_id=1, source_target_pairs={{0,1},{1,0},{2,3},{3,2},{4,5},{5,4},{6,7},{7,6},{8,9},{9,8},{10,11... | collective-permute-start | bytes 3145736 | tf_op jit(solution)/shard_map/ppermute | solution.py:988
  134.2 28.0 %collective-permute-start.25 = (bf16[1,128,1024]{2,1,0:T(8,128)(2,1)}, bf16[1,128,1024]{2,1,0:T(8,128)(2,1)}, u32[]{:S(2)}, u32[]{:S(2)}) collective-permute-start(bf16[1,128,1024]{2,1,0:T(8,128)(2,1)} %collective-permute-done.16.refs_1_), channel_id=1, source_target_pairs={{0,2},{1,3},{2,0},{3,1},{4,6},{5,7},{6,4},{7,5},{8,10},{9,11},{10,... | collective-permute-start | bytes 786440 | tf_op jit(solution)/shard_map/ppermute | solution.py:988
  156.0 6.2 %copy-start.23 = (bf16[1,128,1024]{2,1,0:T(8,128)(2,1)S(1)}, bf16[1,128,1024]{2,1,0:T(8,128)(2,1)}, u32[]{:S(2)}) copy-start(bf16[1,128,1024]{2,1,0:T(8,128)(2,1)} %copy-done.22) | copy-start | bytes 786436
  156.0 7.8 %copy-start.35 = (bf16[1024,512]{1,0:T(8,128)(2,1)S(1)}, bf16[1024,512]{1,0:T(8,128)(2,1)}, u32[]{:S(2)}) copy-start(bf16[1024,512]{1,0:T(8,128)(2,1)} %convolution_convert_fusion.2.q_ref.refs_6_) | copy-start | bytes 3145732
  156.0 7.8 %copy-start.36 = (bf16[1024,512]{1,0:T(8,128)(2,1)S(1)}, bf16[1024,512]{1,0:T(8,128)(2,1)}, u32[]{:S(2)}) copy-start(bf16[1024,512]{1,0:T(8,128)(2,1)} %fusion.6.k_ref.refs_7_) | copy-start | bytes 3145732
  156.0 7.8 %copy-start.37 = (bf16[1024,512]{1,0:T(8,128)(2,1)S(1)}, bf16[1024,512]{1,0:T(8,128)(2,1)}, u32[]{:S(2)}) copy-start(bf16[1024,512]{1,0:T(8,128)(2,1)} %fusion.7.v_ref.refs_8_) | copy-start | bytes 3145732
  156.3 5.9 %copy-start.11 = (bf16[1,256,2048]{2,1,0:T(8,128)(2,1)}, bf16[1,256,2048]{2,1,0:T(8,128)(2,1)S(1)}, u32[]{:S(2)}) copy-start(bf16[1,256,2048]{2,1,0:T(8,128)(2,1)S(1)} %collective-permute-done.21.refs_2_) | copy-start | bytes 3145732
  156.3 23.3 %collective-permute-start.24 = (bf16[1,512,1024]{2,1,0:T(8,128)(2,1)}, bf16[1,512,1024]{2,1,0:T(8,128)(2,1)S(1)}, u32[]{:S(2)}, u32[]{:S(2)}) collective-permute-start(bf16[1,512,1024]{2,1,0:T(8,128)(2,1)} %collective-permute-done.22.refs_0_), channel_id=1, source_target_pairs={{0,2},{1,3},{2,0},{3,1},{4,6},{5,7},{6,4},{7,5},{8,10},{9,11},{10,... | collective-permute-start | bytes 3145736 | tf_op jit(solution)/shard_map/ppermute | solution.py:988
  156.6 25.7 %collective-permute-start.23 = (bf16[1,512,1024]{2,1,0:T(8,128)(2,1)}, bf16[1,512,1024]{2,1,0:T(8,128)(2,1)}, u32[]{:S(2)}, u32[]{:S(2)}) collective-permute-start(bf16[1,512,1024]{2,1,0:T(8,128)(2,1)} %collective-permute-done.22.refs_0_), channel_id=1, source_target_pairs={{0,4},{1,5},{2,6},{3,7},{4,0},{5,1},{6,2},{7,3},{8,12},{9,13},{10,... | collective-permute-start | bytes 3145736 | tf_op jit(solution)/shard_map/ppermute | solution.py:988
  163.4 18.8 %copy-start.2 = (bf16[1,512,1024]{2,1,0:T(8,128)(2,1)}, bf16[1,512,1024]{2,1,0:T(8,128)(2,1)S(1)}, u32[]{:S(2)}) copy-start(bf16[1,512,1024]{2,1,0:T(8,128)(2,1)S(1)} %arrange.11) | copy-start | bytes 3145732
  163.5 18.8 %copy-start.43 = (f32[1024,1024]{1,0:T(8,128)S(1)}, f32[1024,1024]{1,0:T(8,128)}, u32[]{:S(2)}) copy-start(f32[1024,1024]{1,0:T(8,128)} %copy-done.42) | copy-start | bytes 12582916
  163.5 47.6 %collective-permute-start.26 = (bf16[1,256,2048]{2,1,0:T(8,128)(2,1)S(1)}, bf16[1,256,2048]{2,1,0:T(8,128)(2,1)}, u32[]{:S(2)}, u32[]{:S(2)}) collective-permute-start(bf16[1,256,2048]{2,1,0:T(8,128)(2,1)S(1)} %collective-permute-done.20.refs_1_), channel_id=1, source_target_pairs={{0,2},{1,3},{2,0},{3,1},{4,6},{5,7},{6,4},{7,5},{8,10},{9,11},{10,... | collective-permute-start | bytes 3145736 | tf_op jit(solution)/shard_map/ppermute | solution.py:988
  179.6 6.5 %copy-start.10 = (bf16[1024,512]{1,0:T(8,128)(2,1)}, bf16[1024,512]{1,0:T(8,128)(2,1)S(1)}, u32[]{:S(2)}) copy-start(bf16[1024,512]{1,0:T(8,128)(2,1)S(1)} %get-tuple-element.124.refs_9_) | copy-start | bytes 3145732
  179.6 6.5 %copy-start.41 = (bf16[1024,512]{1,0:T(8,128)(2,1)}, bf16[1024,512]{1,0:T(8,128)(2,1)S(1)}, u32[]{:S(2)}) copy-start(bf16[1024,512]{1,0:T(8,128)(2,1)S(1)} %get-tuple-element.137.refs_10_) | copy-start | bytes 3145732
  179.6 6.5 %copy-start.13 = (bf16[1,512,1024]{2,1,0:T(8,128)(2,1)}, bf16[1,512,1024]{2,1,0:T(8,128)(2,1)S(1)}, u32[]{:S(2)}) copy-start(bf16[1,512,1024]{2,1,0:T(8,128)(2,1)S(1)} %collective-permute-done.24.refs_2_) | copy-start | bytes 3145732
  182.3 32.5 %collective-permute-start.27 = (bf16[1,512,1024]{2,1,0:T(8,128)(2,1)}, bf16[1,512,1024]{2,1,0:T(8,128)(2,1)}, u32[]{:S(2)}, u32[]{:S(2)}) collective-permute-start(bf16[1,512,1024]{2,1,0:T(8,128)(2,1)} %collective-permute-done.23.refs_1_), channel_id=1, source_target_pairs={{0,2},{1,3},{2,0},{3,1},{4,6},{5,7},{6,4},{7,5},{8,10},{9,11},{10,... | collective-permute-start | bytes 3145736 | tf_op jit(solution)/shard_map/ppermute | solution.py:988
  194.5 16.5 %copy-start.9 = (bf16[1,256,2048]{2,1,0:T(8,128)(2,1)S(1)}, bf16[1,256,2048]{2,1,0:T(8,128)(2,1)}, u32[]{:S(2)}) copy-start(bf16[1,256,2048]{2,1,0:T(8,128)(2,1)} %copy-done.8) | copy-start | bytes 3145732
  194.5 16.5 %copy-start.12 = (bf16[1,256,2048]{2,1,0:T(8,128)(2,1)S(1)}, bf16[1,256,2048]{2,1,0:T(8,128)(2,1)}, u32[]{:S(2)}) copy-start(bf16[1,256,2048]{2,1,0:T(8,128)(2,1)} %copy-done.11) | copy-start | bytes 3145732
  219.1 16.4 %copy-start.45 = (f32[1024,1024]{1,0:T(8,128)S(1)}, f32[1024,1024]{1,0:T(8,128)}, u32[]{:S(2)}) copy-start(f32[1024,1024]{1,0:T(8,128)} %copy-done.44) | copy-start | bytes 12582916
  219.1 16.4 %copy-start.50 = (f32[1024,1024]{1,0:T(8,128)S(1)}, f32[1024,1024]{1,0:T(8,128)}, u32[]{:S(2)}) copy-start(f32[1024,1024]{1,0:T(8,128)} %get-tuple-element.127) | copy-start | bytes 12582916
  557.4 11.2 %copy-start.58 = (f32[8,1024]{1,0:T(8,128)S(1)}, f32[8,1024]{1,0:T(8,128)}, u32[]{:S(2)}) copy-start(f32[8,1024]{1,0:T(8,128)} %get-tuple-element.157) | copy-start | bytes 98308
  557.4 11.9 %copy-start.53 = (bf16[1024,1024]{1,0:T(8,128)(2,1)S(1)}, bf16[1024,1024]{1,0:T(8,128)(2,1)}, u32[]{:S(2)}) copy-start(bf16[1024,1024]{1,0:T(8,128)(2,1)} %get-tuple-element.193) | copy-start | bytes 6291460
  (26 other events, 59.3 us)

commit v6 on v5

--- a/solution.py
+++ b/solution.py
@@ -1240,8 +1240,7 @@
     so_s, cq_s, kv_s, co_s = [slab_of(x) for x in (so3, cq3, cross_kv, co3)]
     mem, so_s, cq_s, kv_s, _ = pipe.cut(memory, so_s, cq_s, kv_s, at1[0][0])
     pipe.put(fetch(got, "so", so_s, (1, 1)))
-    pipe.put(fetch(got, "cq", cq_s, (1, 1)))
-    pipe.put(fetch(got, "kv", kv_s, (1, 1)))
+    pipe.put(fetch(got, "kv", jnp.concatenate([kv_s, cq_s]), (1, 1)))
     kv = [[dot(mem, cross_kv[m]).astype(bf16) for m in range(2)], None]
     up_s, down_s = slab_of(ffn_up[None]), slab_of(ffn_down[None])
     target_t = flip(target)
@@ -1262,8 +1261,8 @@
     sum1 = alpha_res * target.astype(f32) + b1
     h1 = norm_rows(sum1, ln_gain[0], ln_bias[0])
     h1_low = h1.astype(bf16)
-    cq_oth = arrange(got["cq"])[0]
     kv_oth = arrange(got["kv"])
+    cq_oth = kv_oth[2]
     q2 = [dot(h1_low, cross_query).astype(bf16), dot(h1_low, cq_oth).astype(bf16)]
     kv[1] = [dot(memory, kv_oth[m]).astype(bf16) for m in range(2)]
     q2[0], kv[1][0], down_s = pipe.cut(q2[0], kv[1][0], down_s)

time: 577 us -> 570 us (0.988)
    ppermute x28 -> x24, waiting for transfers between devices: 26.7 us -> 22.6 us  [swap(): return lax.ppermute(x, ALL, [(i, i ^ flip) for i in range(DEVICES)])]
    unnamed x126 -> x124, local copies, waits for them, and re-layouts: 17.8 us -> 15.2 us
    ppermute x28 -> x24, starting transfers between devices: 17.7 us -> 15.8 us  [swap(): return lax.ppermute(x, ALL, [(i, i ^ flip) for i in range(DEVICES)])]
  transfers between devices with their start and end apart: 28 -> 24, of which waited for: 7 -> 5; matrix products, arithmetic and copies ran while one was open for 10% -> 11% of each run, Pallas kernels for 17% -> 17%
where the time goes in v6:
time: 570 us; the launch traced here: 566 us
  Pallas kernels  434 us (76%)
  matrix products  42.4 us (7%)
  local copies, waits for them, and re-layouts  31.7 us (6%)
  waiting for transfers between devices  22.6 us (4%)
  other arithmetic  17 us (3%)
  starting transfers between devices  15.8 us (3%)
    pallas_call x1, Pallas kernels, layer_back(): pl.pallas_call(back_kernel, grid=(3 * STEPS,), in_specs=[pl.BlockSpec(mem...  289 us
    pallas_call x4, Pallas kernels, attend_fwd(): pl.pallas_call(functools.partial(fwd_kernel, causal), grid=(width // 128,...  58 us
    dot_general x16, matrix products, dot(): return lax.dot_general(a, b, dims, preferred_element_type=f32)  42.4 us
    pallas_call x2, Pallas kernels, ffn_forward(): pl.pallas_call(ffn_kernel, grid=(seq // ROWS,), in_specs=[rows(width)] +...  32.9 us
    ppermute x24, waiting for transfers between devices, swap(): return lax.ppermute(x, ALL, [(i, i ^ flip) for i in range(DEVICES)])  22.6 us
    pallas_call x5, Pallas kernels, flip(): pl.pallas_call(flip_kernel, grid=(4,), in_specs=[pl.BlockSpec((rows // 4,...  20.7 us
    ppermute x24, starting transfers between devices, swap(): return lax.ppermute(x, ALL, [(i, i ^ flip) for i in range(DEVICES)])  15.8 us
    unnamed x124, local copies, waits for them, and re-layouts  15.2 us
  transfers between devices with their start and end apart: 24, of which 5 were waited for; matrix products, arithmetic and copies ran while one was open for 11% of the time, Pallas kernels for 17%

profile of v6, /device:TPU:0, one launch (start us, length us, event | category | flops | bytes accessed | tf_op | source)
XLA Modules:
  0.0 565.6 jit_solution(3168378492209113820)
XLA Ops:
  0.7 2.1 constant_dynamic-slice_fusion
  2.8 2.9 collective-permute-start
  5.7 3.1 convolution_convert_fusion.9.v_ref.refs_13_
  10.1 2.3 convolution_convert_fusion.11.q_ref.refs_11_
  12.4 1.7 dynamic-slice_bitcast_fusion.3
  14.0 1.9 constant_dynamic-slice_fusion.1
  15.9 1.7 dynamic-slice_bitcast_fusion.4
  18.1 2.3 dynamic-slice_bitcast_fusion.1
  21.7 13.2 %attend_causal.2 = (bf16[1024,512]{1,0:T(8,128)(2,1)S(1)}, bf16[1024,512]{1,0:T(8,128)(2,1)S(1)}) custom-call(s32[1]{0:T(128)} %dynamic_slice.24.len_ref.refs_0_, bf16[1024,512]{1,0:T(8,128)(2,1)S(1)} %copy-done.23, bf16[1024,512]{1,0:T(8,128)(2,1)S(1)} %convolution_convert_fusion.10.k_ref.refs_12_, ...), custom_call_target="tpu_custom_call" | custom-call | flops 5368709120 | bytes 8388608 | tf_op jit(solution)/shard_map/attend_causal/pallas_call | solution.py:422
  35.0 1.7 collective-permute-start.1
  38.3 1.7 dynamic-slice_bitcast_fusion.2
  40.0 4.2 flip.5.refs_38_
  44.2 1.3 collective-permute-start.3
  45.5 4.1 flip.6.refs_37_
  49.6 4.2 convolution_convert_fusion.8.k_ref.refs_2_
  53.8 2.2 convolution_convert_fusion.7.v_ref.refs_3_
  56.0 7.0 %collective-permute-done.3.refs_0_ = bf16[1,128,1024]{2,1,0:T(8,128)(2,1)S(1)} collective-permute-done((bf16[1,128,1024]{2,1,0:T(8,128)(2,1)}, bf16[1,128,1024]{2,1,0:T(8,128)(2,1)S(1)}, u32[]{:S(2)}, u32[]{:S(2)}) %collective-permute-start.3) | collective-permute-done | bytes 262176 | tf_op jit(solution)/shard_map/ppermute | solution.py:988
  63.2 4.8 fusion.28
  69.3 1.7 collective-permute-start.8
  71.0 1.7 arrange.6.refs_49_
  72.7 1.3 convolution_convert_fusion.4.v_ref.refs_18_
  74.0 1.2 convolution_convert_fusion.6.q_ref.refs_16_
  75.3 1.2 convolution_convert_fusion.5.k_ref.refs_17_
  76.6 13.3 %attend_causal.3 = (bf16[1024,512]{1,0:T(8,128)(2,1)S(1)}, bf16[1024,512]{1,0:T(8,128)(2,1)S(1)}) custom-call(s32[1]{0:T(128)} %dynamic_slice.24.len_ref.refs_0_, bf16[1024,512]{1,0:T(8,128)(2,1)S(1)} %convolution_convert_fusion.6.q_ref.refs_16_, bf16[1024,512]{1,0:T(8,128)(2,1)S(1)} %convolution_convert_fusion.5.k_ref.refs_17_, ...), custom_call_target="tpu_custom_call" | custom-call | flops 5368709120 | bytes 8388608 | tf_op jit(solution)/shard_map/attend_causal/pallas_call | solution.py:422
  90.0 4.3 collective-permute-done.8.refs_1_
  94.4 2.3 dynamic-slice_bitcast_fusion
  97.5 1.5 collective-permute-start.15
  99.2 4.2 fusion.26
  106.0 1.2 convolution_convert_fusion.3.q_ref.refs_1_
  107.9 1.4 copy-done.48
  109.3 2.2 fusion.7.v_ref.refs_8_
  111.5 2.2 fusion.6.k_ref.refs_7_
  113.7 2.2 convolution_convert_fusion.2.q_ref.refs_6_
  115.9 6.5 %collective-permute-done.15.refs_0_ = bf16[1,256,2048]{2,1,0:T(8,128)(2,1)S(1)} collective-permute-done((bf16[1,256,2048]{2,1,0:T(8,128)(2,1)S(1)}, bf16[1,256,2048]{2,1,0:T(8,128)(2,1)S(1)}, u32[]{:S(2)}, u32[]{:S(2)}) %collective-permute-start.15) | collective-permute-done | bytes 1048608 | tf_op jit(solution)/shard_map/ppermute | solution.py:988
  122.4 1.7 collective-permute-start.16
  124.1 1.3 collective-permute-start.18
  126.5 15.7 %attend_memory.2 = (bf16[1024,512]{1,0:T(8,128)(2,1)S(1)}, bf16[1024,512]{1,0:T(8,128)(2,1)S(1)}) custom-call(s32[1]{0:T(128)} %dynamic_slice.24.len_ref.refs_0_, bf16[1024,512]{1,0:T(8,128)(2,1)S(1)} %convolution_convert_fusion.3.q_ref.refs_1_, bf16[1024,512]{1,0:T(8,128)(2,1)S(1)} %copy-done.24, bf16[1024,512]{1,0:T(8,128)(2,1)S(1)} %copy-done.25), custom_call_target="tpu_custom_call" | custom-call | flops 8589934592 | bytes 8388608 | tf_op jit(solution)/shard_map/attend_memory/pallas_call | solution.py:422
  144.2 4.1 flip.7.refs_36_
  148.3 1.4 collective-permute-done.18.refs_0_
  150.2 4.8 fusion.29
  155.1 1.2 arrange.9
  156.6 15.8 %attend_memory.3 = (bf16[1024,512]{1,0:T(8,128)(2,1)S(1)}, bf16[1024,512]{1,0:T(8,128)(2,1)S(1)}) custom-call(s32[1]{0:T(128)} %dynamic_slice.24.len_ref.refs_0_, bf16[1024,512]{1,0:T(8,128)(2,1)S(1)} %copy-done.32, bf16[1024,512]{1,0:T(8,128)(2,1)S(1)} %copy-done.31, bf16[1024,512]{1,0:T(8,128)(2,1)S(1)} %copy-done.30), custom_call_target="tpu_custom_call" | custom-call | flops 8589934592 | bytes 8388608 | tf_op jit(solution)/shard_map/attend_memory/pallas_call | solution.py:422
  172.4 3.3 collective-permute-done.19.refs_1_
  175.7 3.9 fusion.27
  180.2 1.5 copy-done.39
  181.7 2.0 fusion.5.h_ref.x_ref
  183.7 4.2 flip.8.refs_35_
  188.0 16.5 %feed_forward.2 = (bf16[1024,2048]{1,0:T(8,128)(2,1)}, bf16[1024,2048]{1,0:T(8,128)(2,1)}, f32[1024,1024]{1,0:T(8,128)}) custom-call(bf16[1024,1024]{1,0:T(8,128)(2,1)S(1)} %copy-done, bf16[1024,2048]{1,0:T(8,128)(2,1)} %refs_27_.1, bf16[2048,1024]{1,0:T(8,128)(2,1)} %refs_28_.1), custom_call_target="tpu_custom_call" | custom-call | flops 8589934592 | bytes 23068672 | tf_op jit(solution)/shard_map/feed_forward/pallas_call | solution.py:1096
  204.5 1.7 arrange.10
  206.2 2.0 copy-done.4
  208.2 2.3 arrange.11
  210.5 2.0 copy-done.5
  212.5 16.5 %feed_forward.3 = (bf16[1024,2048]{1,0:T(8,128)(2,1)}, bf16[1024,2048]{1,0:T(8,128)(2,1)}, f32[1024,1024]{1,0:T(8,128)}) custom-call(bf16[1024,1024]{1,0:T(8,128)(2,1)S(1)} %copy-done, bf16[1024,2048]{1,0:T(8,128)(2,1)} %bitcast.91, bf16[2048,1024]{1,0:T(8,128)(2,1)} %bitcast.93), custom_call_target="tpu_custom_call" | custom-call | flops 8589934592 | bytes 23068672 | tf_op jit(solution)/shard_map/feed_forward/pallas_call | solution.py:1096
  229.0 3.3 fusion.22
  233.9 2.0 fusion.2
  235.9 3.2 fusion.21
  239.1 3.2 add_multiply_fusion
  242.2 4.1 flip.9.refs_34_
  247.0 289.1 %layer_back.1 = (bf16[1024,1024]{1,0:T(8,128)(2,1)}, bf16[1024,1024]{1,0:T(8,128)(2,1)}, bf16[16,2,2,4,64,512]{5,4,3,2,1,0:T(8,128)(2,1)}, bf16[16,2,2,2,4,64,512]{6,5,4,3,2,1,0:T(8,128)(2,1)}, f32[8,1024]{1,0:T(8,128)}) custom-call(s32[1]{0:T(128)} %dynamic_slice.24.len_ref.refs_0_, bf16[1024,512]{1,0:T(8,128)(2,1)} %copy-done.29, ...), custom_call_target="tpu_custom_call" | custom-call | flops 137438953472 | bytes 16777216 | tf_op jit(solution)/shard_map/layer_back/pallas_call | solution.py:941
  536.1 7.3 %spread.3 = (f32[1,1024,512]{2,1,0:T(8,128)}, f32[2,1024,512]{2,1,0:T(8,128)}, f32[512,1024]{1,0:T(8,128)}) custom-call(bf16[16,1024,512]{2,1,0:T(8,128)(2,1)} %bitcast.95), custom_call_target="tpu_custom_call" | custom-call | bytes 12582912 | tf_op jit(solution)/shard_map/spread/pallas_call | solution.py:1159
  543.5 7.4 %spread.2 = (f32[3,1024,512]{2,1,0:T(8,128)}, f32[512,1024]{1,0:T(8,128)}) custom-call(bf16[16,1024,512]{2,1,0:T(8,128)(2,1)} %bitcast.96), custom_call_target="tpu_custom_call" | custom-call | bytes 12582912 | tf_op jit(solution)/shard_map/spread/pallas_call | solution.py:1159
  550.9 11.2 %spread_feed.1 = (f32[2048,1024]{1,0:T(8,128)}, f32[1024,2048]{1,0:T(8,128)}) custom-call(bf16[16,1024,512]{2,1,0:T(8,128)(2,1)} %bitcast.97), custom_call_target="tpu_custom_call" | custom-call | bytes 25165824 | tf_op jit(solution)/shard_map/spread_feed/pallas_call | solution.py:1202
  562.7 1.3 copy.39
  564.0 1.3 copy.40
  (177 shorter events, 17.8 us)
Async XLA Ops:
  2.8 6.0 %copy-start.42 = (bf16[1024,1024]{1,0:T(8,128)(2,1)S(1)}, bf16[1024,1024]{1,0:T(8,128)(2,1)}, u32[]{:S(2)}) copy-start(bf16[1024,1024]{1,0:T(8,128)(2,1)} %x_ref.1) | copy-start | bytes 6291460
  2.8 6.1 %copy-start.54 = (bf16[3,1024,512]{2,1,0:T(8,128)(2,1)S(1)}, bf16[3,1024,512]{2,1,0:T(8,128)(2,1)}, u32[]{:S(2)}) copy-start(bf16[3,1024,512]{2,1,0:T(8,128)(2,1)} %refs_48_.1) | copy-start | bytes 9437188
  2.8 32.1 %collective-permute-start = (bf16[3,256,512]{2,1,0:T(8,128)(2,1)}, bf16[3,256,512]{2,1,0:T(8,128)(2,1)S(1)}, u32[]{:S(2)}, u32[]{:S(2)}) collective-permute-start(bf16[3,256,512]{2,1,0:T(8,128)(2,1)} %constant_dynamic-slice_fusion), channel_id=1, source_target_pairs={{0,1},{1,0},{2,3},{3,2},{4,5},{5,4},{6,7},{7,6},{8,9},{9,8},{10,11... | collective-permute-start | bytes 2359304 | tf_op jit(solution)/shard_map/ppermute | solution.py:988
  8.8 11.6 %copy-start.21 = (bf16[1024,512]{1,0:T(8,128)(2,1)}, bf16[1024,512]{1,0:T(8,128)(2,1)S(1)}, u32[]{:S(2)}) copy-start(bf16[1024,512]{1,0:T(8,128)(2,1)S(1)} %convolution_convert_fusion.9.v_ref.refs_13_) | copy-start | bytes 3145732
  10.1 10.4 %copy-start.22 = (bf16[1024,512]{1,0:T(8,128)(2,1)}, bf16[1024,512]{1,0:T(8,128)(2,1)S(1)}, u32[]{:S(2)}) copy-start(bf16[1024,512]{1,0:T(8,128)(2,1)S(1)} %convolution_convert_fusion.10.k_ref.refs_12_) | copy-start | bytes 3145732
  10.1 7.5 %copy-start.60 = (s32[2]{0:T(128)S(1)}, s32[2]{0:T(128)}, u32[]{:S(2)}) copy-start(s32[2]{0:T(128)} %param.15) | copy-start | bytes 28
  21.7 15.0 %copy-start.46 = (bf16[2,256,512]{2,1,0:T(8,128)(2,1)S(1)}, bf16[2,256,512]{2,1,0:T(8,128)(2,1)}, u32[]{:S(2)}) copy-start(bf16[2,256,512]{2,1,0:T(8,128)(2,1)} %constant_dynamic-slice_fusion.1) | copy-start | bytes 1572868
  21.7 15.0 %copy-start.52 = (bf16[1,256,512]{2,1,0:T(8,128)(2,1)S(1)}, bf16[1,256,512]{2,1,0:T(8,128)(2,1)}, u32[]{:S(2)}) copy-start(bf16[1,256,512]{2,1,0:T(8,128)(2,1)} %dynamic-slice_bitcast_fusion.3) | copy-start | bytes 786436
  34.9 28.1 %collective-permute-start.2 = (bf16[3,256,512]{2,1,0:T(8,128)(2,1)S(1)}, bf16[3,256,512]{2,1,0:T(8,128)(2,1)S(1)}, u32[]{:S(2)}, u32[]{:S(2)}) collective-permute-start(bf16[3,256,512]{2,1,0:T(8,128)(2,1)S(1)} %collective-permute-done.refs_0_), channel_id=1, source_target_pairs={{0,2},{1,3},{2,0},{3,1},{4,6},{5,7},{6,4},{7,5},{8,10},{9,11},{10,... | collective-permute-start | bytes 2359304 | tf_op jit(solution)/shard_map/ppermute | solution.py:988
  35.0 28.1 %collective-permute-start.1 = (bf16[3,256,512]{2,1,0:T(8,128)(2,1)S(1)}, bf16[3,256,512]{2,1,0:T(8,128)(2,1)S(1)}, u32[]{:S(2)}, u32[]{:S(2)}) collective-permute-start(bf16[3,256,512]{2,1,0:T(8,128)(2,1)S(1)} %collective-permute-done.refs_0_), channel_id=1, source_target_pairs={{0,4},{1,5},{2,6},{3,7},{4,0},{5,1},{6,2},{7,3},{8,12},{9,13},{10,... | collective-permute-start | bytes 2359304 | tf_op jit(solution)/shard_map/ppermute | solution.py:988
  37.6 25.4 %collective-permute-start.4 = (bf16[3,256,512]{2,1,0:T(8,128)(2,1)}, bf16[3,256,512]{2,1,0:T(8,128)(2,1)S(1)}, u32[]{:S(2)}, u32[]{:S(2)}) collective-permute-start(bf16[3,256,512]{2,1,0:T(8,128)(2,1)} %pad_maximum_fusion), channel_id=1, source_target_pairs={{0,1},{1,0},{2,3},{3,2},{4,5},{5,4},{6,7},{7,6},{8,9},{9,8},{10,11... | collective-permute-start | bytes 2359304 | tf_op jit(solution)/shard_map/ppermute | solution.py:988
  44.2 18.9 %collective-permute-start.3 = (bf16[1,128,1024]{2,1,0:T(8,128)(2,1)}, bf16[1,128,1024]{2,1,0:T(8,128)(2,1)S(1)}, u32[]{:S(2)}, u32[]{:S(2)}) collective-permute-start(bf16[1,128,1024]{2,1,0:T(8,128)(2,1)} %dynamic-slice_bitcast_fusion.4), channel_id=1, source_target_pairs={{0,1},{1,0},{2,3},{3,2},{4,5},{5,4},{6,7},{7,6},{8,9},{9,8},{10,11... | collective-permute-start | bytes 786440 | tf_op jit(solution)/shard_map/ppermute | solution.py:988
  53.8 9.3 %copy-start.58 = (f32[3,1024]{1,0:T(4,128)S(1)}, f32[3,1024]{1,0:T(4,128)}, u32[]{:S(2)}) copy-start(f32[3,1024]{1,0:T(4,128)} %param.25) | copy-start | bytes 36868
  63.0 5.9 %copy-start.17 = (bf16[1,128,1024]{2,1,0:T(8,128)(2,1)}, bf16[1,128,1024]{2,1,0:T(8,128)(2,1)S(1)}, u32[]{:S(2)}) copy-start(bf16[1,128,1024]{2,1,0:T(8,128)(2,1)S(1)} %collective-permute-done.3.refs_0_) | copy-start | bytes 786436
  63.1 6.2 %collective-permute-start.5 = (bf16[3,256,512]{2,1,0:T(8,128)(2,1)S(1)}, bf16[3,256,512]{2,1,0:T(8,128)(2,1)}, u32[]{:S(2)}, u32[]{:S(2)}) collective-permute-start(bf16[3,256,512]{2,1,0:T(8,128)(2,1)S(1)} %collective-permute-done.1.refs_1_), channel_id=1, source_target_pairs={{0,2},{1,3},{2,0},{3,1},{4,6},{5,7},{6,4},{7,5},{8,10},{9,11},{10,... | collective-permute-start | bytes 2359304 | tf_op jit(solution)/shard_map/ppermute | solution.py:988
  63.2 4.9 copy-start.53
  68.1 4.7 copy-start.43
  68.1 21.9 %collective-permute-start.10 = (bf16[1,128,1024]{2,1,0:T(8,128)(2,1)S(1)}, bf16[1,128,1024]{2,1,0:T(8,128)(2,1)S(1)}, u32[]{:S(2)}, u32[]{:S(2)}) collective-permute-start(bf16[1,128,1024]{2,1,0:T(8,128)(2,1)S(1)} %copy-done.53), channel_id=1, source_target_pairs={{0,1},{1,0},{2,3},{3,2},{4,5},{5,4},{6,7},{7,6},{8,9},{9,8},{10,11... | collective-permute-start | bytes 786440 | tf_op jit(solution)/shard_map/ppermute | solution.py:988
  68.8 21.2 %collective-permute-start.7 = (bf16[1,128,1024]{2,1,0:T(8,128)(2,1)S(1)}, bf16[1,128,1024]{2,1,0:T(8,128)(2,1)S(1)}, u32[]{:S(2)}, u32[]{:S(2)}) collective-permute-start(bf16[1,128,1024]{2,1,0:T(8,128)(2,1)S(1)} %collective-permute-done.3.refs_0_), channel_id=1, source_target_pairs={{0,2},{1,3},{2,0},{3,1},{4,6},{5,7},{6,4},{7,5},{8,10},{9,11},{10,... | collective-permute-start | bytes 786440 | tf_op jit(solution)/shard_map/ppermute | solution.py:988
  69.0 21.0 %collective-permute-start.6 = (bf16[1,128,1024]{2,1,0:T(8,128)(2,1)S(1)}, bf16[1,128,1024]{2,1,0:T(8,128)(2,1)S(1)}, u32[]{:S(2)}, u32[]{:S(2)}) collective-permute-start(bf16[1,128,1024]{2,1,0:T(8,128)(2,1)S(1)} %collective-permute-done.3.refs_0_), channel_id=1, source_target_pairs={{0,4},{1,5},{2,6},{3,7},{4,0},{5,1},{6,2},{7,3},{8,12},{9,13},{10,... | collective-permute-start | bytes 786440 | tf_op jit(solution)/shard_map/ppermute | solution.py:988
  69.3 20.8 %collective-permute-start.9 = (bf16[3,256,512]{2,1,0:T(8,128)(2,1)S(1)}, bf16[3,256,512]{2,1,0:T(8,128)(2,1)S(1)}, u32[]{:S(2)}, u32[]{:S(2)}) collective-permute-start(bf16[3,256,512]{2,1,0:T(8,128)(2,1)S(1)} %collective-permute-done.4.refs_0_), channel_id=1, source_target_pairs={{0,2},{1,3},{2,0},{3,1},{4,6},{5,7},{6,4},{7,5},{8,10},{9,11},{10,... | collective-permute-start | bytes 2359304 | tf_op jit(solution)/shard_map/ppermute | solution.py:988
  69.3 25.1 %collective-permute-start.8 = (bf16[3,256,512]{2,1,0:T(8,128)(2,1)S(1)}, bf16[3,256,512]{2,1,0:T(8,128)(2,1)S(1)}, u32[]{:S(2)}, u32[]{:S(2)}) collective-permute-start(bf16[3,256,512]{2,1,0:T(8,128)(2,1)S(1)} %collective-permute-done.4.refs_0_), channel_id=1, source_target_pairs={{0,4},{1,5},{2,6},{3,7},{4,0},{5,1},{6,2},{7,3},{8,12},{9,13},{10,... | collective-permute-start | bytes 2359304 | tf_op jit(solution)/shard_map/ppermute | solution.py:988
  76.6 13.4 %copy-start.28 = (bf16[1024,512]{1,0:T(8,128)(2,1)}, bf16[1024,512]{1,0:T(8,128)(2,1)S(1)}, u32[]{:S(2)}) copy-start(bf16[1024,512]{1,0:T(8,128)(2,1)S(1)} %convolution_convert_fusion.5.k_ref.refs_17_) | copy-start | bytes 3145732
  76.6 20.1 %copy-start.59 = (f32[3,1024]{1,0:T(4,128)S(1)}, f32[3,1024]{1,0:T(4,128)}, u32[]{:S(2)}) copy-start(f32[3,1024]{1,0:T(4,128)} %refs_23_.1) | copy-start | bytes 36868
  76.6 20.9 %copy-start.51 = (bf16[1,256,2048]{2,1,0:T(8,128)(2,1)S(1)}, bf16[1,256,2048]{2,1,0:T(8,128)(2,1)}, u32[]{:S(2)}) copy-start(bf16[1,256,2048]{2,1,0:T(8,128)(2,1)} %dynamic-slice_bitcast_fusion.1) | copy-start | bytes 3145732
  76.6 22.4 %copy-start.18 = (bf16[1,128,1024]{2,1,0:T(8,128)(2,1)S(1)}, bf16[1,128,1024]{2,1,0:T(8,128)(2,1)}, u32[]{:S(2)}) copy-start(bf16[1,128,1024]{2,1,0:T(8,128)(2,1)} %copy-done.17) | copy-start | bytes 786436
  90.0 13.4 %copy-start.7 = (bf16[1024,512]{1,0:T(8,128)(2,1)}, bf16[1024,512]{1,0:T(8,128)(2,1)S(1)}, u32[]{:S(2)}) copy-start(bf16[1024,512]{1,0:T(8,128)(2,1)S(1)} %get-tuple-element.100.refs_19_) | copy-start | bytes 3145732
  90.0 13.4 %copy-start.34 = (bf16[1024,512]{1,0:T(8,128)(2,1)}, bf16[1024,512]{1,0:T(8,128)(2,1)S(1)}, u32[]{:S(2)}) copy-start(bf16[1024,512]{1,0:T(8,128)(2,1)S(1)} %get-tuple-element.133.refs_20_) | copy-start | bytes 3145732
  90.0 13.4 %copy-start.15 = (bf16[1,128,1024]{2,1,0:T(8,128)(2,1)}, bf16[1,128,1024]{2,1,0:T(8,128)(2,1)S(1)}, u32[]{:S(2)}) copy-start(bf16[1,128,1024]{2,1,0:T(8,128)(2,1)S(1)} %collective-permute-done.10.refs_0_) | copy-start | bytes 786436
  94.4 4.7 collective-permute-start.11
  96.6 19.3 %collective-permute-start.14 = (bf16[1,128,1024]{2,1,0:T(8,128)(2,1)S(1)}, bf16[1,128,1024]{2,1,0:T(8,128)(2,1)S(1)}, u32[]{:S(2)}, u32[]{:S(2)}) collective-permute-start(bf16[1,128,1024]{2,1,0:T(8,128)(2,1)S(1)} %collective-permute-done.10.refs_0_), channel_id=1, source_target_pairs={{0,2},{1,3},{2,0},{3,1},{4,6},{5,7},{6,4},{7,5},{8,10},{9,11},{10,... | collective-permute-start | bytes 786440 | tf_op jit(solution)/shard_map/ppermute | solution.py:988
  97.2 18.7 %collective-permute-start.13 = (bf16[1,128,1024]{2,1,0:T(8,128)(2,1)S(1)}, bf16[1,128,1024]{2,1,0:T(8,128)(2,1)}, u32[]{:S(2)}, u32[]{:S(2)}) collective-permute-start(bf16[1,128,1024]{2,1,0:T(8,128)(2,1)S(1)} %collective-permute-done.10.refs_0_), channel_id=1, source_target_pairs={{0,4},{1,5},{2,6},{3,7},{4,0},{5,1},{6,2},{7,3},{8,12},{9,13},{10,... | collective-permute-start | bytes 786440 | tf_op jit(solution)/shard_map/ppermute | solution.py:988
  97.5 24.9 %collective-permute-start.15 = (bf16[1,256,2048]{2,1,0:T(8,128)(2,1)S(1)}, bf16[1,256,2048]{2,1,0:T(8,128)(2,1)S(1)}, u32[]{:S(2)}, u32[]{:S(2)}) collective-permute-start(bf16[1,256,2048]{2,1,0:T(8,128)(2,1)S(1)} %copy-done.51), channel_id=1, source_target_pairs={{0,1},{1,0},{2,3},{3,2},{4,5},{5,4},{6,7},{7,6},{8,9},{9,8},{10,11... | collective-permute-start | bytes 3145736 | tf_op jit(solution)/shard_map/ppermute | solution.py:988
  99.0 8.3 %collective-permute-start.12 = (bf16[3,256,512]{2,1,0:T(8,128)(2,1)S(1)}, bf16[3,256,512]{2,1,0:T(8,128)(2,1)S(1)}, u32[]{:S(2)}, u32[]{:S(2)}) collective-permute-start(bf16[3,256,512]{2,1,0:T(8,128)(2,1)S(1)} %collective-permute-done.8.refs_1_), channel_id=1, source_target_pairs={{0,2},{1,3},{2,0},{3,1},{4,6},{5,7},{6,4},{7,5},{8,10},{9,11},{10,... | collective-permute-start | bytes 2359304 | tf_op jit(solution)/shard_map/ppermute | solution.py:988
  106.0 7.7 %copy-start.41 = (bf16[1024,1024]{1,0:T(8,128)(2,1)}, bf16[1024,1024]{1,0:T(8,128)(2,1)S(1)}, u32[]{:S(2)}) copy-start(bf16[1024,1024]{1,0:T(8,128)(2,1)S(1)} %fusion.4.x_ref) | copy-start | bytes 6291460
  107.3 19.2 %copy-start.29 = (bf16[1024,512]{1,0:T(8,128)(2,1)}, bf16[1024,512]{1,0:T(8,128)(2,1)S(1)}, u32[]{:S(2)}) copy-start(bf16[1024,512]{1,0:T(8,128)(2,1)S(1)} %convolution_convert_fusion.3.q_ref.refs_1_) | copy-start | bytes 3145732
  109.3 16.1 %copy-start.1 = (bf16[3,1024,512]{2,1,0:T(8,128)(2,1)}, bf16[3,1024,512]{2,1,0:T(8,128)(2,1)S(1)}, u32[]{:S(2)}) copy-start(bf16[3,1024,512]{2,1,0:T(8,128)(2,1)S(1)} %arrange.8.refs_47_) | copy-start | bytes 9437188
  113.7 12.8 %copy-start.24 = (bf16[1024,512]{1,0:T(8,128)(2,1)S(1)}, bf16[1024,512]{1,0:T(8,128)(2,1)}, u32[]{:S(2)}) copy-start(bf16[1024,512]{1,0:T(8,128)(2,1)} %convolution_convert_fusion.8.k_ref.refs_2_) | copy-start | bytes 3145732
  113.7 12.8 %copy-start.25 = (bf16[1024,512]{1,0:T(8,128)(2,1)S(1)}, bf16[1024,512]{1,0:T(8,128)(2,1)}, u32[]{:S(2)}) copy-start(bf16[1024,512]{1,0:T(8,128)(2,1)} %convolution_convert_fusion.7.v_ref.refs_3_) | copy-start | bytes 3145732
  122.4 19.7 %copy-start.9 = (bf16[1,256,2048]{2,1,0:T(8,128)(2,1)}, bf16[1,256,2048]{2,1,0:T(8,128)(2,1)S(1)}, u32[]{:S(2)}) copy-start(bf16[1,256,2048]{2,1,0:T(8,128)(2,1)S(1)} %collective-permute-done.15.refs_0_) | copy-start | bytes 3145732
  122.4 27.3 %collective-permute-start.17 = (bf16[1,256,2048]{2,1,0:T(8,128)(2,1)S(1)}, bf16[1,256,2048]{2,1,0:T(8,128)(2,1)S(1)}, u32[]{:S(2)}, u32[]{:S(2)}) collective-permute-start(bf16[1,256,2048]{2,1,0:T(8,128)(2,1)S(1)} %collective-permute-done.15.refs_0_), channel_id=1, source_target_pairs={{0,2},{1,3},{2,0},{3,1},{4,6},{5,7},{6,4},{7,5},{8,10},{9,11},{10,... | collective-permute-start | bytes 3145736 | tf_op jit(solution)/shard_map/ppermute | solution.py:988
  122.4 27.3 %collective-permute-start.16 = (bf16[1,256,2048]{2,1,0:T(8,128)(2,1)S(1)}, bf16[1,256,2048]{2,1,0:T(8,128)(2,1)S(1)}, u32[]{:S(2)}, u32[]{:S(2)}) collective-permute-start(bf16[1,256,2048]{2,1,0:T(8,128)(2,1)S(1)} %collective-permute-done.15.refs_0_), channel_id=1, source_target_pairs={{0,4},{1,5},{2,6},{3,7},{4,0},{5,1},{6,2},{7,3},{8,12},{9,13},{10,... | collective-permute-start | bytes 3145736 | tf_op jit(solution)/shard_map/ppermute | solution.py:988
  124.1 25.6 %collective-permute-start.18 = (bf16[1,512,1024]{2,1,0:T(8,128)(2,1)}, bf16[1,512,1024]{2,1,0:T(8,128)(2,1)}, u32[]{:S(2)}, u32[]{:S(2)}) collective-permute-start(bf16[1,512,1024]{2,1,0:T(8,128)(2,1)} %dynamic-slice_bitcast_fusion), channel_id=1, source_target_pairs={{0,1},{1,0},{2,3},{3,2},{4,5},{5,4},{6,7},{7,6},{8,9},{9,8},{10,11... | collective-permute-start | bytes 3145736 | tf_op jit(solution)/shard_map/ppermute | solution.py:988
  126.5 28.6 %collective-permute-start.21 = (bf16[1,128,1024]{2,1,0:T(8,128)(2,1)}, bf16[1,128,1024]{2,1,0:T(8,128)(2,1)}, u32[]{:S(2)}, u32[]{:S(2)}) collective-permute-start(bf16[1,128,1024]{2,1,0:T(8,128)(2,1)} %collective-permute-done.13.refs_1_), channel_id=1, source_target_pairs={{0,2},{1,3},{2,0},{3,1},{4,6},{5,7},{6,4},{7,5},{8,10},{9,11},{10,... | collective-permute-start | bytes 786440 | tf_op jit(solution)/shard_map/ppermute | solution.py:988
  148.3 6.8 %copy-start.16 = (bf16[1,128,1024]{2,1,0:T(8,128)(2,1)S(1)}, bf16[1,128,1024]{2,1,0:T(8,128)(2,1)}, u32[]{:S(2)}) copy-start(bf16[1,128,1024]{2,1,0:T(8,128)(2,1)} %copy-done.15) | copy-start | bytes 786436
  148.3 8.3 %copy-start.30 = (bf16[1024,512]{1,0:T(8,128)(2,1)S(1)}, bf16[1024,512]{1,0:T(8,128)(2,1)}, u32[]{:S(2)}) copy-start(bf16[1024,512]{1,0:T(8,128)(2,1)} %fusion.7.v_ref.refs_8_) | copy-start | bytes 3145732
  148.3 8.3 %copy-start.31 = (bf16[1024,512]{1,0:T(8,128)(2,1)S(1)}, bf16[1024,512]{1,0:T(8,128)(2,1)}, u32[]{:S(2)}) copy-start(bf16[1024,512]{1,0:T(8,128)(2,1)} %fusion.6.k_ref.refs_7_) | copy-start | bytes 3145732
  148.3 8.3 %copy-start.32 = (bf16[1024,512]{1,0:T(8,128)(2,1)S(1)}, bf16[1024,512]{1,0:T(8,128)(2,1)}, u32[]{:S(2)}) copy-start(bf16[1024,512]{1,0:T(8,128)(2,1)} %convolution_convert_fusion.2.q_ref.refs_6_) | copy-start | bytes 3145732
  149.7 5.3 copy-start.11
  149.7 22.6 %collective-permute-start.20 = (bf16[1,512,1024]{2,1,0:T(8,128)(2,1)}, bf16[1,512,1024]{2,1,0:T(8,128)(2,1)S(1)}, u32[]{:S(2)}, u32[]{:S(2)}) collective-permute-start(bf16[1,512,1024]{2,1,0:T(8,128)(2,1)} %collective-permute-done.18.refs_0_), channel_id=1, source_target_pairs={{0,2},{1,3},{2,0},{3,1},{4,6},{5,7},{6,4},{7,5},{8,10},{9,11},{10,... | collective-permute-start | bytes 3145736 | tf_op jit(solution)/shard_map/ppermute | solution.py:988
  149.8 25.9 %collective-permute-start.19 = (bf16[1,512,1024]{2,1,0:T(8,128)(2,1)}, bf16[1,512,1024]{2,1,0:T(8,128)(2,1)}, u32[]{:S(2)}, u32[]{:S(2)}) collective-permute-start(bf16[1,512,1024]{2,1,0:T(8,128)(2,1)} %collective-permute-done.18.refs_0_), channel_id=1, source_target_pairs={{0,4},{1,5},{2,6},{3,7},{4,0},{5,1},{6,2},{7,3},{8,12},{9,13},{10,... | collective-permute-start | bytes 3145736 | tf_op jit(solution)/shard_map/ppermute | solution.py:988
  156.3 19.4 %copy-start.3 = (bf16[1,512,1024]{2,1,0:T(8,128)(2,1)}, bf16[1,512,1024]{2,1,0:T(8,128)(2,1)S(1)}, u32[]{:S(2)}) copy-start(bf16[1,512,1024]{2,1,0:T(8,128)(2,1)S(1)} %arrange.9) | copy-start | bytes 3145732
  156.3 19.4 %copy-start.38 = (f32[1024,1024]{1,0:T(8,128)S(1)}, f32[1024,1024]{1,0:T(8,128)}, u32[]{:S(2)}) copy-start(f32[1024,1024]{1,0:T(8,128)} %copy-done.37) | copy-start | bytes 12582916
  156.3 48.1 %collective-permute-start.22 = (bf16[1,256,2048]{2,1,0:T(8,128)(2,1)S(1)}, bf16[1,256,2048]{2,1,0:T(8,128)(2,1)}, u32[]{:S(2)}, u32[]{:S(2)}) collective-permute-start(bf16[1,256,2048]{2,1,0:T(8,128)(2,1)S(1)} %collective-permute-done.16.refs_1_), channel_id=1, source_target_pairs={{0,2},{1,3},{2,0},{3,1},{4,6},{5,7},{6,4},{7,5},{8,10},{9,11},{10,... | collective-permute-start | bytes 3145736 | tf_op jit(solution)/shard_map/ppermute | solution.py:988
  172.3 7.2 %copy-start.8 = (bf16[1024,512]{1,0:T(8,128)(2,1)}, bf16[1024,512]{1,0:T(8,128)(2,1)S(1)}, u32[]{:S(2)}) copy-start(bf16[1024,512]{1,0:T(8,128)(2,1)S(1)} %get-tuple-element.118.refs_9_) | copy-start | bytes 3145732
  172.4 7.2 %copy-start.36 = (bf16[1024,512]{1,0:T(8,128)(2,1)}, bf16[1024,512]{1,0:T(8,128)(2,1)S(1)}, u32[]{:S(2)}) copy-start(bf16[1024,512]{1,0:T(8,128)(2,1)S(1)} %get-tuple-element.131.refs_10_) | copy-start | bytes 3145732
  172.4 7.2 %copy-start.13 = (bf16[1,512,1024]{2,1,0:T(8,128)(2,1)}, bf16[1,512,1024]{2,1,0:T(8,128)(2,1)S(1)}, u32[]{:S(2)}) copy-start(bf16[1,512,1024]{2,1,0:T(8,128)(2,1)S(1)} %collective-permute-done.20.refs_2_) | copy-start | bytes 3145732
  175.7 32.5 %collective-permute-start.23 = (bf16[1,512,1024]{2,1,0:T(8,128)(2,1)}, bf16[1,512,1024]{2,1,0:T(8,128)(2,1)}, u32[]{:S(2)}, u32[]{:S(2)}) collective-permute-start(bf16[1,512,1024]{2,1,0:T(8,128)(2,1)} %collective-permute-done.19.refs_1_), channel_id=1, source_target_pairs={{0,2},{1,3},{2,0},{3,1},{4,6},{5,7},{6,4},{7,5},{8,10},{9,11},{10,... | collective-permute-start | bytes 3145736 | tf_op jit(solution)/shard_map/ppermute | solution.py:988
  188.0 16.5 %copy-start.10 = (bf16[1,256,2048]{2,1,0:T(8,128)(2,1)S(1)}, bf16[1,256,2048]{2,1,0:T(8,128)(2,1)}, u32[]{:S(2)}) copy-start(bf16[1,256,2048]{2,1,0:T(8,128)(2,1)} %copy-done.9) | copy-start | bytes 3145732
  188.0 16.5 %copy-start.12 = (bf16[1,256,2048]{2,1,0:T(8,128)(2,1)S(1)}, bf16[1,256,2048]{2,1,0:T(8,128)(2,1)}, u32[]{:S(2)}) copy-start(bf16[1,256,2048]{2,1,0:T(8,128)(2,1)} %copy-done.11) | copy-start | bytes 3145732
  212.5 16.5 %copy-start.40 = (f32[1024,1024]{1,0:T(8,128)S(1)}, f32[1024,1024]{1,0:T(8,128)}, u32[]{:S(2)}) copy-start(f32[1024,1024]{1,0:T(8,128)} %copy-done.39) | copy-start | bytes 12582916
  212.5 16.5 %copy-start.45 = (f32[1024,1024]{1,0:T(8,128)S(1)}, f32[1024,1024]{1,0:T(8,128)}, u32[]{:S(2)}) copy-start(f32[1024,1024]{1,0:T(8,128)} %get-tuple-element.121) | copy-start | bytes 12582916
  550.9 11.2 %copy-start.57 = (f32[8,1024]{1,0:T(8,128)S(1)}, f32[8,1024]{1,0:T(8,128)}, u32[]{:S(2)}) copy-start(f32[8,1024]{1,0:T(8,128)} %get-tuple-element.151) | copy-start | bytes 98308
  550.9 11.9 %copy-start.50 = (bf16[1024,1024]{1,0:T(8,128)(2,1)S(1)}, bf16[1024,1024]{1,0:T(8,128)(2,1)}, u32[]{:S(2)}) copy-start(bf16[1024,1024]{1,0:T(8,128)(2,1)} %get-tuple-element.187) | copy-start | bytes 6291460
  (21 other events, 50.4 us)
